TPU v7x, 32 devices: a whole 2x2x4 slice. The times are simulated.
32 devices in a mesh: scen: 4 (over y, core), fac: 8 (over z, x).
Axes of the slice: x: 2, y: 2, z: 4, core: 2. Of those that a mesh axis runs over, the one named last changes fastest.
Arguments:
- shocks: bfloat16 [2, 1024, 256], P(None, 'scen'), may hold values from -6 to 6
- loadings: bfloat16 [256, 2048], P(None, 'fac'), may hold values from -0.375 to 0.375
- vol: float32 [2048], P('fac'), may hold values from 0.1 to 0.5
- jump_counts: int32 [2, 1024, 2048], P(None, 'scen', 'fac'), may hold values from 0 to 3
- jump_noise: bfloat16 [2, 1024, 2048], P(None, 'scen', 'fac'), may hold values from -6 to 6
- jump_mean: float32 [2048], P('fac'), may hold values from -0.15 to 0.1
- jump_vol: float32 [2048], P('fac'), may hold values from 0.05 to 0.3
- dependencies: int32 [2048, 2], P('fac'), may hold values from 0 to 15, as said below
- block_slot: int32 [16], replicated, may hold values from 0 to 15, each once
- trade_weights: bfloat16 [2048, 2, 128], P('fac'), may hold values from -0.375 to 0.375
- netting: int32 [2048], P('fac'), may hold values from 0 to 511
Outputs:
- exposure: float32 [2, 512, 1024], P(None, 'fac', 'scen')
- expected: float32 [2, 512], P(None, 'fac')
Inputs may be any that keep to these rules, and one draw needn't show every extreme that they name: `dependencies`: each trade names 2 different blocks.
All inputs are finite; a program needn't handle non-finite values.
Results may differ from a plain program's by a relative error of at most 0.0056.
Values may be sent and summed in bfloat16 or wider, within the bound.
No kernel may reach another device: no remote copies, remote signals or barrier semaphores. Data moves between devices by JAX's collectives and lax.ppermute only.
A program may use at most 192 MiB of HBM per device.

v0:
```python
import jax
import jax.numpy as jnp
from jax import lax
from jax.sharding import PartitionSpec as P

BLOCK = 128
SET_DEV = 64
DATES = 2


def body(
    shocks,
    loadings,
    vol,
    jump_counts,
    jump_noise,
    jump_mean,
    jump_vol,
    dependencies,
    block_slot,
    trade_weights,
    netting,
):
    fac_count = lax.axis_size("fac")
    scen_count = lax.axis_size("scen")
    rows = shocks.shape[1]
    fac_width = loadings.shape[1]
    factors = fac_width * fac_count
    nblocks = factors // BLOCK
    trade_count = trade_weights.shape[0]
    set_total = SET_DEV * fac_count
    slots = block_slot[dependencies]
    marks = (slots[:, :, None] == jnp.arange(nblocks, dtype=jnp.int32)[None, None, :]).astype(
        jnp.bfloat16
    )
    dense = jnp.einsum("tkb,tkj->bjt", marks, trade_weights, preferred_element_type=jnp.float32)
    dense = dense.astype(jnp.bfloat16).reshape(factors, trade_count)
    level = jnp.zeros((rows, fac_width), jnp.float32)
    exposures = []
    totals = []
    for date in range(DATES):
        diffuse = jnp.dot(shocks[date], loadings, preferred_element_type=jnp.float32)
        counts = jump_counts[date].astype(jnp.float32)
        level = (
            level
            + vol * diffuse
            - 0.5 * vol * vol
            + counts * jump_mean
            + jnp.sqrt(counts) * jump_vol * jump_noise[date].astype(jnp.float32)
        )
        prices = (jnp.exp(level) - 1.0).astype(jnp.bfloat16)
        values = jnp.dot(
            lax.all_gather(prices, "fac", axis=1, tiled=True),
            dense,
            preferred_element_type=jnp.float32,
        )
        partial_value = jax.ops.segment_sum(values.T, netting, num_segments=set_total)
        nets = lax.psum_scatter(partial_value, "fac", scatter_dimension=0, tiled=True)
        exposure = jnp.maximum(nets, 0.0)
        exposures.append(exposure)
        totals.append(jnp.sum(exposure, axis=1))
    summed = lax.psum(jnp.stack(totals), "scen")
    return (jnp.stack(exposures), summed / (rows * scen_count))


def solution(mesh):
    placed = (
        P(None, "scen", None),
        P(None, "fac"),
        P("fac"),
        P(None, "scen", "fac"),
        P(None, "scen", "fac"),
        P("fac"),
        P("fac"),
        P("fac", None),
        P(),
        P("fac", None, None),
        P("fac"),
    )
    return jax.shard_map(
        body,
        mesh=mesh,
        in_specs=placed,
        out_specs=(P(None, "fac", "scen"), P(None, "fac")),
        check_vma=False,
    )
```

profile of v0, /device:TPU:0, one launch (start us, length us, event | category | flops | bytes accessed | tf_op | source)
XLA Modules:
  0.0 238.6 jit_solution(10150128285150206504)
XLA Ops:
  7.2 0.0 copy-start
  7.2 0.0 copy-start.6
  7.2 0.0 copy-start.4
  7.2 0.0 copy-start.7
  7.3 0.0 all-gather.5.cloned.1.call-start
  7.3 0.8 multiply_multiply_fusion
  8.1 2.1 add_convert_fusion
  10.2 1.8 fusion.9
  12.0 0.0 all-gather.5.cloned.1.call-update
  12.1 0.0 all-gather.3.cloned.1.call-start
  12.1 0.7 all-gather.3.cloned.1.call-update
  12.8 0.0 reduce-scatter.5.cloned.1.call-start
  12.9 0.7 fusion.29
  13.6 9.9 %compare_select_fusion.1 = s32[256,2]{0,1:T(2,128)S(1)} fusion(s32[256,2]{0,1:T(2,128)S(1)} %copy-done.2, s32[]{:T(128)} %bitcast, s32[]{:T(128)} %bitcast.1, s32[]{:T(128)} %bitcast.2, s32[]{:T(128)} %bitcast.3, s32[]{:T(128)} %bitcast.4, s32[]{:T(128)} %bitcast.5, s32[]{:T(128)} %bitcast.6, s32[]{:T(128)} %bitcast.7, s32[]{:T(128)} %bitcast.8, s32[]{:T(128)} %bitcast.9, ...), kind=kLoop, calls=%fused_computation.47 | loop fusion | flops 16896 | bytes 4160 | tf_op jit(solution)/shard_map/gather | solution.py:32
  23.5 0.1 copy.13
  23.7 1.1 convolution_convert_fusion
  24.7 29.7 %all-gather.5.cloned.1.call-done = bf16[256,2048]{1,0:T(8,128)(2,1)} async-done(((bf16[256,256]{1,0:T(8,128)(2,1)}), bf16[256,2048]{1,0:T(8,128)(2,1)}) %all-gather.5.cloned.1.call-update) | async-done | bytes 1048592 | tf_op jit(solution)/shard_map/all_gather | solution.py:53
  54.4 1.7 fusion.10
  56.1 2.9 %scatter_custom_fusion.1 = f32[512,256]{1,0:T(8,128)} fusion(s32[256]{0:T(256)} %param.21, f32[256,256]{1,0:T(8,128)S(1)} %fusion.10, f32[]{:T(128)} %constant.6.clone.1), kind=kCustom, calls=%fused_computation.32 | custom fusion | flops 65536 | bytes 524800 | tf_op jit(solution)/shard_map/scatter-add | solution.py:57
  59.0 0.0 reduce-scatter.5.cloned.1.call-update
  59.0 0.0 reduce-scatter.3.cloned.1.call-start
  59.1 36.4 %all-gather.3.cloned.1.call-done = bf16[256,2048]{1,0:T(8,128)(2,1)} async-done(((bf16[256,256]{1,0:T(8,128)(2,1)}), bf16[256,2048]{1,0:T(8,128)(2,1)}) %all-gather.3.cloned.1.call-update) | async-done | bytes 1048592 | tf_op jit(solution)/shard_map/all_gather | solution.py:53
  95.5 1.7 fusion.12
  97.2 2.9 %scatter_custom_fusion = f32[512,256]{1,0:T(8,128)} fusion(s32[256]{0:T(256)} %param.21, f32[256,256]{1,0:T(8,128)S(1)} %fusion.12, f32[]{:T(128)} %constant.6.clone.1), kind=kCustom, calls=%fused_computation.34 | custom fusion | flops 65536 | bytes 524800 | tf_op jit(solution)/shard_map/scatter-add | solution.py:57
  100.1 0.0 reduce-scatter.3.cloned.1.call-update
  100.1 59.6 %reduce-scatter.5.cloned.1.call-done = f32[64,256]{1,0:T(8,128)} async-done(((f32[512,256]{1,0:T(8,128)}), f32[64,256]{1,0:T(8,128)}) %reduce-scatter.5.cloned.1.call-update) | async-done | bytes 65552 | tf_op jit(solution)/shard_map/reduce_scatter | solution.py:58
  159.7 0.9 maximum_reduce_fusion
  160.6 63.6 %reduce-scatter.3.cloned.1.call-done = f32[64,256]{1,0:T(8,128)} async-done(((f32[512,256]{1,0:T(8,128)}), f32[64,256]{1,0:T(8,128)}) %reduce-scatter.3.cloned.1.call-update) | async-done | bytes 65552 | tf_op jit(solution)/shard_map/reduce_scatter | solution.py:58
  224.2 0.9 maximum_reduce_fusion.1
  225.2 5.7 %psum.7 = f32[2,64]{1,0:T(2,128)S(1)} all-reduce(f32[2,64]{1,0:T(2,128)S(1)} %pad_maximum_fusion.1), channel_id=1, replica_groups=mesh['scen'=4,'fac'=8] {'scen'}, use_global_device_ids=true, to_apply=%region_6.0 | all-reduce | flops 128 | bytes 1024 | tf_op jit(solution)/shard_map/psum | solution.py:62
  230.9 0.6 broadcast_multiply_fusion
  231.4 0.7 pad_maximum_fusion
  (15 shorter events, 0.0 us)
Async XLA Ops:
  7.2 16.5 %copy-start = (bf16[256,2,128]{2,1,0:T(2,128)(2,1)S(1)}, bf16[256,2,128]{2,1,0:T(2,128)(2,1)}, u32[]{:S(2)}) copy-start(bf16[256,2,128]{2,1,0:T(2,128)(2,1)} %param.20) | copy-start | bytes 393220
  7.2 3.0 %copy-start.3 = (f32[256]{0:T(256)S(1)}, f32[256]{0:T(256)}, u32[]{:S(2)}) copy-start(f32[256]{0:T(256)} %param.13) | copy-start | bytes 3076
  7.2 3.0 %copy-start.6 = (bf16[2,256,256]{2,1,0:T(8,128)(2,1)S(1)}, bf16[2,256,256]{2,1,0:T(8,128)(2,1)}, u32[]{:S(2)}) copy-start(bf16[2,256,256]{2,1,0:T(8,128)(2,1)} %param.11) | copy-start | bytes 786436
  7.2 3.0 %copy-start.4 = (s32[2,256,256]{2,1,0:T(8,128)S(1)}, s32[2,256,256]{2,1,0:T(8,128)}, u32[]{:S(2)}) copy-start(s32[2,256,256]{2,1,0:T(8,128)} %param.14) | copy-start | bytes 1572868
  7.2 2.9 %copy-start.5 = (bf16[2,256,256]{2,1,0:T(8,128)(2,1)S(1)}, bf16[2,256,256]{2,1,0:T(8,128)(2,1)}, u32[]{:S(2)}) copy-start(bf16[2,256,256]{2,1,0:T(8,128)(2,1)} %param.15) | copy-start | bytes 786436
  7.2 2.9 %copy-start.8 = (f32[256]{0:T(256)S(1)}, f32[256]{0:T(256)}, u32[]{:S(2)}) copy-start(f32[256]{0:T(256)} %param.16) | copy-start | bytes 3076
  7.2 2.9 %copy-start.7 = (f32[256]{0:T(256)S(1)}, f32[256]{0:T(256)}, u32[]{:S(2)}) copy-start(f32[256]{0:T(256)} %param.17) | copy-start | bytes 3076
  7.3 47.2 %all-gather.5.cloned.1.call-start = ((), (), s32[]{:S(2)}) async-start(), calls=%async_computation.4 | async-start | bytes 1179648 | tf_op jit(solution)/shard_map/all_gather | solution.py:53
  8.1 4.8 %copy-start.1 = (s32[16]{0:T(128)S(1)}, s32[16]{0:T(128)}, u32[]{:S(2)}) copy-start(s32[16]{0:T(128)} %param.19) | copy-start | bytes 196
  8.1 5.5 %copy-start.2 = (s32[256,2]{0,1:T(2,128)S(1)}, s32[256,2]{0,1:T(2,128)}, u32[]{:S(2)}) copy-start(s32[256,2]{0,1:T(2,128)} %param.18) | copy-start | bytes 6148
  12.1 83.5 %all-gather.3.cloned.1.call-start = ((), (), s32[]{:S(2)}) async-start(), calls=%async_computation.2 | async-start | bytes 1179648 | tf_op jit(solution)/shard_map/all_gather | solution.py:53
  12.8 146.9 %reduce-scatter.5.cloned.1.call-start = ((), (), s32[]{:S(2)}) async-start(), calls=%async_computation.5 | async-start | bytes 589824 | tf_op jit(solution)/shard_map/reduce_scatter | solution.py:58
  59.0 165.2 %reduce-scatter.3.cloned.1.call-start = ((), (), s32[]{:S(2)}) async-start(), calls=%async_computation.3 | async-start | bytes 589824 | tf_op jit(solution)/shard_map/reduce_scatter | solution.py:58
Sparse Core Ops, SparseCore 0:
  12.2 42.2 all-gather.4
  57.1 38.4 all-gather.2
  98.9 60.7 reduce-scatter.4
  163.3 60.9 reduce-scatter.2
where the time goes:
time: 239 us
  waiting for transfers between devices  190 us (79%)
  other arithmetic  19.6 us (8%)
  between operations  13.9 us (6%)
  matrix products  8.37 us (4%)
  blocking collectives  5.67 us (2%)
    reduce_scatter x2, waiting for transfers between devices, body(): lax.psum_scatter(partial_value, 'fac', scatter_dimension=0, tiled=True)  123 us
    all_gather x2, waiting for transfers between devices, body(): lax.all_gather(prices, 'fac', axis=1, tiled=True)  66.1 us
    gather x1, other arithmetic, body(): slots = block_slot[dependencies]  9.92 us
    scatter-add x2, other arithmetic, body(): jax.ops.segment_sum(values.T, netting, num_segments=set_total)  5.73 us
    psum x1, blocking collectives, body(): summed = lax.psum(jnp.stack(totals), 'scen')  5.67 us
  transfers between devices with their start and end apart: 4, of which 4 were waited for; matrix products, arithmetic and copies ran while one was open for 9% of the time, Pallas kernels for 0%

commit v1 on v0

v1 whole, which is shorter than its diff:
```python
import functools

import jax
import jax.numpy as jnp
from jax import lax
from jax.experimental import pallas as pl
from jax.experimental.pallas import tpu as pltpu
from jax.sharding import PartitionSpec as P

BLOCK = 128
SET_DEV = 64
DATES = 2
SIDE_FLIP = 1
PRICE_FLIP = 2
TAGS = 16
CHUNK = 64

VMEM = pl.BlockSpec(memory_space=pltpu.VMEM)
HBM = pl.BlockSpec(memory_space=pltpu.HBM)
SMEM = pl.BlockSpec(memory_space=pltpu.SMEM)
PARAMS = pltpu.CompilerParams(vmem_limit_bytes=16 * 1024 * 1024)
FETCH_PARAMS = pltpu.CompilerParams(vmem_limit_bytes=60 * 1024 * 1024)
NT = (((1,), (1,)), ((), ()))


def f32_dot(a, b, dims):
    return lax.dot_general(a, b, dims, preferred_element_type=jnp.float32)


def fetch(pairs, sems):
    copies = [pltpu.make_async_copy(src, dst, sems.at[i]) for i, (src, dst) in enumerate(pairs)]
    for copy in copies:
        copy.start()
    for copy in copies:
        copy.wait()


def pack_kernel(part, weights_hbm, deps_hbm, netting_hbm, packet_ref, weights_ref, deps_ref, netting_ref, sems):
    fetch([(weights_hbm, weights_ref), (deps_hbm, deps_ref), (netting_hbm, netting_ref)], sems)
    scen = lax.axis_index("scen")
    row = lax.broadcasted_iota(jnp.int32, (part, BLOCK), 0)
    column = lax.broadcasted_iota(jnp.int32, (part, BLOCK), 1)
    pick = (column == scen * part + row).astype(jnp.float32).astype(jnp.bfloat16)
    for k in range(2):
        share = f32_dot(pick, weights_ref[:, k, :], NT)
        packet_ref[k * part : (k + 1) * part, :] = share.astype(jnp.bfloat16)
    netting = netting_ref[...]
    tags = jnp.concatenate(
        [
            deps_ref[...],
            netting // SET_DEV,
            netting % SET_DEV,
            jnp.zeros((TAGS - 4, netting.shape[1]), jnp.int32),
        ],
        axis=0,
    )
    packet_ref[2 * part :, :] = tags.astype(jnp.float32).astype(jnp.bfloat16)


def price_kernel(*refs):
    count = 7
    out_ref, sems = refs[count], refs[-1]
    refs_in = refs[count + 1 : -1]
    fetch(list(zip(refs[:count], refs_in)), sems)
    shocks_ref, loadings_ref, vol_ref, counts_ref, noise_ref, mean_ref, dev_ref = refs_in
    rows = shocks_ref.shape[1]
    vol = vol_ref[...]
    drift = 0.5 * vol * vol
    mean = mean_ref[...]
    dev = dev_ref[...]
    loadings = loadings_ref[...]

    def step(i, carry):
        at = pl.ds(pl.multiple_of(i * CHUNK, CHUNK), CHUNK)
        level = jnp.zeros((CHUNK, vol.shape[1]), jnp.float32)
        for date in range(DATES):
            diffuse = jnp.dot(shocks_ref[date, at, :], loadings, preferred_element_type=jnp.float32)
            counts = counts_ref[date, at, :].astype(jnp.float32)
            noise = noise_ref[date, at, :].astype(jnp.float32)
            level = level + vol * diffuse - drift + counts * mean + jnp.sqrt(counts) * dev * noise
            out_ref[date, at, :] = (jnp.exp(level) - 1.0).astype(jnp.bfloat16)
        return carry

    lax.fori_loop(0, rows // CHUNK, step, 0)


def combine_kernel(part, held, flips, *refs):
    slot_ref, packet_refs = refs[0], refs[1:-4]
    own_ref, other_ref, chosen_ref, marks_ref = refs[-4:]
    fac = lax.axis_index("fac")
    names = []
    for flip in (0, PRICE_FLIP, SIDE_FLIP, SIDE_FLIP ^ PRICE_FLIP):
        for h in range(held):
            slot = (fac ^ flip) * held + h

            def find(b, name):
                return jnp.where(slot_ref[b] == slot, b, name)

            names.append(lax.fori_loop(0, slot_ref.shape[0], find, 0, unroll=True).astype(jnp.float32))
    trades = packet_refs[0].shape[1]
    place = lax.broadcasted_iota(jnp.int32, (SET_DEV, trades), 0).astype(jnp.float32)
    for source, packet_ref in enumerate(packet_refs):
        at = slice(source * trades, (source + 1) * trades)
        tags = packet_ref[2 * part :, :].astype(jnp.float32)
        weights = [packet_ref[k * part : (k + 1) * part, :].astype(jnp.float32) for k in range(2)]
        for b, name in enumerate(names):
            picked = jnp.where(tags[0:1] == name, weights[0], 0.0)
            picked = jnp.where(tags[1:2] == name, weights[1], picked)
            chosen_ref[b * part : (b + 1) * part, at] = picked.astype(jnp.bfloat16)
        for i, flip in enumerate(flips):
            owner = (fac ^ flip).astype(jnp.float32)
            local = jnp.where(tags[2:3] == owner, tags[3:4], -1.0)
            mark = jnp.where(local == place, 1.0, 0.0)
            marks_ref[i * SET_DEV : (i + 1) * SET_DEV, at] = mark.astype(jnp.bfloat16)
    sums = f32_dot(chosen_ref[...], marks_ref[...], NT)
    half = own_ref.shape[0]
    own_ref[...] = sums[:half]
    other_ref[...] = sums[half:].astype(jnp.bfloat16)


def merge_kernel(own_ref, other_ref, share_ref):
    pair = 2 * SET_DEV
    for at in range(0, own_ref.shape[1], pair):
        other = pltpu.roll(other_ref[:, at : at + pair].astype(jnp.float32), SET_DEV, 1)
        share_ref[:, at : at + pair] = (own_ref[:, at : at + pair] + other).astype(jnp.bfloat16)


def value_kernel(part, held, scen_count, *refs):
    share_refs, price_refs = refs[:scen_count], refs[scen_count : scen_count + 2]
    out_refs, whole_ref = refs[scen_count + 2 : -1], refs[-1]
    scen = lax.axis_index("scen")
    for i, share_ref in enumerate(share_refs):
        column = (scen ^ i) * part
        for b in range(2 * held):
            at = pl.ds(pl.multiple_of(b * BLOCK + column, part), part)
            whole_ref[at, :] = share_ref[b * part : (b + 1) * part, :].astype(jnp.float32)
    width = held * BLOCK
    total = None
    for i, price_ref in enumerate(price_refs):
        whole = whole_ref[i * width : (i + 1) * width, :].T.astype(jnp.bfloat16)
        term = f32_dot(whole, price_ref[...], NT)
        total = term if total is None else total + term
    for p, out_ref in enumerate(out_refs):
        out_ref[...] = total[p * SET_DEV : (p + 1) * SET_DEV].astype(out_ref.dtype)


def expose_kernel(rows, *refs):
    part_refs, exposure_ref, totals_ref = refs[:-2], refs[-2], refs[-1]
    for date in range(DATES):
        at = slice(date * rows, (date + 1) * rows)
        nets = part_refs[0][:, at]
        for ref in part_refs[1:]:
            nets = nets + ref[:, at].astype(jnp.float32)
        exposure = jnp.maximum(nets, 0.0)
        exposure_ref[date] = exposure
        totals_ref[date] = jnp.sum(exposure, axis=1)


def from_partner(x, axis, flip):
    count = lax.axis_size(axis)
    return lax.ppermute(x, axis, [(i, i ^ flip) for i in range(count)])


def body(
    shocks,
    loadings,
    vol,
    jump_counts,
    jump_noise,
    jump_mean,
    jump_vol,
    dependencies,
    block_slot,
    trade_weights,
    netting,
):
    fac_count = lax.axis_size("fac")
    scen_count = lax.axis_size("scen")
    rows = shocks.shape[1]
    width = loadings.shape[1]
    held = width // BLOCK
    trades = trade_weights.shape[0]
    part = BLOCK // scen_count
    column_flips = [i for i in range(fac_count) if not i & SIDE_FLIP]
    owner_flips = [i for i in range(fac_count) if not i & PRICE_FLIP]

    inputs = (trade_weights, dependencies.T, netting[None])
    packet = pl.pallas_call(
        functools.partial(pack_kernel, part),
        out_shape=jax.ShapeDtypeStruct((2 * part + TAGS, trades), jnp.bfloat16),
        in_specs=[HBM] * len(inputs),
        out_specs=VMEM,
        scratch_shapes=[pltpu.VMEM(x.shape, x.dtype) for x in inputs]
        + [pltpu.SemaphoreType.DMA((len(inputs),))],
        compiler_params=FETCH_PARAMS,
        name="pack",
    )(*inputs)
    packets = [packet] + [from_partner(packet, "fac", i) for i in column_flips[1:]]

    packet, shocks = lax.optimization_barrier((packet, shocks))
    inputs = (shocks, loadings, vol[None], jump_counts, jump_noise, jump_mean[None], jump_vol[None])
    prices = pl.pallas_call(
        price_kernel,
        out_shape=jax.ShapeDtypeStruct((DATES, rows, width), jnp.bfloat16),
        in_specs=[HBM] * len(inputs),
        out_specs=VMEM,
        scratch_shapes=[pltpu.VMEM(x.shape, x.dtype) for x in inputs]
        + [pltpu.SemaphoreType.DMA((len(inputs),))],
        compiler_params=FETCH_PARAMS,
        name="price",
    )(*inputs)
    prices = prices.reshape(DATES * rows, width)
    share_shape = (2 * held * part, len(owner_flips) * SET_DEV)
    column_trades = len(column_flips) * trades
    own, other = pl.pallas_call(
        functools.partial(combine_kernel, part, held, owner_flips),
        out_shape=[
            jax.ShapeDtypeStruct(share_shape, jnp.float32),
            jax.ShapeDtypeStruct(share_shape, jnp.bfloat16),
        ],
        in_specs=[SMEM] + [VMEM] * len(packets),
        out_specs=[VMEM] * 2,
        scratch_shapes=[
            pltpu.VMEM((2 * share_shape[0], column_trades), jnp.bfloat16),
            pltpu.VMEM((share_shape[1], column_trades), jnp.bfloat16),
        ],
        compiler_params=PARAMS,
        name="combine",
    )(block_slot, *packets)
    prices, other = lax.optimization_barrier((prices, other))
    pair_prices = [prices, from_partner(prices, "fac", PRICE_FLIP)]
    share = pl.pallas_call(
        merge_kernel,
        out_shape=jax.ShapeDtypeStruct(share_shape, jnp.bfloat16),
        in_specs=[VMEM] * 2,
        out_specs=VMEM,
        compiler_params=PARAMS,
        name="merge",
    )(own, from_partner(other, "fac", SIDE_FLIP))
    shares = [share] + [from_partner(share, "scen", i) for i in range(1, scen_count)]

    parts = pl.pallas_call(
        functools.partial(value_kernel, part, held, scen_count),
        out_shape=[
            jax.ShapeDtypeStruct((SET_DEV, DATES * rows), jnp.bfloat16 if flip else jnp.float32)
            for flip in owner_flips
        ],
        in_specs=[VMEM] * (scen_count + 2),
        out_specs=[VMEM] * len(owner_flips),
        scratch_shapes=[pltpu.VMEM((2 * width, share_shape[1]), jnp.float32)],
        compiler_params=PARAMS,
        name="value",
    )(*shares, *pair_prices)
    parts = [parts[0]] + [from_partner(x, "fac", i) for x, i in zip(parts[1:], owner_flips[1:])]

    exposure, totals = pl.pallas_call(
        functools.partial(expose_kernel, rows),
        out_shape=[
            jax.ShapeDtypeStruct((DATES, SET_DEV, rows), jnp.float32),
            jax.ShapeDtypeStruct((DATES, SET_DEV), jnp.float32),
        ],
        in_specs=[VMEM] * len(parts),
        out_specs=[VMEM] * 2,
        compiler_params=PARAMS,
        name="expose",
    )(*parts)
    sums = [totals] + [from_partner(totals, "scen", i) for i in range(1, scen_count)]
    while len(sums) > 1:
        sums = [sums[i] + sums[i + 1] for i in range(0, len(sums), 2)]
    return (exposure, sums[0] / (rows * scen_count))


def solution(mesh):
    placed = (
        P(None, "scen", None),
        P(None, "fac"),
        P("fac"),
        P(None, "scen", "fac"),
        P(None, "scen", "fac"),
        P("fac"),
        P("fac"),
        P("fac", None),
        P(),
        P("fac", None, None),
        P("fac"),
    )
    return jax.shard_map(
        body,
        mesh=mesh,
        in_specs=placed,
        out_specs=(P(None, "fac", "scen"), P(None, "fac")),
        check_vma=False,
    )
```

time: 239 us -> 39.9 us (0.17)
  waiting for transfers between devices: 190 us -> 15.8 us
  other arithmetic: 19.6 us -> 0.57 us
  starting transfers between devices: 0.16 us -> 15.7 us
  between operations: 13.9 us -> 0.71 us
  matrix products: 8.37 us -> 0 us
  Pallas kernels: 0 us -> 6.89 us
  blocking collectives: 5.67 us -> 0 us
    reduce_scatter x2 -> x0, waiting for transfers between devices: 123 us -> none  [body(): lax.psum_scatter(partial_value, 'fac', scatter_dimension=0, tiled=True)]
    all_gather x2 -> x0, waiting for transfers between devices: 66.1 us -> none  [body(): lax.all_gather(prices, 'fac', axis=1, tiled=True)]
    ppermute x0 -> x14, waiting for transfers between devices: none -> 15.8 us  [from_partner(): return lax.ppermute(x, axis, [(i, i ^ flip) for i in range(count)])]
    ppermute x0 -> x14, starting transfers between devices: none -> 15.7 us  [from_partner(): return lax.ppermute(x, axis, [(i, i ^ flip) for i in range(count)])]
    gather x1 -> x0, other arithmetic: 9.92 us -> none  [body(): slots = block_slot[dependencies]]
    dot_general x5 -> x0, matrix products: 8.37 us -> none  [the longest x2 3.91 us: body(): jnp.dot(shocks[date], loadings, preferred_element_type=jnp.float32)]
    pallas_call x0 -> x6, Pallas kernels: none -> 6.89 us  [the longest x1 2.85 us: body(): pl.pallas_call(price_kernel, out_shape=jax.ShapeDtypeStruct((DATES, rows,...]
    scatter-add x2 -> x0, other arithmetic: 5.73 us -> none  [body(): jax.ops.segment_sum(values.T, netting, num_segments=set_total)]
  transfers between devices with their start and end apart: 4 -> 14, of which waited for: 4 -> 8; matrix products, arithmetic and copies ran while one was open for 9% -> 0% of each run, Pallas kernels for 0% -> 7%
where the time goes in v1:
time: 39.9 us; the launch traced here: 39.7 us
  waiting for transfers between devices  15.8 us (40%)
  starting transfers between devices  15.7 us (39%)
  Pallas kernels  6.89 us (17%)
  between operations  0.71 us (2%)
  other arithmetic  0.57 us (1%)
    ppermute x14, waiting for transfers between devices, from_partner(): return lax.ppermute(x, axis, [(i, i ^ flip) for i in range(count)])  15.8 us
    ppermute x14, starting transfers between devices, from_partner(): return lax.ppermute(x, axis, [(i, i ^ flip) for i in range(count)])  15.7 us
    pallas_call x1, Pallas kernels, body(): pl.pallas_call(price_kernel, out_shape=jax.ShapeDtypeStruct((DATES, rows,...  2.85 us
    pallas_call x1, Pallas kernels, body(): pl.pallas_call(functools.partial(pack_kernel, part), out_shape=jax.ShapeD...  1.97 us
    pallas_call x1, Pallas kernels, body(): pl.pallas_call(functools.partial(combine_kernel, part, held, owner_flips)...  0.9 us
  transfers between devices with their start and end apart: 14, of which 8 were waited for; matrix products, arithmetic and copies ran while one was open for 0% of the time, Pallas kernels for 7%

profile of v1, /device:TPU:0, one launch (start us, length us, event | category | flops | bytes accessed | tf_op | source)
XLA Modules:
  0.0 39.7 jit_solution(12815564212142812948)
XLA Ops:
  0.6 2.0 %pack.1.refs_1_ = bf16[80,256]{1,0:T(8,128)(2,1)} custom-call(bf16[256,2,128]{2,1,0:T(2,128)(2,1)} %weights_hbm.1, s32[2,256]{1,0:T(2,128)} %bitcast.8, s32[1,256]{1,0:T(1,128)} %bitcast.9), custom_call_target="tpu_custom_call" | custom-call | tf_op jit(solution)/shard_map/pack/pallas_call | solution.py:188
  2.6 5.1 %collective-permute-start.2 = (bf16[80,256]{1,0:T(8,128)(2,1)}, bf16[80,256]{1,0:T(8,128)(2,1)S(1)}, u32[]{:S(2)}, u32[]{:S(2)}) collective-permute-start(bf16[80,256]{1,0:T(8,128)(2,1)} %pack.1.refs_1_), channel_id=1, source_target_pairs={{0,6},{1,7},{2,4},{3,5},{4,2},{5,3},{6,0},{7,1},{8,14},{9,15},{10,... | collective-permute-start | bytes 122888 | tf_op jit(solution)/shard_map/ppermute | solution.py:161
  7.7 0.0 collective-permute-start.1
  7.7 0.6 %collective-permute-start = (bf16[80,256]{1,0:T(8,128)(2,1)}, bf16[80,256]{1,0:T(8,128)(2,1)S(1)}, u32[]{:S(2)}, u32[]{:S(2)}) collective-permute-start(bf16[80,256]{1,0:T(8,128)(2,1)} %pack.1.refs_1_), channel_id=1, source_target_pairs={{0,2},{1,3},{2,0},{3,1},{4,6},{5,7},{6,4},{7,5},{8,10},{9,11},{10,... | collective-permute-start | bytes 122888 | tf_op jit(solution)/shard_map/ppermute | solution.py:161
  8.4 2.8 %price.1 = bf16[2,256,256]{2,1,0:T(8,128)(2,1)} custom-call(bf16[2,256,256]{2,1,0:T(8,128)(2,1)} %refs_0_.2, bf16[256,256]{1,0:T(8,128)(2,1)} %refs_1_.1, f32[1,256]{1,0:T(1,128)} %bitcast.10, s32[2,256,256]{2,1,0:T(8,128)} %refs_3_.1, bf16[2,256,256]{2,1,0:T(8,128)(2,1)} %refs_4_.1, f32[1,256]{1,0:T(1,128)} %bitcast.11, f32[1,256]{1,0:T(1,128)} %bitcast.12), custom_call_target="tpu_custom_call" | custom-call | tf_op jit(solution)/shard_map/price/pallas_call | solution.py:202
  11.2 0.0 collective-permute-done.2.refs_4_
  11.2 1.6 %collective-permute-done.1.refs_3_ = bf16[80,256]{1,0:T(8,128)(2,1)S(1)} collective-permute-done((bf16[80,256]{1,0:T(8,128)(2,1)}, bf16[80,256]{1,0:T(8,128)(2,1)S(1)}, u32[]{:S(2)}, u32[]{:S(2)}) %collective-permute-start.1) | collective-permute-done | bytes 40992 | tf_op jit(solution)/shard_map/ppermute | solution.py:161
  12.8 0.0 collective-permute-done.refs_2_
  12.8 0.9 %combine.1 = (f32[128,256]{1,0:T(8,128)S(1)}, bf16[128,256]{1,0:T(8,128)(2,1)S(1)}) custom-call(s32[16]{0:T(128)S(1)} %copy-done.2, bf16[80,256]{1,0:T(8,128)(2,1)S(1)} %copy-done.1, bf16[80,256]{1,0:T(8,128)(2,1)S(1)} %collective-permute-done.refs_2_, bf16[80,256]{1,0:T(8,128)(2,1)S(1)} %collective-permute-done.1.refs_3_, ...), custom_call_target="tpu_custom_call" | custom-call | tf_op jit(solution)/shard_map/combine/pallas_call | solution.py:215
  13.8 0.2 collective-permute-start.7
  14.0 1.5 %collective-permute-start.3 = (bf16[128,256]{1,0:T(8,128)(2,1)S(1)}, bf16[128,256]{1,0:T(8,128)(2,1)S(1)}, u32[]{:S(2)}, u32[]{:S(2)}) collective-permute-start(bf16[128,256]{1,0:T(8,128)(2,1)S(1)} %get-tuple-element.16), channel_id=1, source_target_pairs={{0,1},{1,0},{2,3},{3,2},{4,5},{5,4},{6,7},{7,6},{8,9},{9,8},{10,11... | collective-permute-start | bytes 196616 | tf_op jit(solution)/shard_map/ppermute | solution.py:161
  15.5 2.8 %collective-permute-done.3.other_ref = bf16[128,256]{1,0:T(8,128)(2,1)S(1)} collective-permute-done((bf16[128,256]{1,0:T(8,128)(2,1)S(1)}, bf16[128,256]{1,0:T(8,128)(2,1)S(1)}, u32[]{:S(2)}, u32[]{:S(2)}) %collective-permute-start.3) | collective-permute-done | bytes 65568 | tf_op jit(solution)/shard_map/ppermute | solution.py:161
  18.2 0.1 merge.1.refs_0_
  18.3 0.1 collective-permute-start.6
  18.4 1.6 %collective-permute-start.5 = (bf16[128,256]{1,0:T(8,128)(2,1)S(1)}, bf16[128,256]{1,0:T(8,128)(2,1)S(1)}, u32[]{:S(2)}, u32[]{:S(2)}) collective-permute-start(bf16[128,256]{1,0:T(8,128)(2,1)S(1)} %merge.1.refs_0_), channel_id=1, source_target_pairs={{0,16},{8,24},{16,0},{24,8},{1,17},{9,25},{17,1},{25,9},{2,18},{10... | collective-permute-start | bytes 196616 | tf_op jit(solution)/shard_map/ppermute | solution.py:161
  20.0 0.3 collective-permute-start.4
  20.3 2.5 %collective-permute-done.6.refs_3_ = bf16[128,256]{1,0:T(8,128)(2,1)S(1)} collective-permute-done((bf16[128,256]{1,0:T(8,128)(2,1)S(1)}, bf16[128,256]{1,0:T(8,128)(2,1)S(1)}, u32[]{:S(2)}, u32[]{:S(2)}) %collective-permute-start.6) | collective-permute-done | bytes 65568 | tf_op jit(solution)/shard_map/ppermute | solution.py:161
  22.7 1.5 %collective-permute-done.5.refs_2_ = bf16[128,256]{1,0:T(8,128)(2,1)S(1)} collective-permute-done((bf16[128,256]{1,0:T(8,128)(2,1)S(1)}, bf16[128,256]{1,0:T(8,128)(2,1)S(1)}, u32[]{:S(2)}, u32[]{:S(2)}) %collective-permute-start.5) | collective-permute-done | bytes 65568 | tf_op jit(solution)/shard_map/ppermute | solution.py:161
  24.2 0.0 collective-permute-done.4.refs_1_
  24.2 0.0 collective-permute-done.7.refs_5_
  24.2 0.4 value.1
  24.6 1.6 %collective-permute-start.8 = (bf16[64,512]{1,0:T(8,128)(2,1)S(1)}, bf16[64,512]{1,0:T(8,128)(2,1)S(1)}, u32[]{:S(2)}, u32[]{:S(2)}) collective-permute-start(bf16[64,512]{1,0:T(8,128)(2,1)S(1)} %get-tuple-element.19), channel_id=1, source_target_pairs={{0,1},{1,0},{2,3},{3,2},{4,5},{5,4},{6,7},{7,6},{8,9},{9,8},{10,11... | collective-permute-start | bytes 196616 | tf_op jit(solution)/shard_map/ppermute | solution.py:161
  26.2 2.6 %collective-permute-start.9 = (bf16[64,512]{1,0:T(8,128)(2,1)S(1)}, bf16[64,512]{1,0:T(8,128)(2,1)S(1)}, u32[]{:S(2)}, u32[]{:S(2)}) collective-permute-start(bf16[64,512]{1,0:T(8,128)(2,1)S(1)} %get-tuple-element.20), channel_id=1, source_target_pairs={{0,4},{1,5},{2,6},{3,7},{4,0},{5,1},{6,2},{7,3},{8,12},{9,13},{10,... | collective-permute-start | bytes 196616 | tf_op jit(solution)/shard_map/ppermute | solution.py:161
  28.8 0.3 collective-permute-start.10
  29.1 4.7 %collective-permute-done.9.refs_2_ = bf16[64,512]{1,0:T(8,128)(2,1)S(1)} collective-permute-done((bf16[64,512]{1,0:T(8,128)(2,1)S(1)}, bf16[64,512]{1,0:T(8,128)(2,1)S(1)}, u32[]{:S(2)}, u32[]{:S(2)}) %collective-permute-start.9) | collective-permute-done | bytes 65568 | tf_op jit(solution)/shard_map/ppermute | solution.py:161
  33.7 1.1 %collective-permute-done.10.refs_3_ = bf16[64,512]{1,0:T(8,128)(2,1)S(1)} collective-permute-done((bf16[64,512]{1,0:T(8,128)(2,1)S(1)}, bf16[64,512]{1,0:T(8,128)(2,1)S(1)}, u32[]{:S(2)}, u32[]{:S(2)}) %collective-permute-start.10) | collective-permute-done | bytes 65568 | tf_op jit(solution)/shard_map/ppermute | solution.py:161
  34.8 0.7 %expose.1 = (f32[2,64,256]{2,1,0:T(8,128)}, f32[2,64]{1,0:T(2,128)S(1)}) custom-call(f32[64,512]{1,0:T(8,128)S(1)} %get-tuple-element.18.refs_0_, bf16[64,512]{1,0:T(8,128)(2,1)S(1)} %collective-permute-done.8.refs_1_, bf16[64,512]{1,0:T(8,128)(2,1)S(1)} %collective-permute-done.9.refs_2_, bf16[64,512]{1,0:T(8,128)(2,1)S(1)} %collective-permute-done.10.refs_3_), custom_call_target="tpu_custom_call" | custom-call | tf_op jit(solution)/shard_map/expose/pallas_call | solution.py:256
  35.5 0.8 %collective-permute-start.12 = (f32[2,64]{1,0:T(2,128)S(1)}, f32[2,64]{1,0:T(2,128)S(1)}, u32[]{:S(2)}, u32[]{:S(2)}) collective-permute-start(f32[2,64]{1,0:T(2,128)S(1)} %get-tuple-element.23), channel_id=1, source_target_pairs={{0,16},{8,24},{16,0},{24,8},{1,17},{9,25},{17,1},{25,9},{2,18},{10... | collective-permute-start | bytes 1544 | tf_op jit(solution)/shard_map/ppermute | solution.py:161
  36.3 1.1 %collective-permute-start.11 = (f32[2,64]{1,0:T(2,128)S(1)}, f32[2,64]{1,0:T(2,128)S(1)}, u32[]{:S(2)}, u32[]{:S(2)}) collective-permute-start(f32[2,64]{1,0:T(2,128)S(1)} %get-tuple-element.23), channel_id=1, source_target_pairs={{0,8},{8,0},{16,24},{24,16},{1,9},{9,1},{17,25},{25,17},{2,10},{10... | collective-permute-start | bytes 1544 | tf_op jit(solution)/shard_map/ppermute | solution.py:161
  37.4 1.1 %collective-permute-done.13 = f32[2,64]{1,0:T(2,128)S(1)} collective-permute-done((f32[2,64]{1,0:T(2,128)S(1)}, f32[2,64]{1,0:T(2,128)S(1)}, u32[]{:S(2)}, u32[]{:S(2)}) %collective-permute-start.13) | collective-permute-done | bytes 544 | tf_op jit(solution)/shard_map/ppermute | solution.py:161
  38.5 0.6 %collective-permute-done.12 = f32[2,64]{1,0:T(2,128)S(1)} collective-permute-done((f32[2,64]{1,0:T(2,128)S(1)}, f32[2,64]{1,0:T(2,128)S(1)}, u32[]{:S(2)}, u32[]{:S(2)}) %collective-permute-start.12) | collective-permute-done | bytes 544 | tf_op jit(solution)/shard_map/ppermute | solution.py:161
  39.1 0.6 %add_multiply_fusion = f32[2,64]{1,0:T(2,128)} fusion(f32[2,64]{1,0:T(2,128)S(1)} %collective-permute-done.12, f32[2,64]{1,0:T(2,128)S(1)} %collective-permute-done.13, f32[2,64]{1,0:T(2,128)S(1)} %get-tuple-element.23, f32[2,64]{1,0:T(2,128)S(1)} %collective-permute-done.11), kind=kLoop, calls=%fused_computation | loop fusion | flops 512 | bytes 2560 | tf_op jit(solution)/shard_map/div | solution.py:270
  (9 shorter events, 0.0 us)
Async XLA Ops:
  2.6 8.6 %collective-permute-start.2 = (bf16[80,256]{1,0:T(8,128)(2,1)}, bf16[80,256]{1,0:T(8,128)(2,1)S(1)}, u32[]{:S(2)}, u32[]{:S(2)}) collective-permute-start(bf16[80,256]{1,0:T(8,128)(2,1)} %pack.1.refs_1_), channel_id=1, source_target_pairs={{0,6},{1,7},{2,4},{3,5},{4,2},{5,3},{6,0},{7,1},{8,14},{9,15},{10,... | collective-permute-start | bytes 122888 | tf_op jit(solution)/shard_map/ppermute | solution.py:161
  7.7 5.1 %collective-permute-start.1 = (bf16[80,256]{1,0:T(8,128)(2,1)}, bf16[80,256]{1,0:T(8,128)(2,1)S(1)}, u32[]{:S(2)}, u32[]{:S(2)}) collective-permute-start(bf16[80,256]{1,0:T(8,128)(2,1)} %pack.1.refs_1_), channel_id=1, source_target_pairs={{0,4},{1,5},{2,6},{3,7},{4,0},{5,1},{6,2},{7,3},{8,12},{9,13},{10,... | collective-permute-start | bytes 122888 | tf_op jit(solution)/shard_map/ppermute | solution.py:161
  7.7 5.1 %collective-permute-start = (bf16[80,256]{1,0:T(8,128)(2,1)}, bf16[80,256]{1,0:T(8,128)(2,1)S(1)}, u32[]{:S(2)}, u32[]{:S(2)}) collective-permute-start(bf16[80,256]{1,0:T(8,128)(2,1)} %pack.1.refs_1_), channel_id=1, source_target_pairs={{0,2},{1,3},{2,0},{3,1},{4,6},{5,7},{6,4},{7,5},{8,10},{9,11},{10,... | collective-permute-start | bytes 122888 | tf_op jit(solution)/shard_map/ppermute | solution.py:161
  8.4 4.5 %copy-start.1 = (bf16[80,256]{1,0:T(8,128)(2,1)S(1)}, bf16[80,256]{1,0:T(8,128)(2,1)}, u32[]{:S(2)}) copy-start(bf16[80,256]{1,0:T(8,128)(2,1)} %pack.1.refs_1_) | copy-start | bytes 122884
  8.4 4.5 %copy-start.2 = (s32[16]{0:T(128)S(1)}, s32[16]{0:T(128)}, u32[]{:S(2)}) copy-start(s32[16]{0:T(128)} %refs_0_.1) | copy-start | bytes 196
  11.2 13.0 %copy-start = (bf16[2,256,256]{2,1,0:T(8,128)(2,1)S(1)}, bf16[2,256,256]{2,1,0:T(8,128)(2,1)}, u32[]{:S(2)}) copy-start(bf16[2,256,256]{2,1,0:T(8,128)(2,1)} %price.1) | copy-start | bytes 786436
  13.8 10.4 %collective-permute-start.7 = (bf16[512,256]{1,0:T(8,128)(2,1)}, bf16[512,256]{1,0:T(8,128)(2,1)S(1)}, u32[]{:S(2)}, u32[]{:S(2)}) collective-permute-start(bf16[512,256]{1,0:T(8,128)(2,1)} %bitcast.6), channel_id=1, source_target_pairs={{0,2},{1,3},{2,0},{3,1},{4,6},{5,7},{6,4},{7,5},{8,10},{9,11},{10,... | collective-permute-start | bytes 786440 | tf_op jit(solution)/shard_map/ppermute | solution.py:161
  14.0 4.3 %collective-permute-start.3 = (bf16[128,256]{1,0:T(8,128)(2,1)S(1)}, bf16[128,256]{1,0:T(8,128)(2,1)S(1)}, u32[]{:S(2)}, u32[]{:S(2)}) collective-permute-start(bf16[128,256]{1,0:T(8,128)(2,1)S(1)} %get-tuple-element.16), channel_id=1, source_target_pairs={{0,1},{1,0},{2,3},{3,2},{4,5},{5,4},{6,7},{7,6},{8,9},{9,8},{10,11... | collective-permute-start | bytes 196616 | tf_op jit(solution)/shard_map/ppermute | solution.py:161
  18.3 4.4 %collective-permute-start.6 = (bf16[128,256]{1,0:T(8,128)(2,1)S(1)}, bf16[128,256]{1,0:T(8,128)(2,1)S(1)}, u32[]{:S(2)}, u32[]{:S(2)}) collective-permute-start(bf16[128,256]{1,0:T(8,128)(2,1)S(1)} %merge.1.refs_0_), channel_id=1, source_target_pairs={{0,24},{8,16},{16,8},{24,0},{1,25},{9,17},{17,9},{25,1},{2,26},{10... | collective-permute-start | bytes 196616 | tf_op jit(solution)/shard_map/ppermute | solution.py:161
  18.4 5.8 %collective-permute-start.5 = (bf16[128,256]{1,0:T(8,128)(2,1)S(1)}, bf16[128,256]{1,0:T(8,128)(2,1)S(1)}, u32[]{:S(2)}, u32[]{:S(2)}) collective-permute-start(bf16[128,256]{1,0:T(8,128)(2,1)S(1)} %merge.1.refs_0_), channel_id=1, source_target_pairs={{0,16},{8,24},{16,0},{24,8},{1,17},{9,25},{17,1},{25,9},{2,18},{10... | collective-permute-start | bytes 196616 | tf_op jit(solution)/shard_map/ppermute | solution.py:161
  20.0 4.2 %collective-permute-start.4 = (bf16[128,256]{1,0:T(8,128)(2,1)S(1)}, bf16[128,256]{1,0:T(8,128)(2,1)S(1)}, u32[]{:S(2)}, u32[]{:S(2)}) collective-permute-start(bf16[128,256]{1,0:T(8,128)(2,1)S(1)} %merge.1.refs_0_), channel_id=1, source_target_pairs={{0,8},{8,0},{16,24},{24,16},{1,9},{9,1},{17,25},{25,17},{2,10},{10... | collective-permute-start | bytes 196616 | tf_op jit(solution)/shard_map/ppermute | solution.py:161
  24.6 4.5 %collective-permute-start.8 = (bf16[64,512]{1,0:T(8,128)(2,1)S(1)}, bf16[64,512]{1,0:T(8,128)(2,1)S(1)}, u32[]{:S(2)}, u32[]{:S(2)}) collective-permute-start(bf16[64,512]{1,0:T(8,128)(2,1)S(1)} %get-tuple-element.19), channel_id=1, source_target_pairs={{0,1},{1,0},{2,3},{3,2},{4,5},{5,4},{6,7},{7,6},{8,9},{9,8},{10,11... | collective-permute-start | bytes 196616 | tf_op jit(solution)/shard_map/ppermute | solution.py:161
  26.2 7.6 %collective-permute-start.9 = (bf16[64,512]{1,0:T(8,128)(2,1)S(1)}, bf16[64,512]{1,0:T(8,128)(2,1)S(1)}, u32[]{:S(2)}, u32[]{:S(2)}) collective-permute-start(bf16[64,512]{1,0:T(8,128)(2,1)S(1)} %get-tuple-element.20), channel_id=1, source_target_pairs={{0,4},{1,5},{2,6},{3,7},{4,0},{5,1},{6,2},{7,3},{8,12},{9,13},{10,... | collective-permute-start | bytes 196616 | tf_op jit(solution)/shard_map/ppermute | solution.py:161
  28.8 6.1 %collective-permute-start.10 = (bf16[64,512]{1,0:T(8,128)(2,1)S(1)}, bf16[64,512]{1,0:T(8,128)(2,1)S(1)}, u32[]{:S(2)}, u32[]{:S(2)}) collective-permute-start(bf16[64,512]{1,0:T(8,128)(2,1)S(1)} %get-tuple-element.21), channel_id=1, source_target_pairs={{0,5},{1,4},{2,7},{3,6},{4,1},{5,0},{6,3},{7,2},{8,13},{9,12},{10,... | collective-permute-start | bytes 196616 | tf_op jit(solution)/shard_map/ppermute | solution.py:161
  35.5 3.0 %collective-permute-start.13 = (f32[2,64]{1,0:T(2,128)S(1)}, f32[2,64]{1,0:T(2,128)S(1)}, u32[]{:S(2)}, u32[]{:S(2)}) collective-permute-start(f32[2,64]{1,0:T(2,128)S(1)} %get-tuple-element.23), channel_id=1, source_target_pairs={{0,24},{8,16},{16,8},{24,0},{1,25},{9,17},{17,9},{25,1},{2,26},{10... | collective-permute-start | bytes 1544 | tf_op jit(solution)/shard_map/ppermute | solution.py:161
  35.5 3.6 %collective-permute-start.12 = (f32[2,64]{1,0:T(2,128)S(1)}, f32[2,64]{1,0:T(2,128)S(1)}, u32[]{:S(2)}, u32[]{:S(2)}) collective-permute-start(f32[2,64]{1,0:T(2,128)S(1)} %get-tuple-element.23), channel_id=1, source_target_pairs={{0,16},{8,24},{16,0},{24,8},{1,17},{9,25},{17,1},{25,9},{2,18},{10... | collective-permute-start | bytes 1544 | tf_op jit(solution)/shard_map/ppermute | solution.py:161
  36.3 2.8 %collective-permute-start.11 = (f32[2,64]{1,0:T(2,128)S(1)}, f32[2,64]{1,0:T(2,128)S(1)}, u32[]{:S(2)}, u32[]{:S(2)}) collective-permute-start(f32[2,64]{1,0:T(2,128)S(1)} %get-tuple-element.23), channel_id=1, source_target_pairs={{0,8},{8,0},{16,24},{24,16},{1,9},{9,1},{17,25},{25,17},{2,10},{10... | collective-permute-start | bytes 1544 | tf_op jit(solution)/shard_map/ppermute | solution.py:161

commit v2 on v1

--- a/solution.py
+++ b/solution.py
@@ -58,20 +58,38 @@
 
 
 def price_kernel(*refs):
-    count = 7
-    out_ref, sems = refs[count], refs[-1]
-    refs_in = refs[count + 1 : -1]
-    fetch(list(zip(refs[:count], refs_in)), sems)
-    shocks_ref, loadings_ref, vol_ref, counts_ref, noise_ref, mean_ref, dev_ref = refs_in
+    sources, out_hbm, held_refs, out_ref = refs[:7], refs[7], refs[8:15], refs[15]
+    sems, chunk_sems, out_sems = refs[16:]
+    loadings_ref, vol_ref, mean_ref, dev_ref, shocks_ref, counts_ref, noise_ref = held_refs
     rows = shocks_ref.shape[1]
+    fixed = [
+        pltpu.make_async_copy(src, dst, sems.at[i])
+        for i, (src, dst) in enumerate(zip(sources[:4], held_refs[:4]))
+    ]
+    chunks = [
+        [
+            pltpu.make_async_copy(src.at[:, pl.ds(at, CHUNK)], dst.at[:, pl.ds(at, CHUNK)], chunk_sems.at[i, j])
+            for j, (src, dst) in enumerate(zip(sources[4:], held_refs[4:]))
+        ]
+        for i, at in enumerate(range(0, rows, CHUNK))
+    ]
+    results = [
+        pltpu.make_async_copy(out_ref.at[:, pl.ds(at, CHUNK)], out_hbm.at[:, pl.ds(at, CHUNK)], out_sems.at[i])
+        for i, at in enumerate(range(0, rows, CHUNK))
+    ]
+    for copy in fixed + sum(chunks, []):
+        copy.start()
+    for copy in fixed:
+        copy.wait()
     vol = vol_ref[...]
     drift = 0.5 * vol * vol
     mean = mean_ref[...]
     dev = dev_ref[...]
     loadings = loadings_ref[...]
-
-    def step(i, carry):
-        at = pl.ds(pl.multiple_of(i * CHUNK, CHUNK), CHUNK)
+    for i, copies in enumerate(chunks):
+        for copy in copies:
+            copy.wait()
+        at = slice(i * CHUNK, (i + 1) * CHUNK)
         level = jnp.zeros((CHUNK, vol.shape[1]), jnp.float32)
         for date in range(DATES):
             diffuse = jnp.dot(shocks_ref[date, at, :], loadings, preferred_element_type=jnp.float32)
@@ -79,9 +97,9 @@
             noise = noise_ref[date, at, :].astype(jnp.float32)
             level = level + vol * diffuse - drift + counts * mean + jnp.sqrt(counts) * dev * noise
             out_ref[date, at, :] = (jnp.exp(level) - 1.0).astype(jnp.bfloat16)
-        return carry
-
-    lax.fori_loop(0, rows // CHUNK, step, 0)
+        results[i].start()
+    for copy in results:
+        copy.wait()
 
 
 def combine_kernel(part, held, flips, *refs):
@@ -144,16 +162,22 @@
         out_ref[...] = total[p * SET_DEV : (p + 1) * SET_DEV].astype(out_ref.dtype)
 
 
+def exposure_of(part_refs, date, rows):
+    at = slice(date * rows, (date + 1) * rows)
+    nets = part_refs[0][:, at]
+    for ref in part_refs[1:]:
+        nets = nets + ref[:, at].astype(jnp.float32)
+    return jnp.maximum(nets, 0.0)
+
+
+def totals_kernel(rows, *refs):
+    for date in range(DATES):
+        refs[-1][date] = jnp.sum(exposure_of(refs[:-1], date, rows), axis=1)
+
+
 def expose_kernel(rows, *refs):
-    part_refs, exposure_ref, totals_ref = refs[:-2], refs[-2], refs[-1]
     for date in range(DATES):
-        at = slice(date * rows, (date + 1) * rows)
-        nets = part_refs[0][:, at]
-        for ref in part_refs[1:]:
-            nets = nets + ref[:, at].astype(jnp.float32)
-        exposure = jnp.maximum(nets, 0.0)
-        exposure_ref[date] = exposure
-        totals_ref[date] = jnp.sum(exposure, axis=1)
+        refs[-1][date] = exposure_of(refs[:-1], date, rows)
 
 
 def from_partner(x, axis, flip):
@@ -198,14 +222,19 @@
     packets = [packet] + [from_partner(packet, "fac", i) for i in column_flips[1:]]
 
     packet, shocks = lax.optimization_barrier((packet, shocks))
-    inputs = (shocks, loadings, vol[None], jump_counts, jump_noise, jump_mean[None], jump_vol[None])
+    inputs = (loadings, vol[None], jump_mean[None], jump_vol[None], shocks, jump_counts, jump_noise)
+    prices_shape = jax.ShapeDtypeStruct((DATES, rows, width), jnp.bfloat16)
     prices = pl.pallas_call(
         price_kernel,
-        out_shape=jax.ShapeDtypeStruct((DATES, rows, width), jnp.bfloat16),
+        out_shape=prices_shape,
         in_specs=[HBM] * len(inputs),
-        out_specs=VMEM,
-        scratch_shapes=[pltpu.VMEM(x.shape, x.dtype) for x in inputs]
-        + [pltpu.SemaphoreType.DMA((len(inputs),))],
+        out_specs=HBM,
+        scratch_shapes=[pltpu.VMEM(x.shape, x.dtype) for x in inputs + (prices_shape,)]
+        + [
+            pltpu.SemaphoreType.DMA((4,)),
+            pltpu.SemaphoreType.DMA((rows // CHUNK, 3)),
+            pltpu.SemaphoreType.DMA((rows // CHUNK,)),
+        ],
         compiler_params=FETCH_PARAMS,
         name="price",
     )(*inputs)
@@ -235,6 +264,7 @@
         in_specs=[VMEM] * 2,
         out_specs=VMEM,
         compiler_params=PARAMS,
+        cost_estimate=pl.CostEstimate(flops=10**10, bytes_accessed=0, transcendentals=0),
         name="merge",
     )(own, from_partner(other, "fac", SIDE_FLIP))
     shares = [share] + [from_partner(share, "scen", i) for i in range(1, scen_count)]
@@ -251,16 +281,22 @@
         compiler_params=PARAMS,
         name="value",
     )(*shares, *pair_prices)
-    parts = [parts[0]] + [from_partner(x, "fac", i) for x, i in zip(parts[1:], owner_flips[1:])]
-
-    exposure, totals = pl.pallas_call(
+    sends = list(zip(parts[1:], owner_flips[1:]))
+    parts = [parts[0]] + [from_partner(x, "fac", i) for x, i in sends[::-1]]
+
+    totals = pl.pallas_call(
+        functools.partial(totals_kernel, rows),
+        out_shape=jax.ShapeDtypeStruct((DATES, SET_DEV), jnp.float32),
+        in_specs=[VMEM] * len(parts),
+        out_specs=VMEM,
+        compiler_params=PARAMS,
+        name="totals",
+    )(*parts)
+    exposure = pl.pallas_call(
         functools.partial(expose_kernel, rows),
-        out_shape=[
-            jax.ShapeDtypeStruct((DATES, SET_DEV, rows), jnp.float32),
-            jax.ShapeDtypeStruct((DATES, SET_DEV), jnp.float32),
-        ],
+        out_shape=jax.ShapeDtypeStruct((DATES, SET_DEV, rows), jnp.float32),
         in_specs=[VMEM] * len(parts),
-        out_specs=[VMEM] * 2,
+        out_specs=VMEM,
         compiler_params=PARAMS,
         name="expose",
     )(*parts)

time: 39.9 us -> 39 us (0.977)
  waiting for transfers between devices: 15.8 us -> 14.8 us
    ppermute x14, waiting for transfers between devices: 15.8 us -> 14.8 us  [from_partner(): return lax.ppermute(x, axis, [(i, i ^ flip) for i in range(count)])]
    pallas_call x2 -> x3, Pallas kernels: 3.54 us -> 3.68 us  [the longest x1 2.88 us: body(): pl.pallas_call(price_kernel, out_shape=prices_shape, in_specs=[HBM] * len...]
  transfers between devices with their start and end apart: 14 -> 14, of which waited for: 8 -> 8; matrix products, arithmetic and copies ran while one was open for 0% -> 0% of each run, Pallas kernels for 7% -> 9%
where the time goes in v2:
time: 39 us; the launch traced here: 38.9 us
  starting transfers between devices  15.8 us (41%)
  waiting for transfers between devices  14.8 us (38%)
  Pallas kernels  7.03 us (18%)
  between operations  0.71 us (2%)
  other arithmetic  0.57 us (1%)
    ppermute x14, starting transfers between devices, from_partner(): return lax.ppermute(x, axis, [(i, i ^ flip) for i in range(count)])  15.8 us
    ppermute x14, waiting for transfers between devices, from_partner(): return lax.ppermute(x, axis, [(i, i ^ flip) for i in range(count)])  14.8 us
    pallas_call x1, Pallas kernels, body(): pl.pallas_call(price_kernel, out_shape=prices_shape, in_specs=[HBM] * len...  2.88 us
    pallas_call x1, Pallas kernels, body(): pl.pallas_call(functools.partial(pack_kernel, part), out_shape=jax.ShapeD...  1.97 us
    pallas_call x1, Pallas kernels, body(): pl.pallas_call(functools.partial(combine_kernel, part, held, owner_flips)...  0.9 us
  transfers between devices with their start and end apart: 14, of which 8 were waited for; matrix products, arithmetic and copies ran while one was open for 0% of the time, Pallas kernels for 9%

profile of v2, /device:TPU:0, one launch (start us, length us, event | category | flops | bytes accessed | tf_op | source)
XLA Modules:
  0.0 38.9 jit_solution(13913114663572711475)
XLA Ops:
  0.6 2.0 %pack.1.refs_1_ = bf16[80,256]{1,0:T(8,128)(2,1)} custom-call(bf16[256,2,128]{2,1,0:T(2,128)(2,1)} %weights_hbm.1, s32[2,256]{1,0:T(2,128)} %bitcast.8, s32[1,256]{1,0:T(1,128)} %bitcast.9), custom_call_target="tpu_custom_call" | custom-call | tf_op jit(solution)/shard_map/pack/pallas_call | solution.py:212
  2.6 5.1 %collective-permute-start.2 = (bf16[80,256]{1,0:T(8,128)(2,1)}, bf16[80,256]{1,0:T(8,128)(2,1)S(1)}, u32[]{:S(2)}, u32[]{:S(2)}) collective-permute-start(bf16[80,256]{1,0:T(8,128)(2,1)} %pack.1.refs_1_), channel_id=1, source_target_pairs={{0,6},{1,7},{2,4},{3,5},{4,2},{5,3},{6,0},{7,1},{8,14},{9,15},{10,... | collective-permute-start | bytes 122888 | tf_op jit(solution)/shard_map/ppermute | solution.py:185
  7.7 0.0 collective-permute-start.1
  7.7 0.6 %collective-permute-start = (bf16[80,256]{1,0:T(8,128)(2,1)}, bf16[80,256]{1,0:T(8,128)(2,1)S(1)}, u32[]{:S(2)}, u32[]{:S(2)}) collective-permute-start(bf16[80,256]{1,0:T(8,128)(2,1)} %pack.1.refs_1_), channel_id=1, source_target_pairs={{0,2},{1,3},{2,0},{3,1},{4,6},{5,7},{6,4},{7,5},{8,10},{9,11},{10,... | collective-permute-start | bytes 122888 | tf_op jit(solution)/shard_map/ppermute | solution.py:185
  8.4 2.9 %price.1 = bf16[2,256,256]{2,1,0:T(8,128)(2,1)} custom-call(bf16[256,256]{1,0:T(8,128)(2,1)} %refs_0_.3, f32[1,256]{1,0:T(1,128)} %bitcast.10, f32[1,256]{1,0:T(1,128)} %bitcast.11, f32[1,256]{1,0:T(1,128)} %bitcast.12, bf16[2,256,256]{2,1,0:T(8,128)(2,1)} %refs_4_, s32[2,256,256]{2,1,0:T(8,128)} %refs_5_.1, bf16[2,256,256]{2,1,0:T(8,128)(2,1)} %refs_6_.1), custom_call_target="tpu_custom_call" | custom-call | tf_op jit(solution)/shard_map/price/pallas_call | solution.py:227
  11.3 0.0 collective-permute-done.2.refs_4_
  11.3 1.6 %collective-permute-done.1.refs_3_ = bf16[80,256]{1,0:T(8,128)(2,1)S(1)} collective-permute-done((bf16[80,256]{1,0:T(8,128)(2,1)}, bf16[80,256]{1,0:T(8,128)(2,1)S(1)}, u32[]{:S(2)}, u32[]{:S(2)}) %collective-permute-start.1) | collective-permute-done | bytes 40992 | tf_op jit(solution)/shard_map/ppermute | solution.py:185
  12.8 0.9 %combine.1 = (f32[128,256]{1,0:T(8,128)S(1)}, bf16[128,256]{1,0:T(8,128)(2,1)S(1)}) custom-call(s32[16]{0:T(128)S(1)} %copy-done.2, bf16[80,256]{1,0:T(8,128)(2,1)S(1)} %copy-done.1, bf16[80,256]{1,0:T(8,128)(2,1)S(1)} %collective-permute-done.refs_2_, bf16[80,256]{1,0:T(8,128)(2,1)S(1)} %collective-permute-done.1.refs_3_, ...), custom_call_target="tpu_custom_call" | custom-call | tf_op jit(solution)/shard_map/combine/pallas_call | solution.py:244
  13.8 1.6 %collective-permute-start.3 = (bf16[128,256]{1,0:T(8,128)(2,1)S(1)}, bf16[128,256]{1,0:T(8,128)(2,1)S(1)}, u32[]{:S(2)}, u32[]{:S(2)}) collective-permute-start(bf16[128,256]{1,0:T(8,128)(2,1)S(1)} %get-tuple-element.14), channel_id=1, source_target_pairs={{0,1},{1,0},{2,3},{3,2},{4,5},{5,4},{6,7},{7,6},{8,9},{9,8},{10,11... | collective-permute-start | bytes 196616 | tf_op jit(solution)/shard_map/ppermute | solution.py:185
  15.3 0.2 collective-permute-start.7
  15.5 2.6 %collective-permute-done.3.other_ref = bf16[128,256]{1,0:T(8,128)(2,1)S(1)} collective-permute-done((bf16[128,256]{1,0:T(8,128)(2,1)S(1)}, bf16[128,256]{1,0:T(8,128)(2,1)S(1)}, u32[]{:S(2)}, u32[]{:S(2)}) %collective-permute-start.3) | collective-permute-done | bytes 65568 | tf_op jit(solution)/shard_map/ppermute | solution.py:185
  18.1 0.1 merge.1.refs_0_
  18.2 0.1 collective-permute-start.6
  18.3 1.6 %collective-permute-start.5 = (bf16[128,256]{1,0:T(8,128)(2,1)S(1)}, bf16[128,256]{1,0:T(8,128)(2,1)S(1)}, u32[]{:S(2)}, u32[]{:S(2)}) collective-permute-start(bf16[128,256]{1,0:T(8,128)(2,1)S(1)} %merge.1.refs_0_), channel_id=1, source_target_pairs={{0,16},{8,24},{16,0},{24,8},{1,17},{9,25},{17,1},{25,9},{2,18},{10... | collective-permute-start | bytes 196616 | tf_op jit(solution)/shard_map/ppermute | solution.py:185
  19.8 0.3 collective-permute-start.4
  20.1 2.5 %collective-permute-done.6.refs_3_ = bf16[128,256]{1,0:T(8,128)(2,1)S(1)} collective-permute-done((bf16[128,256]{1,0:T(8,128)(2,1)S(1)}, bf16[128,256]{1,0:T(8,128)(2,1)S(1)}, u32[]{:S(2)}, u32[]{:S(2)}) %collective-permute-start.6) | collective-permute-done | bytes 65568 | tf_op jit(solution)/shard_map/ppermute | solution.py:185
  22.6 1.5 %collective-permute-done.5.refs_2_ = bf16[128,256]{1,0:T(8,128)(2,1)S(1)} collective-permute-done((bf16[128,256]{1,0:T(8,128)(2,1)S(1)}, bf16[128,256]{1,0:T(8,128)(2,1)S(1)}, u32[]{:S(2)}, u32[]{:S(2)}) %collective-permute-start.5) | collective-permute-done | bytes 65568 | tf_op jit(solution)/shard_map/ppermute | solution.py:185
  24.1 0.4 %value.1 = (f32[64,512]{1,0:T(8,128)S(1)}, bf16[64,512]{1,0:T(8,128)(2,1)S(1)}, bf16[64,512]{1,0:T(8,128)(2,1)S(1)}, bf16[64,512]{1,0:T(8,128)(2,1)S(1)}) custom-call(bf16[128,256]{1,0:T(8,128)(2,1)S(1)} %merge.1.refs_0_, bf16[128,256]{1,0:T(8,128)(2,1)S(1)} %collective-permute-done.4.refs_1_, bf16[128,256]{1,0:T(8,128)(2,1)S(1)} %collective-permute-done.5.refs_2_, ...), custom_call_target="tpu_custom_call" | custom-call | tf_op jit(solution)/shard_map/value/pallas_call | solution.py:272
  24.5 3.0 %collective-permute-start.8 = (bf16[64,512]{1,0:T(8,128)(2,1)S(1)}, bf16[64,512]{1,0:T(8,128)(2,1)S(1)}, u32[]{:S(2)}, u32[]{:S(2)}) collective-permute-start(bf16[64,512]{1,0:T(8,128)(2,1)S(1)} %get-tuple-element.17), channel_id=1, source_target_pairs={{0,5},{1,4},{2,7},{3,6},{4,1},{5,0},{6,3},{7,2},{8,13},{9,12},{10,... | collective-permute-start | bytes 196616 | tf_op jit(solution)/shard_map/ppermute | solution.py:185
  27.5 0.9 %collective-permute-start.9 = (bf16[64,512]{1,0:T(8,128)(2,1)S(1)}, bf16[64,512]{1,0:T(8,128)(2,1)S(1)}, u32[]{:S(2)}, u32[]{:S(2)}) collective-permute-start(bf16[64,512]{1,0:T(8,128)(2,1)S(1)} %get-tuple-element.18), channel_id=1, source_target_pairs={{0,4},{1,5},{2,6},{3,7},{4,0},{5,1},{6,2},{7,3},{8,12},{9,13},{10,... | collective-permute-start | bytes 196616 | tf_op jit(solution)/shard_map/ppermute | solution.py:185
  28.4 0.5 %collective-permute-start.10 = (bf16[64,512]{1,0:T(8,128)(2,1)S(1)}, bf16[64,512]{1,0:T(8,128)(2,1)S(1)}, u32[]{:S(2)}, u32[]{:S(2)}) collective-permute-start(bf16[64,512]{1,0:T(8,128)(2,1)S(1)} %get-tuple-element.19), channel_id=1, source_target_pairs={{0,1},{1,0},{2,3},{3,2},{4,5},{5,4},{6,7},{7,6},{8,9},{9,8},{10,11... | collective-permute-start | bytes 196616 | tf_op jit(solution)/shard_map/ppermute | solution.py:185
  28.9 4.1 %collective-permute-done.8.refs_1_ = bf16[64,512]{1,0:T(8,128)(2,1)S(1)} collective-permute-done((bf16[64,512]{1,0:T(8,128)(2,1)S(1)}, bf16[64,512]{1,0:T(8,128)(2,1)S(1)}, u32[]{:S(2)}, u32[]{:S(2)}) %collective-permute-start.8) | collective-permute-done | bytes 65568 | tf_op jit(solution)/shard_map/ppermute | solution.py:185
  33.0 1.2 %collective-permute-done.9.refs_2_ = bf16[64,512]{1,0:T(8,128)(2,1)S(1)} collective-permute-done((bf16[64,512]{1,0:T(8,128)(2,1)S(1)}, bf16[64,512]{1,0:T(8,128)(2,1)S(1)}, u32[]{:S(2)}, u32[]{:S(2)}) %collective-permute-start.9) | collective-permute-done | bytes 65568 | tf_op jit(solution)/shard_map/ppermute | solution.py:185
  34.2 0.0 collective-permute-done.10.refs_3_
  34.2 0.1 totals.1
  34.3 0.4 %collective-permute-start.13 = (f32[2,64]{1,0:T(2,128)S(1)}, f32[2,64]{1,0:T(2,128)S(1)}, u32[]{:S(2)}, u32[]{:S(2)}) collective-permute-start(f32[2,64]{1,0:T(2,128)S(1)} %totals.1), channel_id=1, source_target_pairs={{0,24},{8,16},{16,8},{24,0},{1,25},{9,17},{17,9},{25,1},{2,26},{10... | collective-permute-start | bytes 1544 | tf_op jit(solution)/shard_map/ppermute | solution.py:185
  34.7 1.2 %collective-permute-start.12 = (f32[2,64]{1,0:T(2,128)S(1)}, f32[2,64]{1,0:T(2,128)S(1)}, u32[]{:S(2)}, u32[]{:S(2)}) collective-permute-start(f32[2,64]{1,0:T(2,128)S(1)} %totals.1), channel_id=1, source_target_pairs={{0,16},{8,24},{16,0},{24,8},{1,17},{9,25},{17,1},{25,9},{2,18},{10... | collective-permute-start | bytes 1544 | tf_op jit(solution)/shard_map/ppermute | solution.py:185
  35.9 0.3 collective-permute-start.11
  36.2 0.7 %expose.1 = f32[2,64,256]{2,1,0:T(8,128)} custom-call(f32[64,512]{1,0:T(8,128)S(1)} %get-tuple-element.16.refs_0_, bf16[64,512]{1,0:T(8,128)(2,1)S(1)} %collective-permute-done.8.refs_1_, bf16[64,512]{1,0:T(8,128)(2,1)S(1)} %collective-permute-done.9.refs_2_, bf16[64,512]{1,0:T(8,128)(2,1)S(1)} %collective-permute-done.10.refs_3_), custom_call_target="tpu_custom_call" | custom-call | tf_op jit(solution)/shard_map/expose/pallas_call | solution.py:295
  36.9 0.4 %collective-permute-done.13 = f32[2,64]{1,0:T(2,128)S(1)} collective-permute-done((f32[2,64]{1,0:T(2,128)S(1)}, f32[2,64]{1,0:T(2,128)S(1)}, u32[]{:S(2)}, u32[]{:S(2)}) %collective-permute-start.13) | collective-permute-done | bytes 544 | tf_op jit(solution)/shard_map/ppermute | solution.py:185
  37.4 0.9 %collective-permute-done.12 = f32[2,64]{1,0:T(2,128)S(1)} collective-permute-done((f32[2,64]{1,0:T(2,128)S(1)}, f32[2,64]{1,0:T(2,128)S(1)}, u32[]{:S(2)}, u32[]{:S(2)}) %collective-permute-start.12) | collective-permute-done | bytes 544 | tf_op jit(solution)/shard_map/ppermute | solution.py:185
  38.3 0.6 %add_multiply_fusion = f32[2,64]{1,0:T(2,128)} fusion(f32[2,64]{1,0:T(2,128)S(1)} %collective-permute-done.12, f32[2,64]{1,0:T(2,128)S(1)} %collective-permute-done.13, f32[2,64]{1,0:T(2,128)S(1)} %totals.1, f32[2,64]{1,0:T(2,128)S(1)} %collective-permute-done.11), kind=kLoop, calls=%fused_computation | loop fusion | flops 512 | bytes 2560 | tf_op jit(solution)/shard_map/div | solution.py:306
  (10 shorter events, 0.0 us)
Async XLA Ops:
  2.6 8.7 %collective-permute-start.2 = (bf16[80,256]{1,0:T(8,128)(2,1)}, bf16[80,256]{1,0:T(8,128)(2,1)S(1)}, u32[]{:S(2)}, u32[]{:S(2)}) collective-permute-start(bf16[80,256]{1,0:T(8,128)(2,1)} %pack.1.refs_1_), channel_id=1, source_target_pairs={{0,6},{1,7},{2,4},{3,5},{4,2},{5,3},{6,0},{7,1},{8,14},{9,15},{10,... | collective-permute-start | bytes 122888 | tf_op jit(solution)/shard_map/ppermute | solution.py:185
  7.7 5.1 %collective-permute-start.1 = (bf16[80,256]{1,0:T(8,128)(2,1)}, bf16[80,256]{1,0:T(8,128)(2,1)S(1)}, u32[]{:S(2)}, u32[]{:S(2)}) collective-permute-start(bf16[80,256]{1,0:T(8,128)(2,1)} %pack.1.refs_1_), channel_id=1, source_target_pairs={{0,4},{1,5},{2,6},{3,7},{4,0},{5,1},{6,2},{7,3},{8,12},{9,13},{10,... | collective-permute-start | bytes 122888 | tf_op jit(solution)/shard_map/ppermute | solution.py:185
  7.7 5.1 %collective-permute-start = (bf16[80,256]{1,0:T(8,128)(2,1)}, bf16[80,256]{1,0:T(8,128)(2,1)S(1)}, u32[]{:S(2)}, u32[]{:S(2)}) collective-permute-start(bf16[80,256]{1,0:T(8,128)(2,1)} %pack.1.refs_1_), channel_id=1, source_target_pairs={{0,2},{1,3},{2,0},{3,1},{4,6},{5,7},{6,4},{7,5},{8,10},{9,11},{10,... | collective-permute-start | bytes 122888 | tf_op jit(solution)/shard_map/ppermute | solution.py:185
  8.4 4.5 %copy-start.1 = (bf16[80,256]{1,0:T(8,128)(2,1)S(1)}, bf16[80,256]{1,0:T(8,128)(2,1)}, u32[]{:S(2)}) copy-start(bf16[80,256]{1,0:T(8,128)(2,1)} %pack.1.refs_1_) | copy-start | bytes 122884
  8.4 4.5 %copy-start.2 = (s32[16]{0:T(128)S(1)}, s32[16]{0:T(128)}, u32[]{:S(2)}) copy-start(s32[16]{0:T(128)} %refs_0_.2) | copy-start | bytes 196
  13.8 4.3 %collective-permute-start.3 = (bf16[128,256]{1,0:T(8,128)(2,1)S(1)}, bf16[128,256]{1,0:T(8,128)(2,1)S(1)}, u32[]{:S(2)}, u32[]{:S(2)}) collective-permute-start(bf16[128,256]{1,0:T(8,128)(2,1)S(1)} %get-tuple-element.14), channel_id=1, source_target_pairs={{0,1},{1,0},{2,3},{3,2},{4,5},{5,4},{6,7},{7,6},{8,9},{9,8},{10,11... | collective-permute-start | bytes 196616 | tf_op jit(solution)/shard_map/ppermute | solution.py:185
  15.3 8.7 %collective-permute-start.7 = (bf16[512,256]{1,0:T(8,128)(2,1)}, bf16[512,256]{1,0:T(8,128)(2,1)S(1)}, u32[]{:S(2)}, u32[]{:S(2)}) collective-permute-start(bf16[512,256]{1,0:T(8,128)(2,1)} %bitcast.6), channel_id=1, source_target_pairs={{0,2},{1,3},{2,0},{3,1},{4,6},{5,7},{6,4},{7,5},{8,10},{9,11},{10,... | collective-permute-start | bytes 786440 | tf_op jit(solution)/shard_map/ppermute | solution.py:185
  18.1 6.0 %copy-start = (bf16[2,256,256]{2,1,0:T(8,128)(2,1)S(1)}, bf16[2,256,256]{2,1,0:T(8,128)(2,1)}, u32[]{:S(2)}) copy-start(bf16[2,256,256]{2,1,0:T(8,128)(2,1)} %price.1) | copy-start | bytes 786436
  18.2 4.4 %collective-permute-start.6 = (bf16[128,256]{1,0:T(8,128)(2,1)S(1)}, bf16[128,256]{1,0:T(8,128)(2,1)S(1)}, u32[]{:S(2)}, u32[]{:S(2)}) collective-permute-start(bf16[128,256]{1,0:T(8,128)(2,1)S(1)} %merge.1.refs_0_), channel_id=1, source_target_pairs={{0,24},{8,16},{16,8},{24,0},{1,25},{9,17},{17,9},{25,1},{2,26},{10... | collective-permute-start | bytes 196616 | tf_op jit(solution)/shard_map/ppermute | solution.py:185
  18.3 5.8 %collective-permute-start.5 = (bf16[128,256]{1,0:T(8,128)(2,1)S(1)}, bf16[128,256]{1,0:T(8,128)(2,1)S(1)}, u32[]{:S(2)}, u32[]{:S(2)}) collective-permute-start(bf16[128,256]{1,0:T(8,128)(2,1)S(1)} %merge.1.refs_0_), channel_id=1, source_target_pairs={{0,16},{8,24},{16,0},{24,8},{1,17},{9,25},{17,1},{25,9},{2,18},{10... | collective-permute-start | bytes 196616 | tf_op jit(solution)/shard_map/ppermute | solution.py:185
  19.8 4.2 %collective-permute-start.4 = (bf16[128,256]{1,0:T(8,128)(2,1)S(1)}, bf16[128,256]{1,0:T(8,128)(2,1)S(1)}, u32[]{:S(2)}, u32[]{:S(2)}) collective-permute-start(bf16[128,256]{1,0:T(8,128)(2,1)S(1)} %merge.1.refs_0_), channel_id=1, source_target_pairs={{0,8},{8,0},{16,24},{24,16},{1,9},{9,1},{17,25},{25,17},{2,10},{10... | collective-permute-start | bytes 196616 | tf_op jit(solution)/shard_map/ppermute | solution.py:185
  24.5 8.5 %collective-permute-start.8 = (bf16[64,512]{1,0:T(8,128)(2,1)S(1)}, bf16[64,512]{1,0:T(8,128)(2,1)S(1)}, u32[]{:S(2)}, u32[]{:S(2)}) collective-permute-start(bf16[64,512]{1,0:T(8,128)(2,1)S(1)} %get-tuple-element.17), channel_id=1, source_target_pairs={{0,5},{1,4},{2,7},{3,6},{4,1},{5,0},{6,3},{7,2},{8,13},{9,12},{10,... | collective-permute-start | bytes 196616 | tf_op jit(solution)/shard_map/ppermute | solution.py:185
  27.5 6.7 %collective-permute-start.9 = (bf16[64,512]{1,0:T(8,128)(2,1)S(1)}, bf16[64,512]{1,0:T(8,128)(2,1)S(1)}, u32[]{:S(2)}, u32[]{:S(2)}) collective-permute-start(bf16[64,512]{1,0:T(8,128)(2,1)S(1)} %get-tuple-element.18), channel_id=1, source_target_pairs={{0,4},{1,5},{2,6},{3,7},{4,0},{5,1},{6,2},{7,3},{8,12},{9,13},{10,... | collective-permute-start | bytes 196616 | tf_op jit(solution)/shard_map/ppermute | solution.py:185
  28.4 5.8 %collective-permute-start.10 = (bf16[64,512]{1,0:T(8,128)(2,1)S(1)}, bf16[64,512]{1,0:T(8,128)(2,1)S(1)}, u32[]{:S(2)}, u32[]{:S(2)}) collective-permute-start(bf16[64,512]{1,0:T(8,128)(2,1)S(1)} %get-tuple-element.19), channel_id=1, source_target_pairs={{0,1},{1,0},{2,3},{3,2},{4,5},{5,4},{6,7},{7,6},{8,9},{9,8},{10,11... | collective-permute-start | bytes 196616 | tf_op jit(solution)/shard_map/ppermute | solution.py:185
  34.3 3.1 %collective-permute-start.13 = (f32[2,64]{1,0:T(2,128)S(1)}, f32[2,64]{1,0:T(2,128)S(1)}, u32[]{:S(2)}, u32[]{:S(2)}) collective-permute-start(f32[2,64]{1,0:T(2,128)S(1)} %totals.1), channel_id=1, source_target_pairs={{0,24},{8,16},{16,8},{24,0},{1,25},{9,17},{17,9},{25,1},{2,26},{10... | collective-permute-start | bytes 1544 | tf_op jit(solution)/shard_map/ppermute | solution.py:185
  34.7 3.6 %collective-permute-start.12 = (f32[2,64]{1,0:T(2,128)S(1)}, f32[2,64]{1,0:T(2,128)S(1)}, u32[]{:S(2)}, u32[]{:S(2)}) collective-permute-start(f32[2,64]{1,0:T(2,128)S(1)} %totals.1), channel_id=1, source_target_pairs={{0,16},{8,24},{16,0},{24,8},{1,17},{9,25},{17,1},{25,9},{2,18},{10... | collective-permute-start | bytes 1544 | tf_op jit(solution)/shard_map/ppermute | solution.py:185
  35.9 2.4 %collective-permute-start.11 = (f32[2,64]{1,0:T(2,128)S(1)}, f32[2,64]{1,0:T(2,128)S(1)}, u32[]{:S(2)}, u32[]{:S(2)}) collective-permute-start(f32[2,64]{1,0:T(2,128)S(1)} %totals.1), channel_id=1, source_target_pairs={{0,8},{8,0},{16,24},{24,16},{1,9},{9,1},{17,25},{25,17},{2,10},{10... | collective-permute-start | bytes 1544 | tf_op jit(solution)/shard_map/ppermute | solution.py:185

commit v3 on v2

--- a/solution.py
+++ b/solution.py
@@ -27,16 +27,7 @@
     return lax.dot_general(a, b, dims, preferred_element_type=jnp.float32)
 
 
-def fetch(pairs, sems):
-    copies = [pltpu.make_async_copy(src, dst, sems.at[i]) for i, (src, dst) in enumerate(pairs)]
-    for copy in copies:
-        copy.start()
-    for copy in copies:
-        copy.wait()
-
-
-def pack_kernel(part, weights_hbm, deps_hbm, netting_hbm, packet_ref, weights_ref, deps_ref, netting_ref, sems):
-    fetch([(weights_hbm, weights_ref), (deps_hbm, deps_ref), (netting_hbm, netting_ref)], sems)
+def pack_kernel(part, weights_ref, trades_ref, packet_ref):
     scen = lax.axis_index("scen")
     row = lax.broadcasted_iota(jnp.int32, (part, BLOCK), 0)
     column = lax.broadcasted_iota(jnp.int32, (part, BLOCK), 1)
@@ -44,10 +35,10 @@
     for k in range(2):
         share = f32_dot(pick, weights_ref[:, k, :], NT)
         packet_ref[k * part : (k + 1) * part, :] = share.astype(jnp.bfloat16)
-    netting = netting_ref[...]
+    netting = trades_ref[2:3, :]
     tags = jnp.concatenate(
         [
-            deps_ref[...],
+            trades_ref[:2, :],
             netting // SET_DEV,
             netting % SET_DEV,
             jnp.zeros((TAGS - 4, netting.shape[1]), jnp.int32),
@@ -208,17 +199,14 @@
     column_flips = [i for i in range(fac_count) if not i & SIDE_FLIP]
     owner_flips = [i for i in range(fac_count) if not i & PRICE_FLIP]
 
-    inputs = (trade_weights, dependencies.T, netting[None])
     packet = pl.pallas_call(
         functools.partial(pack_kernel, part),
         out_shape=jax.ShapeDtypeStruct((2 * part + TAGS, trades), jnp.bfloat16),
-        in_specs=[HBM] * len(inputs),
+        in_specs=[VMEM] * 2,
         out_specs=VMEM,
-        scratch_shapes=[pltpu.VMEM(x.shape, x.dtype) for x in inputs]
-        + [pltpu.SemaphoreType.DMA((len(inputs),))],
-        compiler_params=FETCH_PARAMS,
+        compiler_params=PARAMS,
         name="pack",
-    )(*inputs)
+    )(trade_weights, jnp.concatenate([dependencies.T, netting[None]]))
     packets = [packet] + [from_partner(packet, "fac", i) for i in column_flips[1:]]
 
     packet, shocks = lax.optimization_barrier((packet, shocks))
@@ -282,7 +270,8 @@
         name="value",
     )(*shares, *pair_prices)
     sends = list(zip(parts[1:], owner_flips[1:]))
-    parts = [parts[0]] + [from_partner(x, "fac", i) for x, i in sends[::-1]]
+    sends = sends[1:] + sends[:1]
+    parts = [parts[0]] + [from_partner(x, "fac", i) for x, i in sends]
 
     totals = pl.pallas_call(
         functools.partial(totals_kernel, rows),

time: 39 us -> 39.2 us (level)
  local copies, waits for them, and re-layouts: 0.01 us -> 1.59 us
  Pallas kernels: 7.03 us -> 5.48 us
    unnamed x6 -> x10, local copies, waits for them, and re-layouts: 0.01 us -> 1.59 us
    pallas_call x1, Pallas kernels: 1.97 us -> 0.42 us  [body(): pl.pallas_call(functools.partial(pack_kernel, part), out_shape=jax.ShapeD...]
where the time goes in v3:
time: 39.2 us; the launch traced here: 39 us
  starting transfers between devices  15.8 us (40%)
  waiting for transfers between devices  14.8 us (38%)
  Pallas kernels  5.48 us (14%)
  local copies, waits for them, and re-layouts  1.59 us (4%)
  between operations  0.72 us (2%)
  other arithmetic  0.58 us (1%)
    ppermute x14, starting transfers between devices, from_partner(): return lax.ppermute(x, axis, [(i, i ^ flip) for i in range(count)])  15.8 us
    ppermute x14, waiting for transfers between devices, from_partner(): return lax.ppermute(x, axis, [(i, i ^ flip) for i in range(count)])  14.8 us
    pallas_call x1, Pallas kernels, body(): pl.pallas_call(price_kernel, out_shape=prices_shape, in_specs=[HBM] * len...  2.89 us
    unnamed x10, local copies, waits for them, and re-layouts  1.59 us
    pallas_call x1, Pallas kernels, body(): pl.pallas_call(functools.partial(combine_kernel, part, held, owner_flips)...  0.9 us
  transfers between devices with their start and end apart: 14, of which 8 were waited for; matrix products, arithmetic and copies ran while one was open for 0% of the time, Pallas kernels for 9%

profile of v3, /device:TPU:0, one launch (start us, length us, event | category | flops | bytes accessed | tf_op | source)
XLA Modules:
  0.0 39.0 jit_solution(854075492582067753)
XLA Ops:
  0.6 0.7 %copy-done.3 = s32[256,2]{0,1:T(2,128)S(1)} copy-done((s32[256,2]{0,1:T(2,128)S(1)}, s32[256,2]{0,1:T(2,128)}, u32[]{:S(2)}) %copy-start.3) | copy-done | bytes 2072
  1.3 0.0 copy-done.4
  1.3 0.9 %copy-done.1 = bf16[256,2,128]{2,1,0:T(2,128)(2,1)S(1)} copy-done((bf16[256,2,128]{2,1,0:T(2,128)(2,1)S(1)}, bf16[256,2,128]{2,1,0:T(2,128)(2,1)}, u32[]{:S(2)}) %copy-start.1) | copy-done | bytes 131096
  2.2 0.4 %pack.1.refs_1_ = bf16[80,256]{1,0:T(8,128)(2,1)S(1)} custom-call(bf16[256,2,128]{2,1,0:T(2,128)(2,1)S(1)} %copy-done.1, s32[3,256]{1,0:T(4,128)S(1)} %pad_add_fusion.trades_ref), custom_call_target="tpu_custom_call" | custom-call | tf_op jit(solution)/shard_map/pack/pallas_call | solution.py:202
  2.7 5.1 %collective-permute-start.2 = (bf16[80,256]{1,0:T(8,128)(2,1)S(1)}, bf16[80,256]{1,0:T(8,128)(2,1)S(1)}, u32[]{:S(2)}, u32[]{:S(2)}) collective-permute-start(bf16[80,256]{1,0:T(8,128)(2,1)S(1)} %pack.1.refs_1_), channel_id=1, source_target_pairs={{0,6},{1,7},{2,4},{3,5},{4,2},{5,3},{6,0},{7,1},{8,14},{9,15},{10,... | collective-permute-start | bytes 122888 | tf_op jit(solution)/shard_map/ppermute | solution.py:176
  7.8 0.6 %collective-permute-start = (bf16[80,256]{1,0:T(8,128)(2,1)S(1)}, bf16[80,256]{1,0:T(8,128)(2,1)S(1)}, u32[]{:S(2)}, u32[]{:S(2)}) collective-permute-start(bf16[80,256]{1,0:T(8,128)(2,1)S(1)} %pack.1.refs_1_), channel_id=1, source_target_pairs={{0,2},{1,3},{2,0},{3,1},{4,6},{5,7},{6,4},{7,5},{8,10},{9,11},{10,... | collective-permute-start | bytes 122888 | tf_op jit(solution)/shard_map/ppermute | solution.py:176
  8.4 2.9 %price.1 = bf16[2,256,256]{2,1,0:T(8,128)(2,1)} custom-call(bf16[256,256]{1,0:T(8,128)(2,1)} %refs_0_.3, f32[1,256]{1,0:T(1,128)} %bitcast.9, f32[1,256]{1,0:T(1,128)} %bitcast.10, f32[1,256]{1,0:T(1,128)} %bitcast.11, bf16[2,256,256]{2,1,0:T(8,128)(2,1)} %refs_4_, s32[2,256,256]{2,1,0:T(8,128)} %refs_5_.1, bf16[2,256,256]{2,1,0:T(8,128)(2,1)} %refs_6_.1), custom_call_target="tpu_custom_call" | custom-call | tf_op jit(solution)/shard_map/price/pallas_call | solution.py:215
  11.3 1.3 %collective-permute-done.1.refs_3_ = bf16[80,256]{1,0:T(8,128)(2,1)S(1)} collective-permute-done((bf16[80,256]{1,0:T(8,128)(2,1)S(1)}, bf16[80,256]{1,0:T(8,128)(2,1)S(1)}, u32[]{:S(2)}, u32[]{:S(2)}) %collective-permute-start.1) | collective-permute-done | bytes 40992 | tf_op jit(solution)/shard_map/ppermute | solution.py:176
  12.7 0.9 %combine.1 = (f32[128,256]{1,0:T(8,128)S(1)}, bf16[128,256]{1,0:T(8,128)(2,1)S(1)}) custom-call(s32[16]{0:T(128)S(1)} %copy-done.2, bf16[80,256]{1,0:T(8,128)(2,1)S(1)} %pack.1.refs_1_, bf16[80,256]{1,0:T(8,128)(2,1)S(1)} %collective-permute-done.refs_2_, bf16[80,256]{1,0:T(8,128)(2,1)S(1)} %collective-permute-done.1.refs_3_, ...), custom_call_target="tpu_custom_call" | custom-call | tf_op jit(solution)/shard_map/combine/pallas_call | solution.py:232
  13.6 1.6 %collective-permute-start.3 = (bf16[128,256]{1,0:T(8,128)(2,1)S(1)}, bf16[128,256]{1,0:T(8,128)(2,1)S(1)}, u32[]{:S(2)}, u32[]{:S(2)}) collective-permute-start(bf16[128,256]{1,0:T(8,128)(2,1)S(1)} %get-tuple-element.14), channel_id=1, source_target_pairs={{0,1},{1,0},{2,3},{3,2},{4,5},{5,4},{6,7},{7,6},{8,9},{9,8},{10,11... | collective-permute-start | bytes 196616 | tf_op jit(solution)/shard_map/ppermute | solution.py:176
  15.1 0.2 collective-permute-start.7
  15.3 2.6 %collective-permute-done.3.other_ref = bf16[128,256]{1,0:T(8,128)(2,1)S(1)} collective-permute-done((bf16[128,256]{1,0:T(8,128)(2,1)S(1)}, bf16[128,256]{1,0:T(8,128)(2,1)S(1)}, u32[]{:S(2)}, u32[]{:S(2)}) %collective-permute-start.3) | collective-permute-done | bytes 65568 | tf_op jit(solution)/shard_map/ppermute | solution.py:176
  17.9 0.1 merge.1.refs_0_
  18.0 0.1 collective-permute-start.6
  18.1 1.6 %collective-permute-start.5 = (bf16[128,256]{1,0:T(8,128)(2,1)S(1)}, bf16[128,256]{1,0:T(8,128)(2,1)S(1)}, u32[]{:S(2)}, u32[]{:S(2)}) collective-permute-start(bf16[128,256]{1,0:T(8,128)(2,1)S(1)} %merge.1.refs_0_), channel_id=1, source_target_pairs={{0,16},{8,24},{16,0},{24,8},{1,17},{9,25},{17,1},{25,9},{2,18},{10... | collective-permute-start | bytes 196616 | tf_op jit(solution)/shard_map/ppermute | solution.py:176
  19.7 0.3 collective-permute-start.4
  19.9 2.5 %collective-permute-done.6.refs_3_ = bf16[128,256]{1,0:T(8,128)(2,1)S(1)} collective-permute-done((bf16[128,256]{1,0:T(8,128)(2,1)S(1)}, bf16[128,256]{1,0:T(8,128)(2,1)S(1)}, u32[]{:S(2)}, u32[]{:S(2)}) %collective-permute-start.6) | collective-permute-done | bytes 65568 | tf_op jit(solution)/shard_map/ppermute | solution.py:176
  22.4 1.5 %collective-permute-done.5.refs_2_ = bf16[128,256]{1,0:T(8,128)(2,1)S(1)} collective-permute-done((bf16[128,256]{1,0:T(8,128)(2,1)S(1)}, bf16[128,256]{1,0:T(8,128)(2,1)S(1)}, u32[]{:S(2)}, u32[]{:S(2)}) %collective-permute-start.5) | collective-permute-done | bytes 65568 | tf_op jit(solution)/shard_map/ppermute | solution.py:176
  23.9 0.4 %value.1 = (f32[64,512]{1,0:T(8,128)S(1)}, bf16[64,512]{1,0:T(8,128)(2,1)S(1)}, bf16[64,512]{1,0:T(8,128)(2,1)S(1)}, bf16[64,512]{1,0:T(8,128)(2,1)S(1)}) custom-call(bf16[128,256]{1,0:T(8,128)(2,1)S(1)} %merge.1.refs_0_, bf16[128,256]{1,0:T(8,128)(2,1)S(1)} %collective-permute-done.4.refs_1_, bf16[128,256]{1,0:T(8,128)(2,1)S(1)} %collective-permute-done.5.refs_2_, ...), custom_call_target="tpu_custom_call" | custom-call | tf_op jit(solution)/shard_map/value/pallas_call | solution.py:260
  24.3 2.1 %collective-permute-start.8 = (bf16[64,512]{1,0:T(8,128)(2,1)S(1)}, bf16[64,512]{1,0:T(8,128)(2,1)S(1)}, u32[]{:S(2)}, u32[]{:S(2)}) collective-permute-start(bf16[64,512]{1,0:T(8,128)(2,1)S(1)} %get-tuple-element.17), channel_id=1, source_target_pairs={{0,4},{1,5},{2,6},{3,7},{4,0},{5,1},{6,2},{7,3},{8,12},{9,13},{10,... | collective-permute-start | bytes 196616 | tf_op jit(solution)/shard_map/ppermute | solution.py:176
  26.4 1.8 %collective-permute-start.9 = (bf16[64,512]{1,0:T(8,128)(2,1)S(1)}, bf16[64,512]{1,0:T(8,128)(2,1)S(1)}, u32[]{:S(2)}, u32[]{:S(2)}) collective-permute-start(bf16[64,512]{1,0:T(8,128)(2,1)S(1)} %get-tuple-element.18), channel_id=1, source_target_pairs={{0,5},{1,4},{2,7},{3,6},{4,1},{5,0},{6,3},{7,2},{8,13},{9,12},{10,... | collective-permute-start | bytes 196616 | tf_op jit(solution)/shard_map/ppermute | solution.py:176
  28.2 0.5 %collective-permute-start.10 = (bf16[64,512]{1,0:T(8,128)(2,1)S(1)}, bf16[64,512]{1,0:T(8,128)(2,1)S(1)}, u32[]{:S(2)}, u32[]{:S(2)}) collective-permute-start(bf16[64,512]{1,0:T(8,128)(2,1)S(1)} %get-tuple-element.19), channel_id=1, source_target_pairs={{0,1},{1,0},{2,3},{3,2},{4,5},{5,4},{6,7},{7,6},{8,9},{9,8},{10,11... | collective-permute-start | bytes 196616 | tf_op jit(solution)/shard_map/ppermute | solution.py:176
  28.7 1.7 %collective-permute-done.8.refs_1_ = bf16[64,512]{1,0:T(8,128)(2,1)S(1)} collective-permute-done((bf16[64,512]{1,0:T(8,128)(2,1)S(1)}, bf16[64,512]{1,0:T(8,128)(2,1)S(1)}, u32[]{:S(2)}, u32[]{:S(2)}) %collective-permute-start.8) | collective-permute-done | bytes 65568 | tf_op jit(solution)/shard_map/ppermute | solution.py:176
  30.5 3.7 %collective-permute-done.9.refs_2_ = bf16[64,512]{1,0:T(8,128)(2,1)S(1)} collective-permute-done((bf16[64,512]{1,0:T(8,128)(2,1)S(1)}, bf16[64,512]{1,0:T(8,128)(2,1)S(1)}, u32[]{:S(2)}, u32[]{:S(2)}) %collective-permute-start.9) | collective-permute-done | bytes 65568 | tf_op jit(solution)/shard_map/ppermute | solution.py:176
  34.2 0.1 totals.1
  34.3 0.5 %collective-permute-start.13 = (f32[2,64]{1,0:T(2,128)S(1)}, f32[2,64]{1,0:T(2,128)S(1)}, u32[]{:S(2)}, u32[]{:S(2)}) collective-permute-start(f32[2,64]{1,0:T(2,128)S(1)} %totals.1), channel_id=1, source_target_pairs={{0,24},{8,16},{16,8},{24,0},{1,25},{9,17},{17,9},{25,1},{2,26},{10... | collective-permute-start | bytes 1544 | tf_op jit(solution)/shard_map/ppermute | solution.py:176
  34.8 1.2 %collective-permute-start.12 = (f32[2,64]{1,0:T(2,128)S(1)}, f32[2,64]{1,0:T(2,128)S(1)}, u32[]{:S(2)}, u32[]{:S(2)}) collective-permute-start(f32[2,64]{1,0:T(2,128)S(1)} %totals.1), channel_id=1, source_target_pairs={{0,16},{8,24},{16,0},{24,8},{1,17},{9,25},{17,1},{25,9},{2,18},{10... | collective-permute-start | bytes 1544 | tf_op jit(solution)/shard_map/ppermute | solution.py:176
  36.1 0.2 collective-permute-start.11
  36.3 0.7 %expose.1 = f32[2,64,256]{2,1,0:T(8,128)} custom-call(f32[64,512]{1,0:T(8,128)S(1)} %get-tuple-element.16.refs_0_, bf16[64,512]{1,0:T(8,128)(2,1)S(1)} %collective-permute-done.8.refs_1_, bf16[64,512]{1,0:T(8,128)(2,1)S(1)} %collective-permute-done.9.refs_2_, bf16[64,512]{1,0:T(8,128)(2,1)S(1)} %collective-permute-done.10.refs_3_), custom_call_target="tpu_custom_call" | custom-call | tf_op jit(solution)/shard_map/expose/pallas_call | solution.py:284
  36.9 0.4 %collective-permute-done.13 = f32[2,64]{1,0:T(2,128)S(1)} collective-permute-done((f32[2,64]{1,0:T(2,128)S(1)}, f32[2,64]{1,0:T(2,128)S(1)}, u32[]{:S(2)}, u32[]{:S(2)}) %collective-permute-start.13) | collective-permute-done | bytes 544 | tf_op jit(solution)/shard_map/ppermute | solution.py:176
  37.4 1.0 %collective-permute-done.12 = f32[2,64]{1,0:T(2,128)S(1)} collective-permute-done((f32[2,64]{1,0:T(2,128)S(1)}, f32[2,64]{1,0:T(2,128)S(1)}, u32[]{:S(2)}, u32[]{:S(2)}) %collective-permute-start.12) | collective-permute-done | bytes 544 | tf_op jit(solution)/shard_map/ppermute | solution.py:176
  38.4 0.6 %add_multiply_fusion = f32[2,64]{1,0:T(2,128)} fusion(f32[2,64]{1,0:T(2,128)S(1)} %collective-permute-done.12, f32[2,64]{1,0:T(2,128)S(1)} %collective-permute-done.13, f32[2,64]{1,0:T(2,128)S(1)} %totals.1, f32[2,64]{1,0:T(2,128)S(1)} %collective-permute-done.11), kind=kLoop, calls=%fused_computation.1 | loop fusion | flops 512 | bytes 2560 | tf_op jit(solution)/shard_map/div | solution.py:295
  (15 shorter events, 0.0 us)
Async XLA Ops:
  0.6 0.7 %copy-start.3 = (s32[256,2]{0,1:T(2,128)S(1)}, s32[256,2]{0,1:T(2,128)}, u32[]{:S(2)}) copy-start(s32[256,2]{0,1:T(2,128)} %param.18) | copy-start | bytes 6148
  0.6 0.7 %copy-start.4 = (s32[256]{0:T(256)S(1)}, s32[256]{0:T(256)}, u32[]{:S(2)}) copy-start(s32[256]{0:T(256)} %param.21) | copy-start | bytes 3076
  1.3 0.9 %copy-start.1 = (bf16[256,2,128]{2,1,0:T(2,128)(2,1)S(1)}, bf16[256,2,128]{2,1,0:T(2,128)(2,1)}, u32[]{:S(2)}) copy-start(bf16[256,2,128]{2,1,0:T(2,128)(2,1)} %weights_ref.1) | copy-start | bytes 393220
  2.7 8.7 %collective-permute-start.2 = (bf16[80,256]{1,0:T(8,128)(2,1)S(1)}, bf16[80,256]{1,0:T(8,128)(2,1)S(1)}, u32[]{:S(2)}, u32[]{:S(2)}) collective-permute-start(bf16[80,256]{1,0:T(8,128)(2,1)S(1)} %pack.1.refs_1_), channel_id=1, source_target_pairs={{0,6},{1,7},{2,4},{3,5},{4,2},{5,3},{6,0},{7,1},{8,14},{9,15},{10,... | collective-permute-start | bytes 122888 | tf_op jit(solution)/shard_map/ppermute | solution.py:176
  7.8 4.9 %collective-permute-start.1 = (bf16[80,256]{1,0:T(8,128)(2,1)S(1)}, bf16[80,256]{1,0:T(8,128)(2,1)S(1)}, u32[]{:S(2)}, u32[]{:S(2)}) collective-permute-start(bf16[80,256]{1,0:T(8,128)(2,1)S(1)} %pack.1.refs_1_), channel_id=1, source_target_pairs={{0,4},{1,5},{2,6},{3,7},{4,0},{5,1},{6,2},{7,3},{8,12},{9,13},{10,... | collective-permute-start | bytes 122888 | tf_op jit(solution)/shard_map/ppermute | solution.py:176
  7.8 4.9 %collective-permute-start = (bf16[80,256]{1,0:T(8,128)(2,1)S(1)}, bf16[80,256]{1,0:T(8,128)(2,1)S(1)}, u32[]{:S(2)}, u32[]{:S(2)}) collective-permute-start(bf16[80,256]{1,0:T(8,128)(2,1)S(1)} %pack.1.refs_1_), channel_id=1, source_target_pairs={{0,2},{1,3},{2,0},{3,1},{4,6},{5,7},{6,4},{7,5},{8,10},{9,11},{10,... | collective-permute-start | bytes 122888 | tf_op jit(solution)/shard_map/ppermute | solution.py:176
  8.4 4.3 %copy-start.2 = (s32[16]{0:T(128)S(1)}, s32[16]{0:T(128)}, u32[]{:S(2)}) copy-start(s32[16]{0:T(128)} %refs_0_.2) | copy-start | bytes 196
  13.6 4.3 %collective-permute-start.3 = (bf16[128,256]{1,0:T(8,128)(2,1)S(1)}, bf16[128,256]{1,0:T(8,128)(2,1)S(1)}, u32[]{:S(2)}, u32[]{:S(2)}) collective-permute-start(bf16[128,256]{1,0:T(8,128)(2,1)S(1)} %get-tuple-element.14), channel_id=1, source_target_pairs={{0,1},{1,0},{2,3},{3,2},{4,5},{5,4},{6,7},{7,6},{8,9},{9,8},{10,11... | collective-permute-start | bytes 196616 | tf_op jit(solution)/shard_map/ppermute | solution.py:176
  15.1 8.7 %collective-permute-start.7 = (bf16[512,256]{1,0:T(8,128)(2,1)}, bf16[512,256]{1,0:T(8,128)(2,1)S(1)}, u32[]{:S(2)}, u32[]{:S(2)}) collective-permute-start(bf16[512,256]{1,0:T(8,128)(2,1)} %bitcast.6), channel_id=1, source_target_pairs={{0,2},{1,3},{2,0},{3,1},{4,6},{5,7},{6,4},{7,5},{8,10},{9,11},{10,... | collective-permute-start | bytes 786440 | tf_op jit(solution)/shard_map/ppermute | solution.py:176
  17.9 6.0 %copy-start = (bf16[2,256,256]{2,1,0:T(8,128)(2,1)S(1)}, bf16[2,256,256]{2,1,0:T(8,128)(2,1)}, u32[]{:S(2)}) copy-start(bf16[2,256,256]{2,1,0:T(8,128)(2,1)} %price.1) | copy-start | bytes 786436
  18.0 4.4 %collective-permute-start.6 = (bf16[128,256]{1,0:T(8,128)(2,1)S(1)}, bf16[128,256]{1,0:T(8,128)(2,1)S(1)}, u32[]{:S(2)}, u32[]{:S(2)}) collective-permute-start(bf16[128,256]{1,0:T(8,128)(2,1)S(1)} %merge.1.refs_0_), channel_id=1, source_target_pairs={{0,24},{8,16},{16,8},{24,0},{1,25},{9,17},{17,9},{25,1},{2,26},{10... | collective-permute-start | bytes 196616 | tf_op jit(solution)/shard_map/ppermute | solution.py:176
  18.1 5.8 %collective-permute-start.5 = (bf16[128,256]{1,0:T(8,128)(2,1)S(1)}, bf16[128,256]{1,0:T(8,128)(2,1)S(1)}, u32[]{:S(2)}, u32[]{:S(2)}) collective-permute-start(bf16[128,256]{1,0:T(8,128)(2,1)S(1)} %merge.1.refs_0_), channel_id=1, source_target_pairs={{0,16},{8,24},{16,0},{24,8},{1,17},{9,25},{17,1},{25,9},{2,18},{10... | collective-permute-start | bytes 196616 | tf_op jit(solution)/shard_map/ppermute | solution.py:176
  19.7 4.2 %collective-permute-start.4 = (bf16[128,256]{1,0:T(8,128)(2,1)S(1)}, bf16[128,256]{1,0:T(8,128)(2,1)S(1)}, u32[]{:S(2)}, u32[]{:S(2)}) collective-permute-start(bf16[128,256]{1,0:T(8,128)(2,1)S(1)} %merge.1.refs_0_), channel_id=1, source_target_pairs={{0,8},{8,0},{16,24},{24,16},{1,9},{9,1},{17,25},{25,17},{2,10},{10... | collective-permute-start | bytes 196616 | tf_op jit(solution)/shard_map/ppermute | solution.py:176
  24.3 6.2 %collective-permute-start.8 = (bf16[64,512]{1,0:T(8,128)(2,1)S(1)}, bf16[64,512]{1,0:T(8,128)(2,1)S(1)}, u32[]{:S(2)}, u32[]{:S(2)}) collective-permute-start(bf16[64,512]{1,0:T(8,128)(2,1)S(1)} %get-tuple-element.17), channel_id=1, source_target_pairs={{0,4},{1,5},{2,6},{3,7},{4,0},{5,1},{6,2},{7,3},{8,12},{9,13},{10,... | collective-permute-start | bytes 196616 | tf_op jit(solution)/shard_map/ppermute | solution.py:176
  26.4 7.8 %collective-permute-start.9 = (bf16[64,512]{1,0:T(8,128)(2,1)S(1)}, bf16[64,512]{1,0:T(8,128)(2,1)S(1)}, u32[]{:S(2)}, u32[]{:S(2)}) collective-permute-start(bf16[64,512]{1,0:T(8,128)(2,1)S(1)} %get-tuple-element.18), channel_id=1, source_target_pairs={{0,5},{1,4},{2,7},{3,6},{4,1},{5,0},{6,3},{7,2},{8,13},{9,12},{10,... | collective-permute-start | bytes 196616 | tf_op jit(solution)/shard_map/ppermute | solution.py:176
  28.2 6.0 %collective-permute-start.10 = (bf16[64,512]{1,0:T(8,128)(2,1)S(1)}, bf16[64,512]{1,0:T(8,128)(2,1)S(1)}, u32[]{:S(2)}, u32[]{:S(2)}) collective-permute-start(bf16[64,512]{1,0:T(8,128)(2,1)S(1)} %get-tuple-element.19), channel_id=1, source_target_pairs={{0,1},{1,0},{2,3},{3,2},{4,5},{5,4},{6,7},{7,6},{8,9},{9,8},{10,11... | collective-permute-start | bytes 196616 | tf_op jit(solution)/shard_map/ppermute | solution.py:176
  34.3 3.1 %collective-permute-start.13 = (f32[2,64]{1,0:T(2,128)S(1)}, f32[2,64]{1,0:T(2,128)S(1)}, u32[]{:S(2)}, u32[]{:S(2)}) collective-permute-start(f32[2,64]{1,0:T(2,128)S(1)} %totals.1), channel_id=1, source_target_pairs={{0,24},{8,16},{16,8},{24,0},{1,25},{9,17},{17,9},{25,1},{2,26},{10... | collective-permute-start | bytes 1544 | tf_op jit(solution)/shard_map/ppermute | solution.py:176
  34.8 3.6 %collective-permute-start.12 = (f32[2,64]{1,0:T(2,128)S(1)}, f32[2,64]{1,0:T(2,128)S(1)}, u32[]{:S(2)}, u32[]{:S(2)}) collective-permute-start(f32[2,64]{1,0:T(2,128)S(1)} %totals.1), channel_id=1, source_target_pairs={{0,16},{8,24},{16,0},{24,8},{1,17},{9,25},{17,1},{25,9},{2,18},{10... | collective-permute-start | bytes 1544 | tf_op jit(solution)/shard_map/ppermute | solution.py:176
  36.1 2.3 %collective-permute-start.11 = (f32[2,64]{1,0:T(2,128)S(1)}, f32[2,64]{1,0:T(2,128)S(1)}, u32[]{:S(2)}, u32[]{:S(2)}) collective-permute-start(f32[2,64]{1,0:T(2,128)S(1)} %totals.1), channel_id=1, source_target_pairs={{0,8},{8,0},{16,24},{24,16},{1,9},{9,1},{17,25},{25,17},{2,10},{10... | collective-permute-start | bytes 1544 | tf_op jit(solution)/shard_map/ppermute | solution.py:176

commit v4 on v3

--- a/solution.py
+++ b/solution.py
@@ -197,7 +197,7 @@
     trades = trade_weights.shape[0]
     part = BLOCK // scen_count
     column_flips = [i for i in range(fac_count) if not i & SIDE_FLIP]
-    owner_flips = [i for i in range(fac_count) if not i & PRICE_FLIP]
+    owner_flips = [i for i in range(fac_count) if (i // PRICE_FLIP) % 4 in (0, 3)]
 
     packet = pl.pallas_call(
         functools.partial(pack_kernel, part),
@@ -207,7 +207,8 @@
         compiler_params=PARAMS,
         name="pack",
     )(trade_weights, jnp.concatenate([dependencies.T, netting[None]]))
-    packets = [packet] + [from_partner(packet, "fac", i) for i in column_flips[1:]]
+    order = column_flips[1:2] + column_flips[:1:-1]
+    packets = [packet] + [from_partner(packet, "fac", i) for i in order]
 
     packet, shocks = lax.optimization_barrier((packet, shocks))
     inputs = (loadings, vol[None], jump_mean[None], jump_vol[None], shocks, jump_counts, jump_noise)
@@ -255,7 +256,10 @@
         cost_estimate=pl.CostEstimate(flops=10**10, bytes_accessed=0, transcendentals=0),
         name="merge",
     )(own, from_partner(other, "fac", SIDE_FLIP))
-    shares = [share] + [from_partner(share, "scen", i) for i in range(1, scen_count)]
+    shares = [share]
+    for i in range(2, scen_count, 2):
+        shares.append(from_partner(share, "scen", i))
+    shares = sum([[x, from_partner(x, "scen", 1)] for x in shares], [])
 
     parts = pl.pallas_call(
         functools.partial(value_kernel, part, held, scen_count),

time: 39.2 us -> 38.8 us (0.990)
  waiting for transfers between devices: 14.8 us -> 13.6 us
  starting transfers between devices: 15.8 us -> 16.6 us
    ppermute x14, waiting for transfers between devices: 14.8 us -> 13.6 us  [from_partner(): return lax.ppermute(x, axis, [(i, i ^ flip) for i in range(count)])]
    ppermute x14, starting transfers between devices: 15.8 us -> 16.6 us  [from_partner(): return lax.ppermute(x, axis, [(i, i ^ flip) for i in range(count)])]
  transfers between devices with their start and end apart: 14 -> 14, of which waited for: 8 -> 9; matrix products, arithmetic and copies ran while one was open for 0% -> 0% of each run, Pallas kernels for 9% -> 9%
where the time goes in v4:
time: 38.8 us; the launch traced here: 38.6 us
  starting transfers between devices  16.6 us (43%)
  waiting for transfers between devices  13.6 us (35%)
  Pallas kernels  5.48 us (14%)
  local copies, waits for them, and re-layouts  1.59 us (4%)
  between operations  0.71 us (2%)
  other arithmetic  0.58 us (1%)
    ppermute x14, starting transfers between devices, from_partner(): return lax.ppermute(x, axis, [(i, i ^ flip) for i in range(count)])  16.6 us
    ppermute x14, waiting for transfers between devices, from_partner(): return lax.ppermute(x, axis, [(i, i ^ flip) for i in range(count)])  13.6 us
    pallas_call x1, Pallas kernels, body(): pl.pallas_call(price_kernel, out_shape=prices_shape, in_specs=[HBM] * len...  2.89 us
    unnamed x10, local copies, waits for them, and re-layouts  1.59 us
    pallas_call x1, Pallas kernels, body(): pl.pallas_call(functools.partial(combine_kernel, part, held, owner_flips)...  0.9 us
  transfers between devices with their start and end apart: 14, of which 9 were waited for; matrix products, arithmetic and copies ran while one was open for 0% of the time, Pallas kernels for 9%

profile of v4, /device:TPU:0, one launch (start us, length us, event | category | flops | bytes accessed | tf_op | source)
XLA Modules:
  0.0 38.6 jit_solution(14308870171931076402)
XLA Ops:
  0.6 0.7 %copy-done.3 = s32[256,2]{0,1:T(2,128)S(1)} copy-done((s32[256,2]{0,1:T(2,128)S(1)}, s32[256,2]{0,1:T(2,128)}, u32[]{:S(2)}) %copy-start.3) | copy-done | bytes 2072
  1.3 0.0 copy-done.4
  1.3 0.9 %copy-done.1 = bf16[256,2,128]{2,1,0:T(2,128)(2,1)S(1)} copy-done((bf16[256,2,128]{2,1,0:T(2,128)(2,1)S(1)}, bf16[256,2,128]{2,1,0:T(2,128)(2,1)}, u32[]{:S(2)}) %copy-start.1) | copy-done | bytes 131096
  2.2 0.4 %pack.1.refs_1_ = bf16[80,256]{1,0:T(8,128)(2,1)S(1)} custom-call(bf16[256,2,128]{2,1,0:T(2,128)(2,1)S(1)} %copy-done.1, s32[3,256]{1,0:T(4,128)S(1)} %pad_add_fusion.trades_ref), custom_call_target="tpu_custom_call" | custom-call | tf_op jit(solution)/shard_map/pack/pallas_call | solution.py:202
  2.7 4.1 %collective-permute-start.2 = (bf16[80,256]{1,0:T(8,128)(2,1)S(1)}, bf16[80,256]{1,0:T(8,128)(2,1)S(1)}, u32[]{:S(2)}, u32[]{:S(2)}) collective-permute-start(bf16[80,256]{1,0:T(8,128)(2,1)S(1)} %pack.1.refs_1_), channel_id=1, source_target_pairs={{0,4},{1,5},{2,6},{3,7},{4,0},{5,1},{6,2},{7,3},{8,12},{9,13},{10,... | collective-permute-start | bytes 122888 | tf_op jit(solution)/shard_map/ppermute | solution.py:176
  6.8 1.3 %collective-permute-start.1 = (bf16[80,256]{1,0:T(8,128)(2,1)S(1)}, bf16[80,256]{1,0:T(8,128)(2,1)S(1)}, u32[]{:S(2)}, u32[]{:S(2)}) collective-permute-start(bf16[80,256]{1,0:T(8,128)(2,1)S(1)} %pack.1.refs_1_), channel_id=1, source_target_pairs={{0,6},{1,7},{2,4},{3,5},{4,2},{5,3},{6,0},{7,1},{8,14},{9,15},{10,... | collective-permute-start | bytes 122888 | tf_op jit(solution)/shard_map/ppermute | solution.py:176
  8.1 0.2 collective-permute-start
  8.3 2.9 %price.1 = bf16[2,256,256]{2,1,0:T(8,128)(2,1)} custom-call(bf16[256,256]{1,0:T(8,128)(2,1)} %refs_0_.3, f32[1,256]{1,0:T(1,128)} %bitcast.9, f32[1,256]{1,0:T(1,128)} %bitcast.10, f32[1,256]{1,0:T(1,128)} %bitcast.11, bf16[2,256,256]{2,1,0:T(8,128)(2,1)} %refs_4_, s32[2,256,256]{2,1,0:T(8,128)} %refs_5_.1, bf16[2,256,256]{2,1,0:T(8,128)(2,1)} %refs_6_.1), custom_call_target="tpu_custom_call" | custom-call | tf_op jit(solution)/shard_map/price/pallas_call | solution.py:216
  11.2 1.3 %collective-permute-done.1.refs_3_ = bf16[80,256]{1,0:T(8,128)(2,1)S(1)} collective-permute-done((bf16[80,256]{1,0:T(8,128)(2,1)S(1)}, bf16[80,256]{1,0:T(8,128)(2,1)S(1)}, u32[]{:S(2)}, u32[]{:S(2)}) %collective-permute-start.1) | collective-permute-done | bytes 40992 | tf_op jit(solution)/shard_map/ppermute | solution.py:176
  12.6 0.9 %combine.1 = (f32[128,256]{1,0:T(8,128)S(1)}, bf16[128,256]{1,0:T(8,128)(2,1)S(1)}) custom-call(s32[16]{0:T(128)S(1)} %copy-done.2, bf16[80,256]{1,0:T(8,128)(2,1)S(1)} %pack.1.refs_1_, bf16[80,256]{1,0:T(8,128)(2,1)S(1)} %collective-permute-done.refs_2_, bf16[80,256]{1,0:T(8,128)(2,1)S(1)} %collective-permute-done.1.refs_3_, ...), custom_call_target="tpu_custom_call" | custom-call | tf_op jit(solution)/shard_map/combine/pallas_call | solution.py:233
  13.5 1.6 %collective-permute-start.3 = (bf16[128,256]{1,0:T(8,128)(2,1)S(1)}, bf16[128,256]{1,0:T(8,128)(2,1)S(1)}, u32[]{:S(2)}, u32[]{:S(2)}) collective-permute-start(bf16[128,256]{1,0:T(8,128)(2,1)S(1)} %get-tuple-element.14), channel_id=1, source_target_pairs={{0,1},{1,0},{2,3},{3,2},{4,5},{5,4},{6,7},{7,6},{8,9},{9,8},{10,11... | collective-permute-start | bytes 196616 | tf_op jit(solution)/shard_map/ppermute | solution.py:176
  15.0 0.5 %collective-permute-start.7 = (bf16[512,256]{1,0:T(8,128)(2,1)}, bf16[512,256]{1,0:T(8,128)(2,1)S(1)}, u32[]{:S(2)}, u32[]{:S(2)}) collective-permute-start(bf16[512,256]{1,0:T(8,128)(2,1)} %bitcast.6), channel_id=1, source_target_pairs={{0,2},{1,3},{2,0},{3,1},{4,6},{5,7},{6,4},{7,5},{8,10},{9,11},{10,... | collective-permute-start | bytes 786440 | tf_op jit(solution)/shard_map/ppermute | solution.py:176
  15.5 2.3 %collective-permute-done.3.other_ref = bf16[128,256]{1,0:T(8,128)(2,1)S(1)} collective-permute-done((bf16[128,256]{1,0:T(8,128)(2,1)S(1)}, bf16[128,256]{1,0:T(8,128)(2,1)S(1)}, u32[]{:S(2)}, u32[]{:S(2)}) %collective-permute-start.3) | collective-permute-done | bytes 65568 | tf_op jit(solution)/shard_map/ppermute | solution.py:176
  17.8 0.1 merge.1.refs_0_
  17.9 1.6 %collective-permute-start.5 = (bf16[128,256]{1,0:T(8,128)(2,1)S(1)}, bf16[128,256]{1,0:T(8,128)(2,1)S(1)}, u32[]{:S(2)}, u32[]{:S(2)}) collective-permute-start(bf16[128,256]{1,0:T(8,128)(2,1)S(1)} %merge.1.refs_0_), channel_id=1, source_target_pairs={{0,16},{8,24},{16,0},{24,8},{1,17},{9,25},{17,1},{25,9},{2,18},{10... | collective-permute-start | bytes 196616 | tf_op jit(solution)/shard_map/ppermute | solution.py:176
  19.5 2.7 %collective-permute-done.5.refs_2_ = bf16[128,256]{1,0:T(8,128)(2,1)S(1)} collective-permute-done((bf16[128,256]{1,0:T(8,128)(2,1)S(1)}, bf16[128,256]{1,0:T(8,128)(2,1)S(1)}, u32[]{:S(2)}, u32[]{:S(2)}) %collective-permute-start.5) | collective-permute-done | bytes 65568 | tf_op jit(solution)/shard_map/ppermute | solution.py:176
  22.2 1.2 %collective-permute-done.6.refs_3_ = bf16[128,256]{1,0:T(8,128)(2,1)S(1)} collective-permute-done((bf16[128,256]{1,0:T(8,128)(2,1)S(1)}, bf16[128,256]{1,0:T(8,128)(2,1)S(1)}, u32[]{:S(2)}, u32[]{:S(2)}) %collective-permute-start.6) | collective-permute-done | bytes 65568 | tf_op jit(solution)/shard_map/ppermute | solution.py:176
  23.5 0.4 %value.1 = (f32[64,512]{1,0:T(8,128)S(1)}, bf16[64,512]{1,0:T(8,128)(2,1)S(1)}, bf16[64,512]{1,0:T(8,128)(2,1)S(1)}, bf16[64,512]{1,0:T(8,128)(2,1)S(1)}) custom-call(bf16[128,256]{1,0:T(8,128)(2,1)S(1)} %merge.1.refs_0_, bf16[128,256]{1,0:T(8,128)(2,1)S(1)} %collective-permute-done.4.refs_1_, bf16[128,256]{1,0:T(8,128)(2,1)S(1)} %collective-permute-done.5.refs_2_, ...), custom_call_target="tpu_custom_call" | custom-call | tf_op jit(solution)/shard_map/value/pallas_call | solution.py:264
  23.9 2.1 %collective-permute-start.8 = (bf16[64,512]{1,0:T(8,128)(2,1)S(1)}, bf16[64,512]{1,0:T(8,128)(2,1)S(1)}, u32[]{:S(2)}, u32[]{:S(2)}) collective-permute-start(bf16[64,512]{1,0:T(8,128)(2,1)S(1)} %get-tuple-element.17), channel_id=1, source_target_pairs={{0,6},{1,7},{2,4},{3,5},{4,2},{5,3},{6,0},{7,1},{8,14},{9,15},{10,... | collective-permute-start | bytes 196616 | tf_op jit(solution)/shard_map/ppermute | solution.py:176
  26.0 2.7 %collective-permute-start.9 = (bf16[64,512]{1,0:T(8,128)(2,1)S(1)}, bf16[64,512]{1,0:T(8,128)(2,1)S(1)}, u32[]{:S(2)}, u32[]{:S(2)}) collective-permute-start(bf16[64,512]{1,0:T(8,128)(2,1)S(1)} %get-tuple-element.18), channel_id=1, source_target_pairs={{0,7},{1,6},{2,5},{3,4},{4,3},{5,2},{6,1},{7,0},{8,15},{9,14},{10,... | collective-permute-start | bytes 196616 | tf_op jit(solution)/shard_map/ppermute | solution.py:176
  28.7 0.5 %collective-permute-start.10 = (bf16[64,512]{1,0:T(8,128)(2,1)S(1)}, bf16[64,512]{1,0:T(8,128)(2,1)S(1)}, u32[]{:S(2)}, u32[]{:S(2)}) collective-permute-start(bf16[64,512]{1,0:T(8,128)(2,1)S(1)} %get-tuple-element.19), channel_id=1, source_target_pairs={{0,1},{1,0},{2,3},{3,2},{4,5},{5,4},{6,7},{7,6},{8,9},{9,8},{10,11... | collective-permute-start | bytes 196616 | tf_op jit(solution)/shard_map/ppermute | solution.py:176
  29.2 0.8 %collective-permute-done.8.refs_1_ = bf16[64,512]{1,0:T(8,128)(2,1)S(1)} collective-permute-done((bf16[64,512]{1,0:T(8,128)(2,1)S(1)}, bf16[64,512]{1,0:T(8,128)(2,1)S(1)}, u32[]{:S(2)}, u32[]{:S(2)}) %collective-permute-start.8) | collective-permute-done | bytes 65568 | tf_op jit(solution)/shard_map/ppermute | solution.py:176
  30.0 3.0 %collective-permute-done.9.refs_2_ = bf16[64,512]{1,0:T(8,128)(2,1)S(1)} collective-permute-done((bf16[64,512]{1,0:T(8,128)(2,1)S(1)}, bf16[64,512]{1,0:T(8,128)(2,1)S(1)}, u32[]{:S(2)}, u32[]{:S(2)}) %collective-permute-start.9) | collective-permute-done | bytes 65568 | tf_op jit(solution)/shard_map/ppermute | solution.py:176
  33.0 0.7 %collective-permute-done.10.refs_3_ = bf16[64,512]{1,0:T(8,128)(2,1)S(1)} collective-permute-done((bf16[64,512]{1,0:T(8,128)(2,1)S(1)}, bf16[64,512]{1,0:T(8,128)(2,1)S(1)}, u32[]{:S(2)}, u32[]{:S(2)}) %collective-permute-start.10) | collective-permute-done | bytes 65568 | tf_op jit(solution)/shard_map/ppermute | solution.py:176
  33.7 0.1 totals.1
  33.8 0.6 %collective-permute-start.13 = (f32[2,64]{1,0:T(2,128)S(1)}, f32[2,64]{1,0:T(2,128)S(1)}, u32[]{:S(2)}, u32[]{:S(2)}) collective-permute-start(f32[2,64]{1,0:T(2,128)S(1)} %totals.1), channel_id=1, source_target_pairs={{0,24},{8,16},{16,8},{24,0},{1,25},{9,17},{17,9},{25,1},{2,26},{10... | collective-permute-start | bytes 1544 | tf_op jit(solution)/shard_map/ppermute | solution.py:176
  34.4 1.1 %collective-permute-start.12 = (f32[2,64]{1,0:T(2,128)S(1)}, f32[2,64]{1,0:T(2,128)S(1)}, u32[]{:S(2)}, u32[]{:S(2)}) collective-permute-start(f32[2,64]{1,0:T(2,128)S(1)} %totals.1), channel_id=1, source_target_pairs={{0,16},{8,24},{16,0},{24,8},{1,17},{9,25},{17,1},{25,9},{2,18},{10... | collective-permute-start | bytes 1544 | tf_op jit(solution)/shard_map/ppermute | solution.py:176
  35.5 0.3 collective-permute-start.11
  35.7 0.7 %expose.1 = f32[2,64,256]{2,1,0:T(8,128)} custom-call(f32[64,512]{1,0:T(8,128)S(1)} %get-tuple-element.16.refs_0_, bf16[64,512]{1,0:T(8,128)(2,1)S(1)} %collective-permute-done.8.refs_1_, bf16[64,512]{1,0:T(8,128)(2,1)S(1)} %collective-permute-done.9.refs_2_, bf16[64,512]{1,0:T(8,128)(2,1)S(1)} %collective-permute-done.10.refs_3_), custom_call_target="tpu_custom_call" | custom-call | tf_op jit(solution)/shard_map/expose/pallas_call | solution.py:288
  36.4 0.4 %collective-permute-done.13 = f32[2,64]{1,0:T(2,128)S(1)} collective-permute-done((f32[2,64]{1,0:T(2,128)S(1)}, f32[2,64]{1,0:T(2,128)S(1)}, u32[]{:S(2)}, u32[]{:S(2)}) %collective-permute-start.13) | collective-permute-done | bytes 544 | tf_op jit(solution)/shard_map/ppermute | solution.py:176
  36.9 1.1 %collective-permute-done.12 = f32[2,64]{1,0:T(2,128)S(1)} collective-permute-done((f32[2,64]{1,0:T(2,128)S(1)}, f32[2,64]{1,0:T(2,128)S(1)}, u32[]{:S(2)}, u32[]{:S(2)}) %collective-permute-start.12) | collective-permute-done | bytes 544 | tf_op jit(solution)/shard_map/ppermute | solution.py:176
  38.0 0.6 %add_multiply_fusion = f32[2,64]{1,0:T(2,128)} fusion(f32[2,64]{1,0:T(2,128)S(1)} %collective-permute-done.12, f32[2,64]{1,0:T(2,128)S(1)} %collective-permute-done.13, f32[2,64]{1,0:T(2,128)S(1)} %totals.1, f32[2,64]{1,0:T(2,128)S(1)} %collective-permute-done.11), kind=kLoop, calls=%fused_computation.1 | loop fusion | flops 512 | bytes 2560 | tf_op jit(solution)/shard_map/div | solution.py:299
  (15 shorter events, 0.0 us)
Async XLA Ops:
  0.6 0.7 %copy-start.3 = (s32[256,2]{0,1:T(2,128)S(1)}, s32[256,2]{0,1:T(2,128)}, u32[]{:S(2)}) copy-start(s32[256,2]{0,1:T(2,128)} %param.18) | copy-start | bytes 6148
  0.6 0.7 %copy-start.4 = (s32[256]{0:T(256)S(1)}, s32[256]{0:T(256)}, u32[]{:S(2)}) copy-start(s32[256]{0:T(256)} %param.21) | copy-start | bytes 3076
  1.3 0.9 %copy-start.1 = (bf16[256,2,128]{2,1,0:T(2,128)(2,1)S(1)}, bf16[256,2,128]{2,1,0:T(2,128)(2,1)}, u32[]{:S(2)}) copy-start(bf16[256,2,128]{2,1,0:T(2,128)(2,1)} %weights_ref.1) | copy-start | bytes 393220
  2.7 8.6 %collective-permute-start.2 = (bf16[80,256]{1,0:T(8,128)(2,1)S(1)}, bf16[80,256]{1,0:T(8,128)(2,1)S(1)}, u32[]{:S(2)}, u32[]{:S(2)}) collective-permute-start(bf16[80,256]{1,0:T(8,128)(2,1)S(1)} %pack.1.refs_1_), channel_id=1, source_target_pairs={{0,4},{1,5},{2,6},{3,7},{4,0},{5,1},{6,2},{7,3},{8,12},{9,13},{10,... | collective-permute-start | bytes 122888 | tf_op jit(solution)/shard_map/ppermute | solution.py:176
  6.8 5.8 %collective-permute-start.1 = (bf16[80,256]{1,0:T(8,128)(2,1)S(1)}, bf16[80,256]{1,0:T(8,128)(2,1)S(1)}, u32[]{:S(2)}, u32[]{:S(2)}) collective-permute-start(bf16[80,256]{1,0:T(8,128)(2,1)S(1)} %pack.1.refs_1_), channel_id=1, source_target_pairs={{0,6},{1,7},{2,4},{3,5},{4,2},{5,3},{6,0},{7,1},{8,14},{9,15},{10,... | collective-permute-start | bytes 122888 | tf_op jit(solution)/shard_map/ppermute | solution.py:176
  8.1 4.5 %collective-permute-start = (bf16[80,256]{1,0:T(8,128)(2,1)S(1)}, bf16[80,256]{1,0:T(8,128)(2,1)S(1)}, u32[]{:S(2)}, u32[]{:S(2)}) collective-permute-start(bf16[80,256]{1,0:T(8,128)(2,1)S(1)} %pack.1.refs_1_), channel_id=1, source_target_pairs={{0,2},{1,3},{2,0},{3,1},{4,6},{5,7},{6,4},{7,5},{8,10},{9,11},{10,... | collective-permute-start | bytes 122888 | tf_op jit(solution)/shard_map/ppermute | solution.py:176
  8.3 4.2 %copy-start.2 = (s32[16]{0:T(128)S(1)}, s32[16]{0:T(128)}, u32[]{:S(2)}) copy-start(s32[16]{0:T(128)} %refs_0_.2) | copy-start | bytes 196
  13.5 4.3 %collective-permute-start.3 = (bf16[128,256]{1,0:T(8,128)(2,1)S(1)}, bf16[128,256]{1,0:T(8,128)(2,1)S(1)}, u32[]{:S(2)}, u32[]{:S(2)}) collective-permute-start(bf16[128,256]{1,0:T(8,128)(2,1)S(1)} %get-tuple-element.14), channel_id=1, source_target_pairs={{0,1},{1,0},{2,3},{3,2},{4,5},{5,4},{6,7},{7,6},{8,9},{9,8},{10,11... | collective-permute-start | bytes 196616 | tf_op jit(solution)/shard_map/ppermute | solution.py:176
  15.0 8.5 %collective-permute-start.7 = (bf16[512,256]{1,0:T(8,128)(2,1)}, bf16[512,256]{1,0:T(8,128)(2,1)S(1)}, u32[]{:S(2)}, u32[]{:S(2)}) collective-permute-start(bf16[512,256]{1,0:T(8,128)(2,1)} %bitcast.6), channel_id=1, source_target_pairs={{0,2},{1,3},{2,0},{3,1},{4,6},{5,7},{6,4},{7,5},{8,10},{9,11},{10,... | collective-permute-start | bytes 786440 | tf_op jit(solution)/shard_map/ppermute | solution.py:176
  17.8 5.7 %copy-start = (bf16[2,256,256]{2,1,0:T(8,128)(2,1)S(1)}, bf16[2,256,256]{2,1,0:T(8,128)(2,1)}, u32[]{:S(2)}) copy-start(bf16[2,256,256]{2,1,0:T(8,128)(2,1)} %price.1) | copy-start | bytes 786436
  17.9 4.3 %collective-permute-start.5 = (bf16[128,256]{1,0:T(8,128)(2,1)S(1)}, bf16[128,256]{1,0:T(8,128)(2,1)S(1)}, u32[]{:S(2)}, u32[]{:S(2)}) collective-permute-start(bf16[128,256]{1,0:T(8,128)(2,1)S(1)} %merge.1.refs_0_), channel_id=1, source_target_pairs={{0,16},{8,24},{16,0},{24,8},{1,17},{9,25},{17,1},{25,9},{2,18},{10... | collective-permute-start | bytes 196616 | tf_op jit(solution)/shard_map/ppermute | solution.py:176
  19.5 2.8 %collective-permute-start.4 = (bf16[128,256]{1,0:T(8,128)(2,1)S(1)}, bf16[128,256]{1,0:T(8,128)(2,1)S(1)}, u32[]{:S(2)}, u32[]{:S(2)}) collective-permute-start(bf16[128,256]{1,0:T(8,128)(2,1)S(1)} %merge.1.refs_0_), channel_id=1, source_target_pairs={{0,8},{8,0},{16,24},{24,16},{1,9},{9,1},{17,25},{25,17},{2,10},{10... | collective-permute-start | bytes 196616 | tf_op jit(solution)/shard_map/ppermute | solution.py:176
  22.2 1.3 %collective-permute-start.6 = (bf16[128,256]{1,0:T(8,128)(2,1)S(1)}, bf16[128,256]{1,0:T(8,128)(2,1)S(1)}, u32[]{:S(2)}, u32[]{:S(2)}) collective-permute-start(bf16[128,256]{1,0:T(8,128)(2,1)S(1)} %collective-permute-done.5.refs_2_), channel_id=1, source_target_pairs={{0,8},{8,0},{16,24},{24,16},{1,9},{9,1},{17,25},{25,17},{2,10},{10... | collective-permute-start | bytes 196616 | tf_op jit(solution)/shard_map/ppermute | solution.py:176
  23.9 6.1 %collective-permute-start.8 = (bf16[64,512]{1,0:T(8,128)(2,1)S(1)}, bf16[64,512]{1,0:T(8,128)(2,1)S(1)}, u32[]{:S(2)}, u32[]{:S(2)}) collective-permute-start(bf16[64,512]{1,0:T(8,128)(2,1)S(1)} %get-tuple-element.17), channel_id=1, source_target_pairs={{0,6},{1,7},{2,4},{3,5},{4,2},{5,3},{6,0},{7,1},{8,14},{9,15},{10,... | collective-permute-start | bytes 196616 | tf_op jit(solution)/shard_map/ppermute | solution.py:176
  26.0 7.0 %collective-permute-start.9 = (bf16[64,512]{1,0:T(8,128)(2,1)S(1)}, bf16[64,512]{1,0:T(8,128)(2,1)S(1)}, u32[]{:S(2)}, u32[]{:S(2)}) collective-permute-start(bf16[64,512]{1,0:T(8,128)(2,1)S(1)} %get-tuple-element.18), channel_id=1, source_target_pairs={{0,7},{1,6},{2,5},{3,4},{4,3},{5,2},{6,1},{7,0},{8,15},{9,14},{10,... | collective-permute-start | bytes 196616 | tf_op jit(solution)/shard_map/ppermute | solution.py:176
  28.7 5.0 %collective-permute-start.10 = (bf16[64,512]{1,0:T(8,128)(2,1)S(1)}, bf16[64,512]{1,0:T(8,128)(2,1)S(1)}, u32[]{:S(2)}, u32[]{:S(2)}) collective-permute-start(bf16[64,512]{1,0:T(8,128)(2,1)S(1)} %get-tuple-element.19), channel_id=1, source_target_pairs={{0,1},{1,0},{2,3},{3,2},{4,5},{5,4},{6,7},{7,6},{8,9},{9,8},{10,11... | collective-permute-start | bytes 196616 | tf_op jit(solution)/shard_map/ppermute | solution.py:176
  33.8 3.1 %collective-permute-start.13 = (f32[2,64]{1,0:T(2,128)S(1)}, f32[2,64]{1,0:T(2,128)S(1)}, u32[]{:S(2)}, u32[]{:S(2)}) collective-permute-start(f32[2,64]{1,0:T(2,128)S(1)} %totals.1), channel_id=1, source_target_pairs={{0,24},{8,16},{16,8},{24,0},{1,25},{9,17},{17,9},{25,1},{2,26},{10... | collective-permute-start | bytes 1544 | tf_op jit(solution)/shard_map/ppermute | solution.py:176
  34.4 3.6 %collective-permute-start.12 = (f32[2,64]{1,0:T(2,128)S(1)}, f32[2,64]{1,0:T(2,128)S(1)}, u32[]{:S(2)}, u32[]{:S(2)}) collective-permute-start(f32[2,64]{1,0:T(2,128)S(1)} %totals.1), channel_id=1, source_target_pairs={{0,16},{8,24},{16,0},{24,8},{1,17},{9,25},{17,1},{25,9},{2,18},{10... | collective-permute-start | bytes 1544 | tf_op jit(solution)/shard_map/ppermute | solution.py:176
  35.5 2.5 %collective-permute-start.11 = (f32[2,64]{1,0:T(2,128)S(1)}, f32[2,64]{1,0:T(2,128)S(1)}, u32[]{:S(2)}, u32[]{:S(2)}) collective-permute-start(f32[2,64]{1,0:T(2,128)S(1)} %totals.1), channel_id=1, source_target_pairs={{0,8},{8,0},{16,24},{24,16},{1,9},{9,1},{17,25},{25,17},{2,10},{10... | collective-permute-start | bytes 1544 | tf_op jit(solution)/shard_map/ppermute | solution.py:176

commit v5 on v4

--- a/solution.py
+++ b/solution.py
@@ -94,8 +94,8 @@
 
 
 def combine_kernel(part, held, flips, *refs):
-    slot_ref, packet_refs = refs[0], refs[1:-4]
-    own_ref, other_ref, chosen_ref, marks_ref = refs[-4:]
+    slot_ref, packet_refs = refs[0], refs[1:-5]
+    own_ref, narrow_ref, other_ref, chosen_ref, marks_ref = refs[-5:]
     fac = lax.axis_index("fac")
     names = []
     for flip in (0, PRICE_FLIP, SIDE_FLIP, SIDE_FLIP ^ PRICE_FLIP):
@@ -124,25 +124,32 @@
     sums = f32_dot(chosen_ref[...], marks_ref[...], NT)
     half = own_ref.shape[0]
     own_ref[...] = sums[:half]
+    narrow_ref[...] = sums[:half].astype(jnp.bfloat16)
     other_ref[...] = sums[half:].astype(jnp.bfloat16)
 
 
-def merge_kernel(own_ref, other_ref, share_ref):
+def merge_kernel(*refs):
+    part_refs, shares_ref = refs[:-1], refs[-1]
+    rows, columns = part_refs[0].shape
     pair = 2 * SET_DEV
-    for at in range(0, own_ref.shape[1], pair):
-        other = pltpu.roll(other_ref[:, at : at + pair].astype(jnp.float32), SET_DEV, 1)
-        share_ref[:, at : at + pair] = (own_ref[:, at : at + pair] + other).astype(jnp.bfloat16)
+    for i in range(len(part_refs) // 2):
+        own_ref, other_ref = part_refs[2 * i : 2 * i + 2]
+        for at in range(0, columns, pair):
+            own = own_ref[:, at : at + pair].astype(jnp.float32)
+            other = pltpu.roll(other_ref[:, at : at + pair].astype(jnp.float32), SET_DEV, 1)
+            shares_ref[i * rows : (i + 1) * rows, at : at + pair] = (own + other).astype(jnp.bfloat16)
 
 
 def value_kernel(part, held, scen_count, *refs):
-    share_refs, price_refs = refs[:scen_count], refs[scen_count : scen_count + 2]
-    out_refs, whole_ref = refs[scen_count + 2 : -1], refs[-1]
+    cores_refs, price_refs = refs[:2], refs[2:4]
+    out_refs, whole_ref = refs[4:-1], refs[-1]
     scen = lax.axis_index("scen")
-    for i, share_ref in enumerate(share_refs):
+    for i in range(scen_count):
         column = (scen ^ i) * part
         for b in range(2 * held):
+            row = (i // 2 * 2 * held + b) * part
             at = pl.ds(pl.multiple_of(b * BLOCK + column, part), part)
-            whole_ref[at, :] = share_ref[b * part : (b + 1) * part, :].astype(jnp.float32)
+            whole_ref[at, :] = cores_refs[i % 2][row : row + part, :].astype(jnp.float32)
     width = held * BLOCK
     total = None
     for i, price_ref in enumerate(price_refs):
@@ -174,6 +181,16 @@
 def from_partner(x, axis, flip):
     count = lax.axis_size(axis)
     return lax.ppermute(x, axis, [(i, i ^ flip) for i in range(count)])
+
+
+def from_both(x, scen_flip, fac_flip):
+    count = lax.axis_size("fac")
+    pairs = [
+        (i * count + j, (i ^ scen_flip) * count + (j ^ fac_flip))
+        for i in range(lax.axis_size("scen"))
+        for j in range(count)
+    ]
+    return lax.ppermute(x, ("scen", "fac"), pairs)
 
 
 def body(
@@ -228,16 +245,18 @@
         name="price",
     )(*inputs)
     prices = prices.reshape(DATES * rows, width)
+    prices, *packets = lax.optimization_barrier((prices, *packets))
     share_shape = (2 * held * part, len(owner_flips) * SET_DEV)
     column_trades = len(column_flips) * trades
-    own, other = pl.pallas_call(
+    own, narrow, other = pl.pallas_call(
         functools.partial(combine_kernel, part, held, owner_flips),
         out_shape=[
             jax.ShapeDtypeStruct(share_shape, jnp.float32),
             jax.ShapeDtypeStruct(share_shape, jnp.bfloat16),
+            jax.ShapeDtypeStruct(share_shape, jnp.bfloat16),
         ],
         in_specs=[SMEM] + [VMEM] * len(packets),
-        out_specs=[VMEM] * 2,
+        out_specs=[VMEM] * 3,
         scratch_shapes=[
             pltpu.VMEM((2 * share_shape[0], column_trades), jnp.bfloat16),
             pltpu.VMEM((share_shape[1], column_trades), jnp.bfloat16),
@@ -245,21 +264,20 @@
         compiler_params=PARAMS,
         name="combine",
     )(block_slot, *packets)
-    prices, other = lax.optimization_barrier((prices, other))
     pair_prices = [prices, from_partner(prices, "fac", PRICE_FLIP)]
-    share = pl.pallas_call(
+    parts = []
+    for i in range(0, scen_count, 2):
+        parts.append(from_partner(narrow, "scen", i) if i else own)
+        parts.append(from_both(other, i, SIDE_FLIP))
+    shares = pl.pallas_call(
         merge_kernel,
-        out_shape=jax.ShapeDtypeStruct(share_shape, jnp.bfloat16),
-        in_specs=[VMEM] * 2,
+        out_shape=jax.ShapeDtypeStruct((len(parts) // 2 * share_shape[0], share_shape[1]), jnp.bfloat16),
+        in_specs=[VMEM] * len(parts),
         out_specs=VMEM,
         compiler_params=PARAMS,
-        cost_estimate=pl.CostEstimate(flops=10**10, bytes_accessed=0, transcendentals=0),
         name="merge",
-    )(own, from_partner(other, "fac", SIDE_FLIP))
-    shares = [share]
-    for i in range(2, scen_count, 2):
-        shares.append(from_partner(share, "scen", i))
-    shares = sum([[x, from_partner(x, "scen", 1)] for x in shares], [])
+    )(*parts)
+    shares = [shares, from_partner(shares, "scen", 1)]
 
     parts = pl.pallas_call(
         functools.partial(value_kernel, part, held, scen_count),
@@ -267,7 +285,7 @@
             jax.ShapeDtypeStruct((SET_DEV, DATES * rows), jnp.bfloat16 if flip else jnp.float32)
             for flip in owner_flips
         ],
-        in_specs=[VMEM] * (scen_count + 2),
+        in_specs=[VMEM] * 4,
         out_specs=[VMEM] * len(owner_flips),
         scratch_shapes=[pltpu.VMEM((2 * width, share_shape[1]), jnp.float32)],
         compiler_params=PARAMS,
@@ -293,7 +311,9 @@
         compiler_params=PARAMS,
         name="expose",
     )(*parts)
-    sums = [totals] + [from_partner(totals, "scen", i) for i in range(1, scen_count)]
+    sums = [totals] + [None] * (scen_count - 1)
+    for i in [*range(1, scen_count, 2), *range(2, scen_count, 2)]:
+        sums[i] = from_partner(totals, "scen", i)
     while len(sums) > 1:
         sums = [sums[i] + sums[i + 1] for i in range(0, len(sums), 2)]
     return (exposure, sums[0] / (rows * scen_count))

time: 38.8 us -> 37.8 us (0.974)
  waiting for transfers between devices: 13.6 us -> 12 us
  starting transfers between devices: 16.6 us -> 17.1 us
    ppermute x14 -> x12, waiting for transfers between devices: 13.6 us -> 9.69 us  [from_partner(): return lax.ppermute(x, axis, [(i, i ^ flip) for i in range(count)])]
    ppermute x0 -> x2, waiting for transfers between devices: none -> 2.35 us  [from_both(): return lax.ppermute(x, ('scen', 'fac'), pairs)]
    ppermute x0 -> x2, starting transfers between devices: none -> 1.97 us  [from_both(): return lax.ppermute(x, ('scen', 'fac'), pairs)]
    ppermute x14 -> x12, starting transfers between devices: 16.6 us -> 15.2 us  [from_partner(): return lax.ppermute(x, axis, [(i, i ^ flip) for i in range(count)])]
  transfers between devices with their start and end apart: 14 -> 14, of which waited for: 9 -> 10; matrix products, arithmetic and copies ran while one was open for 0% -> 0% of each run, Pallas kernels for 9% -> 12%
where the time goes in v5:
time: 37.8 us; the launch traced here: 37.6 us
  starting transfers between devices  17.1 us (45%)
  waiting for transfers between devices  12 us (32%)
  Pallas kernels  5.48 us (14%)
  local copies, waits for them, and re-layouts  1.59 us (4%)
  between operations  0.73 us (2%)
  other arithmetic  0.58 us (2%)
    ppermute x12, starting transfers between devices, from_partner(): return lax.ppermute(x, axis, [(i, i ^ flip) for i in range(count)])  15.2 us
    ppermute x12, waiting for transfers between devices, from_partner(): return lax.ppermute(x, axis, [(i, i ^ flip) for i in range(count)])  9.69 us
    pallas_call x1, Pallas kernels, body(): pl.pallas_call(price_kernel, out_shape=prices_shape, in_specs=[HBM] * len...  2.87 us
    ppermute x2, waiting for transfers between devices, from_both(): return lax.ppermute(x, ('scen', 'fac'), pairs)  2.35 us
    ppermute x2, starting transfers between devices, from_both(): return lax.ppermute(x, ('scen', 'fac'), pairs)  1.97 us
    unnamed x10, local copies, waits for them, and re-layouts  1.59 us
    pallas_call x1, Pallas kernels, body(): pl.pallas_call(functools.partial(combine_kernel, part, held, owner_flips)...  0.9 us
  transfers between devices with their start and end apart: 14, of which 10 were waited for; matrix products, arithmetic and copies ran while one was open for 0% of the time, Pallas kernels for 12%

profile of v5, /device:TPU:0, one launch (start us, length us, event | category | flops | bytes accessed | tf_op | source)
XLA Modules:
  0.0 37.6 jit_solution(6594772237650312697)
XLA Ops:
  0.6 0.7 %copy-done.3 = s32[256,2]{0,1:T(2,128)S(1)} copy-done((s32[256,2]{0,1:T(2,128)S(1)}, s32[256,2]{0,1:T(2,128)}, u32[]{:S(2)}) %copy-start.3) | copy-done | bytes 2072
  1.3 0.9 %copy-done.1 = bf16[256,2,128]{2,1,0:T(2,128)(2,1)S(1)} copy-done((bf16[256,2,128]{2,1,0:T(2,128)(2,1)S(1)}, bf16[256,2,128]{2,1,0:T(2,128)(2,1)}, u32[]{:S(2)}) %copy-start.1) | copy-done | bytes 131096
  2.2 0.4 %pack.1.refs_1_ = bf16[80,256]{1,0:T(8,128)(2,1)S(1)} custom-call(bf16[256,2,128]{2,1,0:T(2,128)(2,1)S(1)} %copy-done.1, s32[3,256]{1,0:T(4,128)S(1)} %pad_add_fusion.trades_ref), custom_call_target="tpu_custom_call" | custom-call | tf_op jit(solution)/shard_map/pack/pallas_call | solution.py:219
  2.7 4.1 %collective-permute-start.2 = (bf16[80,256]{1,0:T(8,128)(2,1)S(1)}, bf16[80,256]{1,0:T(8,128)(2,1)S(1)}, u32[]{:S(2)}, u32[]{:S(2)}) collective-permute-start(bf16[80,256]{1,0:T(8,128)(2,1)S(1)} %pack.1.refs_1_), channel_id=1, source_target_pairs={{0,4},{1,5},{2,6},{3,7},{4,0},{5,1},{6,2},{7,3},{8,12},{9,13},{10,... | collective-permute-start | bytes 122888 | tf_op jit(solution)/shard_map/ppermute | solution.py:183
  6.8 1.3 %collective-permute-start.1 = (bf16[80,256]{1,0:T(8,128)(2,1)S(1)}, bf16[80,256]{1,0:T(8,128)(2,1)S(1)}, u32[]{:S(2)}, u32[]{:S(2)}) collective-permute-start(bf16[80,256]{1,0:T(8,128)(2,1)S(1)} %pack.1.refs_1_), channel_id=1, source_target_pairs={{0,6},{1,7},{2,4},{3,5},{4,2},{5,3},{6,0},{7,1},{8,14},{9,15},{10,... | collective-permute-start | bytes 122888 | tf_op jit(solution)/shard_map/ppermute | solution.py:183
  8.1 0.2 collective-permute-start
  8.3 2.9 %price.1 = bf16[2,256,256]{2,1,0:T(8,128)(2,1)} custom-call(bf16[256,256]{1,0:T(8,128)(2,1)} %refs_0_.2, f32[1,256]{1,0:T(1,128)} %bitcast.9, f32[1,256]{1,0:T(1,128)} %bitcast.10, f32[1,256]{1,0:T(1,128)} %bitcast.11, bf16[2,256,256]{2,1,0:T(8,128)(2,1)} %refs_4_, s32[2,256,256]{2,1,0:T(8,128)} %refs_5_.1, bf16[2,256,256]{2,1,0:T(8,128)(2,1)} %refs_6_.1), custom_call_target="tpu_custom_call" | custom-call | tf_op jit(solution)/shard_map/price/pallas_call | solution.py:233
  11.2 1.3 %collective-permute-done.1.refs_3_ = bf16[80,256]{1,0:T(8,128)(2,1)S(1)} collective-permute-done((bf16[80,256]{1,0:T(8,128)(2,1)S(1)}, bf16[80,256]{1,0:T(8,128)(2,1)S(1)}, u32[]{:S(2)}, u32[]{:S(2)}) %collective-permute-start.1) | collective-permute-done | bytes 40992 | tf_op jit(solution)/shard_map/ppermute | solution.py:183
  12.6 0.6 %collective-permute-start.7 = (bf16[512,256]{1,0:T(8,128)(2,1)}, bf16[512,256]{1,0:T(8,128)(2,1)S(1)}, u32[]{:S(2)}, u32[]{:S(2)}) collective-permute-start(bf16[512,256]{1,0:T(8,128)(2,1)} %bitcast.6), channel_id=1, source_target_pairs={{0,2},{1,3},{2,0},{3,1},{4,6},{5,7},{6,4},{7,5},{8,10},{9,11},{10,... | collective-permute-start | bytes 786440 | tf_op jit(solution)/shard_map/ppermute | solution.py:183
  13.1 0.9 %combine.1 = (f32[128,256]{1,0:T(8,128)S(1)}, bf16[128,256]{1,0:T(8,128)(2,1)S(1)}, bf16[128,256]{1,0:T(8,128)(2,1)S(1)}) custom-call(s32[16]{0:T(128)S(1)} %copy-done.2, bf16[80,256]{1,0:T(8,128)(2,1)S(1)} %pack.1.refs_1_, bf16[80,256]{1,0:T(8,128)(2,1)S(1)} %collective-permute-done.refs_2_, bf16[80,256]{1,0:T(8,128)(2,1)S(1)} %collective-permute-done.1.refs_3_, ...), custom_call_target="tpu_custom_call" | custom-call | tf_op jit(solution)/shard_map/combine/pallas_call | solution.py:251
  14.0 1.6 %collective-permute-start.4 = (bf16[128,256]{1,0:T(8,128)(2,1)S(1)}, bf16[128,256]{1,0:T(8,128)(2,1)S(1)}, u32[]{:S(2)}, u32[]{:S(2)}) collective-permute-start(bf16[128,256]{1,0:T(8,128)(2,1)S(1)} %get-tuple-element.22), channel_id=1, source_target_pairs={{0,16},{8,24},{16,0},{24,8},{1,17},{9,25},{17,1},{25,9},{2,18},{10... | collective-permute-start | bytes 196616 | tf_op jit(solution)/shard_map/ppermute | solution.py:183
  15.6 1.4 %collective-permute-start.5 = (bf16[128,256]{1,0:T(8,128)(2,1)S(1)}, bf16[128,256]{1,0:T(8,128)(2,1)S(1)}, u32[]{:S(2)}, u32[]{:S(2)}) collective-permute-start(bf16[128,256]{1,0:T(8,128)(2,1)S(1)} %get-tuple-element.21), channel_id=1, source_target_pairs={{0,17},{1,16},{2,19},{3,18},{4,21},{5,20},{6,23},{7,22},{8,25},{9,... | collective-permute-start | bytes 196616 | tf_op jit(solution)/shard_map/ppermute | solution.py:193
  17.1 0.5 %collective-permute-start.3 = (bf16[128,256]{1,0:T(8,128)(2,1)S(1)}, bf16[128,256]{1,0:T(8,128)(2,1)S(1)}, u32[]{:S(2)}, u32[]{:S(2)}) collective-permute-start(bf16[128,256]{1,0:T(8,128)(2,1)S(1)} %get-tuple-element.21), channel_id=1, source_target_pairs={{0,1},{1,0},{2,3},{3,2},{4,5},{5,4},{6,7},{7,6},{8,9},{9,8},{10,11... | collective-permute-start | bytes 196616 | tf_op jit(solution)/shard_map/ppermute | solution.py:193
  17.6 1.4 %collective-permute-done.4.refs_2_ = bf16[128,256]{1,0:T(8,128)(2,1)S(1)} collective-permute-done((bf16[128,256]{1,0:T(8,128)(2,1)S(1)}, bf16[128,256]{1,0:T(8,128)(2,1)S(1)}, u32[]{:S(2)}, u32[]{:S(2)}) %collective-permute-start.4) | collective-permute-done | bytes 65568 | tf_op jit(solution)/shard_map/ppermute | solution.py:183
  19.0 1.8 %collective-permute-done.5.refs_3_ = bf16[128,256]{1,0:T(8,128)(2,1)S(1)} collective-permute-done((bf16[128,256]{1,0:T(8,128)(2,1)S(1)}, bf16[128,256]{1,0:T(8,128)(2,1)S(1)}, u32[]{:S(2)}, u32[]{:S(2)}) %collective-permute-start.5) | collective-permute-done | bytes 65568 | tf_op jit(solution)/shard_map/ppermute | solution.py:193
  20.8 0.5 %collective-permute-done.3.refs_1_ = bf16[128,256]{1,0:T(8,128)(2,1)S(1)} collective-permute-done((bf16[128,256]{1,0:T(8,128)(2,1)S(1)}, bf16[128,256]{1,0:T(8,128)(2,1)S(1)}, u32[]{:S(2)}, u32[]{:S(2)}) %collective-permute-start.3) | collective-permute-done | bytes 65568 | tf_op jit(solution)/shard_map/ppermute | solution.py:193
  21.3 0.1 merge.1.refs_0_
  21.5 1.3 %collective-permute-done.6.refs_1_ = bf16[256,256]{1,0:T(8,128)(2,1)S(1)} collective-permute-done((bf16[256,256]{1,0:T(8,128)(2,1)S(1)}, bf16[256,256]{1,0:T(8,128)(2,1)S(1)}, u32[]{:S(2)}, u32[]{:S(2)}) %collective-permute-start.6) | collective-permute-done | bytes 131104 | tf_op jit(solution)/shard_map/ppermute | solution.py:183
  22.9 0.4 %value.1 = (f32[64,512]{1,0:T(8,128)S(1)}, bf16[64,512]{1,0:T(8,128)(2,1)S(1)}, bf16[64,512]{1,0:T(8,128)(2,1)S(1)}, bf16[64,512]{1,0:T(8,128)(2,1)S(1)}) custom-call(bf16[256,256]{1,0:T(8,128)(2,1)S(1)} %merge.1.refs_0_, bf16[256,256]{1,0:T(8,128)(2,1)S(1)} %collective-permute-done.6.refs_1_, bf16[512,256]{1,0:T(8,128)(2,1)S(1)} %bitcast.7, ...), custom_call_target="tpu_custom_call" | custom-call | tf_op jit(solution)/shard_map/value/pallas_call | solution.py:282
  23.3 2.5 %collective-permute-start.8 = (bf16[64,512]{1,0:T(8,128)(2,1)S(1)}, bf16[64,512]{1,0:T(8,128)(2,1)S(1)}, u32[]{:S(2)}, u32[]{:S(2)}) collective-permute-start(bf16[64,512]{1,0:T(8,128)(2,1)S(1)} %get-tuple-element.25), channel_id=1, source_target_pairs={{0,6},{1,7},{2,4},{3,5},{4,2},{5,3},{6,0},{7,1},{8,14},{9,15},{10,... | collective-permute-start | bytes 196616 | tf_op jit(solution)/shard_map/ppermute | solution.py:183
  25.8 1.7 %collective-permute-start.9 = (bf16[64,512]{1,0:T(8,128)(2,1)S(1)}, bf16[64,512]{1,0:T(8,128)(2,1)S(1)}, u32[]{:S(2)}, u32[]{:S(2)}) collective-permute-start(bf16[64,512]{1,0:T(8,128)(2,1)S(1)} %get-tuple-element.26), channel_id=1, source_target_pairs={{0,7},{1,6},{2,5},{3,4},{4,3},{5,2},{6,1},{7,0},{8,15},{9,14},{10,... | collective-permute-start | bytes 196616 | tf_op jit(solution)/shard_map/ppermute | solution.py:183
  27.5 1.1 %collective-permute-start.10 = (bf16[64,512]{1,0:T(8,128)(2,1)S(1)}, bf16[64,512]{1,0:T(8,128)(2,1)S(1)}, u32[]{:S(2)}, u32[]{:S(2)}) collective-permute-start(bf16[64,512]{1,0:T(8,128)(2,1)S(1)} %get-tuple-element.27), channel_id=1, source_target_pairs={{0,1},{1,0},{2,3},{3,2},{4,5},{5,4},{6,7},{7,6},{8,9},{9,8},{10,11... | collective-permute-start | bytes 196616 | tf_op jit(solution)/shard_map/ppermute | solution.py:183
  28.6 0.8 %collective-permute-done.8.refs_1_ = bf16[64,512]{1,0:T(8,128)(2,1)S(1)} collective-permute-done((bf16[64,512]{1,0:T(8,128)(2,1)S(1)}, bf16[64,512]{1,0:T(8,128)(2,1)S(1)}, u32[]{:S(2)}, u32[]{:S(2)}) %collective-permute-start.8) | collective-permute-done | bytes 65568 | tf_op jit(solution)/shard_map/ppermute | solution.py:183
  29.4 3.4 %collective-permute-done.9.refs_2_ = bf16[64,512]{1,0:T(8,128)(2,1)S(1)} collective-permute-done((bf16[64,512]{1,0:T(8,128)(2,1)S(1)}, bf16[64,512]{1,0:T(8,128)(2,1)S(1)}, u32[]{:S(2)}, u32[]{:S(2)}) %collective-permute-start.9) | collective-permute-done | bytes 65568 | tf_op jit(solution)/shard_map/ppermute | solution.py:183
  32.8 0.3 collective-permute-done.10.refs_3_
  33.2 0.1 totals.1
  33.4 1.4 %collective-permute-start.12 = (f32[2,64]{1,0:T(2,128)S(1)}, f32[2,64]{1,0:T(2,128)S(1)}, u32[]{:S(2)}, u32[]{:S(2)}) collective-permute-start(f32[2,64]{1,0:T(2,128)S(1)} %totals.1), channel_id=1, source_target_pairs={{0,16},{8,24},{16,0},{24,8},{1,17},{9,25},{17,1},{25,9},{2,18},{10... | collective-permute-start | bytes 1544 | tf_op jit(solution)/shard_map/ppermute | solution.py:183
  34.7 0.5 %collective-permute-start.11 = (f32[2,64]{1,0:T(2,128)S(1)}, f32[2,64]{1,0:T(2,128)S(1)}, u32[]{:S(2)}, u32[]{:S(2)}) collective-permute-start(f32[2,64]{1,0:T(2,128)S(1)} %totals.1), channel_id=1, source_target_pairs={{0,8},{8,0},{16,24},{24,16},{1,9},{9,1},{17,25},{25,17},{2,10},{10... | collective-permute-start | bytes 1544 | tf_op jit(solution)/shard_map/ppermute | solution.py:183
  35.2 0.7 %expose.1 = f32[2,64,256]{2,1,0:T(8,128)} custom-call(f32[64,512]{1,0:T(8,128)S(1)} %get-tuple-element.24.refs_0_, bf16[64,512]{1,0:T(8,128)(2,1)S(1)} %collective-permute-done.8.refs_1_, bf16[64,512]{1,0:T(8,128)(2,1)S(1)} %collective-permute-done.9.refs_2_, bf16[64,512]{1,0:T(8,128)(2,1)S(1)} %collective-permute-done.10.refs_3_), custom_call_target="tpu_custom_call" | custom-call | tf_op jit(solution)/shard_map/expose/pallas_call | solution.py:306
  35.9 0.4 %collective-permute-done.13 = f32[2,64]{1,0:T(2,128)S(1)} collective-permute-done((f32[2,64]{1,0:T(2,128)S(1)}, f32[2,64]{1,0:T(2,128)S(1)}, u32[]{:S(2)}, u32[]{:S(2)}) %collective-permute-start.13) | collective-permute-done | bytes 544 | tf_op jit(solution)/shard_map/ppermute | solution.py:183
  36.3 0.7 %collective-permute-done.12 = f32[2,64]{1,0:T(2,128)S(1)} collective-permute-done((f32[2,64]{1,0:T(2,128)S(1)}, f32[2,64]{1,0:T(2,128)S(1)}, u32[]{:S(2)}, u32[]{:S(2)}) %collective-permute-start.12) | collective-permute-done | bytes 544 | tf_op jit(solution)/shard_map/ppermute | solution.py:183
  37.0 0.6 %add_multiply_fusion = f32[2,64]{1,0:T(2,128)} fusion(f32[2,64]{1,0:T(2,128)S(1)} %collective-permute-done.12, f32[2,64]{1,0:T(2,128)S(1)} %collective-permute-done.13, f32[2,64]{1,0:T(2,128)S(1)} %totals.1, f32[2,64]{1,0:T(2,128)S(1)} %collective-permute-done.11), kind=kLoop, calls=%fused_computation.1 | loop fusion | flops 512 | bytes 2560 | tf_op jit(solution)/shard_map/div | solution.py:319
  (15 shorter events, 0.2 us)
Async XLA Ops:
  0.6 0.7 %copy-start.3 = (s32[256,2]{0,1:T(2,128)S(1)}, s32[256,2]{0,1:T(2,128)}, u32[]{:S(2)}) copy-start(s32[256,2]{0,1:T(2,128)} %param.18) | copy-start | bytes 6148
  0.6 0.7 %copy-start.4 = (s32[256]{0:T(256)S(1)}, s32[256]{0:T(256)}, u32[]{:S(2)}) copy-start(s32[256]{0:T(256)} %param.21) | copy-start | bytes 3076
  1.3 0.9 %copy-start.1 = (bf16[256,2,128]{2,1,0:T(2,128)(2,1)S(1)}, bf16[256,2,128]{2,1,0:T(2,128)(2,1)}, u32[]{:S(2)}) copy-start(bf16[256,2,128]{2,1,0:T(2,128)(2,1)} %weights_ref.1) | copy-start | bytes 393220
  2.7 8.6 %collective-permute-start.2 = (bf16[80,256]{1,0:T(8,128)(2,1)S(1)}, bf16[80,256]{1,0:T(8,128)(2,1)S(1)}, u32[]{:S(2)}, u32[]{:S(2)}) collective-permute-start(bf16[80,256]{1,0:T(8,128)(2,1)S(1)} %pack.1.refs_1_), channel_id=1, source_target_pairs={{0,4},{1,5},{2,6},{3,7},{4,0},{5,1},{6,2},{7,3},{8,12},{9,13},{10,... | collective-permute-start | bytes 122888 | tf_op jit(solution)/shard_map/ppermute | solution.py:183
  6.8 5.8 %collective-permute-start.1 = (bf16[80,256]{1,0:T(8,128)(2,1)S(1)}, bf16[80,256]{1,0:T(8,128)(2,1)S(1)}, u32[]{:S(2)}, u32[]{:S(2)}) collective-permute-start(bf16[80,256]{1,0:T(8,128)(2,1)S(1)} %pack.1.refs_1_), channel_id=1, source_target_pairs={{0,6},{1,7},{2,4},{3,5},{4,2},{5,3},{6,0},{7,1},{8,14},{9,15},{10,... | collective-permute-start | bytes 122888 | tf_op jit(solution)/shard_map/ppermute | solution.py:183
  8.1 4.5 %collective-permute-start = (bf16[80,256]{1,0:T(8,128)(2,1)S(1)}, bf16[80,256]{1,0:T(8,128)(2,1)S(1)}, u32[]{:S(2)}, u32[]{:S(2)}) collective-permute-start(bf16[80,256]{1,0:T(8,128)(2,1)S(1)} %pack.1.refs_1_), channel_id=1, source_target_pairs={{0,2},{1,3},{2,0},{3,1},{4,6},{5,7},{6,4},{7,5},{8,10},{9,11},{10,... | collective-permute-start | bytes 122888 | tf_op jit(solution)/shard_map/ppermute | solution.py:183
  11.2 1.9 %copy-start.2 = (s32[16]{0:T(128)S(1)}, s32[16]{0:T(128)}, u32[]{:S(2)}) copy-start(s32[16]{0:T(128)} %refs_0_.3) | copy-start | bytes 196
  12.6 10.3 %collective-permute-start.7 = (bf16[512,256]{1,0:T(8,128)(2,1)}, bf16[512,256]{1,0:T(8,128)(2,1)S(1)}, u32[]{:S(2)}, u32[]{:S(2)}) collective-permute-start(bf16[512,256]{1,0:T(8,128)(2,1)} %bitcast.6), channel_id=1, source_target_pairs={{0,2},{1,3},{2,0},{3,1},{4,6},{5,7},{6,4},{7,5},{8,10},{9,11},{10,... | collective-permute-start | bytes 786440 | tf_op jit(solution)/shard_map/ppermute | solution.py:183
  14.0 8.8 %copy-start = (bf16[2,256,256]{2,1,0:T(8,128)(2,1)S(1)}, bf16[2,256,256]{2,1,0:T(8,128)(2,1)}, u32[]{:S(2)}) copy-start(bf16[2,256,256]{2,1,0:T(8,128)(2,1)} %price.1) | copy-start | bytes 786436
  14.0 4.9 %collective-permute-start.4 = (bf16[128,256]{1,0:T(8,128)(2,1)S(1)}, bf16[128,256]{1,0:T(8,128)(2,1)S(1)}, u32[]{:S(2)}, u32[]{:S(2)}) collective-permute-start(bf16[128,256]{1,0:T(8,128)(2,1)S(1)} %get-tuple-element.22), channel_id=1, source_target_pairs={{0,16},{8,24},{16,0},{24,8},{1,17},{9,25},{17,1},{25,9},{2,18},{10... | collective-permute-start | bytes 196616 | tf_op jit(solution)/shard_map/ppermute | solution.py:183
  15.6 5.2 %collective-permute-start.5 = (bf16[128,256]{1,0:T(8,128)(2,1)S(1)}, bf16[128,256]{1,0:T(8,128)(2,1)S(1)}, u32[]{:S(2)}, u32[]{:S(2)}) collective-permute-start(bf16[128,256]{1,0:T(8,128)(2,1)S(1)} %get-tuple-element.21), channel_id=1, source_target_pairs={{0,17},{1,16},{2,19},{3,18},{4,21},{5,20},{6,23},{7,22},{8,25},{9,... | collective-permute-start | bytes 196616 | tf_op jit(solution)/shard_map/ppermute | solution.py:193
  17.1 4.3 %collective-permute-start.3 = (bf16[128,256]{1,0:T(8,128)(2,1)S(1)}, bf16[128,256]{1,0:T(8,128)(2,1)S(1)}, u32[]{:S(2)}, u32[]{:S(2)}) collective-permute-start(bf16[128,256]{1,0:T(8,128)(2,1)S(1)} %get-tuple-element.21), channel_id=1, source_target_pairs={{0,1},{1,0},{2,3},{3,2},{4,5},{5,4},{6,7},{7,6},{8,9},{9,8},{10,11... | collective-permute-start | bytes 196616 | tf_op jit(solution)/shard_map/ppermute | solution.py:193
  21.4 1.4 %collective-permute-start.6 = (bf16[256,256]{1,0:T(8,128)(2,1)S(1)}, bf16[256,256]{1,0:T(8,128)(2,1)S(1)}, u32[]{:S(2)}, u32[]{:S(2)}) collective-permute-start(bf16[256,256]{1,0:T(8,128)(2,1)S(1)} %merge.1.refs_0_), channel_id=1, source_target_pairs={{0,8},{8,0},{16,24},{24,16},{1,9},{9,1},{17,25},{25,17},{2,10},{10... | collective-permute-start | bytes 393224 | tf_op jit(solution)/shard_map/ppermute | solution.py:183
  23.3 6.1 %collective-permute-start.8 = (bf16[64,512]{1,0:T(8,128)(2,1)S(1)}, bf16[64,512]{1,0:T(8,128)(2,1)S(1)}, u32[]{:S(2)}, u32[]{:S(2)}) collective-permute-start(bf16[64,512]{1,0:T(8,128)(2,1)S(1)} %get-tuple-element.25), channel_id=1, source_target_pairs={{0,6},{1,7},{2,4},{3,5},{4,2},{5,3},{6,0},{7,1},{8,14},{9,15},{10,... | collective-permute-start | bytes 196616 | tf_op jit(solution)/shard_map/ppermute | solution.py:183
  25.8 7.0 %collective-permute-start.9 = (bf16[64,512]{1,0:T(8,128)(2,1)S(1)}, bf16[64,512]{1,0:T(8,128)(2,1)S(1)}, u32[]{:S(2)}, u32[]{:S(2)}) collective-permute-start(bf16[64,512]{1,0:T(8,128)(2,1)S(1)} %get-tuple-element.26), channel_id=1, source_target_pairs={{0,7},{1,6},{2,5},{3,4},{4,3},{5,2},{6,1},{7,0},{8,15},{9,14},{10,... | collective-permute-start | bytes 196616 | tf_op jit(solution)/shard_map/ppermute | solution.py:183
  27.5 5.6 %collective-permute-start.10 = (bf16[64,512]{1,0:T(8,128)(2,1)S(1)}, bf16[64,512]{1,0:T(8,128)(2,1)S(1)}, u32[]{:S(2)}, u32[]{:S(2)}) collective-permute-start(bf16[64,512]{1,0:T(8,128)(2,1)S(1)} %get-tuple-element.27), channel_id=1, source_target_pairs={{0,1},{1,0},{2,3},{3,2},{4,5},{5,4},{6,7},{7,6},{8,9},{9,8},{10,11... | collective-permute-start | bytes 196616 | tf_op jit(solution)/shard_map/ppermute | solution.py:183
  33.3 3.1 %collective-permute-start.13 = (f32[2,64]{1,0:T(2,128)S(1)}, f32[2,64]{1,0:T(2,128)S(1)}, u32[]{:S(2)}, u32[]{:S(2)}) collective-permute-start(f32[2,64]{1,0:T(2,128)S(1)} %totals.1), channel_id=1, source_target_pairs={{0,24},{8,16},{16,8},{24,0},{1,25},{9,17},{17,9},{25,1},{2,26},{10... | collective-permute-start | bytes 1544 | tf_op jit(solution)/shard_map/ppermute | solution.py:183
  33.4 3.6 %collective-permute-start.12 = (f32[2,64]{1,0:T(2,128)S(1)}, f32[2,64]{1,0:T(2,128)S(1)}, u32[]{:S(2)}, u32[]{:S(2)}) collective-permute-start(f32[2,64]{1,0:T(2,128)S(1)} %totals.1), channel_id=1, source_target_pairs={{0,16},{8,24},{16,0},{24,8},{1,17},{9,25},{17,1},{25,9},{2,18},{10... | collective-permute-start | bytes 1544 | tf_op jit(solution)/shard_map/ppermute | solution.py:183
  34.7 2.3 %collective-permute-start.11 = (f32[2,64]{1,0:T(2,128)S(1)}, f32[2,64]{1,0:T(2,128)S(1)}, u32[]{:S(2)}, u32[]{:S(2)}) collective-permute-start(f32[2,64]{1,0:T(2,128)S(1)} %totals.1), channel_id=1, source_target_pairs={{0,8},{8,0},{16,24},{24,16},{1,9},{9,1},{17,25},{25,17},{2,10},{10... | collective-permute-start | bytes 1544 | tf_op jit(solution)/shard_map/ppermute | solution.py:183

commit v6 on v5

--- a/solution.py
+++ b/solution.py
@@ -19,7 +19,6 @@
 HBM = pl.BlockSpec(memory_space=pltpu.HBM)
 SMEM = pl.BlockSpec(memory_space=pltpu.SMEM)
 PARAMS = pltpu.CompilerParams(vmem_limit_bytes=16 * 1024 * 1024)
-FETCH_PARAMS = pltpu.CompilerParams(vmem_limit_bytes=60 * 1024 * 1024)
 NT = (((1,), (1,)), ((), ()))
 
 
@@ -27,18 +26,21 @@
     return lax.dot_general(a, b, dims, preferred_element_type=jnp.float32)
 
 
-def pack_kernel(part, weights_ref, trades_ref, packet_ref):
-    scen = lax.axis_index("scen")
-    row = lax.broadcasted_iota(jnp.int32, (part, BLOCK), 0)
-    column = lax.broadcasted_iota(jnp.int32, (part, BLOCK), 1)
-    pick = (column == scen * part + row).astype(jnp.float32).astype(jnp.bfloat16)
+def pick_kernel(part, pick_ref):
+    row = lax.broadcasted_iota(jnp.int32, pick_ref.shape, 0)
+    column = lax.broadcasted_iota(jnp.int32, pick_ref.shape, 1)
+    pick = column == lax.axis_index("scen") * part + row
+    pick_ref[...] = pick.astype(jnp.float32).astype(jnp.bfloat16)
+
+
+def pack_kernel(part, pick_ref, weights_ref, deps_ref, netting_ref, packet_ref):
     for k in range(2):
-        share = f32_dot(pick, weights_ref[:, k, :], NT)
-        packet_ref[k * part : (k + 1) * part, :] = share.astype(jnp.bfloat16)
-    netting = trades_ref[2:3, :]
+        share = f32_dot(pick_ref[...], weights_ref[:, k, :], NT)
+        packet_ref[k * part : (k + 1) * part, :] = share[:part].astype(jnp.bfloat16)
+    netting = netting_ref[...]
     tags = jnp.concatenate(
         [
-            trades_ref[:2, :],
+            deps_ref[...],
             netting // SET_DEV,
             netting % SET_DEV,
             jnp.zeros((TAGS - 4, netting.shape[1]), jnp.int32),
@@ -48,49 +50,24 @@
     packet_ref[2 * part :, :] = tags.astype(jnp.float32).astype(jnp.bfloat16)
 
 
-def price_kernel(*refs):
-    sources, out_hbm, held_refs, out_ref = refs[:7], refs[7], refs[8:15], refs[15]
-    sems, chunk_sems, out_sems = refs[16:]
-    loadings_ref, vol_ref, mean_ref, dev_ref, shocks_ref, counts_ref, noise_ref = held_refs
+def price_kernel(shocks_ref, loadings_ref, vol_ref, counts_ref, noise_ref, mean_ref, dev_ref, out_ref):
     rows = shocks_ref.shape[1]
-    fixed = [
-        pltpu.make_async_copy(src, dst, sems.at[i])
-        for i, (src, dst) in enumerate(zip(sources[:4], held_refs[:4]))
-    ]
-    chunks = [
-        [
-            pltpu.make_async_copy(src.at[:, pl.ds(at, CHUNK)], dst.at[:, pl.ds(at, CHUNK)], chunk_sems.at[i, j])
-            for j, (src, dst) in enumerate(zip(sources[4:], held_refs[4:]))
-        ]
-        for i, at in enumerate(range(0, rows, CHUNK))
-    ]
-    results = [
-        pltpu.make_async_copy(out_ref.at[:, pl.ds(at, CHUNK)], out_hbm.at[:, pl.ds(at, CHUNK)], out_sems.at[i])
-        for i, at in enumerate(range(0, rows, CHUNK))
-    ]
-    for copy in fixed + sum(chunks, []):
-        copy.start()
-    for copy in fixed:
-        copy.wait()
     vol = vol_ref[...]
     drift = 0.5 * vol * vol
     mean = mean_ref[...]
     dev = dev_ref[...]
     loadings = loadings_ref[...]
-    for i, copies in enumerate(chunks):
-        for copy in copies:
-            copy.wait()
-        at = slice(i * CHUNK, (i + 1) * CHUNK)
+    for i in range(0, rows, CHUNK):
+        at = slice(i, i + CHUNK)
         level = jnp.zeros((CHUNK, vol.shape[1]), jnp.float32)
         for date in range(DATES):
             diffuse = jnp.dot(shocks_ref[date, at, :], loadings, preferred_element_type=jnp.float32)
             counts = counts_ref[date, at, :].astype(jnp.float32)
             noise = noise_ref[date, at, :].astype(jnp.float32)
             level = level + vol * diffuse - drift + counts * mean + jnp.sqrt(counts) * dev * noise
-            out_ref[date, at, :] = (jnp.exp(level) - 1.0).astype(jnp.bfloat16)
-        results[i].start()
-    for copy in results:
-        copy.wait()
+            out_ref[date * rows + i : date * rows + i + CHUNK, :] = (jnp.exp(level) - 1.0).astype(
+                jnp.bfloat16
+            )
 
 
 def combine_kernel(part, held, flips, *refs):
@@ -216,35 +193,34 @@
     column_flips = [i for i in range(fac_count) if not i & SIDE_FLIP]
     owner_flips = [i for i in range(fac_count) if (i // PRICE_FLIP) % 4 in (0, 3)]
 
+    pick = pl.pallas_call(
+        functools.partial(pick_kernel, part),
+        out_shape=jax.ShapeDtypeStruct((max(part, 16), BLOCK), jnp.bfloat16),
+        out_specs=VMEM,
+        compiler_params=PARAMS,
+        cost_estimate=pl.CostEstimate(flops=10**10, bytes_accessed=0, transcendentals=0),
+        name="pick",
+    )()
     packet = pl.pallas_call(
         functools.partial(pack_kernel, part),
         out_shape=jax.ShapeDtypeStruct((2 * part + TAGS, trades), jnp.bfloat16),
-        in_specs=[VMEM] * 2,
+        in_specs=[VMEM] * 4,
         out_specs=VMEM,
         compiler_params=PARAMS,
         name="pack",
-    )(trade_weights, jnp.concatenate([dependencies.T, netting[None]]))
+    )(pick, trade_weights, dependencies.T, netting[None])
     order = column_flips[1:2] + column_flips[:1:-1]
     packets = [packet] + [from_partner(packet, "fac", i) for i in order]
 
     packet, shocks = lax.optimization_barrier((packet, shocks))
-    inputs = (loadings, vol[None], jump_mean[None], jump_vol[None], shocks, jump_counts, jump_noise)
-    prices_shape = jax.ShapeDtypeStruct((DATES, rows, width), jnp.bfloat16)
     prices = pl.pallas_call(
         price_kernel,
-        out_shape=prices_shape,
-        in_specs=[HBM] * len(inputs),
-        out_specs=HBM,
-        scratch_shapes=[pltpu.VMEM(x.shape, x.dtype) for x in inputs + (prices_shape,)]
-        + [
-            pltpu.SemaphoreType.DMA((4,)),
-            pltpu.SemaphoreType.DMA((rows // CHUNK, 3)),
-            pltpu.SemaphoreType.DMA((rows // CHUNK,)),
-        ],
-        compiler_params=FETCH_PARAMS,
+        out_shape=jax.ShapeDtypeStruct((DATES * rows, width), jnp.bfloat16),
+        in_specs=[VMEM] * 7,
+        out_specs=VMEM,
+        compiler_params=PARAMS,
         name="price",
-    )(*inputs)
-    prices = prices.reshape(DATES * rows, width)
+    )(shocks, loadings, vol[None], jump_counts, jump_noise, jump_mean[None], jump_vol[None])
     prices, *packets = lax.optimization_barrier((prices, *packets))
     share_shape = (2 * held * part, len(owner_flips) * SET_DEV)
     column_trades = len(column_flips) * trades

time: 37.8 us -> 36.5 us (0.966)
  Pallas kernels: 5.48 us -> 3.12 us
  waiting for transfers between devices: 12 us -> 13.8 us
  starting transfers between devices: 17.1 us -> 16.6 us
    pallas_call x1 -> x2, Pallas kernels: 2.87 us -> 0.5 us  [the longest x1 0.48 us: body(): pl.pallas_call(price_kernel, out_shape=jax.ShapeDtypeStruct((DATES * rows...]
    ppermute x12, waiting for transfers between devices: 9.69 us -> 11.3 us  [from_partner(): return lax.ppermute(x, axis, [(i, i ^ flip) for i in range(count)])]
    ppermute x12, starting transfers between devices: 15.2 us -> 14.6 us  [from_partner(): return lax.ppermute(x, axis, [(i, i ^ flip) for i in range(count)])]
    unnamed x10 -> x22, local copies, waits for them, and re-layouts: 1.59 us -> 1.47 us
  transfers between devices with their start and end apart: 14 -> 14, of which waited for: 10 -> 10; matrix products, arithmetic and copies ran while one was open for 0% -> 0% of each run, Pallas kernels for 12% -> 6%
where the time goes in v6:
time: 36.5 us; the launch traced here: 36.4 us
  starting transfers between devices  16.6 us (45%)
  waiting for transfers between devices  13.8 us (38%)
  Pallas kernels  3.12 us (9%)
  local copies, waits for them, and re-layouts  1.47 us (4%)
  between operations  0.81 us (2%)
  other arithmetic  0.57 us (2%)
    ppermute x12, starting transfers between devices, from_partner(): return lax.ppermute(x, axis, [(i, i ^ flip) for i in range(count)])  14.6 us
    ppermute x12, waiting for transfers between devices, from_partner(): return lax.ppermute(x, axis, [(i, i ^ flip) for i in range(count)])  11.3 us
    ppermute x2, waiting for transfers between devices, from_both(): return lax.ppermute(x, ('scen', 'fac'), pairs)  2.52 us
    ppermute x2, starting transfers between devices, from_both(): return lax.ppermute(x, ('scen', 'fac'), pairs)  1.97 us
    unnamed x22, local copies, waits for them, and re-layouts  1.47 us
    pallas_call x1, Pallas kernels, body(): pl.pallas_call(functools.partial(combine_kernel, part, held, owner_flips)...  0.9 us
  transfers between devices with their start and end apart: 14, of which 10 were waited for; matrix products, arithmetic and copies ran while one was open for 0% of the time, Pallas kernels for 6%

profile of v6, /device:TPU:0, one launch (start us, length us, event | category | flops | bytes accessed | tf_op | source)
XLA Modules:
  0.0 36.4 jit_solution(13511761334379132621)
XLA Ops:
  0.7 0.8 %copy-done.4 = bf16[256,2,128]{2,1,0:T(2,128)(2,1)S(1)} copy-done((bf16[256,2,128]{2,1,0:T(2,128)(2,1)S(1)}, bf16[256,2,128]{2,1,0:T(2,128)(2,1)}, u32[]{:S(2)}) %copy-start.4) | copy-done | bytes 131096
  1.5 0.4 %pack.1.refs_1_ = bf16[80,256]{1,0:T(8,128)(2,1)S(1)} custom-call(bf16[32,128]{1,0:T(8,128)(2,1)S(1)} %pick.1.pick_ref, bf16[256,2,128]{2,1,0:T(2,128)(2,1)S(1)} %copy-done.4, s32[2,256]{1,0:T(2,128)S(1)} %bitcast.5, s32[1,256]{1,0:T(1,128)S(1)} %bitcast.6), custom_call_target="tpu_custom_call" | custom-call | tf_op jit(solution)/shard_map/pack/pallas_call | solution.py:204
  2.0 4.1 %collective-permute-start.2 = (bf16[80,256]{1,0:T(8,128)(2,1)S(1)}, bf16[80,256]{1,0:T(8,128)(2,1)S(1)}, u32[]{:S(2)}, u32[]{:S(2)}) collective-permute-start(bf16[80,256]{1,0:T(8,128)(2,1)S(1)} %pack.1.refs_1_), channel_id=1, source_target_pairs={{0,4},{1,5},{2,6},{3,7},{4,0},{5,1},{6,2},{7,3},{8,12},{9,13},{10,... | collective-permute-start | bytes 122888 | tf_op jit(solution)/shard_map/ppermute | solution.py:160
  6.1 1.3 %collective-permute-start.1 = (bf16[80,256]{1,0:T(8,128)(2,1)S(1)}, bf16[80,256]{1,0:T(8,128)(2,1)S(1)}, u32[]{:S(2)}, u32[]{:S(2)}) collective-permute-start(bf16[80,256]{1,0:T(8,128)(2,1)S(1)} %pack.1.refs_1_), channel_id=1, source_target_pairs={{0,6},{1,7},{2,4},{3,5},{4,2},{5,3},{6,0},{7,1},{8,14},{9,15},{10,... | collective-permute-start | bytes 122888 | tf_op jit(solution)/shard_map/ppermute | solution.py:160
  7.4 0.2 collective-permute-start
  7.7 0.6 %copy-done.7 = f32[256]{0:T(256)S(1)} copy-done((f32[256]{0:T(256)S(1)}, f32[256]{0:T(256)}, u32[]{:S(2)}) %copy-start.7) | copy-done | bytes 1048
  8.3 0.5 %price.1.refs_2_ = bf16[512,256]{1,0:T(8,128)(2,1)S(1)} custom-call(bf16[2,256,256]{2,1,0:T(8,128)(2,1)S(1)} %copy-done.1, bf16[256,256]{1,0:T(8,128)(2,1)S(1)} %copy-done.3, f32[1,256]{1,0:T(1,128)S(1)} %bitcast.7, s32[2,256,256]{2,1,0:T(8,128)S(1)} %copy-done, bf16[2,256,256]{2,1,0:T(8,128)(2,1)S(1)} %copy-done.2, f32[1,256]{1,0:T(1,128)S(1)} %bitcast.8, ...), custom_call_target="tpu_custom_call" | custom-call | tf_op jit(solution)/shard_map/price/pallas_call | solution.py:216
  8.8 3.0 %collective-permute-done.1.refs_3_ = bf16[80,256]{1,0:T(8,128)(2,1)S(1)} collective-permute-done((bf16[80,256]{1,0:T(8,128)(2,1)S(1)}, bf16[80,256]{1,0:T(8,128)(2,1)S(1)}, u32[]{:S(2)}, u32[]{:S(2)}) %collective-permute-start.1) | collective-permute-done | bytes 40992 | tf_op jit(solution)/shard_map/ppermute | solution.py:160
  11.9 0.9 %combine.1 = (f32[128,256]{1,0:T(8,128)S(1)}, bf16[128,256]{1,0:T(8,128)(2,1)S(1)}, bf16[128,256]{1,0:T(8,128)(2,1)S(1)}) custom-call(s32[16]{0:T(128)S(1)} %copy-done.10, bf16[80,256]{1,0:T(8,128)(2,1)S(1)} %pack.1.refs_1_, bf16[80,256]{1,0:T(8,128)(2,1)S(1)} %collective-permute-done.refs_2_, bf16[80,256]{1,0:T(8,128)(2,1)S(1)} %collective-permute-done.1.refs_3_, ...), custom_call_target="tpu_custom_call" | custom-call | tf_op jit(solution)/shard_map/combine/pallas_call | solution.py:227
  12.8 1.6 %collective-permute-start.4 = (bf16[128,256]{1,0:T(8,128)(2,1)S(1)}, bf16[128,256]{1,0:T(8,128)(2,1)S(1)}, u32[]{:S(2)}, u32[]{:S(2)}) collective-permute-start(bf16[128,256]{1,0:T(8,128)(2,1)S(1)} %get-tuple-element.22), channel_id=1, source_target_pairs={{0,16},{8,24},{16,0},{24,8},{1,17},{9,25},{17,1},{25,9},{2,18},{10... | collective-permute-start | bytes 196616 | tf_op jit(solution)/shard_map/ppermute | solution.py:160
  14.4 1.4 %collective-permute-start.5 = (bf16[128,256]{1,0:T(8,128)(2,1)S(1)}, bf16[128,256]{1,0:T(8,128)(2,1)S(1)}, u32[]{:S(2)}, u32[]{:S(2)}) collective-permute-start(bf16[128,256]{1,0:T(8,128)(2,1)S(1)} %get-tuple-element.21), channel_id=1, source_target_pairs={{0,17},{1,16},{2,19},{3,18},{4,21},{5,20},{6,23},{7,22},{8,25},{9,... | collective-permute-start | bytes 196616 | tf_op jit(solution)/shard_map/ppermute | solution.py:170
  15.8 0.5 %collective-permute-start.3 = (bf16[128,256]{1,0:T(8,128)(2,1)S(1)}, bf16[128,256]{1,0:T(8,128)(2,1)S(1)}, u32[]{:S(2)}, u32[]{:S(2)}) collective-permute-start(bf16[128,256]{1,0:T(8,128)(2,1)S(1)} %get-tuple-element.21), channel_id=1, source_target_pairs={{0,1},{1,0},{2,3},{3,2},{4,5},{5,4},{6,7},{7,6},{8,9},{9,8},{10,11... | collective-permute-start | bytes 196616 | tf_op jit(solution)/shard_map/ppermute | solution.py:170
  16.3 1.2 %collective-permute-done.4.refs_2_ = bf16[128,256]{1,0:T(8,128)(2,1)S(1)} collective-permute-done((bf16[128,256]{1,0:T(8,128)(2,1)S(1)}, bf16[128,256]{1,0:T(8,128)(2,1)S(1)}, u32[]{:S(2)}, u32[]{:S(2)}) %collective-permute-start.4) | collective-permute-done | bytes 65568 | tf_op jit(solution)/shard_map/ppermute | solution.py:160
  17.5 2.0 %collective-permute-done.5.refs_3_ = bf16[128,256]{1,0:T(8,128)(2,1)S(1)} collective-permute-done((bf16[128,256]{1,0:T(8,128)(2,1)S(1)}, bf16[128,256]{1,0:T(8,128)(2,1)S(1)}, u32[]{:S(2)}, u32[]{:S(2)}) %collective-permute-start.5) | collective-permute-done | bytes 65568 | tf_op jit(solution)/shard_map/ppermute | solution.py:170
  19.5 0.5 %collective-permute-done.3.refs_1_ = bf16[128,256]{1,0:T(8,128)(2,1)S(1)} collective-permute-done((bf16[128,256]{1,0:T(8,128)(2,1)S(1)}, bf16[128,256]{1,0:T(8,128)(2,1)S(1)}, u32[]{:S(2)}, u32[]{:S(2)}) %collective-permute-start.3) | collective-permute-done | bytes 65568 | tf_op jit(solution)/shard_map/ppermute | solution.py:170
  20.1 0.1 merge.1.refs_0_
  20.2 0.1 collective-permute-start.6
  20.3 1.3 %collective-permute-done.6.refs_1_ = bf16[256,256]{1,0:T(8,128)(2,1)S(1)} collective-permute-done((bf16[256,256]{1,0:T(8,128)(2,1)S(1)}, bf16[256,256]{1,0:T(8,128)(2,1)S(1)}, u32[]{:S(2)}, u32[]{:S(2)}) %collective-permute-start.6) | collective-permute-done | bytes 131104 | tf_op jit(solution)/shard_map/ppermute | solution.py:160
  21.6 0.4 %value.1 = (f32[64,512]{1,0:T(8,128)S(1)}, bf16[64,512]{1,0:T(8,128)(2,1)S(1)}, bf16[64,512]{1,0:T(8,128)(2,1)S(1)}, bf16[64,512]{1,0:T(8,128)(2,1)S(1)}) custom-call(bf16[256,256]{1,0:T(8,128)(2,1)S(1)} %merge.1.refs_0_, bf16[256,256]{1,0:T(8,128)(2,1)S(1)} %collective-permute-done.6.refs_1_, bf16[512,256]{1,0:T(8,128)(2,1)S(1)} %price.1.refs_2_, ...), custom_call_target="tpu_custom_call" | custom-call | tf_op jit(solution)/shard_map/value/pallas_call | solution.py:258
  22.0 2.8 %collective-permute-start.8 = (bf16[64,512]{1,0:T(8,128)(2,1)S(1)}, bf16[64,512]{1,0:T(8,128)(2,1)S(1)}, u32[]{:S(2)}, u32[]{:S(2)}) collective-permute-start(bf16[64,512]{1,0:T(8,128)(2,1)S(1)} %get-tuple-element.25), channel_id=1, source_target_pairs={{0,6},{1,7},{2,4},{3,5},{4,2},{5,3},{6,0},{7,1},{8,14},{9,15},{10,... | collective-permute-start | bytes 196616 | tf_op jit(solution)/shard_map/ppermute | solution.py:160
  24.8 1.5 %collective-permute-start.9 = (bf16[64,512]{1,0:T(8,128)(2,1)S(1)}, bf16[64,512]{1,0:T(8,128)(2,1)S(1)}, u32[]{:S(2)}, u32[]{:S(2)}) collective-permute-start(bf16[64,512]{1,0:T(8,128)(2,1)S(1)} %get-tuple-element.26), channel_id=1, source_target_pairs={{0,7},{1,6},{2,5},{3,4},{4,3},{5,2},{6,1},{7,0},{8,15},{9,14},{10,... | collective-permute-start | bytes 196616 | tf_op jit(solution)/shard_map/ppermute | solution.py:160
  26.3 1.1 %collective-permute-start.10 = (bf16[64,512]{1,0:T(8,128)(2,1)S(1)}, bf16[64,512]{1,0:T(8,128)(2,1)S(1)}, u32[]{:S(2)}, u32[]{:S(2)}) collective-permute-start(bf16[64,512]{1,0:T(8,128)(2,1)S(1)} %get-tuple-element.27), channel_id=1, source_target_pairs={{0,1},{1,0},{2,3},{3,2},{4,5},{5,4},{6,7},{7,6},{8,9},{9,8},{10,11... | collective-permute-start | bytes 196616 | tf_op jit(solution)/shard_map/ppermute | solution.py:160
  27.4 0.8 %collective-permute-done.8.refs_1_ = bf16[64,512]{1,0:T(8,128)(2,1)S(1)} collective-permute-done((bf16[64,512]{1,0:T(8,128)(2,1)S(1)}, bf16[64,512]{1,0:T(8,128)(2,1)S(1)}, u32[]{:S(2)}, u32[]{:S(2)}) %collective-permute-start.8) | collective-permute-done | bytes 65568 | tf_op jit(solution)/shard_map/ppermute | solution.py:160
  28.2 3.6 %collective-permute-done.9.refs_2_ = bf16[64,512]{1,0:T(8,128)(2,1)S(1)} collective-permute-done((bf16[64,512]{1,0:T(8,128)(2,1)S(1)}, bf16[64,512]{1,0:T(8,128)(2,1)S(1)}, u32[]{:S(2)}, u32[]{:S(2)}) %collective-permute-start.9) | collective-permute-done | bytes 65568 | tf_op jit(solution)/shard_map/ppermute | solution.py:160
  31.8 0.2 collective-permute-done.10.refs_3_
  32.0 0.1 totals.1
  32.2 1.4 %collective-permute-start.12 = (f32[2,64]{1,0:T(2,128)S(1)}, f32[2,64]{1,0:T(2,128)S(1)}, u32[]{:S(2)}, u32[]{:S(2)}) collective-permute-start(f32[2,64]{1,0:T(2,128)S(1)} %totals.1), channel_id=1, source_target_pairs={{0,16},{8,24},{16,0},{24,8},{1,17},{9,25},{17,1},{25,9},{2,18},{10... | collective-permute-start | bytes 1544 | tf_op jit(solution)/shard_map/ppermute | solution.py:160
  33.5 0.5 %collective-permute-start.11 = (f32[2,64]{1,0:T(2,128)S(1)}, f32[2,64]{1,0:T(2,128)S(1)}, u32[]{:S(2)}, u32[]{:S(2)}) collective-permute-start(f32[2,64]{1,0:T(2,128)S(1)} %totals.1), channel_id=1, source_target_pairs={{0,8},{8,0},{16,24},{24,16},{1,9},{9,1},{17,25},{25,17},{2,10},{10... | collective-permute-start | bytes 1544 | tf_op jit(solution)/shard_map/ppermute | solution.py:160
  34.0 0.7 %expose.1 = f32[2,64,256]{2,1,0:T(8,128)} custom-call(f32[64,512]{1,0:T(8,128)S(1)} %get-tuple-element.24.refs_0_, bf16[64,512]{1,0:T(8,128)(2,1)S(1)} %collective-permute-done.8.refs_1_, bf16[64,512]{1,0:T(8,128)(2,1)S(1)} %collective-permute-done.9.refs_2_, bf16[64,512]{1,0:T(8,128)(2,1)S(1)} %collective-permute-done.10.refs_3_), custom_call_target="tpu_custom_call" | custom-call | tf_op jit(solution)/shard_map/expose/pallas_call | solution.py:282
  34.7 0.4 %collective-permute-done.13 = f32[2,64]{1,0:T(2,128)S(1)} collective-permute-done((f32[2,64]{1,0:T(2,128)S(1)}, f32[2,64]{1,0:T(2,128)S(1)}, u32[]{:S(2)}, u32[]{:S(2)}) %collective-permute-start.13) | collective-permute-done | bytes 544 | tf_op jit(solution)/shard_map/ppermute | solution.py:160
  35.1 0.7 %collective-permute-done.12 = f32[2,64]{1,0:T(2,128)S(1)} collective-permute-done((f32[2,64]{1,0:T(2,128)S(1)}, f32[2,64]{1,0:T(2,128)S(1)}, u32[]{:S(2)}, u32[]{:S(2)}) %collective-permute-start.12) | collective-permute-done | bytes 544 | tf_op jit(solution)/shard_map/ppermute | solution.py:160
  35.8 0.6 %add_multiply_fusion = f32[2,64]{1,0:T(2,128)} fusion(f32[2,64]{1,0:T(2,128)S(1)} %collective-permute-done.12, f32[2,64]{1,0:T(2,128)S(1)} %collective-permute-done.13, f32[2,64]{1,0:T(2,128)S(1)} %totals.1, f32[2,64]{1,0:T(2,128)S(1)} %collective-permute-done.11), kind=kLoop, calls=%fused_computation | loop fusion | flops 512 | bytes 2560 | tf_op jit(solution)/shard_map/div | solution.py:295
  (27 shorter events, 0.1 us)
Async XLA Ops:
  0.6 0.9 %copy-start.4 = (bf16[256,2,128]{2,1,0:T(2,128)(2,1)S(1)}, bf16[256,2,128]{2,1,0:T(2,128)(2,1)}, u32[]{:S(2)}) copy-start(bf16[256,2,128]{2,1,0:T(2,128)(2,1)} %weights_ref.1) | copy-start | bytes 393220
  0.6 0.9 %copy-start.5 = (s32[256,2]{0,1:T(2,128)S(1)}, s32[256,2]{0,1:T(2,128)}, u32[]{:S(2)}) copy-start(s32[256,2]{0,1:T(2,128)} %param.18) | copy-start | bytes 6148
  0.7 0.9 %copy-start.6 = (s32[256]{0:T(256)S(1)}, s32[256]{0:T(256)}, u32[]{:S(2)}) copy-start(s32[256]{0:T(256)} %param.21) | copy-start | bytes 3076
  0.7 7.0 %copy-start = (s32[2,256,256]{2,1,0:T(8,128)S(1)}, s32[2,256,256]{2,1,0:T(8,128)}, u32[]{:S(2)}) copy-start(s32[2,256,256]{2,1,0:T(8,128)} %counts_ref.1) | copy-start | bytes 1572868
  0.7 7.0 %copy-start.1 = (bf16[2,256,256]{2,1,0:T(8,128)(2,1)S(1)}, bf16[2,256,256]{2,1,0:T(8,128)(2,1)}, u32[]{:S(2)}) copy-start(bf16[2,256,256]{2,1,0:T(8,128)(2,1)} %shocks_ref) | copy-start | bytes 786436
  0.7 7.0 %copy-start.2 = (bf16[2,256,256]{2,1,0:T(8,128)(2,1)S(1)}, bf16[2,256,256]{2,1,0:T(8,128)(2,1)}, u32[]{:S(2)}) copy-start(bf16[2,256,256]{2,1,0:T(8,128)(2,1)} %noise_ref.1) | copy-start | bytes 786436
  0.7 7.0 %copy-start.8 = (f32[256]{0:T(256)S(1)}, f32[256]{0:T(256)}, u32[]{:S(2)}) copy-start(f32[256]{0:T(256)} %param.16) | copy-start | bytes 3076
  0.7 7.0 %copy-start.9 = (f32[256]{0:T(256)S(1)}, f32[256]{0:T(256)}, u32[]{:S(2)}) copy-start(f32[256]{0:T(256)} %param.17) | copy-start | bytes 3076
  0.7 6.9 %copy-start.3 = (bf16[256,256]{1,0:T(8,128)(2,1)S(1)}, bf16[256,256]{1,0:T(8,128)(2,1)}, u32[]{:S(2)}) copy-start(bf16[256,256]{1,0:T(8,128)(2,1)} %loadings_ref.1) | copy-start | bytes 393220
  2.0 6.9 %collective-permute-start.2 = (bf16[80,256]{1,0:T(8,128)(2,1)S(1)}, bf16[80,256]{1,0:T(8,128)(2,1)S(1)}, u32[]{:S(2)}, u32[]{:S(2)}) collective-permute-start(bf16[80,256]{1,0:T(8,128)(2,1)S(1)} %pack.1.refs_1_), channel_id=1, source_target_pairs={{0,4},{1,5},{2,6},{3,7},{4,0},{5,1},{6,2},{7,3},{8,12},{9,13},{10,... | collective-permute-start | bytes 122888 | tf_op jit(solution)/shard_map/ppermute | solution.py:160
  6.1 5.8 %collective-permute-start.1 = (bf16[80,256]{1,0:T(8,128)(2,1)S(1)}, bf16[80,256]{1,0:T(8,128)(2,1)S(1)}, u32[]{:S(2)}, u32[]{:S(2)}) collective-permute-start(bf16[80,256]{1,0:T(8,128)(2,1)S(1)} %pack.1.refs_1_), channel_id=1, source_target_pairs={{0,6},{1,7},{2,4},{3,5},{4,2},{5,3},{6,0},{7,1},{8,14},{9,15},{10,... | collective-permute-start | bytes 122888 | tf_op jit(solution)/shard_map/ppermute | solution.py:160
  7.4 4.5 %collective-permute-start = (bf16[80,256]{1,0:T(8,128)(2,1)S(1)}, bf16[80,256]{1,0:T(8,128)(2,1)S(1)}, u32[]{:S(2)}, u32[]{:S(2)}) collective-permute-start(bf16[80,256]{1,0:T(8,128)(2,1)S(1)} %pack.1.refs_1_), channel_id=1, source_target_pairs={{0,2},{1,3},{2,0},{3,1},{4,6},{5,7},{6,4},{7,5},{8,10},{9,11},{10,... | collective-permute-start | bytes 122888 | tf_op jit(solution)/shard_map/ppermute | solution.py:160
  7.6 0.7 %copy-start.7 = (f32[256]{0:T(256)S(1)}, f32[256]{0:T(256)}, u32[]{:S(2)}) copy-start(f32[256]{0:T(256)} %param.13) | copy-start | bytes 3076
  8.3 3.5 %copy-start.10 = (s32[16]{0:T(128)S(1)}, s32[16]{0:T(128)}, u32[]{:S(2)}) copy-start(s32[16]{0:T(128)} %refs_0_.1) | copy-start | bytes 196
  11.9 9.7 %collective-permute-start.7 = (bf16[512,256]{1,0:T(8,128)(2,1)S(1)}, bf16[512,256]{1,0:T(8,128)(2,1)S(1)}, u32[]{:S(2)}, u32[]{:S(2)}) collective-permute-start(bf16[512,256]{1,0:T(8,128)(2,1)S(1)} %price.1.refs_2_), channel_id=1, source_target_pairs={{0,2},{1,3},{2,0},{3,1},{4,6},{5,7},{6,4},{7,5},{8,10},{9,11},{10,... | collective-permute-start | bytes 786440 | tf_op jit(solution)/shard_map/ppermute | solution.py:160
  12.8 4.8 %collective-permute-start.4 = (bf16[128,256]{1,0:T(8,128)(2,1)S(1)}, bf16[128,256]{1,0:T(8,128)(2,1)S(1)}, u32[]{:S(2)}, u32[]{:S(2)}) collective-permute-start(bf16[128,256]{1,0:T(8,128)(2,1)S(1)} %get-tuple-element.22), channel_id=1, source_target_pairs={{0,16},{8,24},{16,0},{24,8},{1,17},{9,25},{17,1},{25,9},{2,18},{10... | collective-permute-start | bytes 196616 | tf_op jit(solution)/shard_map/ppermute | solution.py:160
  14.4 5.2 %collective-permute-start.5 = (bf16[128,256]{1,0:T(8,128)(2,1)S(1)}, bf16[128,256]{1,0:T(8,128)(2,1)S(1)}, u32[]{:S(2)}, u32[]{:S(2)}) collective-permute-start(bf16[128,256]{1,0:T(8,128)(2,1)S(1)} %get-tuple-element.21), channel_id=1, source_target_pairs={{0,17},{1,16},{2,19},{3,18},{4,21},{5,20},{6,23},{7,22},{8,25},{9,... | collective-permute-start | bytes 196616 | tf_op jit(solution)/shard_map/ppermute | solution.py:170
  15.8 4.3 %collective-permute-start.3 = (bf16[128,256]{1,0:T(8,128)(2,1)S(1)}, bf16[128,256]{1,0:T(8,128)(2,1)S(1)}, u32[]{:S(2)}, u32[]{:S(2)}) collective-permute-start(bf16[128,256]{1,0:T(8,128)(2,1)S(1)} %get-tuple-element.21), channel_id=1, source_target_pairs={{0,1},{1,0},{2,3},{3,2},{4,5},{5,4},{6,7},{7,6},{8,9},{9,8},{10,11... | collective-permute-start | bytes 196616 | tf_op jit(solution)/shard_map/ppermute | solution.py:170
  20.2 1.4 %collective-permute-start.6 = (bf16[256,256]{1,0:T(8,128)(2,1)S(1)}, bf16[256,256]{1,0:T(8,128)(2,1)S(1)}, u32[]{:S(2)}, u32[]{:S(2)}) collective-permute-start(bf16[256,256]{1,0:T(8,128)(2,1)S(1)} %merge.1.refs_0_), channel_id=1, source_target_pairs={{0,8},{8,0},{16,24},{24,16},{1,9},{9,1},{17,25},{25,17},{2,10},{10... | collective-permute-start | bytes 393224 | tf_op jit(solution)/shard_map/ppermute | solution.py:160
  22.0 6.2 %collective-permute-start.8 = (bf16[64,512]{1,0:T(8,128)(2,1)S(1)}, bf16[64,512]{1,0:T(8,128)(2,1)S(1)}, u32[]{:S(2)}, u32[]{:S(2)}) collective-permute-start(bf16[64,512]{1,0:T(8,128)(2,1)S(1)} %get-tuple-element.25), channel_id=1, source_target_pairs={{0,6},{1,7},{2,4},{3,5},{4,2},{5,3},{6,0},{7,1},{8,14},{9,15},{10,... | collective-permute-start | bytes 196616 | tf_op jit(solution)/shard_map/ppermute | solution.py:160
  24.8 7.0 %collective-permute-start.9 = (bf16[64,512]{1,0:T(8,128)(2,1)S(1)}, bf16[64,512]{1,0:T(8,128)(2,1)S(1)}, u32[]{:S(2)}, u32[]{:S(2)}) collective-permute-start(bf16[64,512]{1,0:T(8,128)(2,1)S(1)} %get-tuple-element.26), channel_id=1, source_target_pairs={{0,7},{1,6},{2,5},{3,4},{4,3},{5,2},{6,1},{7,0},{8,15},{9,14},{10,... | collective-permute-start | bytes 196616 | tf_op jit(solution)/shard_map/ppermute | solution.py:160
  26.3 5.7 %collective-permute-start.10 = (bf16[64,512]{1,0:T(8,128)(2,1)S(1)}, bf16[64,512]{1,0:T(8,128)(2,1)S(1)}, u32[]{:S(2)}, u32[]{:S(2)}) collective-permute-start(bf16[64,512]{1,0:T(8,128)(2,1)S(1)} %get-tuple-element.27), channel_id=1, source_target_pairs={{0,1},{1,0},{2,3},{3,2},{4,5},{5,4},{6,7},{7,6},{8,9},{9,8},{10,11... | collective-permute-start | bytes 196616 | tf_op jit(solution)/shard_map/ppermute | solution.py:160
  32.1 3.1 %collective-permute-start.13 = (f32[2,64]{1,0:T(2,128)S(1)}, f32[2,64]{1,0:T(2,128)S(1)}, u32[]{:S(2)}, u32[]{:S(2)}) collective-permute-start(f32[2,64]{1,0:T(2,128)S(1)} %totals.1), channel_id=1, source_target_pairs={{0,24},{8,16},{16,8},{24,0},{1,25},{9,17},{17,9},{25,1},{2,26},{10... | collective-permute-start | bytes 1544 | tf_op jit(solution)/shard_map/ppermute | solution.py:160
  32.2 3.6 %collective-permute-start.12 = (f32[2,64]{1,0:T(2,128)S(1)}, f32[2,64]{1,0:T(2,128)S(1)}, u32[]{:S(2)}, u32[]{:S(2)}) collective-permute-start(f32[2,64]{1,0:T(2,128)S(1)} %totals.1), channel_id=1, source_target_pairs={{0,16},{8,24},{16,0},{24,8},{1,17},{9,25},{17,1},{25,9},{2,18},{10... | collective-permute-start | bytes 1544 | tf_op jit(solution)/shard_map/ppermute | solution.py:160
  33.5 2.3 %collective-permute-start.11 = (f32[2,64]{1,0:T(2,128)S(1)}, f32[2,64]{1,0:T(2,128)S(1)}, u32[]{:S(2)}, u32[]{:S(2)}) collective-permute-start(f32[2,64]{1,0:T(2,128)S(1)} %totals.1), channel_id=1, source_target_pairs={{0,8},{8,0},{16,24},{24,16},{1,9},{9,1},{17,25},{25,17},{2,10},{10... | collective-permute-start | bytes 1544 | tf_op jit(solution)/shard_map/ppermute | solution.py:160

commit v7 on v6

--- a/solution.py
+++ b/solution.py
@@ -221,7 +221,6 @@
         compiler_params=PARAMS,
         name="price",
     )(shocks, loadings, vol[None], jump_counts, jump_noise, jump_mean[None], jump_vol[None])
-    prices, *packets = lax.optimization_barrier((prices, *packets))
     share_shape = (2 * held * part, len(owner_flips) * SET_DEV)
     column_trades = len(column_flips) * trades
     own, narrow, other = pl.pallas_call(
@@ -238,6 +237,7 @@
             pltpu.VMEM((share_shape[1], column_trades), jnp.bfloat16),
         ],
         compiler_params=PARAMS,
+        cost_estimate=pl.CostEstimate(flops=10**9, bytes_accessed=0, transcendentals=0),
         name="combine",
     )(block_slot, *packets)
     pair_prices = [prices, from_partner(prices, "fac", PRICE_FLIP)]

time: 36.5 us -> 36.3 us (level)
  waiting for transfers between devices: 13.8 us -> 11.8 us
  starting transfers between devices: 16.6 us -> 18.4 us
    ppermute x12, waiting for transfers between devices: 11.3 us -> 8.84 us  [from_partner(): return lax.ppermute(x, axis, [(i, i ^ flip) for i in range(count)])]
    ppermute x12, starting transfers between devices: 14.6 us -> 16.5 us  [from_partner(): return lax.ppermute(x, axis, [(i, i ^ flip) for i in range(count)])]
    ppermute x2, waiting for transfers between devices: 2.52 us -> 2.95 us  [from_both(): return lax.ppermute(x, ('scen', 'fac'), pairs)]
  transfers between devices with their start and end apart: 14 -> 14, of which waited for: 10 -> 11; matrix products, arithmetic and copies ran while one was open for 0% -> 0% of each run, Pallas kernels for 6% -> 6%
where the time goes in v7:
time: 36.3 us; the launch traced here: 36.2 us
  starting transfers between devices  18.4 us (51%)
  waiting for transfers between devices  11.8 us (33%)
  Pallas kernels  3.11 us (9%)
  local copies, waits for them, and re-layouts  1.47 us (4%)
  between operations  0.8 us (2%)
  other arithmetic  0.57 us (2%)
    ppermute x12, starting transfers between devices, from_partner(): return lax.ppermute(x, axis, [(i, i ^ flip) for i in range(count)])  16.5 us
    ppermute x12, waiting for transfers between devices, from_partner(): return lax.ppermute(x, axis, [(i, i ^ flip) for i in range(count)])  8.84 us
    ppermute x2, waiting for transfers between devices, from_both(): return lax.ppermute(x, ('scen', 'fac'), pairs)  2.95 us
    ppermute x2, starting transfers between devices, from_both(): return lax.ppermute(x, ('scen', 'fac'), pairs)  1.97 us
    unnamed x22, local copies, waits for them, and re-layouts  1.47 us
    pallas_call x1, Pallas kernels, body(): pl.pallas_call(functools.partial(combine_kernel, part, held, owner_flips)...  0.9 us
  transfers between devices with their start and end apart: 14, of which 11 were waited for; matrix products, arithmetic and copies ran while one was open for 0% of the time, Pallas kernels for 6%

profile of v7, /device:TPU:0, one launch (start us, length us, event | category | flops | bytes accessed | tf_op | source)
XLA Modules:
  0.0 36.2 jit_solution(1624839336892193939)
XLA Ops:
  0.7 0.8 %copy-done.4 = bf16[256,2,128]{2,1,0:T(2,128)(2,1)S(1)} copy-done((bf16[256,2,128]{2,1,0:T(2,128)(2,1)S(1)}, bf16[256,2,128]{2,1,0:T(2,128)(2,1)}, u32[]{:S(2)}) %copy-start.4) | copy-done | bytes 131096
  1.5 0.4 %pack.1.refs_1_ = bf16[80,256]{1,0:T(8,128)(2,1)S(1)} custom-call(bf16[32,128]{1,0:T(8,128)(2,1)S(1)} %pick.1.pick_ref, bf16[256,2,128]{2,1,0:T(2,128)(2,1)S(1)} %copy-done.4, s32[2,256]{1,0:T(2,128)S(1)} %bitcast.5, s32[1,256]{1,0:T(1,128)S(1)} %bitcast.6), custom_call_target="tpu_custom_call" | custom-call | tf_op jit(solution)/shard_map/pack/pallas_call | solution.py:204
  2.0 4.1 %collective-permute-start.2 = (bf16[80,256]{1,0:T(8,128)(2,1)S(1)}, bf16[80,256]{1,0:T(8,128)(2,1)S(1)}, u32[]{:S(2)}, u32[]{:S(2)}) collective-permute-start(bf16[80,256]{1,0:T(8,128)(2,1)S(1)} %pack.1.refs_1_), channel_id=1, source_target_pairs={{0,4},{1,5},{2,6},{3,7},{4,0},{5,1},{6,2},{7,3},{8,12},{9,13},{10,... | collective-permute-start | bytes 122888 | tf_op jit(solution)/shard_map/ppermute | solution.py:160
  6.1 1.3 %collective-permute-start.1 = (bf16[80,256]{1,0:T(8,128)(2,1)S(1)}, bf16[80,256]{1,0:T(8,128)(2,1)S(1)}, u32[]{:S(2)}, u32[]{:S(2)}) collective-permute-start(bf16[80,256]{1,0:T(8,128)(2,1)S(1)} %pack.1.refs_1_), channel_id=1, source_target_pairs={{0,6},{1,7},{2,4},{3,5},{4,2},{5,3},{6,0},{7,1},{8,14},{9,15},{10,... | collective-permute-start | bytes 122888 | tf_op jit(solution)/shard_map/ppermute | solution.py:160
  7.4 0.2 collective-permute-start
  7.7 0.6 %copy-done.7 = f32[256]{0:T(256)S(1)} copy-done((f32[256]{0:T(256)S(1)}, f32[256]{0:T(256)}, u32[]{:S(2)}) %copy-start.7) | copy-done | bytes 1048
  8.3 0.5 %price.1.refs_2_ = bf16[512,256]{1,0:T(8,128)(2,1)S(1)} custom-call(bf16[2,256,256]{2,1,0:T(8,128)(2,1)S(1)} %copy-done.1, bf16[256,256]{1,0:T(8,128)(2,1)S(1)} %copy-done.3, f32[1,256]{1,0:T(1,128)S(1)} %bitcast.7, s32[2,256,256]{2,1,0:T(8,128)S(1)} %copy-done, bf16[2,256,256]{2,1,0:T(8,128)(2,1)S(1)} %copy-done.2, f32[1,256]{1,0:T(1,128)S(1)} %bitcast.8, ...), custom_call_target="tpu_custom_call" | custom-call | tf_op jit(solution)/shard_map/price/pallas_call | solution.py:216
  8.8 1.9 %collective-permute-start.7 = (bf16[512,256]{1,0:T(8,128)(2,1)S(1)}, bf16[512,256]{1,0:T(8,128)(2,1)S(1)}, u32[]{:S(2)}, u32[]{:S(2)}) collective-permute-start(bf16[512,256]{1,0:T(8,128)(2,1)S(1)} %price.1.refs_2_), channel_id=1, source_target_pairs={{0,2},{1,3},{2,0},{3,1},{4,6},{5,7},{6,4},{7,5},{8,10},{9,11},{10,... | collective-permute-start | bytes 786440 | tf_op jit(solution)/shard_map/ppermute | solution.py:160
  10.7 1.3 %collective-permute-done.1.refs_3_ = bf16[80,256]{1,0:T(8,128)(2,1)S(1)} collective-permute-done((bf16[80,256]{1,0:T(8,128)(2,1)S(1)}, bf16[80,256]{1,0:T(8,128)(2,1)S(1)}, u32[]{:S(2)}, u32[]{:S(2)}) %collective-permute-start.1) | collective-permute-done | bytes 40992 | tf_op jit(solution)/shard_map/ppermute | solution.py:160
  12.0 0.3 collective-permute-done.refs_2_
  12.3 0.9 %combine.1 = (f32[128,256]{1,0:T(8,128)S(1)}, bf16[128,256]{1,0:T(8,128)(2,1)S(1)}, bf16[128,256]{1,0:T(8,128)(2,1)S(1)}) custom-call(s32[16]{0:T(128)S(1)} %copy-done.10, bf16[80,256]{1,0:T(8,128)(2,1)S(1)} %pack.1.refs_1_, bf16[80,256]{1,0:T(8,128)(2,1)S(1)} %collective-permute-done.refs_2_, bf16[80,256]{1,0:T(8,128)(2,1)S(1)} %collective-permute-done.1.refs_3_, ...), custom_call_target="tpu_custom_call" | custom-call | flops 1000000000 | tf_op jit(solution)/shard_map/combine/pallas_call | solution.py:226
  13.2 1.6 %collective-permute-start.4 = (bf16[128,256]{1,0:T(8,128)(2,1)S(1)}, bf16[128,256]{1,0:T(8,128)(2,1)S(1)}, u32[]{:S(2)}, u32[]{:S(2)}) collective-permute-start(bf16[128,256]{1,0:T(8,128)(2,1)S(1)} %get-tuple-element.12), channel_id=1, source_target_pairs={{0,16},{8,24},{16,0},{24,8},{1,17},{9,25},{17,1},{25,9},{2,18},{10... | collective-permute-start | bytes 196616 | tf_op jit(solution)/shard_map/ppermute | solution.py:160
  14.8 1.4 %collective-permute-start.5 = (bf16[128,256]{1,0:T(8,128)(2,1)S(1)}, bf16[128,256]{1,0:T(8,128)(2,1)S(1)}, u32[]{:S(2)}, u32[]{:S(2)}) collective-permute-start(bf16[128,256]{1,0:T(8,128)(2,1)S(1)} %get-tuple-element.11), channel_id=1, source_target_pairs={{0,17},{1,16},{2,19},{3,18},{4,21},{5,20},{6,23},{7,22},{8,25},{9,... | collective-permute-start | bytes 196616 | tf_op jit(solution)/shard_map/ppermute | solution.py:170
  16.2 0.5 %collective-permute-start.3 = (bf16[128,256]{1,0:T(8,128)(2,1)S(1)}, bf16[128,256]{1,0:T(8,128)(2,1)S(1)}, u32[]{:S(2)}, u32[]{:S(2)}) collective-permute-start(bf16[128,256]{1,0:T(8,128)(2,1)S(1)} %get-tuple-element.11), channel_id=1, source_target_pairs={{0,1},{1,0},{2,3},{3,2},{4,5},{5,4},{6,7},{7,6},{8,9},{9,8},{10,11... | collective-permute-start | bytes 196616 | tf_op jit(solution)/shard_map/ppermute | solution.py:170
  16.8 0.8 %collective-permute-done.4.refs_2_ = bf16[128,256]{1,0:T(8,128)(2,1)S(1)} collective-permute-done((bf16[128,256]{1,0:T(8,128)(2,1)S(1)}, bf16[128,256]{1,0:T(8,128)(2,1)S(1)}, u32[]{:S(2)}, u32[]{:S(2)}) %collective-permute-start.4) | collective-permute-done | bytes 65568 | tf_op jit(solution)/shard_map/ppermute | solution.py:160
  17.5 2.4 %collective-permute-done.5.refs_3_ = bf16[128,256]{1,0:T(8,128)(2,1)S(1)} collective-permute-done((bf16[128,256]{1,0:T(8,128)(2,1)S(1)}, bf16[128,256]{1,0:T(8,128)(2,1)S(1)}, u32[]{:S(2)}, u32[]{:S(2)}) %collective-permute-start.5) | collective-permute-done | bytes 65568 | tf_op jit(solution)/shard_map/ppermute | solution.py:170
  19.9 0.5 %collective-permute-done.3.refs_1_ = bf16[128,256]{1,0:T(8,128)(2,1)S(1)} collective-permute-done((bf16[128,256]{1,0:T(8,128)(2,1)S(1)}, bf16[128,256]{1,0:T(8,128)(2,1)S(1)}, u32[]{:S(2)}, u32[]{:S(2)}) %collective-permute-start.3) | collective-permute-done | bytes 65568 | tf_op jit(solution)/shard_map/ppermute | solution.py:170
  20.7 1.3 %collective-permute-done.6.refs_1_ = bf16[256,256]{1,0:T(8,128)(2,1)S(1)} collective-permute-done((bf16[256,256]{1,0:T(8,128)(2,1)S(1)}, bf16[256,256]{1,0:T(8,128)(2,1)S(1)}, u32[]{:S(2)}, u32[]{:S(2)}) %collective-permute-start.6) | collective-permute-done | bytes 131104 | tf_op jit(solution)/shard_map/ppermute | solution.py:160
  22.0 0.4 %value.1 = (f32[64,512]{1,0:T(8,128)S(1)}, bf16[64,512]{1,0:T(8,128)(2,1)S(1)}, bf16[64,512]{1,0:T(8,128)(2,1)S(1)}, bf16[64,512]{1,0:T(8,128)(2,1)S(1)}) custom-call(bf16[256,256]{1,0:T(8,128)(2,1)S(1)} %merge.1.refs_0_, bf16[256,256]{1,0:T(8,128)(2,1)S(1)} %collective-permute-done.6.refs_1_, bf16[512,256]{1,0:T(8,128)(2,1)S(1)} %price.1.refs_2_, ...), custom_call_target="tpu_custom_call" | custom-call | tf_op jit(solution)/shard_map/value/pallas_call | solution.py:258
  22.4 2.1 %collective-permute-start.8 = (bf16[64,512]{1,0:T(8,128)(2,1)S(1)}, bf16[64,512]{1,0:T(8,128)(2,1)S(1)}, u32[]{:S(2)}, u32[]{:S(2)}) collective-permute-start(bf16[64,512]{1,0:T(8,128)(2,1)S(1)} %get-tuple-element.15), channel_id=1, source_target_pairs={{0,6},{1,7},{2,4},{3,5},{4,2},{5,3},{6,0},{7,1},{8,14},{9,15},{10,... | collective-permute-start | bytes 196616 | tf_op jit(solution)/shard_map/ppermute | solution.py:160
  24.5 2.2 %collective-permute-start.9 = (bf16[64,512]{1,0:T(8,128)(2,1)S(1)}, bf16[64,512]{1,0:T(8,128)(2,1)S(1)}, u32[]{:S(2)}, u32[]{:S(2)}) collective-permute-start(bf16[64,512]{1,0:T(8,128)(2,1)S(1)} %get-tuple-element.16), channel_id=1, source_target_pairs={{0,7},{1,6},{2,5},{3,4},{4,3},{5,2},{6,1},{7,0},{8,15},{9,14},{10,... | collective-permute-start | bytes 196616 | tf_op jit(solution)/shard_map/ppermute | solution.py:160
  26.7 1.1 %collective-permute-start.10 = (bf16[64,512]{1,0:T(8,128)(2,1)S(1)}, bf16[64,512]{1,0:T(8,128)(2,1)S(1)}, u32[]{:S(2)}, u32[]{:S(2)}) collective-permute-start(bf16[64,512]{1,0:T(8,128)(2,1)S(1)} %get-tuple-element.17), channel_id=1, source_target_pairs={{0,1},{1,0},{2,3},{3,2},{4,5},{5,4},{6,7},{7,6},{8,9},{9,8},{10,11... | collective-permute-start | bytes 196616 | tf_op jit(solution)/shard_map/ppermute | solution.py:160
  27.8 0.8 %collective-permute-done.8.refs_1_ = bf16[64,512]{1,0:T(8,128)(2,1)S(1)} collective-permute-done((bf16[64,512]{1,0:T(8,128)(2,1)S(1)}, bf16[64,512]{1,0:T(8,128)(2,1)S(1)}, u32[]{:S(2)}, u32[]{:S(2)}) %collective-permute-start.8) | collective-permute-done | bytes 65568 | tf_op jit(solution)/shard_map/ppermute | solution.py:160
  28.5 3.0 %collective-permute-done.9.refs_2_ = bf16[64,512]{1,0:T(8,128)(2,1)S(1)} collective-permute-done((bf16[64,512]{1,0:T(8,128)(2,1)S(1)}, bf16[64,512]{1,0:T(8,128)(2,1)S(1)}, u32[]{:S(2)}, u32[]{:S(2)}) %collective-permute-start.9) | collective-permute-done | bytes 65568 | tf_op jit(solution)/shard_map/ppermute | solution.py:160
  31.5 0.2 collective-permute-done.10.refs_3_
  31.8 0.1 totals.1
  32.0 1.6 %collective-permute-start.12 = (f32[2,64]{1,0:T(2,128)S(1)}, f32[2,64]{1,0:T(2,128)S(1)}, u32[]{:S(2)}, u32[]{:S(2)}) collective-permute-start(f32[2,64]{1,0:T(2,128)S(1)} %totals.1), channel_id=1, source_target_pairs={{0,16},{8,24},{16,0},{24,8},{1,17},{9,25},{17,1},{25,9},{2,18},{10... | collective-permute-start | bytes 1544 | tf_op jit(solution)/shard_map/ppermute | solution.py:160
  33.6 0.3 collective-permute-start.11
  33.8 0.7 %expose.1 = f32[2,64,256]{2,1,0:T(8,128)} custom-call(f32[64,512]{1,0:T(8,128)S(1)} %get-tuple-element.14.refs_0_, bf16[64,512]{1,0:T(8,128)(2,1)S(1)} %collective-permute-done.8.refs_1_, bf16[64,512]{1,0:T(8,128)(2,1)S(1)} %collective-permute-done.9.refs_2_, bf16[64,512]{1,0:T(8,128)(2,1)S(1)} %collective-permute-done.10.refs_3_), custom_call_target="tpu_custom_call" | custom-call | tf_op jit(solution)/shard_map/expose/pallas_call | solution.py:282
  34.5 0.4 %collective-permute-done.13 = f32[2,64]{1,0:T(2,128)S(1)} collective-permute-done((f32[2,64]{1,0:T(2,128)S(1)}, f32[2,64]{1,0:T(2,128)S(1)}, u32[]{:S(2)}, u32[]{:S(2)}) %collective-permute-start.13) | collective-permute-done | bytes 544 | tf_op jit(solution)/shard_map/ppermute | solution.py:160
  35.0 0.7 %collective-permute-done.12 = f32[2,64]{1,0:T(2,128)S(1)} collective-permute-done((f32[2,64]{1,0:T(2,128)S(1)}, f32[2,64]{1,0:T(2,128)S(1)}, u32[]{:S(2)}, u32[]{:S(2)}) %collective-permute-start.12) | collective-permute-done | bytes 544 | tf_op jit(solution)/shard_map/ppermute | solution.py:160
  35.6 0.6 %add_multiply_fusion = f32[2,64]{1,0:T(2,128)} fusion(f32[2,64]{1,0:T(2,128)S(1)} %collective-permute-done.12, f32[2,64]{1,0:T(2,128)S(1)} %collective-permute-done.13, f32[2,64]{1,0:T(2,128)S(1)} %totals.1, f32[2,64]{1,0:T(2,128)S(1)} %collective-permute-done.11), kind=kLoop, calls=%fused_computation | loop fusion | flops 512 | bytes 2560 | tf_op jit(solution)/shard_map/div | solution.py:295
  (27 shorter events, 0.3 us)
Async XLA Ops:
  0.6 0.9 %copy-start.4 = (bf16[256,2,128]{2,1,0:T(2,128)(2,1)S(1)}, bf16[256,2,128]{2,1,0:T(2,128)(2,1)}, u32[]{:S(2)}) copy-start(bf16[256,2,128]{2,1,0:T(2,128)(2,1)} %weights_ref.1) | copy-start | bytes 393220
  0.6 0.9 %copy-start.5 = (s32[256,2]{0,1:T(2,128)S(1)}, s32[256,2]{0,1:T(2,128)}, u32[]{:S(2)}) copy-start(s32[256,2]{0,1:T(2,128)} %param.18) | copy-start | bytes 6148
  0.7 0.9 %copy-start.6 = (s32[256]{0:T(256)S(1)}, s32[256]{0:T(256)}, u32[]{:S(2)}) copy-start(s32[256]{0:T(256)} %param.21) | copy-start | bytes 3076
  0.7 7.0 %copy-start = (s32[2,256,256]{2,1,0:T(8,128)S(1)}, s32[2,256,256]{2,1,0:T(8,128)}, u32[]{:S(2)}) copy-start(s32[2,256,256]{2,1,0:T(8,128)} %counts_ref.1) | copy-start | bytes 1572868
  0.7 7.0 %copy-start.1 = (bf16[2,256,256]{2,1,0:T(8,128)(2,1)S(1)}, bf16[2,256,256]{2,1,0:T(8,128)(2,1)}, u32[]{:S(2)}) copy-start(bf16[2,256,256]{2,1,0:T(8,128)(2,1)} %shocks_ref) | copy-start | bytes 786436
  0.7 7.0 %copy-start.2 = (bf16[2,256,256]{2,1,0:T(8,128)(2,1)S(1)}, bf16[2,256,256]{2,1,0:T(8,128)(2,1)}, u32[]{:S(2)}) copy-start(bf16[2,256,256]{2,1,0:T(8,128)(2,1)} %noise_ref.1) | copy-start | bytes 786436
  0.7 7.0 %copy-start.8 = (f32[256]{0:T(256)S(1)}, f32[256]{0:T(256)}, u32[]{:S(2)}) copy-start(f32[256]{0:T(256)} %param.16) | copy-start | bytes 3076
  0.7 7.0 %copy-start.9 = (f32[256]{0:T(256)S(1)}, f32[256]{0:T(256)}, u32[]{:S(2)}) copy-start(f32[256]{0:T(256)} %param.17) | copy-start | bytes 3076
  0.7 6.9 %copy-start.3 = (bf16[256,256]{1,0:T(8,128)(2,1)S(1)}, bf16[256,256]{1,0:T(8,128)(2,1)}, u32[]{:S(2)}) copy-start(bf16[256,256]{1,0:T(8,128)(2,1)} %loadings_ref.1) | copy-start | bytes 393220
  2.0 8.7 %collective-permute-start.2 = (bf16[80,256]{1,0:T(8,128)(2,1)S(1)}, bf16[80,256]{1,0:T(8,128)(2,1)S(1)}, u32[]{:S(2)}, u32[]{:S(2)}) collective-permute-start(bf16[80,256]{1,0:T(8,128)(2,1)S(1)} %pack.1.refs_1_), channel_id=1, source_target_pairs={{0,4},{1,5},{2,6},{3,7},{4,0},{5,1},{6,2},{7,3},{8,12},{9,13},{10,... | collective-permute-start | bytes 122888 | tf_op jit(solution)/shard_map/ppermute | solution.py:160
  6.1 5.9 %collective-permute-start.1 = (bf16[80,256]{1,0:T(8,128)(2,1)S(1)}, bf16[80,256]{1,0:T(8,128)(2,1)S(1)}, u32[]{:S(2)}, u32[]{:S(2)}) collective-permute-start(bf16[80,256]{1,0:T(8,128)(2,1)S(1)} %pack.1.refs_1_), channel_id=1, source_target_pairs={{0,6},{1,7},{2,4},{3,5},{4,2},{5,3},{6,0},{7,1},{8,14},{9,15},{10,... | collective-permute-start | bytes 122888 | tf_op jit(solution)/shard_map/ppermute | solution.py:160
  7.4 4.9 %collective-permute-start = (bf16[80,256]{1,0:T(8,128)(2,1)S(1)}, bf16[80,256]{1,0:T(8,128)(2,1)S(1)}, u32[]{:S(2)}, u32[]{:S(2)}) collective-permute-start(bf16[80,256]{1,0:T(8,128)(2,1)S(1)} %pack.1.refs_1_), channel_id=1, source_target_pairs={{0,2},{1,3},{2,0},{3,1},{4,6},{5,7},{6,4},{7,5},{8,10},{9,11},{10,... | collective-permute-start | bytes 122888 | tf_op jit(solution)/shard_map/ppermute | solution.py:160
  7.6 0.7 %copy-start.7 = (f32[256]{0:T(256)S(1)}, f32[256]{0:T(256)}, u32[]{:S(2)}) copy-start(f32[256]{0:T(256)} %param.13) | copy-start | bytes 3076
  8.3 4.0 %copy-start.10 = (s32[16]{0:T(128)S(1)}, s32[16]{0:T(128)}, u32[]{:S(2)}) copy-start(s32[16]{0:T(128)} %refs_0_.1) | copy-start | bytes 196
  8.8 13.2 %collective-permute-start.7 = (bf16[512,256]{1,0:T(8,128)(2,1)S(1)}, bf16[512,256]{1,0:T(8,128)(2,1)S(1)}, u32[]{:S(2)}, u32[]{:S(2)}) collective-permute-start(bf16[512,256]{1,0:T(8,128)(2,1)S(1)} %price.1.refs_2_), channel_id=1, source_target_pairs={{0,2},{1,3},{2,0},{3,1},{4,6},{5,7},{6,4},{7,5},{8,10},{9,11},{10,... | collective-permute-start | bytes 786440 | tf_op jit(solution)/shard_map/ppermute | solution.py:160
  13.2 4.3 %collective-permute-start.4 = (bf16[128,256]{1,0:T(8,128)(2,1)S(1)}, bf16[128,256]{1,0:T(8,128)(2,1)S(1)}, u32[]{:S(2)}, u32[]{:S(2)}) collective-permute-start(bf16[128,256]{1,0:T(8,128)(2,1)S(1)} %get-tuple-element.12), channel_id=1, source_target_pairs={{0,16},{8,24},{16,0},{24,8},{1,17},{9,25},{17,1},{25,9},{2,18},{10... | collective-permute-start | bytes 196616 | tf_op jit(solution)/shard_map/ppermute | solution.py:160
  14.8 5.2 %collective-permute-start.5 = (bf16[128,256]{1,0:T(8,128)(2,1)S(1)}, bf16[128,256]{1,0:T(8,128)(2,1)S(1)}, u32[]{:S(2)}, u32[]{:S(2)}) collective-permute-start(bf16[128,256]{1,0:T(8,128)(2,1)S(1)} %get-tuple-element.11), channel_id=1, source_target_pairs={{0,17},{1,16},{2,19},{3,18},{4,21},{5,20},{6,23},{7,22},{8,25},{9,... | collective-permute-start | bytes 196616 | tf_op jit(solution)/shard_map/ppermute | solution.py:170
  16.2 4.3 %collective-permute-start.3 = (bf16[128,256]{1,0:T(8,128)(2,1)S(1)}, bf16[128,256]{1,0:T(8,128)(2,1)S(1)}, u32[]{:S(2)}, u32[]{:S(2)}) collective-permute-start(bf16[128,256]{1,0:T(8,128)(2,1)S(1)} %get-tuple-element.11), channel_id=1, source_target_pairs={{0,1},{1,0},{2,3},{3,2},{4,5},{5,4},{6,7},{7,6},{8,9},{9,8},{10,11... | collective-permute-start | bytes 196616 | tf_op jit(solution)/shard_map/ppermute | solution.py:170
  20.6 1.4 %collective-permute-start.6 = (bf16[256,256]{1,0:T(8,128)(2,1)S(1)}, bf16[256,256]{1,0:T(8,128)(2,1)S(1)}, u32[]{:S(2)}, u32[]{:S(2)}) collective-permute-start(bf16[256,256]{1,0:T(8,128)(2,1)S(1)} %merge.1.refs_0_), channel_id=1, source_target_pairs={{0,8},{8,0},{16,24},{24,16},{1,9},{9,1},{17,25},{25,17},{2,10},{10... | collective-permute-start | bytes 393224 | tf_op jit(solution)/shard_map/ppermute | solution.py:160
  22.4 6.1 %collective-permute-start.8 = (bf16[64,512]{1,0:T(8,128)(2,1)S(1)}, bf16[64,512]{1,0:T(8,128)(2,1)S(1)}, u32[]{:S(2)}, u32[]{:S(2)}) collective-permute-start(bf16[64,512]{1,0:T(8,128)(2,1)S(1)} %get-tuple-element.15), channel_id=1, source_target_pairs={{0,6},{1,7},{2,4},{3,5},{4,2},{5,3},{6,0},{7,1},{8,14},{9,15},{10,... | collective-permute-start | bytes 196616 | tf_op jit(solution)/shard_map/ppermute | solution.py:160
  24.5 7.0 %collective-permute-start.9 = (bf16[64,512]{1,0:T(8,128)(2,1)S(1)}, bf16[64,512]{1,0:T(8,128)(2,1)S(1)}, u32[]{:S(2)}, u32[]{:S(2)}) collective-permute-start(bf16[64,512]{1,0:T(8,128)(2,1)S(1)} %get-tuple-element.16), channel_id=1, source_target_pairs={{0,7},{1,6},{2,5},{3,4},{4,3},{5,2},{6,1},{7,0},{8,15},{9,14},{10,... | collective-permute-start | bytes 196616 | tf_op jit(solution)/shard_map/ppermute | solution.py:160
  26.7 5.1 %collective-permute-start.10 = (bf16[64,512]{1,0:T(8,128)(2,1)S(1)}, bf16[64,512]{1,0:T(8,128)(2,1)S(1)}, u32[]{:S(2)}, u32[]{:S(2)}) collective-permute-start(bf16[64,512]{1,0:T(8,128)(2,1)S(1)} %get-tuple-element.17), channel_id=1, source_target_pairs={{0,1},{1,0},{2,3},{3,2},{4,5},{5,4},{6,7},{7,6},{8,9},{9,8},{10,11... | collective-permute-start | bytes 196616 | tf_op jit(solution)/shard_map/ppermute | solution.py:160
  31.9 3.1 %collective-permute-start.13 = (f32[2,64]{1,0:T(2,128)S(1)}, f32[2,64]{1,0:T(2,128)S(1)}, u32[]{:S(2)}, u32[]{:S(2)}) collective-permute-start(f32[2,64]{1,0:T(2,128)S(1)} %totals.1), channel_id=1, source_target_pairs={{0,24},{8,16},{16,8},{24,0},{1,25},{9,17},{17,9},{25,1},{2,26},{10... | collective-permute-start | bytes 1544 | tf_op jit(solution)/shard_map/ppermute | solution.py:160
  32.0 3.6 %collective-permute-start.12 = (f32[2,64]{1,0:T(2,128)S(1)}, f32[2,64]{1,0:T(2,128)S(1)}, u32[]{:S(2)}, u32[]{:S(2)}) collective-permute-start(f32[2,64]{1,0:T(2,128)S(1)} %totals.1), channel_id=1, source_target_pairs={{0,16},{8,24},{16,0},{24,8},{1,17},{9,25},{17,1},{25,9},{2,18},{10... | collective-permute-start | bytes 1544 | tf_op jit(solution)/shard_map/ppermute | solution.py:160
  33.6 2.0 %collective-permute-start.11 = (f32[2,64]{1,0:T(2,128)S(1)}, f32[2,64]{1,0:T(2,128)S(1)}, u32[]{:S(2)}, u32[]{:S(2)}) collective-permute-start(f32[2,64]{1,0:T(2,128)S(1)} %totals.1), channel_id=1, source_target_pairs={{0,8},{8,0},{16,24},{24,16},{1,9},{9,1},{17,25},{25,17},{2,10},{10... | collective-permute-start | bytes 1544 | tf_op jit(solution)/shard_map/ppermute | solution.py:160

commit v8 on v7

--- a/solution.py
+++ b/solution.py
@@ -209,8 +209,7 @@
         compiler_params=PARAMS,
         name="pack",
     )(pick, trade_weights, dependencies.T, netting[None])
-    order = column_flips[1:2] + column_flips[:1:-1]
-    packets = [packet] + [from_partner(packet, "fac", i) for i in order]
+    packets = [packet] + [from_partner(packet, "fac", i) for i in column_flips[1:]]
 
     packet, shocks = lax.optimization_barrier((packet, shocks))
     prices = pl.pallas_call(

time: 36.3 us -> 36.1 us (level)
  transfers between devices with their start and end apart: 14 -> 14, of which waited for: 11 -> 10; matrix products, arithmetic and copies ran while one was open for 0% -> 0% of each run, Pallas kernels for 6% -> 6%
where the time goes in v8:
time: 36.1 us; the launch traced here: 35.9 us
  starting transfers between devices  18.1 us (50%)
  waiting for transfers between devices  11.8 us (33%)
  Pallas kernels  3.11 us (9%)
  local copies, waits for them, and re-layouts  1.47 us (4%)
  between operations  0.8 us (2%)
  other arithmetic  0.57 us (2%)
    ppermute x12, starting transfers between devices, from_partner(): return lax.ppermute(x, axis, [(i, i ^ flip) for i in range(count)])  16.1 us
    ppermute x12, waiting for transfers between devices, from_partner(): return lax.ppermute(x, axis, [(i, i ^ flip) for i in range(count)])  9.06 us
    ppermute x2, waiting for transfers between devices, from_both(): return lax.ppermute(x, ('scen', 'fac'), pairs)  2.78 us
    ppermute x2, starting transfers between devices, from_both(): return lax.ppermute(x, ('scen', 'fac'), pairs)  1.97 us
    unnamed x22, local copies, waits for them, and re-layouts  1.47 us
    pallas_call x1, Pallas kernels, body(): pl.pallas_call(functools.partial(combine_kernel, part, held, owner_flips)...  0.9 us
  transfers between devices with their start and end apart: 14, of which 10 were waited for; matrix products, arithmetic and copies ran while one was open for 0% of the time, Pallas kernels for 6%

profile of v8, /device:TPU:0, one launch (start us, length us, event | category | flops | bytes accessed | tf_op | source)
XLA Modules:
  0.0 35.9 jit_solution(864562589412397265)
XLA Ops:
  0.7 0.8 %copy-done.4 = bf16[256,2,128]{2,1,0:T(2,128)(2,1)S(1)} copy-done((bf16[256,2,128]{2,1,0:T(2,128)(2,1)S(1)}, bf16[256,2,128]{2,1,0:T(2,128)(2,1)}, u32[]{:S(2)}) %copy-start.4) | copy-done | bytes 131096
  1.5 0.4 %pack.1.refs_1_ = bf16[80,256]{1,0:T(8,128)(2,1)S(1)} custom-call(bf16[32,128]{1,0:T(8,128)(2,1)S(1)} %pick.1.pick_ref, bf16[256,2,128]{2,1,0:T(2,128)(2,1)S(1)} %copy-done.4, s32[2,256]{1,0:T(2,128)S(1)} %bitcast.5, s32[1,256]{1,0:T(1,128)S(1)} %bitcast.6), custom_call_target="tpu_custom_call" | custom-call | tf_op jit(solution)/shard_map/pack/pallas_call | solution.py:204
  2.0 5.1 %collective-permute-start.2 = (bf16[80,256]{1,0:T(8,128)(2,1)S(1)}, bf16[80,256]{1,0:T(8,128)(2,1)S(1)}, u32[]{:S(2)}, u32[]{:S(2)}) collective-permute-start(bf16[80,256]{1,0:T(8,128)(2,1)S(1)} %pack.1.refs_1_), channel_id=1, source_target_pairs={{0,6},{1,7},{2,4},{3,5},{4,2},{5,3},{6,0},{7,1},{8,14},{9,15},{10,... | collective-permute-start | bytes 122888 | tf_op jit(solution)/shard_map/ppermute | solution.py:160
  7.1 0.6 %collective-permute-start = (bf16[80,256]{1,0:T(8,128)(2,1)S(1)}, bf16[80,256]{1,0:T(8,128)(2,1)S(1)}, u32[]{:S(2)}, u32[]{:S(2)}) collective-permute-start(bf16[80,256]{1,0:T(8,128)(2,1)S(1)} %pack.1.refs_1_), channel_id=1, source_target_pairs={{0,2},{1,3},{2,0},{3,1},{4,6},{5,7},{6,4},{7,5},{8,10},{9,11},{10,... | collective-permute-start | bytes 122888 | tf_op jit(solution)/shard_map/ppermute | solution.py:160
  7.8 0.6 %copy-done.7 = f32[256]{0:T(256)S(1)} copy-done((f32[256]{0:T(256)S(1)}, f32[256]{0:T(256)}, u32[]{:S(2)}) %copy-start.7) | copy-done | bytes 1048
  8.4 0.5 %price.1.refs_2_ = bf16[512,256]{1,0:T(8,128)(2,1)S(1)} custom-call(bf16[2,256,256]{2,1,0:T(8,128)(2,1)S(1)} %copy-done.1, bf16[256,256]{1,0:T(8,128)(2,1)S(1)} %copy-done.3, f32[1,256]{1,0:T(1,128)S(1)} %bitcast.7, s32[2,256,256]{2,1,0:T(8,128)S(1)} %copy-done, bf16[2,256,256]{2,1,0:T(8,128)(2,1)S(1)} %copy-done.2, f32[1,256]{1,0:T(1,128)S(1)} %bitcast.8, ...), custom_call_target="tpu_custom_call" | custom-call | tf_op jit(solution)/shard_map/price/pallas_call | solution.py:215
  8.9 1.5 %collective-permute-start.7 = (bf16[512,256]{1,0:T(8,128)(2,1)S(1)}, bf16[512,256]{1,0:T(8,128)(2,1)S(1)}, u32[]{:S(2)}, u32[]{:S(2)}) collective-permute-start(bf16[512,256]{1,0:T(8,128)(2,1)S(1)} %price.1.refs_2_), channel_id=1, source_target_pairs={{0,2},{1,3},{2,0},{3,1},{4,6},{5,7},{6,4},{7,5},{8,10},{9,11},{10,... | collective-permute-start | bytes 786440 | tf_op jit(solution)/shard_map/ppermute | solution.py:160
  10.3 1.7 %collective-permute-done.1.refs_3_ = bf16[80,256]{1,0:T(8,128)(2,1)S(1)} collective-permute-done((bf16[80,256]{1,0:T(8,128)(2,1)S(1)}, bf16[80,256]{1,0:T(8,128)(2,1)S(1)}, u32[]{:S(2)}, u32[]{:S(2)}) %collective-permute-start.1) | collective-permute-done | bytes 40992 | tf_op jit(solution)/shard_map/ppermute | solution.py:160
  12.1 0.9 %combine.1 = (f32[128,256]{1,0:T(8,128)S(1)}, bf16[128,256]{1,0:T(8,128)(2,1)S(1)}, bf16[128,256]{1,0:T(8,128)(2,1)S(1)}) custom-call(s32[16]{0:T(128)S(1)} %copy-done.10, bf16[80,256]{1,0:T(8,128)(2,1)S(1)} %pack.1.refs_1_, bf16[80,256]{1,0:T(8,128)(2,1)S(1)} %collective-permute-done.refs_2_, bf16[80,256]{1,0:T(8,128)(2,1)S(1)} %collective-permute-done.1.refs_3_, ...), custom_call_target="tpu_custom_call" | custom-call | flops 1000000000 | tf_op jit(solution)/shard_map/combine/pallas_call | solution.py:225
  13.0 1.6 %collective-permute-start.4 = (bf16[128,256]{1,0:T(8,128)(2,1)S(1)}, bf16[128,256]{1,0:T(8,128)(2,1)S(1)}, u32[]{:S(2)}, u32[]{:S(2)}) collective-permute-start(bf16[128,256]{1,0:T(8,128)(2,1)S(1)} %get-tuple-element.12), channel_id=1, source_target_pairs={{0,16},{8,24},{16,0},{24,8},{1,17},{9,25},{17,1},{25,9},{2,18},{10... | collective-permute-start | bytes 196616 | tf_op jit(solution)/shard_map/ppermute | solution.py:160
  14.6 1.4 %collective-permute-start.5 = (bf16[128,256]{1,0:T(8,128)(2,1)S(1)}, bf16[128,256]{1,0:T(8,128)(2,1)S(1)}, u32[]{:S(2)}, u32[]{:S(2)}) collective-permute-start(bf16[128,256]{1,0:T(8,128)(2,1)S(1)} %get-tuple-element.11), channel_id=1, source_target_pairs={{0,17},{1,16},{2,19},{3,18},{4,21},{5,20},{6,23},{7,22},{8,25},{9,... | collective-permute-start | bytes 196616 | tf_op jit(solution)/shard_map/ppermute | solution.py:170
  16.0 0.5 %collective-permute-start.3 = (bf16[128,256]{1,0:T(8,128)(2,1)S(1)}, bf16[128,256]{1,0:T(8,128)(2,1)S(1)}, u32[]{:S(2)}, u32[]{:S(2)}) collective-permute-start(bf16[128,256]{1,0:T(8,128)(2,1)S(1)} %get-tuple-element.11), channel_id=1, source_target_pairs={{0,1},{1,0},{2,3},{3,2},{4,5},{5,4},{6,7},{7,6},{8,9},{9,8},{10,11... | collective-permute-start | bytes 196616 | tf_op jit(solution)/shard_map/ppermute | solution.py:170
  16.6 1.0 %collective-permute-done.4.refs_2_ = bf16[128,256]{1,0:T(8,128)(2,1)S(1)} collective-permute-done((bf16[128,256]{1,0:T(8,128)(2,1)S(1)}, bf16[128,256]{1,0:T(8,128)(2,1)S(1)}, u32[]{:S(2)}, u32[]{:S(2)}) %collective-permute-start.4) | collective-permute-done | bytes 65568 | tf_op jit(solution)/shard_map/ppermute | solution.py:160
  17.5 2.2 %collective-permute-done.5.refs_3_ = bf16[128,256]{1,0:T(8,128)(2,1)S(1)} collective-permute-done((bf16[128,256]{1,0:T(8,128)(2,1)S(1)}, bf16[128,256]{1,0:T(8,128)(2,1)S(1)}, u32[]{:S(2)}, u32[]{:S(2)}) %collective-permute-start.5) | collective-permute-done | bytes 65568 | tf_op jit(solution)/shard_map/ppermute | solution.py:170
  19.7 0.5 %collective-permute-done.3.refs_1_ = bf16[128,256]{1,0:T(8,128)(2,1)S(1)} collective-permute-done((bf16[128,256]{1,0:T(8,128)(2,1)S(1)}, bf16[128,256]{1,0:T(8,128)(2,1)S(1)}, u32[]{:S(2)}, u32[]{:S(2)}) %collective-permute-start.3) | collective-permute-done | bytes 65568 | tf_op jit(solution)/shard_map/ppermute | solution.py:170
  20.3 0.1 merge.1.refs_0_
  20.4 0.1 collective-permute-start.6
  20.5 1.3 %collective-permute-done.6.refs_1_ = bf16[256,256]{1,0:T(8,128)(2,1)S(1)} collective-permute-done((bf16[256,256]{1,0:T(8,128)(2,1)S(1)}, bf16[256,256]{1,0:T(8,128)(2,1)S(1)}, u32[]{:S(2)}, u32[]{:S(2)}) %collective-permute-start.6) | collective-permute-done | bytes 131104 | tf_op jit(solution)/shard_map/ppermute | solution.py:160
  21.8 0.4 %value.1 = (f32[64,512]{1,0:T(8,128)S(1)}, bf16[64,512]{1,0:T(8,128)(2,1)S(1)}, bf16[64,512]{1,0:T(8,128)(2,1)S(1)}, bf16[64,512]{1,0:T(8,128)(2,1)S(1)}) custom-call(bf16[256,256]{1,0:T(8,128)(2,1)S(1)} %merge.1.refs_0_, bf16[256,256]{1,0:T(8,128)(2,1)S(1)} %collective-permute-done.6.refs_1_, bf16[512,256]{1,0:T(8,128)(2,1)S(1)} %price.1.refs_2_, ...), custom_call_target="tpu_custom_call" | custom-call | tf_op jit(solution)/shard_map/value/pallas_call | solution.py:257
  22.2 1.5 %collective-permute-start.8 = (bf16[64,512]{1,0:T(8,128)(2,1)S(1)}, bf16[64,512]{1,0:T(8,128)(2,1)S(1)}, u32[]{:S(2)}, u32[]{:S(2)}) collective-permute-start(bf16[64,512]{1,0:T(8,128)(2,1)S(1)} %get-tuple-element.15), channel_id=1, source_target_pairs={{0,6},{1,7},{2,4},{3,5},{4,2},{5,3},{6,0},{7,1},{8,14},{9,15},{10,... | collective-permute-start | bytes 196616 | tf_op jit(solution)/shard_map/ppermute | solution.py:160
  23.8 2.8 %collective-permute-start.9 = (bf16[64,512]{1,0:T(8,128)(2,1)S(1)}, bf16[64,512]{1,0:T(8,128)(2,1)S(1)}, u32[]{:S(2)}, u32[]{:S(2)}) collective-permute-start(bf16[64,512]{1,0:T(8,128)(2,1)S(1)} %get-tuple-element.16), channel_id=1, source_target_pairs={{0,7},{1,6},{2,5},{3,4},{4,3},{5,2},{6,1},{7,0},{8,15},{9,14},{10,... | collective-permute-start | bytes 196616 | tf_op jit(solution)/shard_map/ppermute | solution.py:160
  26.5 1.1 %collective-permute-start.10 = (bf16[64,512]{1,0:T(8,128)(2,1)S(1)}, bf16[64,512]{1,0:T(8,128)(2,1)S(1)}, u32[]{:S(2)}, u32[]{:S(2)}) collective-permute-start(bf16[64,512]{1,0:T(8,128)(2,1)S(1)} %get-tuple-element.17), channel_id=1, source_target_pairs={{0,1},{1,0},{2,3},{3,2},{4,5},{5,4},{6,7},{7,6},{8,9},{9,8},{10,11... | collective-permute-start | bytes 196616 | tf_op jit(solution)/shard_map/ppermute | solution.py:160
  27.6 0.8 %collective-permute-done.8.refs_1_ = bf16[64,512]{1,0:T(8,128)(2,1)S(1)} collective-permute-done((bf16[64,512]{1,0:T(8,128)(2,1)S(1)}, bf16[64,512]{1,0:T(8,128)(2,1)S(1)}, u32[]{:S(2)}, u32[]{:S(2)}) %collective-permute-start.8) | collective-permute-done | bytes 65568 | tf_op jit(solution)/shard_map/ppermute | solution.py:160
  28.4 2.4 %collective-permute-done.9.refs_2_ = bf16[64,512]{1,0:T(8,128)(2,1)S(1)} collective-permute-done((bf16[64,512]{1,0:T(8,128)(2,1)S(1)}, bf16[64,512]{1,0:T(8,128)(2,1)S(1)}, u32[]{:S(2)}, u32[]{:S(2)}) %collective-permute-start.9) | collective-permute-done | bytes 65568 | tf_op jit(solution)/shard_map/ppermute | solution.py:160
  30.8 0.7 %collective-permute-done.10.refs_3_ = bf16[64,512]{1,0:T(8,128)(2,1)S(1)} collective-permute-done((bf16[64,512]{1,0:T(8,128)(2,1)S(1)}, bf16[64,512]{1,0:T(8,128)(2,1)S(1)}, u32[]{:S(2)}, u32[]{:S(2)}) %collective-permute-start.10) | collective-permute-done | bytes 65568 | tf_op jit(solution)/shard_map/ppermute | solution.py:160
  31.5 0.1 totals.1
  31.7 1.3 %collective-permute-start.12 = (f32[2,64]{1,0:T(2,128)S(1)}, f32[2,64]{1,0:T(2,128)S(1)}, u32[]{:S(2)}, u32[]{:S(2)}) collective-permute-start(f32[2,64]{1,0:T(2,128)S(1)} %totals.1), channel_id=1, source_target_pairs={{0,16},{8,24},{16,0},{24,8},{1,17},{9,25},{17,1},{25,9},{2,18},{10... | collective-permute-start | bytes 1544 | tf_op jit(solution)/shard_map/ppermute | solution.py:160
  33.0 0.5 %collective-permute-start.11 = (f32[2,64]{1,0:T(2,128)S(1)}, f32[2,64]{1,0:T(2,128)S(1)}, u32[]{:S(2)}, u32[]{:S(2)}) collective-permute-start(f32[2,64]{1,0:T(2,128)S(1)} %totals.1), channel_id=1, source_target_pairs={{0,8},{8,0},{16,24},{24,16},{1,9},{9,1},{17,25},{25,17},{2,10},{10... | collective-permute-start | bytes 1544 | tf_op jit(solution)/shard_map/ppermute | solution.py:160
  33.5 0.7 %expose.1 = f32[2,64,256]{2,1,0:T(8,128)} custom-call(f32[64,512]{1,0:T(8,128)S(1)} %get-tuple-element.14.refs_0_, bf16[64,512]{1,0:T(8,128)(2,1)S(1)} %collective-permute-done.8.refs_1_, bf16[64,512]{1,0:T(8,128)(2,1)S(1)} %collective-permute-done.9.refs_2_, bf16[64,512]{1,0:T(8,128)(2,1)S(1)} %collective-permute-done.10.refs_3_), custom_call_target="tpu_custom_call" | custom-call | tf_op jit(solution)/shard_map/expose/pallas_call | solution.py:281
  34.2 0.4 %collective-permute-done.13 = f32[2,64]{1,0:T(2,128)S(1)} collective-permute-done((f32[2,64]{1,0:T(2,128)S(1)}, f32[2,64]{1,0:T(2,128)S(1)}, u32[]{:S(2)}, u32[]{:S(2)}) %collective-permute-start.13) | collective-permute-done | bytes 544 | tf_op jit(solution)/shard_map/ppermute | solution.py:160
  34.7 0.7 %collective-permute-done.12 = f32[2,64]{1,0:T(2,128)S(1)} collective-permute-done((f32[2,64]{1,0:T(2,128)S(1)}, f32[2,64]{1,0:T(2,128)S(1)}, u32[]{:S(2)}, u32[]{:S(2)}) %collective-permute-start.12) | collective-permute-done | bytes 544 | tf_op jit(solution)/shard_map/ppermute | solution.py:160
  35.3 0.6 %add_multiply_fusion = f32[2,64]{1,0:T(2,128)} fusion(f32[2,64]{1,0:T(2,128)S(1)} %collective-permute-done.12, f32[2,64]{1,0:T(2,128)S(1)} %collective-permute-done.13, f32[2,64]{1,0:T(2,128)S(1)} %totals.1, f32[2,64]{1,0:T(2,128)S(1)} %collective-permute-done.11), kind=kLoop, calls=%fused_computation | loop fusion | flops 512 | bytes 2560 | tf_op jit(solution)/shard_map/div | solution.py:294
  (27 shorter events, 0.1 us)
Async XLA Ops:
  0.6 0.9 %copy-start.4 = (bf16[256,2,128]{2,1,0:T(2,128)(2,1)S(1)}, bf16[256,2,128]{2,1,0:T(2,128)(2,1)}, u32[]{:S(2)}) copy-start(bf16[256,2,128]{2,1,0:T(2,128)(2,1)} %weights_ref.1) | copy-start | bytes 393220
  0.6 0.9 %copy-start.5 = (s32[256,2]{0,1:T(2,128)S(1)}, s32[256,2]{0,1:T(2,128)}, u32[]{:S(2)}) copy-start(s32[256,2]{0,1:T(2,128)} %param.18) | copy-start | bytes 6148
  0.7 0.9 %copy-start.6 = (s32[256]{0:T(256)S(1)}, s32[256]{0:T(256)}, u32[]{:S(2)}) copy-start(s32[256]{0:T(256)} %param.21) | copy-start | bytes 3076
  0.7 7.1 %copy-start = (s32[2,256,256]{2,1,0:T(8,128)S(1)}, s32[2,256,256]{2,1,0:T(8,128)}, u32[]{:S(2)}) copy-start(s32[2,256,256]{2,1,0:T(8,128)} %counts_ref.1) | copy-start | bytes 1572868
  0.7 7.1 %copy-start.1 = (bf16[2,256,256]{2,1,0:T(8,128)(2,1)S(1)}, bf16[2,256,256]{2,1,0:T(8,128)(2,1)}, u32[]{:S(2)}) copy-start(bf16[2,256,256]{2,1,0:T(8,128)(2,1)} %shocks_ref) | copy-start | bytes 786436
  0.7 7.0 %copy-start.2 = (bf16[2,256,256]{2,1,0:T(8,128)(2,1)S(1)}, bf16[2,256,256]{2,1,0:T(8,128)(2,1)}, u32[]{:S(2)}) copy-start(bf16[2,256,256]{2,1,0:T(8,128)(2,1)} %noise_ref.1) | copy-start | bytes 786436
  0.7 7.0 %copy-start.8 = (f32[256]{0:T(256)S(1)}, f32[256]{0:T(256)}, u32[]{:S(2)}) copy-start(f32[256]{0:T(256)} %param.16) | copy-start | bytes 3076
  0.7 7.0 %copy-start.9 = (f32[256]{0:T(256)S(1)}, f32[256]{0:T(256)}, u32[]{:S(2)}) copy-start(f32[256]{0:T(256)} %param.17) | copy-start | bytes 3076
  0.7 7.0 %copy-start.3 = (bf16[256,256]{1,0:T(8,128)(2,1)S(1)}, bf16[256,256]{1,0:T(8,128)(2,1)}, u32[]{:S(2)}) copy-start(bf16[256,256]{1,0:T(8,128)(2,1)} %loadings_ref.1) | copy-start | bytes 393220
  2.0 8.4 %collective-permute-start.2 = (bf16[80,256]{1,0:T(8,128)(2,1)S(1)}, bf16[80,256]{1,0:T(8,128)(2,1)S(1)}, u32[]{:S(2)}, u32[]{:S(2)}) collective-permute-start(bf16[80,256]{1,0:T(8,128)(2,1)S(1)} %pack.1.refs_1_), channel_id=1, source_target_pairs={{0,6},{1,7},{2,4},{3,5},{4,2},{5,3},{6,0},{7,1},{8,14},{9,15},{10,... | collective-permute-start | bytes 122888 | tf_op jit(solution)/shard_map/ppermute | solution.py:160
  7.1 5.0 %collective-permute-start.1 = (bf16[80,256]{1,0:T(8,128)(2,1)S(1)}, bf16[80,256]{1,0:T(8,128)(2,1)S(1)}, u32[]{:S(2)}, u32[]{:S(2)}) collective-permute-start(bf16[80,256]{1,0:T(8,128)(2,1)S(1)} %pack.1.refs_1_), channel_id=1, source_target_pairs={{0,4},{1,5},{2,6},{3,7},{4,0},{5,1},{6,2},{7,3},{8,12},{9,13},{10,... | collective-permute-start | bytes 122888 | tf_op jit(solution)/shard_map/ppermute | solution.py:160
  7.1 5.0 %collective-permute-start = (bf16[80,256]{1,0:T(8,128)(2,1)S(1)}, bf16[80,256]{1,0:T(8,128)(2,1)S(1)}, u32[]{:S(2)}, u32[]{:S(2)}) collective-permute-start(bf16[80,256]{1,0:T(8,128)(2,1)S(1)} %pack.1.refs_1_), channel_id=1, source_target_pairs={{0,2},{1,3},{2,0},{3,1},{4,6},{5,7},{6,4},{7,5},{8,10},{9,11},{10,... | collective-permute-start | bytes 122888 | tf_op jit(solution)/shard_map/ppermute | solution.py:160
  7.7 0.7 %copy-start.7 = (f32[256]{0:T(256)S(1)}, f32[256]{0:T(256)}, u32[]{:S(2)}) copy-start(f32[256]{0:T(256)} %param.13) | copy-start | bytes 3076
  8.4 3.7 %copy-start.10 = (s32[16]{0:T(128)S(1)}, s32[16]{0:T(128)}, u32[]{:S(2)}) copy-start(s32[16]{0:T(128)} %refs_0_.1) | copy-start | bytes 196
  8.9 12.9 %collective-permute-start.7 = (bf16[512,256]{1,0:T(8,128)(2,1)S(1)}, bf16[512,256]{1,0:T(8,128)(2,1)S(1)}, u32[]{:S(2)}, u32[]{:S(2)}) collective-permute-start(bf16[512,256]{1,0:T(8,128)(2,1)S(1)} %price.1.refs_2_), channel_id=1, source_target_pairs={{0,2},{1,3},{2,0},{3,1},{4,6},{5,7},{6,4},{7,5},{8,10},{9,11},{10,... | collective-permute-start | bytes 786440 | tf_op jit(solution)/shard_map/ppermute | solution.py:160
  13.0 4.5 %collective-permute-start.4 = (bf16[128,256]{1,0:T(8,128)(2,1)S(1)}, bf16[128,256]{1,0:T(8,128)(2,1)S(1)}, u32[]{:S(2)}, u32[]{:S(2)}) collective-permute-start(bf16[128,256]{1,0:T(8,128)(2,1)S(1)} %get-tuple-element.12), channel_id=1, source_target_pairs={{0,16},{8,24},{16,0},{24,8},{1,17},{9,25},{17,1},{25,9},{2,18},{10... | collective-permute-start | bytes 196616 | tf_op jit(solution)/shard_map/ppermute | solution.py:160
  14.6 5.2 %collective-permute-start.5 = (bf16[128,256]{1,0:T(8,128)(2,1)S(1)}, bf16[128,256]{1,0:T(8,128)(2,1)S(1)}, u32[]{:S(2)}, u32[]{:S(2)}) collective-permute-start(bf16[128,256]{1,0:T(8,128)(2,1)S(1)} %get-tuple-element.11), channel_id=1, source_target_pairs={{0,17},{1,16},{2,19},{3,18},{4,21},{5,20},{6,23},{7,22},{8,25},{9,... | collective-permute-start | bytes 196616 | tf_op jit(solution)/shard_map/ppermute | solution.py:170
  16.0 4.3 %collective-permute-start.3 = (bf16[128,256]{1,0:T(8,128)(2,1)S(1)}, bf16[128,256]{1,0:T(8,128)(2,1)S(1)}, u32[]{:S(2)}, u32[]{:S(2)}) collective-permute-start(bf16[128,256]{1,0:T(8,128)(2,1)S(1)} %get-tuple-element.11), channel_id=1, source_target_pairs={{0,1},{1,0},{2,3},{3,2},{4,5},{5,4},{6,7},{7,6},{8,9},{9,8},{10,11... | collective-permute-start | bytes 196616 | tf_op jit(solution)/shard_map/ppermute | solution.py:170
  20.4 1.4 %collective-permute-start.6 = (bf16[256,256]{1,0:T(8,128)(2,1)S(1)}, bf16[256,256]{1,0:T(8,128)(2,1)S(1)}, u32[]{:S(2)}, u32[]{:S(2)}) collective-permute-start(bf16[256,256]{1,0:T(8,128)(2,1)S(1)} %merge.1.refs_0_), channel_id=1, source_target_pairs={{0,8},{8,0},{16,24},{24,16},{1,9},{9,1},{17,25},{25,17},{2,10},{10... | collective-permute-start | bytes 393224 | tf_op jit(solution)/shard_map/ppermute | solution.py:160
  22.2 6.1 %collective-permute-start.8 = (bf16[64,512]{1,0:T(8,128)(2,1)S(1)}, bf16[64,512]{1,0:T(8,128)(2,1)S(1)}, u32[]{:S(2)}, u32[]{:S(2)}) collective-permute-start(bf16[64,512]{1,0:T(8,128)(2,1)S(1)} %get-tuple-element.15), channel_id=1, source_target_pairs={{0,6},{1,7},{2,4},{3,5},{4,2},{5,3},{6,0},{7,1},{8,14},{9,15},{10,... | collective-permute-start | bytes 196616 | tf_op jit(solution)/shard_map/ppermute | solution.py:160
  23.8 7.0 %collective-permute-start.9 = (bf16[64,512]{1,0:T(8,128)(2,1)S(1)}, bf16[64,512]{1,0:T(8,128)(2,1)S(1)}, u32[]{:S(2)}, u32[]{:S(2)}) collective-permute-start(bf16[64,512]{1,0:T(8,128)(2,1)S(1)} %get-tuple-element.16), channel_id=1, source_target_pairs={{0,7},{1,6},{2,5},{3,4},{4,3},{5,2},{6,1},{7,0},{8,15},{9,14},{10,... | collective-permute-start | bytes 196616 | tf_op jit(solution)/shard_map/ppermute | solution.py:160
  26.5 5.0 %collective-permute-start.10 = (bf16[64,512]{1,0:T(8,128)(2,1)S(1)}, bf16[64,512]{1,0:T(8,128)(2,1)S(1)}, u32[]{:S(2)}, u32[]{:S(2)}) collective-permute-start(bf16[64,512]{1,0:T(8,128)(2,1)S(1)} %get-tuple-element.17), channel_id=1, source_target_pairs={{0,1},{1,0},{2,3},{3,2},{4,5},{5,4},{6,7},{7,6},{8,9},{9,8},{10,11... | collective-permute-start | bytes 196616 | tf_op jit(solution)/shard_map/ppermute | solution.py:160
  31.6 3.1 %collective-permute-start.13 = (f32[2,64]{1,0:T(2,128)S(1)}, f32[2,64]{1,0:T(2,128)S(1)}, u32[]{:S(2)}, u32[]{:S(2)}) collective-permute-start(f32[2,64]{1,0:T(2,128)S(1)} %totals.1), channel_id=1, source_target_pairs={{0,24},{8,16},{16,8},{24,0},{1,25},{9,17},{17,9},{25,1},{2,26},{10... | collective-permute-start | bytes 1544 | tf_op jit(solution)/shard_map/ppermute | solution.py:160
  31.7 3.6 %collective-permute-start.12 = (f32[2,64]{1,0:T(2,128)S(1)}, f32[2,64]{1,0:T(2,128)S(1)}, u32[]{:S(2)}, u32[]{:S(2)}) collective-permute-start(f32[2,64]{1,0:T(2,128)S(1)} %totals.1), channel_id=1, source_target_pairs={{0,16},{8,24},{16,0},{24,8},{1,17},{9,25},{17,1},{25,9},{2,18},{10... | collective-permute-start | bytes 1544 | tf_op jit(solution)/shard_map/ppermute | solution.py:160
  33.0 2.3 %collective-permute-start.11 = (f32[2,64]{1,0:T(2,128)S(1)}, f32[2,64]{1,0:T(2,128)S(1)}, u32[]{:S(2)}, u32[]{:S(2)}) collective-permute-start(f32[2,64]{1,0:T(2,128)S(1)} %totals.1), channel_id=1, source_target_pairs={{0,8},{8,0},{16,24},{24,16},{1,9},{9,1},{17,25},{25,17},{2,10},{10... | collective-permute-start | bytes 1544 | tf_op jit(solution)/shard_map/ppermute | solution.py:160

commit v9 on v7

--- a/solution.py
+++ b/solution.py
@@ -191,7 +191,7 @@
     trades = trade_weights.shape[0]
     part = BLOCK // scen_count
     column_flips = [i for i in range(fac_count) if not i & SIDE_FLIP]
-    owner_flips = [i for i in range(fac_count) if (i // PRICE_FLIP) % 4 in (0, 3)]
+    owner_flips = [i for i in range(fac_count) if not i & PRICE_FLIP]
 
     pick = pl.pallas_call(
         functools.partial(pick_kernel, part),

time: 36.3 us -> 36.7 us (1.011)
  waiting for transfers between devices: 11.8 us -> 13.1 us
  starting transfers between devices: 18.4 us -> 17.5 us
    ppermute x12, waiting for transfers between devices: 8.84 us -> 10.1 us  [from_partner(): return lax.ppermute(x, axis, [(i, i ^ flip) for i in range(count)])]
    ppermute x12, starting transfers between devices: 16.5 us -> 15.6 us  [from_partner(): return lax.ppermute(x, axis, [(i, i ^ flip) for i in range(count)])]
  transfers between devices with their start and end apart: 14 -> 14, of which waited for: 11 -> 10; matrix products, arithmetic and copies ran while one was open for 0% -> 0% of each run, Pallas kernels for 6% -> 6%
where the time goes in v9:
time: 36.7 us; the launch traced here: 36.6 us
  starting transfers between devices  17.5 us (48%)
  waiting for transfers between devices  13.1 us (36%)
  Pallas kernels  3.11 us (8%)
  local copies, waits for them, and re-layouts  1.47 us (4%)
  between operations  0.79 us (2%)
  other arithmetic  0.57 us (2%)
    ppermute x12, starting transfers between devices, from_partner(): return lax.ppermute(x, axis, [(i, i ^ flip) for i in range(count)])  15.6 us
    ppermute x12, waiting for transfers between devices, from_partner(): return lax.ppermute(x, axis, [(i, i ^ flip) for i in range(count)])  10.1 us
    ppermute x2, waiting for transfers between devices, from_both(): return lax.ppermute(x, ('scen', 'fac'), pairs)  2.95 us
    ppermute x2, starting transfers between devices, from_both(): return lax.ppermute(x, ('scen', 'fac'), pairs)  1.97 us
    unnamed x22, local copies, waits for them, and re-layouts  1.47 us
    pallas_call x1, Pallas kernels, body(): pl.pallas_call(functools.partial(combine_kernel, part, held, owner_flips)...  0.9 us
  transfers between devices with their start and end apart: 14, of which 10 were waited for; matrix products, arithmetic and copies ran while one was open for 0% of the time, Pallas kernels for 6%

profile of v9, /device:TPU:0, one launch (start us, length us, event | category | flops | bytes accessed | tf_op | source)
XLA Modules:
  0.0 36.6 jit_solution(16658672803808099790)
XLA Ops:
  0.7 0.8 %copy-done.4 = bf16[256,2,128]{2,1,0:T(2,128)(2,1)S(1)} copy-done((bf16[256,2,128]{2,1,0:T(2,128)(2,1)S(1)}, bf16[256,2,128]{2,1,0:T(2,128)(2,1)}, u32[]{:S(2)}) %copy-start.4) | copy-done | bytes 131096
  1.5 0.4 %pack.1.refs_1_ = bf16[80,256]{1,0:T(8,128)(2,1)S(1)} custom-call(bf16[32,128]{1,0:T(8,128)(2,1)S(1)} %pick.1.pick_ref, bf16[256,2,128]{2,1,0:T(2,128)(2,1)S(1)} %copy-done.4, s32[2,256]{1,0:T(2,128)S(1)} %bitcast.5, s32[1,256]{1,0:T(1,128)S(1)} %bitcast.6), custom_call_target="tpu_custom_call" | custom-call | tf_op jit(solution)/shard_map/pack/pallas_call | solution.py:204
  2.0 4.1 %collective-permute-start.2 = (bf16[80,256]{1,0:T(8,128)(2,1)S(1)}, bf16[80,256]{1,0:T(8,128)(2,1)S(1)}, u32[]{:S(2)}, u32[]{:S(2)}) collective-permute-start(bf16[80,256]{1,0:T(8,128)(2,1)S(1)} %pack.1.refs_1_), channel_id=1, source_target_pairs={{0,4},{1,5},{2,6},{3,7},{4,0},{5,1},{6,2},{7,3},{8,12},{9,13},{10,... | collective-permute-start | bytes 122888 | tf_op jit(solution)/shard_map/ppermute | solution.py:160
  6.1 1.3 %collective-permute-start.1 = (bf16[80,256]{1,0:T(8,128)(2,1)S(1)}, bf16[80,256]{1,0:T(8,128)(2,1)S(1)}, u32[]{:S(2)}, u32[]{:S(2)}) collective-permute-start(bf16[80,256]{1,0:T(8,128)(2,1)S(1)} %pack.1.refs_1_), channel_id=1, source_target_pairs={{0,6},{1,7},{2,4},{3,5},{4,2},{5,3},{6,0},{7,1},{8,14},{9,15},{10,... | collective-permute-start | bytes 122888 | tf_op jit(solution)/shard_map/ppermute | solution.py:160
  7.4 0.2 collective-permute-start
  7.7 0.6 %copy-done.7 = f32[256]{0:T(256)S(1)} copy-done((f32[256]{0:T(256)S(1)}, f32[256]{0:T(256)}, u32[]{:S(2)}) %copy-start.7) | copy-done | bytes 1048
  8.3 0.5 %price.1.refs_2_ = bf16[512,256]{1,0:T(8,128)(2,1)S(1)} custom-call(bf16[2,256,256]{2,1,0:T(8,128)(2,1)S(1)} %copy-done.1, bf16[256,256]{1,0:T(8,128)(2,1)S(1)} %copy-done.3, f32[1,256]{1,0:T(1,128)S(1)} %bitcast.7, s32[2,256,256]{2,1,0:T(8,128)S(1)} %copy-done, bf16[2,256,256]{2,1,0:T(8,128)(2,1)S(1)} %copy-done.2, f32[1,256]{1,0:T(1,128)S(1)} %bitcast.8, ...), custom_call_target="tpu_custom_call" | custom-call | tf_op jit(solution)/shard_map/price/pallas_call | solution.py:216
  8.8 1.9 %collective-permute-start.7 = (bf16[512,256]{1,0:T(8,128)(2,1)S(1)}, bf16[512,256]{1,0:T(8,128)(2,1)S(1)}, u32[]{:S(2)}, u32[]{:S(2)}) collective-permute-start(bf16[512,256]{1,0:T(8,128)(2,1)S(1)} %price.1.refs_2_), channel_id=1, source_target_pairs={{0,2},{1,3},{2,0},{3,1},{4,6},{5,7},{6,4},{7,5},{8,10},{9,11},{10,... | collective-permute-start | bytes 786440 | tf_op jit(solution)/shard_map/ppermute | solution.py:160
  10.7 1.3 %collective-permute-done.1.refs_3_ = bf16[80,256]{1,0:T(8,128)(2,1)S(1)} collective-permute-done((bf16[80,256]{1,0:T(8,128)(2,1)S(1)}, bf16[80,256]{1,0:T(8,128)(2,1)S(1)}, u32[]{:S(2)}, u32[]{:S(2)}) %collective-permute-start.1) | collective-permute-done | bytes 40992 | tf_op jit(solution)/shard_map/ppermute | solution.py:160
  12.0 0.3 collective-permute-done.refs_2_
  12.3 0.9 %combine.1 = (f32[128,256]{1,0:T(8,128)S(1)}, bf16[128,256]{1,0:T(8,128)(2,1)S(1)}, bf16[128,256]{1,0:T(8,128)(2,1)S(1)}) custom-call(s32[16]{0:T(128)S(1)} %copy-done.10, bf16[80,256]{1,0:T(8,128)(2,1)S(1)} %pack.1.refs_1_, bf16[80,256]{1,0:T(8,128)(2,1)S(1)} %collective-permute-done.refs_2_, bf16[80,256]{1,0:T(8,128)(2,1)S(1)} %collective-permute-done.1.refs_3_, ...), custom_call_target="tpu_custom_call" | custom-call | flops 1000000000 | tf_op jit(solution)/shard_map/combine/pallas_call | solution.py:226
  13.2 1.6 %collective-permute-start.4 = (bf16[128,256]{1,0:T(8,128)(2,1)S(1)}, bf16[128,256]{1,0:T(8,128)(2,1)S(1)}, u32[]{:S(2)}, u32[]{:S(2)}) collective-permute-start(bf16[128,256]{1,0:T(8,128)(2,1)S(1)} %get-tuple-element.12), channel_id=1, source_target_pairs={{0,16},{8,24},{16,0},{24,8},{1,17},{9,25},{17,1},{25,9},{2,18},{10... | collective-permute-start | bytes 196616 | tf_op jit(solution)/shard_map/ppermute | solution.py:160
  14.8 1.4 %collective-permute-start.5 = (bf16[128,256]{1,0:T(8,128)(2,1)S(1)}, bf16[128,256]{1,0:T(8,128)(2,1)S(1)}, u32[]{:S(2)}, u32[]{:S(2)}) collective-permute-start(bf16[128,256]{1,0:T(8,128)(2,1)S(1)} %get-tuple-element.11), channel_id=1, source_target_pairs={{0,17},{1,16},{2,19},{3,18},{4,21},{5,20},{6,23},{7,22},{8,25},{9,... | collective-permute-start | bytes 196616 | tf_op jit(solution)/shard_map/ppermute | solution.py:170
  16.2 0.5 %collective-permute-start.3 = (bf16[128,256]{1,0:T(8,128)(2,1)S(1)}, bf16[128,256]{1,0:T(8,128)(2,1)S(1)}, u32[]{:S(2)}, u32[]{:S(2)}) collective-permute-start(bf16[128,256]{1,0:T(8,128)(2,1)S(1)} %get-tuple-element.11), channel_id=1, source_target_pairs={{0,1},{1,0},{2,3},{3,2},{4,5},{5,4},{6,7},{7,6},{8,9},{9,8},{10,11... | collective-permute-start | bytes 196616 | tf_op jit(solution)/shard_map/ppermute | solution.py:170
  16.8 0.8 %collective-permute-done.4.refs_2_ = bf16[128,256]{1,0:T(8,128)(2,1)S(1)} collective-permute-done((bf16[128,256]{1,0:T(8,128)(2,1)S(1)}, bf16[128,256]{1,0:T(8,128)(2,1)S(1)}, u32[]{:S(2)}, u32[]{:S(2)}) %collective-permute-start.4) | collective-permute-done | bytes 65568 | tf_op jit(solution)/shard_map/ppermute | solution.py:160
  17.5 2.4 %collective-permute-done.5.refs_3_ = bf16[128,256]{1,0:T(8,128)(2,1)S(1)} collective-permute-done((bf16[128,256]{1,0:T(8,128)(2,1)S(1)}, bf16[128,256]{1,0:T(8,128)(2,1)S(1)}, u32[]{:S(2)}, u32[]{:S(2)}) %collective-permute-start.5) | collective-permute-done | bytes 65568 | tf_op jit(solution)/shard_map/ppermute | solution.py:170
  19.9 0.5 %collective-permute-done.3.refs_1_ = bf16[128,256]{1,0:T(8,128)(2,1)S(1)} collective-permute-done((bf16[128,256]{1,0:T(8,128)(2,1)S(1)}, bf16[128,256]{1,0:T(8,128)(2,1)S(1)}, u32[]{:S(2)}, u32[]{:S(2)}) %collective-permute-start.3) | collective-permute-done | bytes 65568 | tf_op jit(solution)/shard_map/ppermute | solution.py:170
  20.7 1.3 %collective-permute-done.6.refs_1_ = bf16[256,256]{1,0:T(8,128)(2,1)S(1)} collective-permute-done((bf16[256,256]{1,0:T(8,128)(2,1)S(1)}, bf16[256,256]{1,0:T(8,128)(2,1)S(1)}, u32[]{:S(2)}, u32[]{:S(2)}) %collective-permute-start.6) | collective-permute-done | bytes 131104 | tf_op jit(solution)/shard_map/ppermute | solution.py:160
  22.0 0.4 %value.1 = (f32[64,512]{1,0:T(8,128)S(1)}, bf16[64,512]{1,0:T(8,128)(2,1)S(1)}, bf16[64,512]{1,0:T(8,128)(2,1)S(1)}, bf16[64,512]{1,0:T(8,128)(2,1)S(1)}) custom-call(bf16[256,256]{1,0:T(8,128)(2,1)S(1)} %merge.1.refs_0_, bf16[256,256]{1,0:T(8,128)(2,1)S(1)} %collective-permute-done.6.refs_1_, bf16[512,256]{1,0:T(8,128)(2,1)S(1)} %price.1.refs_2_, ...), custom_call_target="tpu_custom_call" | custom-call | tf_op jit(solution)/shard_map/value/pallas_call | solution.py:258
  22.4 0.9 %collective-permute-start.8 = (bf16[64,512]{1,0:T(8,128)(2,1)S(1)}, bf16[64,512]{1,0:T(8,128)(2,1)S(1)}, u32[]{:S(2)}, u32[]{:S(2)}) collective-permute-start(bf16[64,512]{1,0:T(8,128)(2,1)S(1)} %get-tuple-element.15), channel_id=1, source_target_pairs={{0,4},{1,5},{2,6},{3,7},{4,0},{5,1},{6,2},{7,3},{8,12},{9,13},{10,... | collective-permute-start | bytes 196616 | tf_op jit(solution)/shard_map/ppermute | solution.py:160
  23.3 2.5 %collective-permute-start.9 = (bf16[64,512]{1,0:T(8,128)(2,1)S(1)}, bf16[64,512]{1,0:T(8,128)(2,1)S(1)}, u32[]{:S(2)}, u32[]{:S(2)}) collective-permute-start(bf16[64,512]{1,0:T(8,128)(2,1)S(1)} %get-tuple-element.16), channel_id=1, source_target_pairs={{0,5},{1,4},{2,7},{3,6},{4,1},{5,0},{6,3},{7,2},{8,13},{9,12},{10,... | collective-permute-start | bytes 196616 | tf_op jit(solution)/shard_map/ppermute | solution.py:160
  25.8 1.1 %collective-permute-start.10 = (bf16[64,512]{1,0:T(8,128)(2,1)S(1)}, bf16[64,512]{1,0:T(8,128)(2,1)S(1)}, u32[]{:S(2)}, u32[]{:S(2)}) collective-permute-start(bf16[64,512]{1,0:T(8,128)(2,1)S(1)} %get-tuple-element.17), channel_id=1, source_target_pairs={{0,1},{1,0},{2,3},{3,2},{4,5},{5,4},{6,7},{7,6},{8,9},{9,8},{10,11... | collective-permute-start | bytes 196616 | tf_op jit(solution)/shard_map/ppermute | solution.py:160
  26.9 2.2 %collective-permute-done.8.refs_1_ = bf16[64,512]{1,0:T(8,128)(2,1)S(1)} collective-permute-done((bf16[64,512]{1,0:T(8,128)(2,1)S(1)}, bf16[64,512]{1,0:T(8,128)(2,1)S(1)}, u32[]{:S(2)}, u32[]{:S(2)}) %collective-permute-start.8) | collective-permute-done | bytes 65568 | tf_op jit(solution)/shard_map/ppermute | solution.py:160
  29.1 2.4 %collective-permute-done.9.refs_2_ = bf16[64,512]{1,0:T(8,128)(2,1)S(1)} collective-permute-done((bf16[64,512]{1,0:T(8,128)(2,1)S(1)}, bf16[64,512]{1,0:T(8,128)(2,1)S(1)}, u32[]{:S(2)}, u32[]{:S(2)}) %collective-permute-start.9) | collective-permute-done | bytes 65568 | tf_op jit(solution)/shard_map/ppermute | solution.py:160
  31.5 0.1 totals.1
  31.7 0.8 %collective-permute-start.13 = (f32[2,64]{1,0:T(2,128)S(1)}, f32[2,64]{1,0:T(2,128)S(1)}, u32[]{:S(2)}, u32[]{:S(2)}) collective-permute-start(f32[2,64]{1,0:T(2,128)S(1)} %totals.1), channel_id=1, source_target_pairs={{0,24},{8,16},{16,8},{24,0},{1,25},{9,17},{17,9},{25,1},{2,26},{10... | collective-permute-start | bytes 1544 | tf_op jit(solution)/shard_map/ppermute | solution.py:160
  32.4 1.0 %collective-permute-start.12 = (f32[2,64]{1,0:T(2,128)S(1)}, f32[2,64]{1,0:T(2,128)S(1)}, u32[]{:S(2)}, u32[]{:S(2)}) collective-permute-start(f32[2,64]{1,0:T(2,128)S(1)} %totals.1), channel_id=1, source_target_pairs={{0,16},{8,24},{16,0},{24,8},{1,17},{9,25},{17,1},{25,9},{2,18},{10... | collective-permute-start | bytes 1544 | tf_op jit(solution)/shard_map/ppermute | solution.py:160
  33.4 0.2 collective-permute-start.11
  33.6 0.7 %expose.1 = f32[2,64,256]{2,1,0:T(8,128)} custom-call(f32[64,512]{1,0:T(8,128)S(1)} %get-tuple-element.14.refs_0_, bf16[64,512]{1,0:T(8,128)(2,1)S(1)} %collective-permute-done.8.refs_1_, bf16[64,512]{1,0:T(8,128)(2,1)S(1)} %collective-permute-done.9.refs_2_, bf16[64,512]{1,0:T(8,128)(2,1)S(1)} %collective-permute-done.10.refs_3_), custom_call_target="tpu_custom_call" | custom-call | tf_op jit(solution)/shard_map/expose/pallas_call | solution.py:282
  34.3 0.4 %collective-permute-done.13 = f32[2,64]{1,0:T(2,128)S(1)} collective-permute-done((f32[2,64]{1,0:T(2,128)S(1)}, f32[2,64]{1,0:T(2,128)S(1)}, u32[]{:S(2)}, u32[]{:S(2)}) %collective-permute-start.13) | collective-permute-done | bytes 544 | tf_op jit(solution)/shard_map/ppermute | solution.py:160
  34.7 1.3 %collective-permute-done.12 = f32[2,64]{1,0:T(2,128)S(1)} collective-permute-done((f32[2,64]{1,0:T(2,128)S(1)}, f32[2,64]{1,0:T(2,128)S(1)}, u32[]{:S(2)}, u32[]{:S(2)}) %collective-permute-start.12) | collective-permute-done | bytes 544 | tf_op jit(solution)/shard_map/ppermute | solution.py:160
  36.0 0.6 %add_multiply_fusion = f32[2,64]{1,0:T(2,128)} fusion(f32[2,64]{1,0:T(2,128)S(1)} %collective-permute-done.12, f32[2,64]{1,0:T(2,128)S(1)} %collective-permute-done.13, f32[2,64]{1,0:T(2,128)S(1)} %totals.1, f32[2,64]{1,0:T(2,128)S(1)} %collective-permute-done.11), kind=kLoop, calls=%fused_computation | loop fusion | flops 512 | bytes 2560 | tf_op jit(solution)/shard_map/div | solution.py:295
  (27 shorter events, 0.2 us)
Async XLA Ops:
  0.6 0.9 %copy-start.4 = (bf16[256,2,128]{2,1,0:T(2,128)(2,1)S(1)}, bf16[256,2,128]{2,1,0:T(2,128)(2,1)}, u32[]{:S(2)}) copy-start(bf16[256,2,128]{2,1,0:T(2,128)(2,1)} %weights_ref.1) | copy-start | bytes 393220
  0.6 0.9 %copy-start.5 = (s32[256,2]{0,1:T(2,128)S(1)}, s32[256,2]{0,1:T(2,128)}, u32[]{:S(2)}) copy-start(s32[256,2]{0,1:T(2,128)} %param.18) | copy-start | bytes 6148
  0.7 0.9 %copy-start.6 = (s32[256]{0:T(256)S(1)}, s32[256]{0:T(256)}, u32[]{:S(2)}) copy-start(s32[256]{0:T(256)} %param.21) | copy-start | bytes 3076
  0.7 7.0 %copy-start = (s32[2,256,256]{2,1,0:T(8,128)S(1)}, s32[2,256,256]{2,1,0:T(8,128)}, u32[]{:S(2)}) copy-start(s32[2,256,256]{2,1,0:T(8,128)} %counts_ref.1) | copy-start | bytes 1572868
  0.7 7.0 %copy-start.1 = (bf16[2,256,256]{2,1,0:T(8,128)(2,1)S(1)}, bf16[2,256,256]{2,1,0:T(8,128)(2,1)}, u32[]{:S(2)}) copy-start(bf16[2,256,256]{2,1,0:T(8,128)(2,1)} %shocks_ref) | copy-start | bytes 786436
  0.7 7.0 %copy-start.2 = (bf16[2,256,256]{2,1,0:T(8,128)(2,1)S(1)}, bf16[2,256,256]{2,1,0:T(8,128)(2,1)}, u32[]{:S(2)}) copy-start(bf16[2,256,256]{2,1,0:T(8,128)(2,1)} %noise_ref.1) | copy-start | bytes 786436
  0.7 7.0 %copy-start.8 = (f32[256]{0:T(256)S(1)}, f32[256]{0:T(256)}, u32[]{:S(2)}) copy-start(f32[256]{0:T(256)} %param.16) | copy-start | bytes 3076
  0.7 7.0 %copy-start.9 = (f32[256]{0:T(256)S(1)}, f32[256]{0:T(256)}, u32[]{:S(2)}) copy-start(f32[256]{0:T(256)} %param.17) | copy-start | bytes 3076
  0.7 6.9 %copy-start.3 = (bf16[256,256]{1,0:T(8,128)(2,1)S(1)}, bf16[256,256]{1,0:T(8,128)(2,1)}, u32[]{:S(2)}) copy-start(bf16[256,256]{1,0:T(8,128)(2,1)} %loadings_ref.1) | copy-start | bytes 393220
  2.0 8.7 %collective-permute-start.2 = (bf16[80,256]{1,0:T(8,128)(2,1)S(1)}, bf16[80,256]{1,0:T(8,128)(2,1)S(1)}, u32[]{:S(2)}, u32[]{:S(2)}) collective-permute-start(bf16[80,256]{1,0:T(8,128)(2,1)S(1)} %pack.1.refs_1_), channel_id=1, source_target_pairs={{0,4},{1,5},{2,6},{3,7},{4,0},{5,1},{6,2},{7,3},{8,12},{9,13},{10,... | collective-permute-start | bytes 122888 | tf_op jit(solution)/shard_map/ppermute | solution.py:160
  6.1 5.9 %collective-permute-start.1 = (bf16[80,256]{1,0:T(8,128)(2,1)S(1)}, bf16[80,256]{1,0:T(8,128)(2,1)S(1)}, u32[]{:S(2)}, u32[]{:S(2)}) collective-permute-start(bf16[80,256]{1,0:T(8,128)(2,1)S(1)} %pack.1.refs_1_), channel_id=1, source_target_pairs={{0,6},{1,7},{2,4},{3,5},{4,2},{5,3},{6,0},{7,1},{8,14},{9,15},{10,... | collective-permute-start | bytes 122888 | tf_op jit(solution)/shard_map/ppermute | solution.py:160
  7.4 4.9 %collective-permute-start = (bf16[80,256]{1,0:T(8,128)(2,1)S(1)}, bf16[80,256]{1,0:T(8,128)(2,1)S(1)}, u32[]{:S(2)}, u32[]{:S(2)}) collective-permute-start(bf16[80,256]{1,0:T(8,128)(2,1)S(1)} %pack.1.refs_1_), channel_id=1, source_target_pairs={{0,2},{1,3},{2,0},{3,1},{4,6},{5,7},{6,4},{7,5},{8,10},{9,11},{10,... | collective-permute-start | bytes 122888 | tf_op jit(solution)/shard_map/ppermute | solution.py:160
  7.6 0.7 %copy-start.7 = (f32[256]{0:T(256)S(1)}, f32[256]{0:T(256)}, u32[]{:S(2)}) copy-start(f32[256]{0:T(256)} %param.13) | copy-start | bytes 3076
  8.3 4.0 %copy-start.10 = (s32[16]{0:T(128)S(1)}, s32[16]{0:T(128)}, u32[]{:S(2)}) copy-start(s32[16]{0:T(128)} %refs_0_.1) | copy-start | bytes 196
  8.8 13.2 %collective-permute-start.7 = (bf16[512,256]{1,0:T(8,128)(2,1)S(1)}, bf16[512,256]{1,0:T(8,128)(2,1)S(1)}, u32[]{:S(2)}, u32[]{:S(2)}) collective-permute-start(bf16[512,256]{1,0:T(8,128)(2,1)S(1)} %price.1.refs_2_), channel_id=1, source_target_pairs={{0,2},{1,3},{2,0},{3,1},{4,6},{5,7},{6,4},{7,5},{8,10},{9,11},{10,... | collective-permute-start | bytes 786440 | tf_op jit(solution)/shard_map/ppermute | solution.py:160
  13.2 4.3 %collective-permute-start.4 = (bf16[128,256]{1,0:T(8,128)(2,1)S(1)}, bf16[128,256]{1,0:T(8,128)(2,1)S(1)}, u32[]{:S(2)}, u32[]{:S(2)}) collective-permute-start(bf16[128,256]{1,0:T(8,128)(2,1)S(1)} %get-tuple-element.12), channel_id=1, source_target_pairs={{0,16},{8,24},{16,0},{24,8},{1,17},{9,25},{17,1},{25,9},{2,18},{10... | collective-permute-start | bytes 196616 | tf_op jit(solution)/shard_map/ppermute | solution.py:160
  14.8 5.2 %collective-permute-start.5 = (bf16[128,256]{1,0:T(8,128)(2,1)S(1)}, bf16[128,256]{1,0:T(8,128)(2,1)S(1)}, u32[]{:S(2)}, u32[]{:S(2)}) collective-permute-start(bf16[128,256]{1,0:T(8,128)(2,1)S(1)} %get-tuple-element.11), channel_id=1, source_target_pairs={{0,17},{1,16},{2,19},{3,18},{4,21},{5,20},{6,23},{7,22},{8,25},{9,... | collective-permute-start | bytes 196616 | tf_op jit(solution)/shard_map/ppermute | solution.py:170
  16.2 4.3 %collective-permute-start.3 = (bf16[128,256]{1,0:T(8,128)(2,1)S(1)}, bf16[128,256]{1,0:T(8,128)(2,1)S(1)}, u32[]{:S(2)}, u32[]{:S(2)}) collective-permute-start(bf16[128,256]{1,0:T(8,128)(2,1)S(1)} %get-tuple-element.11), channel_id=1, source_target_pairs={{0,1},{1,0},{2,3},{3,2},{4,5},{5,4},{6,7},{7,6},{8,9},{9,8},{10,11... | collective-permute-start | bytes 196616 | tf_op jit(solution)/shard_map/ppermute | solution.py:170
  20.6 1.4 %collective-permute-start.6 = (bf16[256,256]{1,0:T(8,128)(2,1)S(1)}, bf16[256,256]{1,0:T(8,128)(2,1)S(1)}, u32[]{:S(2)}, u32[]{:S(2)}) collective-permute-start(bf16[256,256]{1,0:T(8,128)(2,1)S(1)} %merge.1.refs_0_), channel_id=1, source_target_pairs={{0,8},{8,0},{16,24},{24,16},{1,9},{9,1},{17,25},{25,17},{2,10},{10... | collective-permute-start | bytes 393224 | tf_op jit(solution)/shard_map/ppermute | solution.py:160
  22.4 6.7 %collective-permute-start.8 = (bf16[64,512]{1,0:T(8,128)(2,1)S(1)}, bf16[64,512]{1,0:T(8,128)(2,1)S(1)}, u32[]{:S(2)}, u32[]{:S(2)}) collective-permute-start(bf16[64,512]{1,0:T(8,128)(2,1)S(1)} %get-tuple-element.15), channel_id=1, source_target_pairs={{0,4},{1,5},{2,6},{3,7},{4,0},{5,1},{6,2},{7,3},{8,12},{9,13},{10,... | collective-permute-start | bytes 196616 | tf_op jit(solution)/shard_map/ppermute | solution.py:160
  23.3 8.2 %collective-permute-start.9 = (bf16[64,512]{1,0:T(8,128)(2,1)S(1)}, bf16[64,512]{1,0:T(8,128)(2,1)S(1)}, u32[]{:S(2)}, u32[]{:S(2)}) collective-permute-start(bf16[64,512]{1,0:T(8,128)(2,1)S(1)} %get-tuple-element.16), channel_id=1, source_target_pairs={{0,5},{1,4},{2,7},{3,6},{4,1},{5,0},{6,3},{7,2},{8,13},{9,12},{10,... | collective-permute-start | bytes 196616 | tf_op jit(solution)/shard_map/ppermute | solution.py:160
  25.8 5.7 %collective-permute-start.10 = (bf16[64,512]{1,0:T(8,128)(2,1)S(1)}, bf16[64,512]{1,0:T(8,128)(2,1)S(1)}, u32[]{:S(2)}, u32[]{:S(2)}) collective-permute-start(bf16[64,512]{1,0:T(8,128)(2,1)S(1)} %get-tuple-element.17), channel_id=1, source_target_pairs={{0,1},{1,0},{2,3},{3,2},{4,5},{5,4},{6,7},{7,6},{8,9},{9,8},{10,11... | collective-permute-start | bytes 196616 | tf_op jit(solution)/shard_map/ppermute | solution.py:160
  31.7 3.1 %collective-permute-start.13 = (f32[2,64]{1,0:T(2,128)S(1)}, f32[2,64]{1,0:T(2,128)S(1)}, u32[]{:S(2)}, u32[]{:S(2)}) collective-permute-start(f32[2,64]{1,0:T(2,128)S(1)} %totals.1), channel_id=1, source_target_pairs={{0,24},{8,16},{16,8},{24,0},{1,25},{9,17},{17,9},{25,1},{2,26},{10... | collective-permute-start | bytes 1544 | tf_op jit(solution)/shard_map/ppermute | solution.py:160
  32.4 3.6 %collective-permute-start.12 = (f32[2,64]{1,0:T(2,128)S(1)}, f32[2,64]{1,0:T(2,128)S(1)}, u32[]{:S(2)}, u32[]{:S(2)}) collective-permute-start(f32[2,64]{1,0:T(2,128)S(1)} %totals.1), channel_id=1, source_target_pairs={{0,16},{8,24},{16,0},{24,8},{1,17},{9,25},{17,1},{25,9},{2,18},{10... | collective-permute-start | bytes 1544 | tf_op jit(solution)/shard_map/ppermute | solution.py:160
  33.4 2.6 %collective-permute-start.11 = (f32[2,64]{1,0:T(2,128)S(1)}, f32[2,64]{1,0:T(2,128)S(1)}, u32[]{:S(2)}, u32[]{:S(2)}) collective-permute-start(f32[2,64]{1,0:T(2,128)S(1)} %totals.1), channel_id=1, source_target_pairs={{0,8},{8,0},{16,24},{24,16},{1,9},{9,1},{17,25},{25,17},{2,10},{10... | collective-permute-start | bytes 1544 | tf_op jit(solution)/shard_map/ppermute | solution.py:160

commit v10 on v8

--- a/solution.py
+++ b/solution.py
@@ -11,7 +11,8 @@
 SET_DEV = 64
 DATES = 2
 SIDE_FLIP = 1
-PRICE_FLIP = 2
+PRICE_FLIP = 6
+HALF_FLIP = 4
 TAGS = 16
 CHUNK = 64
 
@@ -191,7 +192,7 @@
     trades = trade_weights.shape[0]
     part = BLOCK // scen_count
     column_flips = [i for i in range(fac_count) if not i & SIDE_FLIP]
-    owner_flips = [i for i in range(fac_count) if (i // PRICE_FLIP) % 4 in (0, 3)]
+    owner_flips = [i for i in range(fac_count) if not i & HALF_FLIP]
 
     pick = pl.pallas_call(
         functools.partial(pick_kernel, part),

time: 36.1 us -> 34.7 us (0.961)
  waiting for transfers between devices: 11.8 us -> 9.88 us
  starting transfers between devices: 18.1 us -> 18.7 us
    ppermute x12, waiting for transfers between devices: 9.06 us -> 7.52 us  [from_partner(): return lax.ppermute(x, axis, [(i, i ^ flip) for i in range(count)])]
    ppermute x12, starting transfers between devices: 16.1 us -> 16.7 us  [from_partner(): return lax.ppermute(x, axis, [(i, i ^ flip) for i in range(count)])]
    ppermute x2, waiting for transfers between devices: 2.78 us -> 2.37 us  [from_both(): return lax.ppermute(x, ('scen', 'fac'), pairs)]
  transfers between devices with their start and end apart: 14 -> 14, of which waited for: 10 -> 9; matrix products, arithmetic and copies ran while one was open for 0% -> 0% of each run, Pallas kernels for 6% -> 6%
where the time goes in v10:
time: 34.7 us; the launch traced here: 34.5 us
  starting transfers between devices  18.7 us (54%)
  waiting for transfers between devices  9.88 us (28%)
  Pallas kernels  3.12 us (9%)
  local copies, waits for them, and re-layouts  1.47 us (4%)
  between operations  0.81 us (2%)
  other arithmetic  0.57 us (2%)
    ppermute x12, starting transfers between devices, from_partner(): return lax.ppermute(x, axis, [(i, i ^ flip) for i in range(count)])  16.7 us
    ppermute x12, waiting for transfers between devices, from_partner(): return lax.ppermute(x, axis, [(i, i ^ flip) for i in range(count)])  7.52 us
    ppermute x2, waiting for transfers between devices, from_both(): return lax.ppermute(x, ('scen', 'fac'), pairs)  2.37 us
    ppermute x2, starting transfers between devices, from_both(): return lax.ppermute(x, ('scen', 'fac'), pairs)  1.97 us
    unnamed x22, local copies, waits for them, and re-layouts  1.47 us
    pallas_call x1, Pallas kernels, body(): pl.pallas_call(functools.partial(combine_kernel, part, held, owner_flips)...  0.9 us
  transfers between devices with their start and end apart: 14, of which 9 were waited for; matrix products, arithmetic and copies ran while one was open for 0% of the time, Pallas kernels for 6%

profile of v10, /device:TPU:0, one launch (start us, length us, event | category | flops | bytes accessed | tf_op | source)
XLA Modules:
  0.0 34.5 jit_solution(9757570025207409882)
XLA Ops:
  0.7 0.8 %copy-done.4 = bf16[256,2,128]{2,1,0:T(2,128)(2,1)S(1)} copy-done((bf16[256,2,128]{2,1,0:T(2,128)(2,1)S(1)}, bf16[256,2,128]{2,1,0:T(2,128)(2,1)}, u32[]{:S(2)}) %copy-start.4) | copy-done | bytes 131096
  1.5 0.4 %pack.1.refs_1_ = bf16[80,256]{1,0:T(8,128)(2,1)S(1)} custom-call(bf16[32,128]{1,0:T(8,128)(2,1)S(1)} %pick.1.pick_ref, bf16[256,2,128]{2,1,0:T(2,128)(2,1)S(1)} %copy-done.4, s32[2,256]{1,0:T(2,128)S(1)} %bitcast.5, s32[1,256]{1,0:T(1,128)S(1)} %bitcast.6), custom_call_target="tpu_custom_call" | custom-call | tf_op jit(solution)/shard_map/pack/pallas_call | solution.py:205
  2.0 5.1 %collective-permute-start.2 = (bf16[80,256]{1,0:T(8,128)(2,1)S(1)}, bf16[80,256]{1,0:T(8,128)(2,1)S(1)}, u32[]{:S(2)}, u32[]{:S(2)}) collective-permute-start(bf16[80,256]{1,0:T(8,128)(2,1)S(1)} %pack.1.refs_1_), channel_id=1, source_target_pairs={{0,6},{1,7},{2,4},{3,5},{4,2},{5,3},{6,0},{7,1},{8,14},{9,15},{10,... | collective-permute-start | bytes 122888 | tf_op jit(solution)/shard_map/ppermute | solution.py:161
  7.1 0.6 %collective-permute-start = (bf16[80,256]{1,0:T(8,128)(2,1)S(1)}, bf16[80,256]{1,0:T(8,128)(2,1)S(1)}, u32[]{:S(2)}, u32[]{:S(2)}) collective-permute-start(bf16[80,256]{1,0:T(8,128)(2,1)S(1)} %pack.1.refs_1_), channel_id=1, source_target_pairs={{0,2},{1,3},{2,0},{3,1},{4,6},{5,7},{6,4},{7,5},{8,10},{9,11},{10,... | collective-permute-start | bytes 122888 | tf_op jit(solution)/shard_map/ppermute | solution.py:161
  7.8 0.6 %copy-done.7 = f32[256]{0:T(256)S(1)} copy-done((f32[256]{0:T(256)S(1)}, f32[256]{0:T(256)}, u32[]{:S(2)}) %copy-start.7) | copy-done | bytes 1048
  8.4 0.5 %price.1.refs_2_ = bf16[512,256]{1,0:T(8,128)(2,1)S(1)} custom-call(bf16[2,256,256]{2,1,0:T(8,128)(2,1)S(1)} %copy-done.1, bf16[256,256]{1,0:T(8,128)(2,1)S(1)} %copy-done.3, f32[1,256]{1,0:T(1,128)S(1)} %bitcast.7, s32[2,256,256]{2,1,0:T(8,128)S(1)} %copy-done, bf16[2,256,256]{2,1,0:T(8,128)(2,1)S(1)} %copy-done.2, f32[1,256]{1,0:T(1,128)S(1)} %bitcast.8, ...), custom_call_target="tpu_custom_call" | custom-call | tf_op jit(solution)/shard_map/price/pallas_call | solution.py:216
  8.9 3.8 %collective-permute-start.7 = (bf16[512,256]{1,0:T(8,128)(2,1)S(1)}, bf16[512,256]{1,0:T(8,128)(2,1)S(1)}, u32[]{:S(2)}, u32[]{:S(2)}) collective-permute-start(bf16[512,256]{1,0:T(8,128)(2,1)S(1)} %price.1.refs_2_), channel_id=1, source_target_pairs={{0,6},{1,7},{2,4},{3,5},{4,2},{5,3},{6,0},{7,1},{8,14},{9,15},{10,... | collective-permute-start | bytes 786440 | tf_op jit(solution)/shard_map/ppermute | solution.py:161
  12.7 0.9 %combine.1 = (f32[128,256]{1,0:T(8,128)S(1)}, bf16[128,256]{1,0:T(8,128)(2,1)S(1)}, bf16[128,256]{1,0:T(8,128)(2,1)S(1)}) custom-call(s32[16]{0:T(128)S(1)} %copy-done.10, bf16[80,256]{1,0:T(8,128)(2,1)S(1)} %pack.1.refs_1_, bf16[80,256]{1,0:T(8,128)(2,1)S(1)} %collective-permute-done.refs_2_, bf16[80,256]{1,0:T(8,128)(2,1)S(1)} %collective-permute-done.1.refs_3_, ...), custom_call_target="tpu_custom_call" | custom-call | flops 1000000000 | tf_op jit(solution)/shard_map/combine/pallas_call | solution.py:226
  13.6 1.6 %collective-permute-start.4 = (bf16[128,256]{1,0:T(8,128)(2,1)S(1)}, bf16[128,256]{1,0:T(8,128)(2,1)S(1)}, u32[]{:S(2)}, u32[]{:S(2)}) collective-permute-start(bf16[128,256]{1,0:T(8,128)(2,1)S(1)} %get-tuple-element.12), channel_id=1, source_target_pairs={{0,16},{8,24},{16,0},{24,8},{1,17},{9,25},{17,1},{25,9},{2,18},{10... | collective-permute-start | bytes 196616 | tf_op jit(solution)/shard_map/ppermute | solution.py:161
  15.2 1.4 %collective-permute-start.5 = (bf16[128,256]{1,0:T(8,128)(2,1)S(1)}, bf16[128,256]{1,0:T(8,128)(2,1)S(1)}, u32[]{:S(2)}, u32[]{:S(2)}) collective-permute-start(bf16[128,256]{1,0:T(8,128)(2,1)S(1)} %get-tuple-element.11), channel_id=1, source_target_pairs={{0,17},{1,16},{2,19},{3,18},{4,21},{5,20},{6,23},{7,22},{8,25},{9,... | collective-permute-start | bytes 196616 | tf_op jit(solution)/shard_map/ppermute | solution.py:171
  16.6 0.5 %collective-permute-start.3 = (bf16[128,256]{1,0:T(8,128)(2,1)S(1)}, bf16[128,256]{1,0:T(8,128)(2,1)S(1)}, u32[]{:S(2)}, u32[]{:S(2)}) collective-permute-start(bf16[128,256]{1,0:T(8,128)(2,1)S(1)} %get-tuple-element.11), channel_id=1, source_target_pairs={{0,1},{1,0},{2,3},{3,2},{4,5},{5,4},{6,7},{7,6},{8,9},{9,8},{10,11... | collective-permute-start | bytes 196616 | tf_op jit(solution)/shard_map/ppermute | solution.py:171
  17.2 1.4 %collective-permute-done.4.refs_2_ = bf16[128,256]{1,0:T(8,128)(2,1)S(1)} collective-permute-done((bf16[128,256]{1,0:T(8,128)(2,1)S(1)}, bf16[128,256]{1,0:T(8,128)(2,1)S(1)}, u32[]{:S(2)}, u32[]{:S(2)}) %collective-permute-start.4) | collective-permute-done | bytes 65568 | tf_op jit(solution)/shard_map/ppermute | solution.py:161
  18.5 1.8 %collective-permute-done.5.refs_3_ = bf16[128,256]{1,0:T(8,128)(2,1)S(1)} collective-permute-done((bf16[128,256]{1,0:T(8,128)(2,1)S(1)}, bf16[128,256]{1,0:T(8,128)(2,1)S(1)}, u32[]{:S(2)}, u32[]{:S(2)}) %collective-permute-start.5) | collective-permute-done | bytes 65568 | tf_op jit(solution)/shard_map/ppermute | solution.py:171
  20.4 0.5 %collective-permute-done.3.refs_1_ = bf16[128,256]{1,0:T(8,128)(2,1)S(1)} collective-permute-done((bf16[128,256]{1,0:T(8,128)(2,1)S(1)}, bf16[128,256]{1,0:T(8,128)(2,1)S(1)}, u32[]{:S(2)}, u32[]{:S(2)}) %collective-permute-start.3) | collective-permute-done | bytes 65568 | tf_op jit(solution)/shard_map/ppermute | solution.py:171
  20.9 0.1 merge.1.refs_0_
  21.0 0.1 collective-permute-start.6
  21.1 1.3 %collective-permute-done.6.refs_1_ = bf16[256,256]{1,0:T(8,128)(2,1)S(1)} collective-permute-done((bf16[256,256]{1,0:T(8,128)(2,1)S(1)}, bf16[256,256]{1,0:T(8,128)(2,1)S(1)}, u32[]{:S(2)}, u32[]{:S(2)}) %collective-permute-start.6) | collective-permute-done | bytes 131104 | tf_op jit(solution)/shard_map/ppermute | solution.py:161
  22.4 0.4 %value.1 = (f32[64,512]{1,0:T(8,128)S(1)}, bf16[64,512]{1,0:T(8,128)(2,1)S(1)}, bf16[64,512]{1,0:T(8,128)(2,1)S(1)}, bf16[64,512]{1,0:T(8,128)(2,1)S(1)}) custom-call(bf16[256,256]{1,0:T(8,128)(2,1)S(1)} %merge.1.refs_0_, bf16[256,256]{1,0:T(8,128)(2,1)S(1)} %collective-permute-done.6.refs_1_, bf16[512,256]{1,0:T(8,128)(2,1)S(1)} %price.1.refs_2_, ...), custom_call_target="tpu_custom_call" | custom-call | tf_op jit(solution)/shard_map/value/pallas_call | solution.py:258
  22.8 1.4 %collective-permute-start.8 = (bf16[64,512]{1,0:T(8,128)(2,1)S(1)}, bf16[64,512]{1,0:T(8,128)(2,1)S(1)}, u32[]{:S(2)}, u32[]{:S(2)}) collective-permute-start(bf16[64,512]{1,0:T(8,128)(2,1)S(1)} %get-tuple-element.15), channel_id=1, source_target_pairs={{0,2},{1,3},{2,0},{3,1},{4,6},{5,7},{6,4},{7,5},{8,10},{9,11},{10,... | collective-permute-start | bytes 196616 | tf_op jit(solution)/shard_map/ppermute | solution.py:161
  24.2 1.1 %collective-permute-start.9 = (bf16[64,512]{1,0:T(8,128)(2,1)S(1)}, bf16[64,512]{1,0:T(8,128)(2,1)S(1)}, u32[]{:S(2)}, u32[]{:S(2)}) collective-permute-start(bf16[64,512]{1,0:T(8,128)(2,1)S(1)} %get-tuple-element.16), channel_id=1, source_target_pairs={{0,3},{1,2},{2,1},{3,0},{4,7},{5,6},{6,5},{7,4},{8,11},{9,10},{10,... | collective-permute-start | bytes 196616 | tf_op jit(solution)/shard_map/ppermute | solution.py:161
  25.3 1.1 %collective-permute-start.10 = (bf16[64,512]{1,0:T(8,128)(2,1)S(1)}, bf16[64,512]{1,0:T(8,128)(2,1)S(1)}, u32[]{:S(2)}, u32[]{:S(2)}) collective-permute-start(bf16[64,512]{1,0:T(8,128)(2,1)S(1)} %get-tuple-element.17), channel_id=1, source_target_pairs={{0,1},{1,0},{2,3},{3,2},{4,5},{5,4},{6,7},{7,6},{8,9},{9,8},{10,11... | collective-permute-start | bytes 196616 | tf_op jit(solution)/shard_map/ppermute | solution.py:161
  26.4 1.3 %collective-permute-done.8.refs_1_ = bf16[64,512]{1,0:T(8,128)(2,1)S(1)} collective-permute-done((bf16[64,512]{1,0:T(8,128)(2,1)S(1)}, bf16[64,512]{1,0:T(8,128)(2,1)S(1)}, u32[]{:S(2)}, u32[]{:S(2)}) %collective-permute-start.8) | collective-permute-done | bytes 65568 | tf_op jit(solution)/shard_map/ppermute | solution.py:161
  27.7 1.8 %collective-permute-done.9.refs_2_ = bf16[64,512]{1,0:T(8,128)(2,1)S(1)} collective-permute-done((bf16[64,512]{1,0:T(8,128)(2,1)S(1)}, bf16[64,512]{1,0:T(8,128)(2,1)S(1)}, u32[]{:S(2)}, u32[]{:S(2)}) %collective-permute-start.9) | collective-permute-done | bytes 65568 | tf_op jit(solution)/shard_map/ppermute | solution.py:161
  29.5 0.6 %collective-permute-done.10.refs_3_ = bf16[64,512]{1,0:T(8,128)(2,1)S(1)} collective-permute-done((bf16[64,512]{1,0:T(8,128)(2,1)S(1)}, bf16[64,512]{1,0:T(8,128)(2,1)S(1)}, u32[]{:S(2)}, u32[]{:S(2)}) %collective-permute-start.10) | collective-permute-done | bytes 65568 | tf_op jit(solution)/shard_map/ppermute | solution.py:161
  30.1 0.1 totals.1
  30.2 0.1 collective-permute-start.13
  30.3 1.6 %collective-permute-start.12 = (f32[2,64]{1,0:T(2,128)S(1)}, f32[2,64]{1,0:T(2,128)S(1)}, u32[]{:S(2)}, u32[]{:S(2)}) collective-permute-start(f32[2,64]{1,0:T(2,128)S(1)} %totals.1), channel_id=1, source_target_pairs={{0,16},{8,24},{16,0},{24,8},{1,17},{9,25},{17,1},{25,9},{2,18},{10... | collective-permute-start | bytes 1544 | tf_op jit(solution)/shard_map/ppermute | solution.py:161
  31.9 0.3 collective-permute-start.11
  32.2 0.7 %expose.1 = f32[2,64,256]{2,1,0:T(8,128)} custom-call(f32[64,512]{1,0:T(8,128)S(1)} %get-tuple-element.14.refs_0_, bf16[64,512]{1,0:T(8,128)(2,1)S(1)} %collective-permute-done.8.refs_1_, bf16[64,512]{1,0:T(8,128)(2,1)S(1)} %collective-permute-done.9.refs_2_, bf16[64,512]{1,0:T(8,128)(2,1)S(1)} %collective-permute-done.10.refs_3_), custom_call_target="tpu_custom_call" | custom-call | tf_op jit(solution)/shard_map/expose/pallas_call | solution.py:282
  32.8 0.4 %collective-permute-done.13 = f32[2,64]{1,0:T(2,128)S(1)} collective-permute-done((f32[2,64]{1,0:T(2,128)S(1)}, f32[2,64]{1,0:T(2,128)S(1)}, u32[]{:S(2)}, u32[]{:S(2)}) %collective-permute-start.13) | collective-permute-done | bytes 544 | tf_op jit(solution)/shard_map/ppermute | solution.py:161
  33.3 0.7 %collective-permute-done.12 = f32[2,64]{1,0:T(2,128)S(1)} collective-permute-done((f32[2,64]{1,0:T(2,128)S(1)}, f32[2,64]{1,0:T(2,128)S(1)}, u32[]{:S(2)}, u32[]{:S(2)}) %collective-permute-start.12) | collective-permute-done | bytes 544 | tf_op jit(solution)/shard_map/ppermute | solution.py:161
  33.9 0.6 %add_multiply_fusion = f32[2,64]{1,0:T(2,128)} fusion(f32[2,64]{1,0:T(2,128)S(1)} %collective-permute-done.12, f32[2,64]{1,0:T(2,128)S(1)} %collective-permute-done.13, f32[2,64]{1,0:T(2,128)S(1)} %totals.1, f32[2,64]{1,0:T(2,128)S(1)} %collective-permute-done.11), kind=kLoop, calls=%fused_computation | loop fusion | flops 512 | bytes 2560 | tf_op jit(solution)/shard_map/div | solution.py:295
  (27 shorter events, 0.1 us)
Async XLA Ops:
  0.6 0.9 %copy-start.4 = (bf16[256,2,128]{2,1,0:T(2,128)(2,1)S(1)}, bf16[256,2,128]{2,1,0:T(2,128)(2,1)}, u32[]{:S(2)}) copy-start(bf16[256,2,128]{2,1,0:T(2,128)(2,1)} %weights_ref.1) | copy-start | bytes 393220
  0.6 0.9 %copy-start.5 = (s32[256,2]{0,1:T(2,128)S(1)}, s32[256,2]{0,1:T(2,128)}, u32[]{:S(2)}) copy-start(s32[256,2]{0,1:T(2,128)} %param.18) | copy-start | bytes 6148
  0.7 0.9 %copy-start.6 = (s32[256]{0:T(256)S(1)}, s32[256]{0:T(256)}, u32[]{:S(2)}) copy-start(s32[256]{0:T(256)} %param.21) | copy-start | bytes 3076
  0.7 7.1 %copy-start = (s32[2,256,256]{2,1,0:T(8,128)S(1)}, s32[2,256,256]{2,1,0:T(8,128)}, u32[]{:S(2)}) copy-start(s32[2,256,256]{2,1,0:T(8,128)} %counts_ref.1) | copy-start | bytes 1572868
  0.7 7.1 %copy-start.1 = (bf16[2,256,256]{2,1,0:T(8,128)(2,1)S(1)}, bf16[2,256,256]{2,1,0:T(8,128)(2,1)}, u32[]{:S(2)}) copy-start(bf16[2,256,256]{2,1,0:T(8,128)(2,1)} %shocks_ref) | copy-start | bytes 786436
  0.7 7.0 %copy-start.2 = (bf16[2,256,256]{2,1,0:T(8,128)(2,1)S(1)}, bf16[2,256,256]{2,1,0:T(8,128)(2,1)}, u32[]{:S(2)}) copy-start(bf16[2,256,256]{2,1,0:T(8,128)(2,1)} %noise_ref.1) | copy-start | bytes 786436
  0.7 7.0 %copy-start.8 = (f32[256]{0:T(256)S(1)}, f32[256]{0:T(256)}, u32[]{:S(2)}) copy-start(f32[256]{0:T(256)} %param.16) | copy-start | bytes 3076
  0.7 7.0 %copy-start.9 = (f32[256]{0:T(256)S(1)}, f32[256]{0:T(256)}, u32[]{:S(2)}) copy-start(f32[256]{0:T(256)} %param.17) | copy-start | bytes 3076
  0.7 7.0 %copy-start.3 = (bf16[256,256]{1,0:T(8,128)(2,1)S(1)}, bf16[256,256]{1,0:T(8,128)(2,1)}, u32[]{:S(2)}) copy-start(bf16[256,256]{1,0:T(8,128)(2,1)} %loadings_ref.1) | copy-start | bytes 393220
  2.0 10.7 %collective-permute-start.2 = (bf16[80,256]{1,0:T(8,128)(2,1)S(1)}, bf16[80,256]{1,0:T(8,128)(2,1)S(1)}, u32[]{:S(2)}, u32[]{:S(2)}) collective-permute-start(bf16[80,256]{1,0:T(8,128)(2,1)S(1)} %pack.1.refs_1_), channel_id=1, source_target_pairs={{0,6},{1,7},{2,4},{3,5},{4,2},{5,3},{6,0},{7,1},{8,14},{9,15},{10,... | collective-permute-start | bytes 122888 | tf_op jit(solution)/shard_map/ppermute | solution.py:161
  7.1 5.6 %collective-permute-start.1 = (bf16[80,256]{1,0:T(8,128)(2,1)S(1)}, bf16[80,256]{1,0:T(8,128)(2,1)S(1)}, u32[]{:S(2)}, u32[]{:S(2)}) collective-permute-start(bf16[80,256]{1,0:T(8,128)(2,1)S(1)} %pack.1.refs_1_), channel_id=1, source_target_pairs={{0,4},{1,5},{2,6},{3,7},{4,0},{5,1},{6,2},{7,3},{8,12},{9,13},{10,... | collective-permute-start | bytes 122888 | tf_op jit(solution)/shard_map/ppermute | solution.py:161
  7.1 5.6 %collective-permute-start = (bf16[80,256]{1,0:T(8,128)(2,1)S(1)}, bf16[80,256]{1,0:T(8,128)(2,1)S(1)}, u32[]{:S(2)}, u32[]{:S(2)}) collective-permute-start(bf16[80,256]{1,0:T(8,128)(2,1)S(1)} %pack.1.refs_1_), channel_id=1, source_target_pairs={{0,2},{1,3},{2,0},{3,1},{4,6},{5,7},{6,4},{7,5},{8,10},{9,11},{10,... | collective-permute-start | bytes 122888 | tf_op jit(solution)/shard_map/ppermute | solution.py:161
  7.7 0.7 %copy-start.7 = (f32[256]{0:T(256)S(1)}, f32[256]{0:T(256)}, u32[]{:S(2)}) copy-start(f32[256]{0:T(256)} %param.13) | copy-start | bytes 3076
  8.4 4.3 %copy-start.10 = (s32[16]{0:T(128)S(1)}, s32[16]{0:T(128)}, u32[]{:S(2)}) copy-start(s32[16]{0:T(128)} %refs_0_.1) | copy-start | bytes 196
  8.9 13.6 %collective-permute-start.7 = (bf16[512,256]{1,0:T(8,128)(2,1)S(1)}, bf16[512,256]{1,0:T(8,128)(2,1)S(1)}, u32[]{:S(2)}, u32[]{:S(2)}) collective-permute-start(bf16[512,256]{1,0:T(8,128)(2,1)S(1)} %price.1.refs_2_), channel_id=1, source_target_pairs={{0,6},{1,7},{2,4},{3,5},{4,2},{5,3},{6,0},{7,1},{8,14},{9,15},{10,... | collective-permute-start | bytes 786440 | tf_op jit(solution)/shard_map/ppermute | solution.py:161
  13.6 4.9 %collective-permute-start.4 = (bf16[128,256]{1,0:T(8,128)(2,1)S(1)}, bf16[128,256]{1,0:T(8,128)(2,1)S(1)}, u32[]{:S(2)}, u32[]{:S(2)}) collective-permute-start(bf16[128,256]{1,0:T(8,128)(2,1)S(1)} %get-tuple-element.12), channel_id=1, source_target_pairs={{0,16},{8,24},{16,0},{24,8},{1,17},{9,25},{17,1},{25,9},{2,18},{10... | collective-permute-start | bytes 196616 | tf_op jit(solution)/shard_map/ppermute | solution.py:161
  15.2 5.2 %collective-permute-start.5 = (bf16[128,256]{1,0:T(8,128)(2,1)S(1)}, bf16[128,256]{1,0:T(8,128)(2,1)S(1)}, u32[]{:S(2)}, u32[]{:S(2)}) collective-permute-start(bf16[128,256]{1,0:T(8,128)(2,1)S(1)} %get-tuple-element.11), channel_id=1, source_target_pairs={{0,17},{1,16},{2,19},{3,18},{4,21},{5,20},{6,23},{7,22},{8,25},{9,... | collective-permute-start | bytes 196616 | tf_op jit(solution)/shard_map/ppermute | solution.py:171
  16.6 4.3 %collective-permute-start.3 = (bf16[128,256]{1,0:T(8,128)(2,1)S(1)}, bf16[128,256]{1,0:T(8,128)(2,1)S(1)}, u32[]{:S(2)}, u32[]{:S(2)}) collective-permute-start(bf16[128,256]{1,0:T(8,128)(2,1)S(1)} %get-tuple-element.11), channel_id=1, source_target_pairs={{0,1},{1,0},{2,3},{3,2},{4,5},{5,4},{6,7},{7,6},{8,9},{9,8},{10,11... | collective-permute-start | bytes 196616 | tf_op jit(solution)/shard_map/ppermute | solution.py:171
  21.0 1.4 %collective-permute-start.6 = (bf16[256,256]{1,0:T(8,128)(2,1)S(1)}, bf16[256,256]{1,0:T(8,128)(2,1)S(1)}, u32[]{:S(2)}, u32[]{:S(2)}) collective-permute-start(bf16[256,256]{1,0:T(8,128)(2,1)S(1)} %merge.1.refs_0_), channel_id=1, source_target_pairs={{0,8},{8,0},{16,24},{24,16},{1,9},{9,1},{17,25},{25,17},{2,10},{10... | collective-permute-start | bytes 393224 | tf_op jit(solution)/shard_map/ppermute | solution.py:161
  22.8 4.8 %collective-permute-start.8 = (bf16[64,512]{1,0:T(8,128)(2,1)S(1)}, bf16[64,512]{1,0:T(8,128)(2,1)S(1)}, u32[]{:S(2)}, u32[]{:S(2)}) collective-permute-start(bf16[64,512]{1,0:T(8,128)(2,1)S(1)} %get-tuple-element.15), channel_id=1, source_target_pairs={{0,2},{1,3},{2,0},{3,1},{4,6},{5,7},{6,4},{7,5},{8,10},{9,11},{10,... | collective-permute-start | bytes 196616 | tf_op jit(solution)/shard_map/ppermute | solution.py:161
  24.2 5.2 %collective-permute-start.9 = (bf16[64,512]{1,0:T(8,128)(2,1)S(1)}, bf16[64,512]{1,0:T(8,128)(2,1)S(1)}, u32[]{:S(2)}, u32[]{:S(2)}) collective-permute-start(bf16[64,512]{1,0:T(8,128)(2,1)S(1)} %get-tuple-element.16), channel_id=1, source_target_pairs={{0,3},{1,2},{2,1},{3,0},{4,7},{5,6},{6,5},{7,4},{8,11},{9,10},{10,... | collective-permute-start | bytes 196616 | tf_op jit(solution)/shard_map/ppermute | solution.py:161
  25.3 4.8 %collective-permute-start.10 = (bf16[64,512]{1,0:T(8,128)(2,1)S(1)}, bf16[64,512]{1,0:T(8,128)(2,1)S(1)}, u32[]{:S(2)}, u32[]{:S(2)}) collective-permute-start(bf16[64,512]{1,0:T(8,128)(2,1)S(1)} %get-tuple-element.17), channel_id=1, source_target_pairs={{0,1},{1,0},{2,3},{3,2},{4,5},{5,4},{6,7},{7,6},{8,9},{9,8},{10,11... | collective-permute-start | bytes 196616 | tf_op jit(solution)/shard_map/ppermute | solution.py:161
  30.2 3.1 %collective-permute-start.13 = (f32[2,64]{1,0:T(2,128)S(1)}, f32[2,64]{1,0:T(2,128)S(1)}, u32[]{:S(2)}, u32[]{:S(2)}) collective-permute-start(f32[2,64]{1,0:T(2,128)S(1)} %totals.1), channel_id=1, source_target_pairs={{0,24},{8,16},{16,8},{24,0},{1,25},{9,17},{17,9},{25,1},{2,26},{10... | collective-permute-start | bytes 1544 | tf_op jit(solution)/shard_map/ppermute | solution.py:161
  30.3 3.6 %collective-permute-start.12 = (f32[2,64]{1,0:T(2,128)S(1)}, f32[2,64]{1,0:T(2,128)S(1)}, u32[]{:S(2)}, u32[]{:S(2)}) collective-permute-start(f32[2,64]{1,0:T(2,128)S(1)} %totals.1), channel_id=1, source_target_pairs={{0,16},{8,24},{16,0},{24,8},{1,17},{9,25},{17,1},{25,9},{2,18},{10... | collective-permute-start | bytes 1544 | tf_op jit(solution)/shard_map/ppermute | solution.py:161
  31.9 2.1 %collective-permute-start.11 = (f32[2,64]{1,0:T(2,128)S(1)}, f32[2,64]{1,0:T(2,128)S(1)}, u32[]{:S(2)}, u32[]{:S(2)}) collective-permute-start(f32[2,64]{1,0:T(2,128)S(1)} %totals.1), channel_id=1, source_target_pairs={{0,8},{8,0},{16,24},{24,16},{1,9},{9,1},{17,25},{25,17},{2,10},{10... | collective-permute-start | bytes 1544 | tf_op jit(solution)/shard_map/ppermute | solution.py:161

commit v11 on v9

--- a/solution.py
+++ b/solution.py
@@ -11,7 +11,7 @@
 SET_DEV = 64
 DATES = 2
 SIDE_FLIP = 1
-PRICE_FLIP = 2
+PRICE_FLIP = 4
 TAGS = 16
 CHUNK = 64
 

time: 36.7 us -> 35.3 us (0.962)
  waiting for transfers between devices: 13.1 us -> 11.6 us
    ppermute x12, waiting for transfers between devices: 10.1 us -> 9.04 us  [from_partner(): return lax.ppermute(x, axis, [(i, i ^ flip) for i in range(count)])]
    ppermute x2, waiting for transfers between devices: 2.95 us -> 2.55 us  [from_both(): return lax.ppermute(x, ('scen', 'fac'), pairs)]
  transfers between devices with their start and end apart: 14 -> 14, of which waited for: 10 -> 11; matrix products, arithmetic and copies ran while one was open for 0% -> 0% of each run, Pallas kernels for 6% -> 6%
where the time goes in v11:
time: 35.3 us; the launch traced here: 35.2 us
  starting transfers between devices  17.6 us (50%)
  waiting for transfers between devices  11.6 us (33%)
  Pallas kernels  3.11 us (9%)
  local copies, waits for them, and re-layouts  1.47 us (4%)
  between operations  0.81 us (2%)
  other arithmetic  0.57 us (2%)
    ppermute x12, starting transfers between devices, from_partner(): return lax.ppermute(x, axis, [(i, i ^ flip) for i in range(count)])  15.7 us
    ppermute x12, waiting for transfers between devices, from_partner(): return lax.ppermute(x, axis, [(i, i ^ flip) for i in range(count)])  9.04 us
    ppermute x2, waiting for transfers between devices, from_both(): return lax.ppermute(x, ('scen', 'fac'), pairs)  2.55 us
    ppermute x2, starting transfers between devices, from_both(): return lax.ppermute(x, ('scen', 'fac'), pairs)  1.97 us
    unnamed x22, local copies, waits for them, and re-layouts  1.47 us
    pallas_call x1, Pallas kernels, body(): pl.pallas_call(functools.partial(combine_kernel, part, held, owner_flips)...  0.9 us
  transfers between devices with their start and end apart: 14, of which 11 were waited for; matrix products, arithmetic and copies ran while one was open for 0% of the time, Pallas kernels for 6%

profile of v11, /device:TPU:0, one launch (start us, length us, event | category | flops | bytes accessed | tf_op | source)
XLA Modules:
  0.0 35.2 jit_solution(148439040964432488)
XLA Ops:
  0.7 0.8 %copy-done.4 = bf16[256,2,128]{2,1,0:T(2,128)(2,1)S(1)} copy-done((bf16[256,2,128]{2,1,0:T(2,128)(2,1)S(1)}, bf16[256,2,128]{2,1,0:T(2,128)(2,1)}, u32[]{:S(2)}) %copy-start.4) | copy-done | bytes 131096
  1.5 0.4 %pack.1.refs_1_ = bf16[80,256]{1,0:T(8,128)(2,1)S(1)} custom-call(bf16[32,128]{1,0:T(8,128)(2,1)S(1)} %pick.1.pick_ref, bf16[256,2,128]{2,1,0:T(2,128)(2,1)S(1)} %copy-done.4, s32[2,256]{1,0:T(2,128)S(1)} %bitcast.5, s32[1,256]{1,0:T(1,128)S(1)} %bitcast.6), custom_call_target="tpu_custom_call" | custom-call | tf_op jit(solution)/shard_map/pack/pallas_call | solution.py:204
  2.0 4.1 %collective-permute-start.2 = (bf16[80,256]{1,0:T(8,128)(2,1)S(1)}, bf16[80,256]{1,0:T(8,128)(2,1)S(1)}, u32[]{:S(2)}, u32[]{:S(2)}) collective-permute-start(bf16[80,256]{1,0:T(8,128)(2,1)S(1)} %pack.1.refs_1_), channel_id=1, source_target_pairs={{0,4},{1,5},{2,6},{3,7},{4,0},{5,1},{6,2},{7,3},{8,12},{9,13},{10,... | collective-permute-start | bytes 122888 | tf_op jit(solution)/shard_map/ppermute | solution.py:160
  6.1 1.3 %collective-permute-start.1 = (bf16[80,256]{1,0:T(8,128)(2,1)S(1)}, bf16[80,256]{1,0:T(8,128)(2,1)S(1)}, u32[]{:S(2)}, u32[]{:S(2)}) collective-permute-start(bf16[80,256]{1,0:T(8,128)(2,1)S(1)} %pack.1.refs_1_), channel_id=1, source_target_pairs={{0,6},{1,7},{2,4},{3,5},{4,2},{5,3},{6,0},{7,1},{8,14},{9,15},{10,... | collective-permute-start | bytes 122888 | tf_op jit(solution)/shard_map/ppermute | solution.py:160
  7.4 0.2 collective-permute-start
  7.7 0.6 %copy-done.7 = f32[256]{0:T(256)S(1)} copy-done((f32[256]{0:T(256)S(1)}, f32[256]{0:T(256)}, u32[]{:S(2)}) %copy-start.7) | copy-done | bytes 1048
  8.3 0.5 %price.1.refs_2_ = bf16[512,256]{1,0:T(8,128)(2,1)S(1)} custom-call(bf16[2,256,256]{2,1,0:T(8,128)(2,1)S(1)} %copy-done.1, bf16[256,256]{1,0:T(8,128)(2,1)S(1)} %copy-done.3, f32[1,256]{1,0:T(1,128)S(1)} %bitcast.7, s32[2,256,256]{2,1,0:T(8,128)S(1)} %copy-done, bf16[2,256,256]{2,1,0:T(8,128)(2,1)S(1)} %copy-done.2, f32[1,256]{1,0:T(1,128)S(1)} %bitcast.8, ...), custom_call_target="tpu_custom_call" | custom-call | tf_op jit(solution)/shard_map/price/pallas_call | solution.py:216
  8.8 2.9 %collective-permute-start.7 = (bf16[512,256]{1,0:T(8,128)(2,1)S(1)}, bf16[512,256]{1,0:T(8,128)(2,1)S(1)}, u32[]{:S(2)}, u32[]{:S(2)}) collective-permute-start(bf16[512,256]{1,0:T(8,128)(2,1)S(1)} %price.1.refs_2_), channel_id=1, source_target_pairs={{0,4},{1,5},{2,6},{3,7},{4,0},{5,1},{6,2},{7,3},{8,12},{9,13},{10,... | collective-permute-start | bytes 786440 | tf_op jit(solution)/shard_map/ppermute | solution.py:160
  11.7 0.2 collective-permute-done.1.refs_3_
  11.9 0.9 %combine.1 = (f32[128,256]{1,0:T(8,128)S(1)}, bf16[128,256]{1,0:T(8,128)(2,1)S(1)}, bf16[128,256]{1,0:T(8,128)(2,1)S(1)}) custom-call(s32[16]{0:T(128)S(1)} %copy-done.10, bf16[80,256]{1,0:T(8,128)(2,1)S(1)} %pack.1.refs_1_, bf16[80,256]{1,0:T(8,128)(2,1)S(1)} %collective-permute-done.refs_2_, bf16[80,256]{1,0:T(8,128)(2,1)S(1)} %collective-permute-done.1.refs_3_, ...), custom_call_target="tpu_custom_call" | custom-call | flops 1000000000 | tf_op jit(solution)/shard_map/combine/pallas_call | solution.py:226
  12.8 1.6 %collective-permute-start.4 = (bf16[128,256]{1,0:T(8,128)(2,1)S(1)}, bf16[128,256]{1,0:T(8,128)(2,1)S(1)}, u32[]{:S(2)}, u32[]{:S(2)}) collective-permute-start(bf16[128,256]{1,0:T(8,128)(2,1)S(1)} %get-tuple-element.12), channel_id=1, source_target_pairs={{0,16},{8,24},{16,0},{24,8},{1,17},{9,25},{17,1},{25,9},{2,18},{10... | collective-permute-start | bytes 196616 | tf_op jit(solution)/shard_map/ppermute | solution.py:160
  14.4 1.4 %collective-permute-start.5 = (bf16[128,256]{1,0:T(8,128)(2,1)S(1)}, bf16[128,256]{1,0:T(8,128)(2,1)S(1)}, u32[]{:S(2)}, u32[]{:S(2)}) collective-permute-start(bf16[128,256]{1,0:T(8,128)(2,1)S(1)} %get-tuple-element.11), channel_id=1, source_target_pairs={{0,17},{1,16},{2,19},{3,18},{4,21},{5,20},{6,23},{7,22},{8,25},{9,... | collective-permute-start | bytes 196616 | tf_op jit(solution)/shard_map/ppermute | solution.py:170
  15.8 0.5 %collective-permute-start.3 = (bf16[128,256]{1,0:T(8,128)(2,1)S(1)}, bf16[128,256]{1,0:T(8,128)(2,1)S(1)}, u32[]{:S(2)}, u32[]{:S(2)}) collective-permute-start(bf16[128,256]{1,0:T(8,128)(2,1)S(1)} %get-tuple-element.11), channel_id=1, source_target_pairs={{0,1},{1,0},{2,3},{3,2},{4,5},{5,4},{6,7},{7,6},{8,9},{9,8},{10,11... | collective-permute-start | bytes 196616 | tf_op jit(solution)/shard_map/ppermute | solution.py:170
  16.4 1.2 %collective-permute-done.4.refs_2_ = bf16[128,256]{1,0:T(8,128)(2,1)S(1)} collective-permute-done((bf16[128,256]{1,0:T(8,128)(2,1)S(1)}, bf16[128,256]{1,0:T(8,128)(2,1)S(1)}, u32[]{:S(2)}, u32[]{:S(2)}) %collective-permute-start.4) | collective-permute-done | bytes 65568 | tf_op jit(solution)/shard_map/ppermute | solution.py:160
  17.5 2.0 %collective-permute-done.5.refs_3_ = bf16[128,256]{1,0:T(8,128)(2,1)S(1)} collective-permute-done((bf16[128,256]{1,0:T(8,128)(2,1)S(1)}, bf16[128,256]{1,0:T(8,128)(2,1)S(1)}, u32[]{:S(2)}, u32[]{:S(2)}) %collective-permute-start.5) | collective-permute-done | bytes 65568 | tf_op jit(solution)/shard_map/ppermute | solution.py:170
  19.5 0.5 %collective-permute-done.3.refs_1_ = bf16[128,256]{1,0:T(8,128)(2,1)S(1)} collective-permute-done((bf16[128,256]{1,0:T(8,128)(2,1)S(1)}, bf16[128,256]{1,0:T(8,128)(2,1)S(1)}, u32[]{:S(2)}, u32[]{:S(2)}) %collective-permute-start.3) | collective-permute-done | bytes 65568 | tf_op jit(solution)/shard_map/ppermute | solution.py:170
  20.1 0.1 merge.1.refs_0_
  20.3 1.3 %collective-permute-done.6.refs_1_ = bf16[256,256]{1,0:T(8,128)(2,1)S(1)} collective-permute-done((bf16[256,256]{1,0:T(8,128)(2,1)S(1)}, bf16[256,256]{1,0:T(8,128)(2,1)S(1)}, u32[]{:S(2)}, u32[]{:S(2)}) %collective-permute-start.6) | collective-permute-done | bytes 131104 | tf_op jit(solution)/shard_map/ppermute | solution.py:160
  21.6 1.5 %collective-permute-done.7.refs_3_ = bf16[512,256]{1,0:T(8,128)(2,1)S(1)} collective-permute-done((bf16[512,256]{1,0:T(8,128)(2,1)S(1)}, bf16[512,256]{1,0:T(8,128)(2,1)S(1)}, u32[]{:S(2)}, u32[]{:S(2)}) %collective-permute-start.7) | collective-permute-done | bytes 262176 | tf_op jit(solution)/shard_map/ppermute | solution.py:160
  23.1 0.4 %value.1 = (f32[64,512]{1,0:T(8,128)S(1)}, bf16[64,512]{1,0:T(8,128)(2,1)S(1)}, bf16[64,512]{1,0:T(8,128)(2,1)S(1)}, bf16[64,512]{1,0:T(8,128)(2,1)S(1)}) custom-call(bf16[256,256]{1,0:T(8,128)(2,1)S(1)} %merge.1.refs_0_, bf16[256,256]{1,0:T(8,128)(2,1)S(1)} %collective-permute-done.6.refs_1_, bf16[512,256]{1,0:T(8,128)(2,1)S(1)} %price.1.refs_2_, ...), custom_call_target="tpu_custom_call" | custom-call | tf_op jit(solution)/shard_map/value/pallas_call | solution.py:258
  23.6 2.9 %collective-permute-start.9 = (bf16[64,512]{1,0:T(8,128)(2,1)S(1)}, bf16[64,512]{1,0:T(8,128)(2,1)S(1)}, u32[]{:S(2)}, u32[]{:S(2)}) collective-permute-start(bf16[64,512]{1,0:T(8,128)(2,1)S(1)} %get-tuple-element.16), channel_id=1, source_target_pairs={{0,3},{1,2},{2,1},{3,0},{4,7},{5,6},{6,5},{7,4},{8,11},{9,10},{10,... | collective-permute-start | bytes 196616 | tf_op jit(solution)/shard_map/ppermute | solution.py:160
  26.5 0.5 %collective-permute-start.10 = (bf16[64,512]{1,0:T(8,128)(2,1)S(1)}, bf16[64,512]{1,0:T(8,128)(2,1)S(1)}, u32[]{:S(2)}, u32[]{:S(2)}) collective-permute-start(bf16[64,512]{1,0:T(8,128)(2,1)S(1)} %get-tuple-element.17), channel_id=1, source_target_pairs={{0,1},{1,0},{2,3},{3,2},{4,5},{5,4},{6,7},{7,6},{8,9},{9,8},{10,11... | collective-permute-start | bytes 196616 | tf_op jit(solution)/shard_map/ppermute | solution.py:160
  27.1 0.8 %collective-permute-done.8.refs_1_ = bf16[64,512]{1,0:T(8,128)(2,1)S(1)} collective-permute-done((bf16[64,512]{1,0:T(8,128)(2,1)S(1)}, bf16[64,512]{1,0:T(8,128)(2,1)S(1)}, u32[]{:S(2)}, u32[]{:S(2)}) %collective-permute-start.8) | collective-permute-done | bytes 65568 | tf_op jit(solution)/shard_map/ppermute | solution.py:160
  27.8 1.6 %collective-permute-done.9.refs_2_ = bf16[64,512]{1,0:T(8,128)(2,1)S(1)} collective-permute-done((bf16[64,512]{1,0:T(8,128)(2,1)S(1)}, bf16[64,512]{1,0:T(8,128)(2,1)S(1)}, u32[]{:S(2)}, u32[]{:S(2)}) %collective-permute-start.9) | collective-permute-done | bytes 65568 | tf_op jit(solution)/shard_map/ppermute | solution.py:160
  29.5 1.3 %collective-permute-done.10.refs_3_ = bf16[64,512]{1,0:T(8,128)(2,1)S(1)} collective-permute-done((bf16[64,512]{1,0:T(8,128)(2,1)S(1)}, bf16[64,512]{1,0:T(8,128)(2,1)S(1)}, u32[]{:S(2)}, u32[]{:S(2)}) %collective-permute-start.10) | collective-permute-done | bytes 65568 | tf_op jit(solution)/shard_map/ppermute | solution.py:160
  30.8 0.1 totals.1
  31.0 1.6 %collective-permute-start.12 = (f32[2,64]{1,0:T(2,128)S(1)}, f32[2,64]{1,0:T(2,128)S(1)}, u32[]{:S(2)}, u32[]{:S(2)}) collective-permute-start(f32[2,64]{1,0:T(2,128)S(1)} %totals.1), channel_id=1, source_target_pairs={{0,16},{8,24},{16,0},{24,8},{1,17},{9,25},{17,1},{25,9},{2,18},{10... | collective-permute-start | bytes 1544 | tf_op jit(solution)/shard_map/ppermute | solution.py:160
  32.6 0.3 collective-permute-start.11
  32.8 0.7 %expose.1 = f32[2,64,256]{2,1,0:T(8,128)} custom-call(f32[64,512]{1,0:T(8,128)S(1)} %get-tuple-element.14.refs_0_, bf16[64,512]{1,0:T(8,128)(2,1)S(1)} %collective-permute-done.8.refs_1_, bf16[64,512]{1,0:T(8,128)(2,1)S(1)} %collective-permute-done.9.refs_2_, bf16[64,512]{1,0:T(8,128)(2,1)S(1)} %collective-permute-done.10.refs_3_), custom_call_target="tpu_custom_call" | custom-call | tf_op jit(solution)/shard_map/expose/pallas_call | solution.py:282
  33.5 0.4 %collective-permute-done.13 = f32[2,64]{1,0:T(2,128)S(1)} collective-permute-done((f32[2,64]{1,0:T(2,128)S(1)}, f32[2,64]{1,0:T(2,128)S(1)}, u32[]{:S(2)}, u32[]{:S(2)}) %collective-permute-start.13) | collective-permute-done | bytes 544 | tf_op jit(solution)/shard_map/ppermute | solution.py:160
  34.0 0.7 %collective-permute-done.12 = f32[2,64]{1,0:T(2,128)S(1)} collective-permute-done((f32[2,64]{1,0:T(2,128)S(1)}, f32[2,64]{1,0:T(2,128)S(1)}, u32[]{:S(2)}, u32[]{:S(2)}) %collective-permute-start.12) | collective-permute-done | bytes 544 | tf_op jit(solution)/shard_map/ppermute | solution.py:160
  34.6 0.6 %add_multiply_fusion = f32[2,64]{1,0:T(2,128)} fusion(f32[2,64]{1,0:T(2,128)S(1)} %collective-permute-done.12, f32[2,64]{1,0:T(2,128)S(1)} %collective-permute-done.13, f32[2,64]{1,0:T(2,128)S(1)} %totals.1, f32[2,64]{1,0:T(2,128)S(1)} %collective-permute-done.11), kind=kLoop, calls=%fused_computation | loop fusion | flops 512 | bytes 2560 | tf_op jit(solution)/shard_map/div | solution.py:295
  (27 shorter events, 0.3 us)
Async XLA Ops:
  0.6 0.9 %copy-start.4 = (bf16[256,2,128]{2,1,0:T(2,128)(2,1)S(1)}, bf16[256,2,128]{2,1,0:T(2,128)(2,1)}, u32[]{:S(2)}) copy-start(bf16[256,2,128]{2,1,0:T(2,128)(2,1)} %weights_ref.1) | copy-start | bytes 393220
  0.6 0.9 %copy-start.5 = (s32[256,2]{0,1:T(2,128)S(1)}, s32[256,2]{0,1:T(2,128)}, u32[]{:S(2)}) copy-start(s32[256,2]{0,1:T(2,128)} %param.18) | copy-start | bytes 6148
  0.7 0.9 %copy-start.6 = (s32[256]{0:T(256)S(1)}, s32[256]{0:T(256)}, u32[]{:S(2)}) copy-start(s32[256]{0:T(256)} %param.21) | copy-start | bytes 3076
  0.7 7.0 %copy-start = (s32[2,256,256]{2,1,0:T(8,128)S(1)}, s32[2,256,256]{2,1,0:T(8,128)}, u32[]{:S(2)}) copy-start(s32[2,256,256]{2,1,0:T(8,128)} %counts_ref.1) | copy-start | bytes 1572868
  0.7 7.0 %copy-start.1 = (bf16[2,256,256]{2,1,0:T(8,128)(2,1)S(1)}, bf16[2,256,256]{2,1,0:T(8,128)(2,1)}, u32[]{:S(2)}) copy-start(bf16[2,256,256]{2,1,0:T(8,128)(2,1)} %shocks_ref) | copy-start | bytes 786436
  0.7 7.0 %copy-start.2 = (bf16[2,256,256]{2,1,0:T(8,128)(2,1)S(1)}, bf16[2,256,256]{2,1,0:T(8,128)(2,1)}, u32[]{:S(2)}) copy-start(bf16[2,256,256]{2,1,0:T(8,128)(2,1)} %noise_ref.1) | copy-start | bytes 786436
  0.7 7.0 %copy-start.8 = (f32[256]{0:T(256)S(1)}, f32[256]{0:T(256)}, u32[]{:S(2)}) copy-start(f32[256]{0:T(256)} %param.16) | copy-start | bytes 3076
  0.7 7.0 %copy-start.9 = (f32[256]{0:T(256)S(1)}, f32[256]{0:T(256)}, u32[]{:S(2)}) copy-start(f32[256]{0:T(256)} %param.17) | copy-start | bytes 3076
  0.7 6.9 %copy-start.3 = (bf16[256,256]{1,0:T(8,128)(2,1)S(1)}, bf16[256,256]{1,0:T(8,128)(2,1)}, u32[]{:S(2)}) copy-start(bf16[256,256]{1,0:T(8,128)(2,1)} %loadings_ref.1) | copy-start | bytes 393220
  2.0 9.7 %collective-permute-start.2 = (bf16[80,256]{1,0:T(8,128)(2,1)S(1)}, bf16[80,256]{1,0:T(8,128)(2,1)S(1)}, u32[]{:S(2)}, u32[]{:S(2)}) collective-permute-start(bf16[80,256]{1,0:T(8,128)(2,1)S(1)} %pack.1.refs_1_), channel_id=1, source_target_pairs={{0,4},{1,5},{2,6},{3,7},{4,0},{5,1},{6,2},{7,3},{8,12},{9,13},{10,... | collective-permute-start | bytes 122888 | tf_op jit(solution)/shard_map/ppermute | solution.py:160
  6.1 5.8 %collective-permute-start.1 = (bf16[80,256]{1,0:T(8,128)(2,1)S(1)}, bf16[80,256]{1,0:T(8,128)(2,1)S(1)}, u32[]{:S(2)}, u32[]{:S(2)}) collective-permute-start(bf16[80,256]{1,0:T(8,128)(2,1)S(1)} %pack.1.refs_1_), channel_id=1, source_target_pairs={{0,6},{1,7},{2,4},{3,5},{4,2},{5,3},{6,0},{7,1},{8,14},{9,15},{10,... | collective-permute-start | bytes 122888 | tf_op jit(solution)/shard_map/ppermute | solution.py:160
  7.4 4.5 %collective-permute-start = (bf16[80,256]{1,0:T(8,128)(2,1)S(1)}, bf16[80,256]{1,0:T(8,128)(2,1)S(1)}, u32[]{:S(2)}, u32[]{:S(2)}) collective-permute-start(bf16[80,256]{1,0:T(8,128)(2,1)S(1)} %pack.1.refs_1_), channel_id=1, source_target_pairs={{0,2},{1,3},{2,0},{3,1},{4,6},{5,7},{6,4},{7,5},{8,10},{9,11},{10,... | collective-permute-start | bytes 122888 | tf_op jit(solution)/shard_map/ppermute | solution.py:160
  7.6 0.7 %copy-start.7 = (f32[256]{0:T(256)S(1)}, f32[256]{0:T(256)}, u32[]{:S(2)}) copy-start(f32[256]{0:T(256)} %param.13) | copy-start | bytes 3076
  8.3 3.6 %copy-start.10 = (s32[16]{0:T(128)S(1)}, s32[16]{0:T(128)}, u32[]{:S(2)}) copy-start(s32[16]{0:T(128)} %refs_0_.1) | copy-start | bytes 196
  8.8 14.3 %collective-permute-start.7 = (bf16[512,256]{1,0:T(8,128)(2,1)S(1)}, bf16[512,256]{1,0:T(8,128)(2,1)S(1)}, u32[]{:S(2)}, u32[]{:S(2)}) collective-permute-start(bf16[512,256]{1,0:T(8,128)(2,1)S(1)} %price.1.refs_2_), channel_id=1, source_target_pairs={{0,4},{1,5},{2,6},{3,7},{4,0},{5,1},{6,2},{7,3},{8,12},{9,13},{10,... | collective-permute-start | bytes 786440 | tf_op jit(solution)/shard_map/ppermute | solution.py:160
  12.8 4.7 %collective-permute-start.4 = (bf16[128,256]{1,0:T(8,128)(2,1)S(1)}, bf16[128,256]{1,0:T(8,128)(2,1)S(1)}, u32[]{:S(2)}, u32[]{:S(2)}) collective-permute-start(bf16[128,256]{1,0:T(8,128)(2,1)S(1)} %get-tuple-element.12), channel_id=1, source_target_pairs={{0,16},{8,24},{16,0},{24,8},{1,17},{9,25},{17,1},{25,9},{2,18},{10... | collective-permute-start | bytes 196616 | tf_op jit(solution)/shard_map/ppermute | solution.py:160
  14.4 5.2 %collective-permute-start.5 = (bf16[128,256]{1,0:T(8,128)(2,1)S(1)}, bf16[128,256]{1,0:T(8,128)(2,1)S(1)}, u32[]{:S(2)}, u32[]{:S(2)}) collective-permute-start(bf16[128,256]{1,0:T(8,128)(2,1)S(1)} %get-tuple-element.11), channel_id=1, source_target_pairs={{0,17},{1,16},{2,19},{3,18},{4,21},{5,20},{6,23},{7,22},{8,25},{9,... | collective-permute-start | bytes 196616 | tf_op jit(solution)/shard_map/ppermute | solution.py:170
  15.8 4.3 %collective-permute-start.3 = (bf16[128,256]{1,0:T(8,128)(2,1)S(1)}, bf16[128,256]{1,0:T(8,128)(2,1)S(1)}, u32[]{:S(2)}, u32[]{:S(2)}) collective-permute-start(bf16[128,256]{1,0:T(8,128)(2,1)S(1)} %get-tuple-element.11), channel_id=1, source_target_pairs={{0,1},{1,0},{2,3},{3,2},{4,5},{5,4},{6,7},{7,6},{8,9},{9,8},{10,11... | collective-permute-start | bytes 196616 | tf_op jit(solution)/shard_map/ppermute | solution.py:170
  20.2 1.4 %collective-permute-start.6 = (bf16[256,256]{1,0:T(8,128)(2,1)S(1)}, bf16[256,256]{1,0:T(8,128)(2,1)S(1)}, u32[]{:S(2)}, u32[]{:S(2)}) collective-permute-start(bf16[256,256]{1,0:T(8,128)(2,1)S(1)} %merge.1.refs_0_), channel_id=1, source_target_pairs={{0,8},{8,0},{16,24},{24,16},{1,9},{9,1},{17,25},{25,17},{2,10},{10... | collective-permute-start | bytes 393224 | tf_op jit(solution)/shard_map/ppermute | solution.py:160
  23.5 4.3 %collective-permute-start.8 = (bf16[64,512]{1,0:T(8,128)(2,1)S(1)}, bf16[64,512]{1,0:T(8,128)(2,1)S(1)}, u32[]{:S(2)}, u32[]{:S(2)}) collective-permute-start(bf16[64,512]{1,0:T(8,128)(2,1)S(1)} %get-tuple-element.15), channel_id=1, source_target_pairs={{0,2},{1,3},{2,0},{3,1},{4,6},{5,7},{6,4},{7,5},{8,10},{9,11},{10,... | collective-permute-start | bytes 196616 | tf_op jit(solution)/shard_map/ppermute | solution.py:160
  23.6 5.9 %collective-permute-start.9 = (bf16[64,512]{1,0:T(8,128)(2,1)S(1)}, bf16[64,512]{1,0:T(8,128)(2,1)S(1)}, u32[]{:S(2)}, u32[]{:S(2)}) collective-permute-start(bf16[64,512]{1,0:T(8,128)(2,1)S(1)} %get-tuple-element.16), channel_id=1, source_target_pairs={{0,3},{1,2},{2,1},{3,0},{4,7},{5,6},{6,5},{7,4},{8,11},{9,10},{10,... | collective-permute-start | bytes 196616 | tf_op jit(solution)/shard_map/ppermute | solution.py:160
  26.5 4.3 %collective-permute-start.10 = (bf16[64,512]{1,0:T(8,128)(2,1)S(1)}, bf16[64,512]{1,0:T(8,128)(2,1)S(1)}, u32[]{:S(2)}, u32[]{:S(2)}) collective-permute-start(bf16[64,512]{1,0:T(8,128)(2,1)S(1)} %get-tuple-element.17), channel_id=1, source_target_pairs={{0,1},{1,0},{2,3},{3,2},{4,5},{5,4},{6,7},{7,6},{8,9},{9,8},{10,11... | collective-permute-start | bytes 196616 | tf_op jit(solution)/shard_map/ppermute | solution.py:160
  30.9 3.1 %collective-permute-start.13 = (f32[2,64]{1,0:T(2,128)S(1)}, f32[2,64]{1,0:T(2,128)S(1)}, u32[]{:S(2)}, u32[]{:S(2)}) collective-permute-start(f32[2,64]{1,0:T(2,128)S(1)} %totals.1), channel_id=1, source_target_pairs={{0,24},{8,16},{16,8},{24,0},{1,25},{9,17},{17,9},{25,1},{2,26},{10... | collective-permute-start | bytes 1544 | tf_op jit(solution)/shard_map/ppermute | solution.py:160
  31.0 3.6 %collective-permute-start.12 = (f32[2,64]{1,0:T(2,128)S(1)}, f32[2,64]{1,0:T(2,128)S(1)}, u32[]{:S(2)}, u32[]{:S(2)}) collective-permute-start(f32[2,64]{1,0:T(2,128)S(1)} %totals.1), channel_id=1, source_target_pairs={{0,16},{8,24},{16,0},{24,8},{1,17},{9,25},{17,1},{25,9},{2,18},{10... | collective-permute-start | bytes 1544 | tf_op jit(solution)/shard_map/ppermute | solution.py:160
  32.6 2.1 %collective-permute-start.11 = (f32[2,64]{1,0:T(2,128)S(1)}, f32[2,64]{1,0:T(2,128)S(1)}, u32[]{:S(2)}, u32[]{:S(2)}) collective-permute-start(f32[2,64]{1,0:T(2,128)S(1)} %totals.1), channel_id=1, source_target_pairs={{0,8},{8,0},{16,24},{24,16},{1,9},{9,1},{17,25},{25,17},{2,10},{10... | collective-permute-start | bytes 1544 | tf_op jit(solution)/shard_map/ppermute | solution.py:160

commit v12 on v10

--- a/solution.py
+++ b/solution.py
@@ -210,7 +210,8 @@
         compiler_params=PARAMS,
         name="pack",
     )(pick, trade_weights, dependencies.T, netting[None])
-    packets = [packet] + [from_partner(packet, "fac", i) for i in column_flips[1:]]
+    order = column_flips[1:2] + column_flips[:1:-1]
+    packets = [packet] + [from_partner(packet, "fac", i) for i in order]
 
     packet, shocks = lax.optimization_barrier((packet, shocks))
     prices = pl.pallas_call(
@@ -268,7 +269,7 @@
         name="value",
     )(*shares, *pair_prices)
     sends = list(zip(parts[1:], owner_flips[1:]))
-    sends = sends[1:] + sends[:1]
+    sends = sends[1:2] + sends[:1] + sends[2:]
     parts = [parts[0]] + [from_partner(x, "fac", i) for x, i in sends]
 
     totals = pl.pallas_call(

time: 34.7 us -> 35.3 us (1.017)
  waiting for transfers between devices: 9.88 us -> 11.4 us
  starting transfers between devices: 18.7 us -> 17.9 us
    ppermute x12, waiting for transfers between devices: 7.52 us -> 8.93 us  [from_partner(): return lax.ppermute(x, axis, [(i, i ^ flip) for i in range(count)])]
    ppermute x12, starting transfers between devices: 16.7 us -> 15.9 us  [from_partner(): return lax.ppermute(x, axis, [(i, i ^ flip) for i in range(count)])]
  transfers between devices with their start and end apart: 14 -> 14, of which waited for: 9 -> 10; matrix products, arithmetic and copies ran while one was open for 0% -> 0% of each run, Pallas kernels for 6% -> 6%
where the time goes in v12:
time: 35.3 us; the launch traced here: 35.2 us
  starting transfers between devices  17.9 us (51%)
  waiting for transfers between devices  11.4 us (32%)
  Pallas kernels  3.11 us (9%)
  local copies, waits for them, and re-layouts  1.47 us (4%)
  between operations  0.8 us (2%)
  other arithmetic  0.57 us (2%)
    ppermute x12, starting transfers between devices, from_partner(): return lax.ppermute(x, axis, [(i, i ^ flip) for i in range(count)])  15.9 us
    ppermute x12, waiting for transfers between devices, from_partner(): return lax.ppermute(x, axis, [(i, i ^ flip) for i in range(count)])  8.93 us
    ppermute x2, waiting for transfers between devices, from_both(): return lax.ppermute(x, ('scen', 'fac'), pairs)  2.43 us
    ppermute x2, starting transfers between devices, from_both(): return lax.ppermute(x, ('scen', 'fac'), pairs)  1.97 us
    unnamed x22, local copies, waits for them, and re-layouts  1.47 us
    pallas_call x1, Pallas kernels, body(): pl.pallas_call(functools.partial(combine_kernel, part, held, owner_flips)...  0.9 us
  transfers between devices with their start and end apart: 14, of which 10 were waited for; matrix products, arithmetic and copies ran while one was open for 0% of the time, Pallas kernels for 6%

profile of v12, /device:TPU:0, one launch (start us, length us, event | category | flops | bytes accessed | tf_op | source)
XLA Modules:
  0.0 35.2 jit_solution(12809660730503679138)
XLA Ops:
  0.7 0.8 %copy-done.4 = bf16[256,2,128]{2,1,0:T(2,128)(2,1)S(1)} copy-done((bf16[256,2,128]{2,1,0:T(2,128)(2,1)S(1)}, bf16[256,2,128]{2,1,0:T(2,128)(2,1)}, u32[]{:S(2)}) %copy-start.4) | copy-done | bytes 131096
  1.5 0.4 %pack.1.refs_1_ = bf16[80,256]{1,0:T(8,128)(2,1)S(1)} custom-call(bf16[32,128]{1,0:T(8,128)(2,1)S(1)} %pick.1.pick_ref, bf16[256,2,128]{2,1,0:T(2,128)(2,1)S(1)} %copy-done.4, s32[2,256]{1,0:T(2,128)S(1)} %bitcast.5, s32[1,256]{1,0:T(1,128)S(1)} %bitcast.6), custom_call_target="tpu_custom_call" | custom-call | tf_op jit(solution)/shard_map/pack/pallas_call | solution.py:205
  2.0 4.1 %collective-permute-start.2 = (bf16[80,256]{1,0:T(8,128)(2,1)S(1)}, bf16[80,256]{1,0:T(8,128)(2,1)S(1)}, u32[]{:S(2)}, u32[]{:S(2)}) collective-permute-start(bf16[80,256]{1,0:T(8,128)(2,1)S(1)} %pack.1.refs_1_), channel_id=1, source_target_pairs={{0,4},{1,5},{2,6},{3,7},{4,0},{5,1},{6,2},{7,3},{8,12},{9,13},{10,... | collective-permute-start | bytes 122888 | tf_op jit(solution)/shard_map/ppermute | solution.py:161
  6.1 1.3 %collective-permute-start.1 = (bf16[80,256]{1,0:T(8,128)(2,1)S(1)}, bf16[80,256]{1,0:T(8,128)(2,1)S(1)}, u32[]{:S(2)}, u32[]{:S(2)}) collective-permute-start(bf16[80,256]{1,0:T(8,128)(2,1)S(1)} %pack.1.refs_1_), channel_id=1, source_target_pairs={{0,6},{1,7},{2,4},{3,5},{4,2},{5,3},{6,0},{7,1},{8,14},{9,15},{10,... | collective-permute-start | bytes 122888 | tf_op jit(solution)/shard_map/ppermute | solution.py:161
  7.4 0.2 collective-permute-start
  7.7 0.6 %copy-done.7 = f32[256]{0:T(256)S(1)} copy-done((f32[256]{0:T(256)S(1)}, f32[256]{0:T(256)}, u32[]{:S(2)}) %copy-start.7) | copy-done | bytes 1048
  8.3 0.5 %price.1.refs_2_ = bf16[512,256]{1,0:T(8,128)(2,1)S(1)} custom-call(bf16[2,256,256]{2,1,0:T(8,128)(2,1)S(1)} %copy-done.1, bf16[256,256]{1,0:T(8,128)(2,1)S(1)} %copy-done.3, f32[1,256]{1,0:T(1,128)S(1)} %bitcast.7, s32[2,256,256]{2,1,0:T(8,128)S(1)} %copy-done, bf16[2,256,256]{2,1,0:T(8,128)(2,1)S(1)} %copy-done.2, f32[1,256]{1,0:T(1,128)S(1)} %bitcast.8, ...), custom_call_target="tpu_custom_call" | custom-call | tf_op jit(solution)/shard_map/price/pallas_call | solution.py:217
  8.8 3.0 %collective-permute-start.7 = (bf16[512,256]{1,0:T(8,128)(2,1)S(1)}, bf16[512,256]{1,0:T(8,128)(2,1)S(1)}, u32[]{:S(2)}, u32[]{:S(2)}) collective-permute-start(bf16[512,256]{1,0:T(8,128)(2,1)S(1)} %price.1.refs_2_), channel_id=1, source_target_pairs={{0,6},{1,7},{2,4},{3,5},{4,2},{5,3},{6,0},{7,1},{8,14},{9,15},{10,... | collective-permute-start | bytes 786440 | tf_op jit(solution)/shard_map/ppermute | solution.py:161
  11.8 0.1 collective-permute-done.1.refs_3_
  11.9 0.9 %combine.1 = (f32[128,256]{1,0:T(8,128)S(1)}, bf16[128,256]{1,0:T(8,128)(2,1)S(1)}, bf16[128,256]{1,0:T(8,128)(2,1)S(1)}) custom-call(s32[16]{0:T(128)S(1)} %copy-done.10, bf16[80,256]{1,0:T(8,128)(2,1)S(1)} %pack.1.refs_1_, bf16[80,256]{1,0:T(8,128)(2,1)S(1)} %collective-permute-done.refs_2_, bf16[80,256]{1,0:T(8,128)(2,1)S(1)} %collective-permute-done.1.refs_3_, ...), custom_call_target="tpu_custom_call" | custom-call | flops 1000000000 | tf_op jit(solution)/shard_map/combine/pallas_call | solution.py:227
  12.8 1.6 %collective-permute-start.4 = (bf16[128,256]{1,0:T(8,128)(2,1)S(1)}, bf16[128,256]{1,0:T(8,128)(2,1)S(1)}, u32[]{:S(2)}, u32[]{:S(2)}) collective-permute-start(bf16[128,256]{1,0:T(8,128)(2,1)S(1)} %get-tuple-element.12), channel_id=1, source_target_pairs={{0,16},{8,24},{16,0},{24,8},{1,17},{9,25},{17,1},{25,9},{2,18},{10... | collective-permute-start | bytes 196616 | tf_op jit(solution)/shard_map/ppermute | solution.py:161
  14.4 1.4 %collective-permute-start.5 = (bf16[128,256]{1,0:T(8,128)(2,1)S(1)}, bf16[128,256]{1,0:T(8,128)(2,1)S(1)}, u32[]{:S(2)}, u32[]{:S(2)}) collective-permute-start(bf16[128,256]{1,0:T(8,128)(2,1)S(1)} %get-tuple-element.11), channel_id=1, source_target_pairs={{0,17},{1,16},{2,19},{3,18},{4,21},{5,20},{6,23},{7,22},{8,25},{9,... | collective-permute-start | bytes 196616 | tf_op jit(solution)/shard_map/ppermute | solution.py:171
  15.8 0.5 %collective-permute-start.3 = (bf16[128,256]{1,0:T(8,128)(2,1)S(1)}, bf16[128,256]{1,0:T(8,128)(2,1)S(1)}, u32[]{:S(2)}, u32[]{:S(2)}) collective-permute-start(bf16[128,256]{1,0:T(8,128)(2,1)S(1)} %get-tuple-element.11), channel_id=1, source_target_pairs={{0,1},{1,0},{2,3},{3,2},{4,5},{5,4},{6,7},{7,6},{8,9},{9,8},{10,11... | collective-permute-start | bytes 196616 | tf_op jit(solution)/shard_map/ppermute | solution.py:171
  16.3 1.3 %collective-permute-done.4.refs_2_ = bf16[128,256]{1,0:T(8,128)(2,1)S(1)} collective-permute-done((bf16[128,256]{1,0:T(8,128)(2,1)S(1)}, bf16[128,256]{1,0:T(8,128)(2,1)S(1)}, u32[]{:S(2)}, u32[]{:S(2)}) %collective-permute-start.4) | collective-permute-done | bytes 65568 | tf_op jit(solution)/shard_map/ppermute | solution.py:161
  17.6 1.9 %collective-permute-done.5.refs_3_ = bf16[128,256]{1,0:T(8,128)(2,1)S(1)} collective-permute-done((bf16[128,256]{1,0:T(8,128)(2,1)S(1)}, bf16[128,256]{1,0:T(8,128)(2,1)S(1)}, u32[]{:S(2)}, u32[]{:S(2)}) %collective-permute-start.5) | collective-permute-done | bytes 65568 | tf_op jit(solution)/shard_map/ppermute | solution.py:171
  19.5 0.5 %collective-permute-done.3.refs_1_ = bf16[128,256]{1,0:T(8,128)(2,1)S(1)} collective-permute-done((bf16[128,256]{1,0:T(8,128)(2,1)S(1)}, bf16[128,256]{1,0:T(8,128)(2,1)S(1)}, u32[]{:S(2)}, u32[]{:S(2)}) %collective-permute-start.3) | collective-permute-done | bytes 65568 | tf_op jit(solution)/shard_map/ppermute | solution.py:171
  20.1 0.1 merge.1.refs_0_
  20.2 0.1 collective-permute-start.6
  20.3 1.3 %collective-permute-done.6.refs_1_ = bf16[256,256]{1,0:T(8,128)(2,1)S(1)} collective-permute-done((bf16[256,256]{1,0:T(8,128)(2,1)S(1)}, bf16[256,256]{1,0:T(8,128)(2,1)S(1)}, u32[]{:S(2)}, u32[]{:S(2)}) %collective-permute-start.6) | collective-permute-done | bytes 131104 | tf_op jit(solution)/shard_map/ppermute | solution.py:161
  21.6 0.4 %value.1 = (f32[64,512]{1,0:T(8,128)S(1)}, bf16[64,512]{1,0:T(8,128)(2,1)S(1)}, bf16[64,512]{1,0:T(8,128)(2,1)S(1)}, bf16[64,512]{1,0:T(8,128)(2,1)S(1)}) custom-call(bf16[256,256]{1,0:T(8,128)(2,1)S(1)} %merge.1.refs_0_, bf16[256,256]{1,0:T(8,128)(2,1)S(1)} %collective-permute-done.6.refs_1_, bf16[512,256]{1,0:T(8,128)(2,1)S(1)} %price.1.refs_2_, ...), custom_call_target="tpu_custom_call" | custom-call | tf_op jit(solution)/shard_map/value/pallas_call | solution.py:259
  22.0 2.1 %collective-permute-start.8 = (bf16[64,512]{1,0:T(8,128)(2,1)S(1)}, bf16[64,512]{1,0:T(8,128)(2,1)S(1)}, u32[]{:S(2)}, u32[]{:S(2)}) collective-permute-start(bf16[64,512]{1,0:T(8,128)(2,1)S(1)} %get-tuple-element.15), channel_id=1, source_target_pairs={{0,2},{1,3},{2,0},{3,1},{4,6},{5,7},{6,4},{7,5},{8,10},{9,11},{10,... | collective-permute-start | bytes 196616 | tf_op jit(solution)/shard_map/ppermute | solution.py:161
  24.1 1.5 %collective-permute-start.9 = (bf16[64,512]{1,0:T(8,128)(2,1)S(1)}, bf16[64,512]{1,0:T(8,128)(2,1)S(1)}, u32[]{:S(2)}, u32[]{:S(2)}) collective-permute-start(bf16[64,512]{1,0:T(8,128)(2,1)S(1)} %get-tuple-element.16), channel_id=1, source_target_pairs={{0,1},{1,0},{2,3},{3,2},{4,5},{5,4},{6,7},{7,6},{8,9},{9,8},{10,11... | collective-permute-start | bytes 196616 | tf_op jit(solution)/shard_map/ppermute | solution.py:161
  25.7 0.9 %collective-permute-done.8.refs_1_ = bf16[64,512]{1,0:T(8,128)(2,1)S(1)} collective-permute-done((bf16[64,512]{1,0:T(8,128)(2,1)S(1)}, bf16[64,512]{1,0:T(8,128)(2,1)S(1)}, u32[]{:S(2)}, u32[]{:S(2)}) %collective-permute-start.8) | collective-permute-done | bytes 65568 | tf_op jit(solution)/shard_map/ppermute | solution.py:161
  26.6 2.5 %collective-permute-done.9.refs_2_ = bf16[64,512]{1,0:T(8,128)(2,1)S(1)} collective-permute-done((bf16[64,512]{1,0:T(8,128)(2,1)S(1)}, bf16[64,512]{1,0:T(8,128)(2,1)S(1)}, u32[]{:S(2)}, u32[]{:S(2)}) %collective-permute-start.9) | collective-permute-done | bytes 65568 | tf_op jit(solution)/shard_map/ppermute | solution.py:161
  29.1 1.7 %collective-permute-done.10.refs_3_ = bf16[64,512]{1,0:T(8,128)(2,1)S(1)} collective-permute-done((bf16[64,512]{1,0:T(8,128)(2,1)S(1)}, bf16[64,512]{1,0:T(8,128)(2,1)S(1)}, u32[]{:S(2)}, u32[]{:S(2)}) %collective-permute-start.10) | collective-permute-done | bytes 65568 | tf_op jit(solution)/shard_map/ppermute | solution.py:161
  30.8 0.1 totals.1
  31.0 1.6 %collective-permute-start.12 = (f32[2,64]{1,0:T(2,128)S(1)}, f32[2,64]{1,0:T(2,128)S(1)}, u32[]{:S(2)}, u32[]{:S(2)}) collective-permute-start(f32[2,64]{1,0:T(2,128)S(1)} %totals.1), channel_id=1, source_target_pairs={{0,16},{8,24},{16,0},{24,8},{1,17},{9,25},{17,1},{25,9},{2,18},{10... | collective-permute-start | bytes 1544 | tf_op jit(solution)/shard_map/ppermute | solution.py:161
  32.6 0.3 collective-permute-start.11
  32.8 0.7 %expose.1 = f32[2,64,256]{2,1,0:T(8,128)} custom-call(f32[64,512]{1,0:T(8,128)S(1)} %get-tuple-element.14.refs_0_, bf16[64,512]{1,0:T(8,128)(2,1)S(1)} %collective-permute-done.8.refs_1_, bf16[64,512]{1,0:T(8,128)(2,1)S(1)} %collective-permute-done.9.refs_2_, bf16[64,512]{1,0:T(8,128)(2,1)S(1)} %collective-permute-done.10.refs_3_), custom_call_target="tpu_custom_call" | custom-call | tf_op jit(solution)/shard_map/expose/pallas_call | solution.py:283
  33.5 0.4 %collective-permute-done.13 = f32[2,64]{1,0:T(2,128)S(1)} collective-permute-done((f32[2,64]{1,0:T(2,128)S(1)}, f32[2,64]{1,0:T(2,128)S(1)}, u32[]{:S(2)}, u32[]{:S(2)}) %collective-permute-start.13) | collective-permute-done | bytes 544 | tf_op jit(solution)/shard_map/ppermute | solution.py:161
  34.0 0.7 %collective-permute-done.12 = f32[2,64]{1,0:T(2,128)S(1)} collective-permute-done((f32[2,64]{1,0:T(2,128)S(1)}, f32[2,64]{1,0:T(2,128)S(1)}, u32[]{:S(2)}, u32[]{:S(2)}) %collective-permute-start.12) | collective-permute-done | bytes 544 | tf_op jit(solution)/shard_map/ppermute | solution.py:161
  34.6 0.6 %add_multiply_fusion = f32[2,64]{1,0:T(2,128)} fusion(f32[2,64]{1,0:T(2,128)S(1)} %collective-permute-done.12, f32[2,64]{1,0:T(2,128)S(1)} %collective-permute-done.13, f32[2,64]{1,0:T(2,128)S(1)} %totals.1, f32[2,64]{1,0:T(2,128)S(1)} %collective-permute-done.11), kind=kLoop, calls=%fused_computation | loop fusion | flops 512 | bytes 2560 | tf_op jit(solution)/shard_map/div | solution.py:296
  (27 shorter events, 0.2 us)
Async XLA Ops:
  0.6 0.9 %copy-start.4 = (bf16[256,2,128]{2,1,0:T(2,128)(2,1)S(1)}, bf16[256,2,128]{2,1,0:T(2,128)(2,1)}, u32[]{:S(2)}) copy-start(bf16[256,2,128]{2,1,0:T(2,128)(2,1)} %weights_ref.1) | copy-start | bytes 393220
  0.6 0.9 %copy-start.5 = (s32[256,2]{0,1:T(2,128)S(1)}, s32[256,2]{0,1:T(2,128)}, u32[]{:S(2)}) copy-start(s32[256,2]{0,1:T(2,128)} %param.18) | copy-start | bytes 6148
  0.7 0.9 %copy-start.6 = (s32[256]{0:T(256)S(1)}, s32[256]{0:T(256)}, u32[]{:S(2)}) copy-start(s32[256]{0:T(256)} %param.21) | copy-start | bytes 3076
  0.7 7.0 %copy-start = (s32[2,256,256]{2,1,0:T(8,128)S(1)}, s32[2,256,256]{2,1,0:T(8,128)}, u32[]{:S(2)}) copy-start(s32[2,256,256]{2,1,0:T(8,128)} %counts_ref.1) | copy-start | bytes 1572868
  0.7 7.0 %copy-start.1 = (bf16[2,256,256]{2,1,0:T(8,128)(2,1)S(1)}, bf16[2,256,256]{2,1,0:T(8,128)(2,1)}, u32[]{:S(2)}) copy-start(bf16[2,256,256]{2,1,0:T(8,128)(2,1)} %shocks_ref) | copy-start | bytes 786436
  0.7 7.0 %copy-start.2 = (bf16[2,256,256]{2,1,0:T(8,128)(2,1)S(1)}, bf16[2,256,256]{2,1,0:T(8,128)(2,1)}, u32[]{:S(2)}) copy-start(bf16[2,256,256]{2,1,0:T(8,128)(2,1)} %noise_ref.1) | copy-start | bytes 786436
  0.7 7.0 %copy-start.8 = (f32[256]{0:T(256)S(1)}, f32[256]{0:T(256)}, u32[]{:S(2)}) copy-start(f32[256]{0:T(256)} %param.16) | copy-start | bytes 3076
  0.7 7.0 %copy-start.9 = (f32[256]{0:T(256)S(1)}, f32[256]{0:T(256)}, u32[]{:S(2)}) copy-start(f32[256]{0:T(256)} %param.17) | copy-start | bytes 3076
  0.7 6.9 %copy-start.3 = (bf16[256,256]{1,0:T(8,128)(2,1)S(1)}, bf16[256,256]{1,0:T(8,128)(2,1)}, u32[]{:S(2)}) copy-start(bf16[256,256]{1,0:T(8,128)(2,1)} %loadings_ref.1) | copy-start | bytes 393220
  2.0 9.8 %collective-permute-start.2 = (bf16[80,256]{1,0:T(8,128)(2,1)S(1)}, bf16[80,256]{1,0:T(8,128)(2,1)S(1)}, u32[]{:S(2)}, u32[]{:S(2)}) collective-permute-start(bf16[80,256]{1,0:T(8,128)(2,1)S(1)} %pack.1.refs_1_), channel_id=1, source_target_pairs={{0,4},{1,5},{2,6},{3,7},{4,0},{5,1},{6,2},{7,3},{8,12},{9,13},{10,... | collective-permute-start | bytes 122888 | tf_op jit(solution)/shard_map/ppermute | solution.py:161
  6.1 5.8 %collective-permute-start.1 = (bf16[80,256]{1,0:T(8,128)(2,1)S(1)}, bf16[80,256]{1,0:T(8,128)(2,1)S(1)}, u32[]{:S(2)}, u32[]{:S(2)}) collective-permute-start(bf16[80,256]{1,0:T(8,128)(2,1)S(1)} %pack.1.refs_1_), channel_id=1, source_target_pairs={{0,6},{1,7},{2,4},{3,5},{4,2},{5,3},{6,0},{7,1},{8,14},{9,15},{10,... | collective-permute-start | bytes 122888 | tf_op jit(solution)/shard_map/ppermute | solution.py:161
  7.4 4.5 %collective-permute-start = (bf16[80,256]{1,0:T(8,128)(2,1)S(1)}, bf16[80,256]{1,0:T(8,128)(2,1)S(1)}, u32[]{:S(2)}, u32[]{:S(2)}) collective-permute-start(bf16[80,256]{1,0:T(8,128)(2,1)S(1)} %pack.1.refs_1_), channel_id=1, source_target_pairs={{0,2},{1,3},{2,0},{3,1},{4,6},{5,7},{6,4},{7,5},{8,10},{9,11},{10,... | collective-permute-start | bytes 122888 | tf_op jit(solution)/shard_map/ppermute | solution.py:161
  7.6 0.7 %copy-start.7 = (f32[256]{0:T(256)S(1)}, f32[256]{0:T(256)}, u32[]{:S(2)}) copy-start(f32[256]{0:T(256)} %param.13) | copy-start | bytes 3076
  8.3 3.6 %copy-start.10 = (s32[16]{0:T(128)S(1)}, s32[16]{0:T(128)}, u32[]{:S(2)}) copy-start(s32[16]{0:T(128)} %refs_0_.1) | copy-start | bytes 196
  8.8 12.8 %collective-permute-start.7 = (bf16[512,256]{1,0:T(8,128)(2,1)S(1)}, bf16[512,256]{1,0:T(8,128)(2,1)S(1)}, u32[]{:S(2)}, u32[]{:S(2)}) collective-permute-start(bf16[512,256]{1,0:T(8,128)(2,1)S(1)} %price.1.refs_2_), channel_id=1, source_target_pairs={{0,6},{1,7},{2,4},{3,5},{4,2},{5,3},{6,0},{7,1},{8,14},{9,15},{10,... | collective-permute-start | bytes 786440 | tf_op jit(solution)/shard_map/ppermute | solution.py:161
  12.8 4.9 %collective-permute-start.4 = (bf16[128,256]{1,0:T(8,128)(2,1)S(1)}, bf16[128,256]{1,0:T(8,128)(2,1)S(1)}, u32[]{:S(2)}, u32[]{:S(2)}) collective-permute-start(bf16[128,256]{1,0:T(8,128)(2,1)S(1)} %get-tuple-element.12), channel_id=1, source_target_pairs={{0,16},{8,24},{16,0},{24,8},{1,17},{9,25},{17,1},{25,9},{2,18},{10... | collective-permute-start | bytes 196616 | tf_op jit(solution)/shard_map/ppermute | solution.py:161
  14.4 5.2 %collective-permute-start.5 = (bf16[128,256]{1,0:T(8,128)(2,1)S(1)}, bf16[128,256]{1,0:T(8,128)(2,1)S(1)}, u32[]{:S(2)}, u32[]{:S(2)}) collective-permute-start(bf16[128,256]{1,0:T(8,128)(2,1)S(1)} %get-tuple-element.11), channel_id=1, source_target_pairs={{0,17},{1,16},{2,19},{3,18},{4,21},{5,20},{6,23},{7,22},{8,25},{9,... | collective-permute-start | bytes 196616 | tf_op jit(solution)/shard_map/ppermute | solution.py:171
  15.8 4.3 %collective-permute-start.3 = (bf16[128,256]{1,0:T(8,128)(2,1)S(1)}, bf16[128,256]{1,0:T(8,128)(2,1)S(1)}, u32[]{:S(2)}, u32[]{:S(2)}) collective-permute-start(bf16[128,256]{1,0:T(8,128)(2,1)S(1)} %get-tuple-element.11), channel_id=1, source_target_pairs={{0,1},{1,0},{2,3},{3,2},{4,5},{5,4},{6,7},{7,6},{8,9},{9,8},{10,11... | collective-permute-start | bytes 196616 | tf_op jit(solution)/shard_map/ppermute | solution.py:171
  20.2 1.4 %collective-permute-start.6 = (bf16[256,256]{1,0:T(8,128)(2,1)S(1)}, bf16[256,256]{1,0:T(8,128)(2,1)S(1)}, u32[]{:S(2)}, u32[]{:S(2)}) collective-permute-start(bf16[256,256]{1,0:T(8,128)(2,1)S(1)} %merge.1.refs_0_), channel_id=1, source_target_pairs={{0,8},{8,0},{16,24},{24,16},{1,9},{9,1},{17,25},{25,17},{2,10},{10... | collective-permute-start | bytes 393224 | tf_op jit(solution)/shard_map/ppermute | solution.py:161
  22.0 4.6 %collective-permute-start.8 = (bf16[64,512]{1,0:T(8,128)(2,1)S(1)}, bf16[64,512]{1,0:T(8,128)(2,1)S(1)}, u32[]{:S(2)}, u32[]{:S(2)}) collective-permute-start(bf16[64,512]{1,0:T(8,128)(2,1)S(1)} %get-tuple-element.15), channel_id=1, source_target_pairs={{0,2},{1,3},{2,0},{3,1},{4,6},{5,7},{6,4},{7,5},{8,10},{9,11},{10,... | collective-permute-start | bytes 196616 | tf_op jit(solution)/shard_map/ppermute | solution.py:161
  24.1 5.0 %collective-permute-start.9 = (bf16[64,512]{1,0:T(8,128)(2,1)S(1)}, bf16[64,512]{1,0:T(8,128)(2,1)S(1)}, u32[]{:S(2)}, u32[]{:S(2)}) collective-permute-start(bf16[64,512]{1,0:T(8,128)(2,1)S(1)} %get-tuple-element.16), channel_id=1, source_target_pairs={{0,1},{1,0},{2,3},{3,2},{4,5},{5,4},{6,7},{7,6},{8,9},{9,8},{10,11... | collective-permute-start | bytes 196616 | tf_op jit(solution)/shard_map/ppermute | solution.py:161
  25.6 5.2 %collective-permute-start.10 = (bf16[64,512]{1,0:T(8,128)(2,1)S(1)}, bf16[64,512]{1,0:T(8,128)(2,1)S(1)}, u32[]{:S(2)}, u32[]{:S(2)}) collective-permute-start(bf16[64,512]{1,0:T(8,128)(2,1)S(1)} %get-tuple-element.17), channel_id=1, source_target_pairs={{0,3},{1,2},{2,1},{3,0},{4,7},{5,6},{6,5},{7,4},{8,11},{9,10},{10,... | collective-permute-start | bytes 196616 | tf_op jit(solution)/shard_map/ppermute | solution.py:161
  30.9 3.1 %collective-permute-start.13 = (f32[2,64]{1,0:T(2,128)S(1)}, f32[2,64]{1,0:T(2,128)S(1)}, u32[]{:S(2)}, u32[]{:S(2)}) collective-permute-start(f32[2,64]{1,0:T(2,128)S(1)} %totals.1), channel_id=1, source_target_pairs={{0,24},{8,16},{16,8},{24,0},{1,25},{9,17},{17,9},{25,1},{2,26},{10... | collective-permute-start | bytes 1544 | tf_op jit(solution)/shard_map/ppermute | solution.py:161
  31.0 3.6 %collective-permute-start.12 = (f32[2,64]{1,0:T(2,128)S(1)}, f32[2,64]{1,0:T(2,128)S(1)}, u32[]{:S(2)}, u32[]{:S(2)}) collective-permute-start(f32[2,64]{1,0:T(2,128)S(1)} %totals.1), channel_id=1, source_target_pairs={{0,16},{8,24},{16,0},{24,8},{1,17},{9,25},{17,1},{25,9},{2,18},{10... | collective-permute-start | bytes 1544 | tf_op jit(solution)/shard_map/ppermute | solution.py:161
  32.6 2.1 %collective-permute-start.11 = (f32[2,64]{1,0:T(2,128)S(1)}, f32[2,64]{1,0:T(2,128)S(1)}, u32[]{:S(2)}, u32[]{:S(2)}) collective-permute-start(f32[2,64]{1,0:T(2,128)S(1)} %totals.1), channel_id=1, source_target_pairs={{0,8},{8,0},{16,24},{24,16},{1,9},{9,1},{17,25},{25,17},{2,10},{10... | collective-permute-start | bytes 1544 | tf_op jit(solution)/shard_map/ppermute | solution.py:161

commit v13 on v12

--- a/solution.py
+++ b/solution.py
@@ -269,7 +269,7 @@
         name="value",
     )(*shares, *pair_prices)
     sends = list(zip(parts[1:], owner_flips[1:]))
-    sends = sends[1:2] + sends[:1] + sends[2:]
+    sends = sends[1:] + sends[:1]
     parts = [parts[0]] + [from_partner(x, "fac", i) for x, i in sends]
 
     totals = pl.pallas_call(

time: 35.3 us -> 34.6 us (0.980)
  waiting for transfers between devices: 11.4 us -> 10.6 us
    ppermute x12, waiting for transfers between devices: 8.93 us -> 8.14 us  [from_partner(): return lax.ppermute(x, axis, [(i, i ^ flip) for i in range(count)])]
where the time goes in v13:
time: 34.6 us; the launch traced here: 34.4 us
  starting transfers between devices  17.9 us (52%)
  waiting for transfers between devices  10.6 us (31%)
  Pallas kernels  3.11 us (9%)
  local copies, waits for them, and re-layouts  1.47 us (4%)
  between operations  0.8 us (2%)
  other arithmetic  0.57 us (2%)
    ppermute x12, starting transfers between devices, from_partner(): return lax.ppermute(x, axis, [(i, i ^ flip) for i in range(count)])  15.9 us
    ppermute x12, waiting for transfers between devices, from_partner(): return lax.ppermute(x, axis, [(i, i ^ flip) for i in range(count)])  8.14 us
    ppermute x2, waiting for transfers between devices, from_both(): return lax.ppermute(x, ('scen', 'fac'), pairs)  2.43 us
    ppermute x2, starting transfers between devices, from_both(): return lax.ppermute(x, ('scen', 'fac'), pairs)  1.97 us
    unnamed x22, local copies, waits for them, and re-layouts  1.47 us
    pallas_call x1, Pallas kernels, body(): pl.pallas_call(functools.partial(combine_kernel, part, held, owner_flips)...  0.9 us
  transfers between devices with their start and end apart: 14, of which 10 were waited for; matrix products, arithmetic and copies ran while one was open for 0% of the time, Pallas kernels for 6%

profile of v13, /device:TPU:0, one launch (start us, length us, event | category | flops | bytes accessed | tf_op | source)
XLA Modules:
  0.0 34.4 jit_solution(2343744735209062086)
XLA Ops:
  0.7 0.8 %copy-done.4 = bf16[256,2,128]{2,1,0:T(2,128)(2,1)S(1)} copy-done((bf16[256,2,128]{2,1,0:T(2,128)(2,1)S(1)}, bf16[256,2,128]{2,1,0:T(2,128)(2,1)}, u32[]{:S(2)}) %copy-start.4) | copy-done | bytes 131096
  1.5 0.4 %pack.1.refs_1_ = bf16[80,256]{1,0:T(8,128)(2,1)S(1)} custom-call(bf16[32,128]{1,0:T(8,128)(2,1)S(1)} %pick.1.pick_ref, bf16[256,2,128]{2,1,0:T(2,128)(2,1)S(1)} %copy-done.4, s32[2,256]{1,0:T(2,128)S(1)} %bitcast.5, s32[1,256]{1,0:T(1,128)S(1)} %bitcast.6), custom_call_target="tpu_custom_call" | custom-call | tf_op jit(solution)/shard_map/pack/pallas_call | solution.py:205
  2.0 4.1 %collective-permute-start.2 = (bf16[80,256]{1,0:T(8,128)(2,1)S(1)}, bf16[80,256]{1,0:T(8,128)(2,1)S(1)}, u32[]{:S(2)}, u32[]{:S(2)}) collective-permute-start(bf16[80,256]{1,0:T(8,128)(2,1)S(1)} %pack.1.refs_1_), channel_id=1, source_target_pairs={{0,4},{1,5},{2,6},{3,7},{4,0},{5,1},{6,2},{7,3},{8,12},{9,13},{10,... | collective-permute-start | bytes 122888 | tf_op jit(solution)/shard_map/ppermute | solution.py:161
  6.1 1.3 %collective-permute-start.1 = (bf16[80,256]{1,0:T(8,128)(2,1)S(1)}, bf16[80,256]{1,0:T(8,128)(2,1)S(1)}, u32[]{:S(2)}, u32[]{:S(2)}) collective-permute-start(bf16[80,256]{1,0:T(8,128)(2,1)S(1)} %pack.1.refs_1_), channel_id=1, source_target_pairs={{0,6},{1,7},{2,4},{3,5},{4,2},{5,3},{6,0},{7,1},{8,14},{9,15},{10,... | collective-permute-start | bytes 122888 | tf_op jit(solution)/shard_map/ppermute | solution.py:161
  7.4 0.2 collective-permute-start
  7.7 0.6 %copy-done.7 = f32[256]{0:T(256)S(1)} copy-done((f32[256]{0:T(256)S(1)}, f32[256]{0:T(256)}, u32[]{:S(2)}) %copy-start.7) | copy-done | bytes 1048
  8.3 0.5 %price.1.refs_2_ = bf16[512,256]{1,0:T(8,128)(2,1)S(1)} custom-call(bf16[2,256,256]{2,1,0:T(8,128)(2,1)S(1)} %copy-done.1, bf16[256,256]{1,0:T(8,128)(2,1)S(1)} %copy-done.3, f32[1,256]{1,0:T(1,128)S(1)} %bitcast.7, s32[2,256,256]{2,1,0:T(8,128)S(1)} %copy-done, bf16[2,256,256]{2,1,0:T(8,128)(2,1)S(1)} %copy-done.2, f32[1,256]{1,0:T(1,128)S(1)} %bitcast.8, ...), custom_call_target="tpu_custom_call" | custom-call | tf_op jit(solution)/shard_map/price/pallas_call | solution.py:217
  8.8 3.0 %collective-permute-start.7 = (bf16[512,256]{1,0:T(8,128)(2,1)S(1)}, bf16[512,256]{1,0:T(8,128)(2,1)S(1)}, u32[]{:S(2)}, u32[]{:S(2)}) collective-permute-start(bf16[512,256]{1,0:T(8,128)(2,1)S(1)} %price.1.refs_2_), channel_id=1, source_target_pairs={{0,6},{1,7},{2,4},{3,5},{4,2},{5,3},{6,0},{7,1},{8,14},{9,15},{10,... | collective-permute-start | bytes 786440 | tf_op jit(solution)/shard_map/ppermute | solution.py:161
  11.8 0.1 collective-permute-done.1.refs_3_
  11.9 0.9 %combine.1 = (f32[128,256]{1,0:T(8,128)S(1)}, bf16[128,256]{1,0:T(8,128)(2,1)S(1)}, bf16[128,256]{1,0:T(8,128)(2,1)S(1)}) custom-call(s32[16]{0:T(128)S(1)} %copy-done.10, bf16[80,256]{1,0:T(8,128)(2,1)S(1)} %pack.1.refs_1_, bf16[80,256]{1,0:T(8,128)(2,1)S(1)} %collective-permute-done.refs_2_, bf16[80,256]{1,0:T(8,128)(2,1)S(1)} %collective-permute-done.1.refs_3_, ...), custom_call_target="tpu_custom_call" | custom-call | flops 1000000000 | tf_op jit(solution)/shard_map/combine/pallas_call | solution.py:227
  12.8 1.6 %collective-permute-start.4 = (bf16[128,256]{1,0:T(8,128)(2,1)S(1)}, bf16[128,256]{1,0:T(8,128)(2,1)S(1)}, u32[]{:S(2)}, u32[]{:S(2)}) collective-permute-start(bf16[128,256]{1,0:T(8,128)(2,1)S(1)} %get-tuple-element.12), channel_id=1, source_target_pairs={{0,16},{8,24},{16,0},{24,8},{1,17},{9,25},{17,1},{25,9},{2,18},{10... | collective-permute-start | bytes 196616 | tf_op jit(solution)/shard_map/ppermute | solution.py:161
  14.4 1.4 %collective-permute-start.5 = (bf16[128,256]{1,0:T(8,128)(2,1)S(1)}, bf16[128,256]{1,0:T(8,128)(2,1)S(1)}, u32[]{:S(2)}, u32[]{:S(2)}) collective-permute-start(bf16[128,256]{1,0:T(8,128)(2,1)S(1)} %get-tuple-element.11), channel_id=1, source_target_pairs={{0,17},{1,16},{2,19},{3,18},{4,21},{5,20},{6,23},{7,22},{8,25},{9,... | collective-permute-start | bytes 196616 | tf_op jit(solution)/shard_map/ppermute | solution.py:171
  15.8 0.5 %collective-permute-start.3 = (bf16[128,256]{1,0:T(8,128)(2,1)S(1)}, bf16[128,256]{1,0:T(8,128)(2,1)S(1)}, u32[]{:S(2)}, u32[]{:S(2)}) collective-permute-start(bf16[128,256]{1,0:T(8,128)(2,1)S(1)} %get-tuple-element.11), channel_id=1, source_target_pairs={{0,1},{1,0},{2,3},{3,2},{4,5},{5,4},{6,7},{7,6},{8,9},{9,8},{10,11... | collective-permute-start | bytes 196616 | tf_op jit(solution)/shard_map/ppermute | solution.py:171
  16.3 1.3 %collective-permute-done.4.refs_2_ = bf16[128,256]{1,0:T(8,128)(2,1)S(1)} collective-permute-done((bf16[128,256]{1,0:T(8,128)(2,1)S(1)}, bf16[128,256]{1,0:T(8,128)(2,1)S(1)}, u32[]{:S(2)}, u32[]{:S(2)}) %collective-permute-start.4) | collective-permute-done | bytes 65568 | tf_op jit(solution)/shard_map/ppermute | solution.py:161
  17.6 1.9 %collective-permute-done.5.refs_3_ = bf16[128,256]{1,0:T(8,128)(2,1)S(1)} collective-permute-done((bf16[128,256]{1,0:T(8,128)(2,1)S(1)}, bf16[128,256]{1,0:T(8,128)(2,1)S(1)}, u32[]{:S(2)}, u32[]{:S(2)}) %collective-permute-start.5) | collective-permute-done | bytes 65568 | tf_op jit(solution)/shard_map/ppermute | solution.py:171
  19.5 0.5 %collective-permute-done.3.refs_1_ = bf16[128,256]{1,0:T(8,128)(2,1)S(1)} collective-permute-done((bf16[128,256]{1,0:T(8,128)(2,1)S(1)}, bf16[128,256]{1,0:T(8,128)(2,1)S(1)}, u32[]{:S(2)}, u32[]{:S(2)}) %collective-permute-start.3) | collective-permute-done | bytes 65568 | tf_op jit(solution)/shard_map/ppermute | solution.py:171
  20.1 0.1 merge.1.refs_0_
  20.3 1.3 %collective-permute-done.6.refs_1_ = bf16[256,256]{1,0:T(8,128)(2,1)S(1)} collective-permute-done((bf16[256,256]{1,0:T(8,128)(2,1)S(1)}, bf16[256,256]{1,0:T(8,128)(2,1)S(1)}, u32[]{:S(2)}, u32[]{:S(2)}) %collective-permute-start.6) | collective-permute-done | bytes 131104 | tf_op jit(solution)/shard_map/ppermute | solution.py:161
  21.6 0.4 %value.1 = (f32[64,512]{1,0:T(8,128)S(1)}, bf16[64,512]{1,0:T(8,128)(2,1)S(1)}, bf16[64,512]{1,0:T(8,128)(2,1)S(1)}, bf16[64,512]{1,0:T(8,128)(2,1)S(1)}) custom-call(bf16[256,256]{1,0:T(8,128)(2,1)S(1)} %merge.1.refs_0_, bf16[256,256]{1,0:T(8,128)(2,1)S(1)} %collective-permute-done.6.refs_1_, bf16[512,256]{1,0:T(8,128)(2,1)S(1)} %price.1.refs_2_, ...), custom_call_target="tpu_custom_call" | custom-call | tf_op jit(solution)/shard_map/value/pallas_call | solution.py:259
  22.0 2.1 %collective-permute-start.8 = (bf16[64,512]{1,0:T(8,128)(2,1)S(1)}, bf16[64,512]{1,0:T(8,128)(2,1)S(1)}, u32[]{:S(2)}, u32[]{:S(2)}) collective-permute-start(bf16[64,512]{1,0:T(8,128)(2,1)S(1)} %get-tuple-element.15), channel_id=1, source_target_pairs={{0,2},{1,3},{2,0},{3,1},{4,6},{5,7},{6,4},{7,5},{8,10},{9,11},{10,... | collective-permute-start | bytes 196616 | tf_op jit(solution)/shard_map/ppermute | solution.py:161
  24.1 1.0 %collective-permute-start.9 = (bf16[64,512]{1,0:T(8,128)(2,1)S(1)}, bf16[64,512]{1,0:T(8,128)(2,1)S(1)}, u32[]{:S(2)}, u32[]{:S(2)}) collective-permute-start(bf16[64,512]{1,0:T(8,128)(2,1)S(1)} %get-tuple-element.16), channel_id=1, source_target_pairs={{0,3},{1,2},{2,1},{3,0},{4,7},{5,6},{6,5},{7,4},{8,11},{9,10},{10,... | collective-permute-start | bytes 196616 | tf_op jit(solution)/shard_map/ppermute | solution.py:161
  25.1 0.5 %collective-permute-start.10 = (bf16[64,512]{1,0:T(8,128)(2,1)S(1)}, bf16[64,512]{1,0:T(8,128)(2,1)S(1)}, u32[]{:S(2)}, u32[]{:S(2)}) collective-permute-start(bf16[64,512]{1,0:T(8,128)(2,1)S(1)} %get-tuple-element.17), channel_id=1, source_target_pairs={{0,1},{1,0},{2,3},{3,2},{4,5},{5,4},{6,7},{7,6},{8,9},{9,8},{10,11... | collective-permute-start | bytes 196616 | tf_op jit(solution)/shard_map/ppermute | solution.py:161
  25.7 0.7 %collective-permute-done.8.refs_1_ = bf16[64,512]{1,0:T(8,128)(2,1)S(1)} collective-permute-done((bf16[64,512]{1,0:T(8,128)(2,1)S(1)}, bf16[64,512]{1,0:T(8,128)(2,1)S(1)}, u32[]{:S(2)}, u32[]{:S(2)}) %collective-permute-start.8) | collective-permute-done | bytes 65568 | tf_op jit(solution)/shard_map/ppermute | solution.py:161
  26.4 3.0 %collective-permute-done.9.refs_2_ = bf16[64,512]{1,0:T(8,128)(2,1)S(1)} collective-permute-done((bf16[64,512]{1,0:T(8,128)(2,1)S(1)}, bf16[64,512]{1,0:T(8,128)(2,1)S(1)}, u32[]{:S(2)}, u32[]{:S(2)}) %collective-permute-start.9) | collective-permute-done | bytes 65568 | tf_op jit(solution)/shard_map/ppermute | solution.py:161
  29.4 0.6 %collective-permute-done.10.refs_3_ = bf16[64,512]{1,0:T(8,128)(2,1)S(1)} collective-permute-done((bf16[64,512]{1,0:T(8,128)(2,1)S(1)}, bf16[64,512]{1,0:T(8,128)(2,1)S(1)}, u32[]{:S(2)}, u32[]{:S(2)}) %collective-permute-start.10) | collective-permute-done | bytes 65568 | tf_op jit(solution)/shard_map/ppermute | solution.py:161
  30.0 0.1 totals.1
  30.2 1.6 %collective-permute-start.12 = (f32[2,64]{1,0:T(2,128)S(1)}, f32[2,64]{1,0:T(2,128)S(1)}, u32[]{:S(2)}, u32[]{:S(2)}) collective-permute-start(f32[2,64]{1,0:T(2,128)S(1)} %totals.1), channel_id=1, source_target_pairs={{0,16},{8,24},{16,0},{24,8},{1,17},{9,25},{17,1},{25,9},{2,18},{10... | collective-permute-start | bytes 1544 | tf_op jit(solution)/shard_map/ppermute | solution.py:161
  31.8 0.3 collective-permute-start.11
  32.0 0.7 %expose.1 = f32[2,64,256]{2,1,0:T(8,128)} custom-call(f32[64,512]{1,0:T(8,128)S(1)} %get-tuple-element.14.refs_0_, bf16[64,512]{1,0:T(8,128)(2,1)S(1)} %collective-permute-done.8.refs_1_, bf16[64,512]{1,0:T(8,128)(2,1)S(1)} %collective-permute-done.9.refs_2_, bf16[64,512]{1,0:T(8,128)(2,1)S(1)} %collective-permute-done.10.refs_3_), custom_call_target="tpu_custom_call" | custom-call | tf_op jit(solution)/shard_map/expose/pallas_call | solution.py:283
  32.7 0.4 %collective-permute-done.13 = f32[2,64]{1,0:T(2,128)S(1)} collective-permute-done((f32[2,64]{1,0:T(2,128)S(1)}, f32[2,64]{1,0:T(2,128)S(1)}, u32[]{:S(2)}, u32[]{:S(2)}) %collective-permute-start.13) | collective-permute-done | bytes 544 | tf_op jit(solution)/shard_map/ppermute | solution.py:161
  33.2 0.7 %collective-permute-done.12 = f32[2,64]{1,0:T(2,128)S(1)} collective-permute-done((f32[2,64]{1,0:T(2,128)S(1)}, f32[2,64]{1,0:T(2,128)S(1)}, u32[]{:S(2)}, u32[]{:S(2)}) %collective-permute-start.12) | collective-permute-done | bytes 544 | tf_op jit(solution)/shard_map/ppermute | solution.py:161
  33.8 0.6 %add_multiply_fusion = f32[2,64]{1,0:T(2,128)} fusion(f32[2,64]{1,0:T(2,128)S(1)} %collective-permute-done.12, f32[2,64]{1,0:T(2,128)S(1)} %collective-permute-done.13, f32[2,64]{1,0:T(2,128)S(1)} %totals.1, f32[2,64]{1,0:T(2,128)S(1)} %collective-permute-done.11), kind=kLoop, calls=%fused_computation | loop fusion | flops 512 | bytes 2560 | tf_op jit(solution)/shard_map/div | solution.py:296
  (27 shorter events, 0.2 us)
Async XLA Ops:
  0.6 0.9 %copy-start.4 = (bf16[256,2,128]{2,1,0:T(2,128)(2,1)S(1)}, bf16[256,2,128]{2,1,0:T(2,128)(2,1)}, u32[]{:S(2)}) copy-start(bf16[256,2,128]{2,1,0:T(2,128)(2,1)} %weights_ref.1) | copy-start | bytes 393220
  0.6 0.9 %copy-start.5 = (s32[256,2]{0,1:T(2,128)S(1)}, s32[256,2]{0,1:T(2,128)}, u32[]{:S(2)}) copy-start(s32[256,2]{0,1:T(2,128)} %param.18) | copy-start | bytes 6148
  0.7 0.9 %copy-start.6 = (s32[256]{0:T(256)S(1)}, s32[256]{0:T(256)}, u32[]{:S(2)}) copy-start(s32[256]{0:T(256)} %param.21) | copy-start | bytes 3076
  0.7 7.0 %copy-start = (s32[2,256,256]{2,1,0:T(8,128)S(1)}, s32[2,256,256]{2,1,0:T(8,128)}, u32[]{:S(2)}) copy-start(s32[2,256,256]{2,1,0:T(8,128)} %counts_ref.1) | copy-start | bytes 1572868
  0.7 7.0 %copy-start.1 = (bf16[2,256,256]{2,1,0:T(8,128)(2,1)S(1)}, bf16[2,256,256]{2,1,0:T(8,128)(2,1)}, u32[]{:S(2)}) copy-start(bf16[2,256,256]{2,1,0:T(8,128)(2,1)} %shocks_ref) | copy-start | bytes 786436
  0.7 7.0 %copy-start.2 = (bf16[2,256,256]{2,1,0:T(8,128)(2,1)S(1)}, bf16[2,256,256]{2,1,0:T(8,128)(2,1)}, u32[]{:S(2)}) copy-start(bf16[2,256,256]{2,1,0:T(8,128)(2,1)} %noise_ref.1) | copy-start | bytes 786436
  0.7 7.0 %copy-start.8 = (f32[256]{0:T(256)S(1)}, f32[256]{0:T(256)}, u32[]{:S(2)}) copy-start(f32[256]{0:T(256)} %param.16) | copy-start | bytes 3076
  0.7 7.0 %copy-start.9 = (f32[256]{0:T(256)S(1)}, f32[256]{0:T(256)}, u32[]{:S(2)}) copy-start(f32[256]{0:T(256)} %param.17) | copy-start | bytes 3076
  0.7 6.9 %copy-start.3 = (bf16[256,256]{1,0:T(8,128)(2,1)S(1)}, bf16[256,256]{1,0:T(8,128)(2,1)}, u32[]{:S(2)}) copy-start(bf16[256,256]{1,0:T(8,128)(2,1)} %loadings_ref.1) | copy-start | bytes 393220
  2.0 9.8 %collective-permute-start.2 = (bf16[80,256]{1,0:T(8,128)(2,1)S(1)}, bf16[80,256]{1,0:T(8,128)(2,1)S(1)}, u32[]{:S(2)}, u32[]{:S(2)}) collective-permute-start(bf16[80,256]{1,0:T(8,128)(2,1)S(1)} %pack.1.refs_1_), channel_id=1, source_target_pairs={{0,4},{1,5},{2,6},{3,7},{4,0},{5,1},{6,2},{7,3},{8,12},{9,13},{10,... | collective-permute-start | bytes 122888 | tf_op jit(solution)/shard_map/ppermute | solution.py:161
  6.1 5.8 %collective-permute-start.1 = (bf16[80,256]{1,0:T(8,128)(2,1)S(1)}, bf16[80,256]{1,0:T(8,128)(2,1)S(1)}, u32[]{:S(2)}, u32[]{:S(2)}) collective-permute-start(bf16[80,256]{1,0:T(8,128)(2,1)S(1)} %pack.1.refs_1_), channel_id=1, source_target_pairs={{0,6},{1,7},{2,4},{3,5},{4,2},{5,3},{6,0},{7,1},{8,14},{9,15},{10,... | collective-permute-start | bytes 122888 | tf_op jit(solution)/shard_map/ppermute | solution.py:161
  7.4 4.5 %collective-permute-start = (bf16[80,256]{1,0:T(8,128)(2,1)S(1)}, bf16[80,256]{1,0:T(8,128)(2,1)S(1)}, u32[]{:S(2)}, u32[]{:S(2)}) collective-permute-start(bf16[80,256]{1,0:T(8,128)(2,1)S(1)} %pack.1.refs_1_), channel_id=1, source_target_pairs={{0,2},{1,3},{2,0},{3,1},{4,6},{5,7},{6,4},{7,5},{8,10},{9,11},{10,... | collective-permute-start | bytes 122888 | tf_op jit(solution)/shard_map/ppermute | solution.py:161
  7.6 0.7 %copy-start.7 = (f32[256]{0:T(256)S(1)}, f32[256]{0:T(256)}, u32[]{:S(2)}) copy-start(f32[256]{0:T(256)} %param.13) | copy-start | bytes 3076
  8.3 3.6 %copy-start.10 = (s32[16]{0:T(128)S(1)}, s32[16]{0:T(128)}, u32[]{:S(2)}) copy-start(s32[16]{0:T(128)} %refs_0_.1) | copy-start | bytes 196
  8.8 12.8 %collective-permute-start.7 = (bf16[512,256]{1,0:T(8,128)(2,1)S(1)}, bf16[512,256]{1,0:T(8,128)(2,1)S(1)}, u32[]{:S(2)}, u32[]{:S(2)}) collective-permute-start(bf16[512,256]{1,0:T(8,128)(2,1)S(1)} %price.1.refs_2_), channel_id=1, source_target_pairs={{0,6},{1,7},{2,4},{3,5},{4,2},{5,3},{6,0},{7,1},{8,14},{9,15},{10,... | collective-permute-start | bytes 786440 | tf_op jit(solution)/shard_map/ppermute | solution.py:161
  12.8 4.9 %collective-permute-start.4 = (bf16[128,256]{1,0:T(8,128)(2,1)S(1)}, bf16[128,256]{1,0:T(8,128)(2,1)S(1)}, u32[]{:S(2)}, u32[]{:S(2)}) collective-permute-start(bf16[128,256]{1,0:T(8,128)(2,1)S(1)} %get-tuple-element.12), channel_id=1, source_target_pairs={{0,16},{8,24},{16,0},{24,8},{1,17},{9,25},{17,1},{25,9},{2,18},{10... | collective-permute-start | bytes 196616 | tf_op jit(solution)/shard_map/ppermute | solution.py:161
  14.4 5.2 %collective-permute-start.5 = (bf16[128,256]{1,0:T(8,128)(2,1)S(1)}, bf16[128,256]{1,0:T(8,128)(2,1)S(1)}, u32[]{:S(2)}, u32[]{:S(2)}) collective-permute-start(bf16[128,256]{1,0:T(8,128)(2,1)S(1)} %get-tuple-element.11), channel_id=1, source_target_pairs={{0,17},{1,16},{2,19},{3,18},{4,21},{5,20},{6,23},{7,22},{8,25},{9,... | collective-permute-start | bytes 196616 | tf_op jit(solution)/shard_map/ppermute | solution.py:171
  15.8 4.3 %collective-permute-start.3 = (bf16[128,256]{1,0:T(8,128)(2,1)S(1)}, bf16[128,256]{1,0:T(8,128)(2,1)S(1)}, u32[]{:S(2)}, u32[]{:S(2)}) collective-permute-start(bf16[128,256]{1,0:T(8,128)(2,1)S(1)} %get-tuple-element.11), channel_id=1, source_target_pairs={{0,1},{1,0},{2,3},{3,2},{4,5},{5,4},{6,7},{7,6},{8,9},{9,8},{10,11... | collective-permute-start | bytes 196616 | tf_op jit(solution)/shard_map/ppermute | solution.py:171
  20.2 1.4 %collective-permute-start.6 = (bf16[256,256]{1,0:T(8,128)(2,1)S(1)}, bf16[256,256]{1,0:T(8,128)(2,1)S(1)}, u32[]{:S(2)}, u32[]{:S(2)}) collective-permute-start(bf16[256,256]{1,0:T(8,128)(2,1)S(1)} %merge.1.refs_0_), channel_id=1, source_target_pairs={{0,8},{8,0},{16,24},{24,16},{1,9},{9,1},{17,25},{25,17},{2,10},{10... | collective-permute-start | bytes 393224 | tf_op jit(solution)/shard_map/ppermute | solution.py:161
  22.0 4.4 %collective-permute-start.8 = (bf16[64,512]{1,0:T(8,128)(2,1)S(1)}, bf16[64,512]{1,0:T(8,128)(2,1)S(1)}, u32[]{:S(2)}, u32[]{:S(2)}) collective-permute-start(bf16[64,512]{1,0:T(8,128)(2,1)S(1)} %get-tuple-element.15), channel_id=1, source_target_pairs={{0,2},{1,3},{2,0},{3,1},{4,6},{5,7},{6,4},{7,5},{8,10},{9,11},{10,... | collective-permute-start | bytes 196616 | tf_op jit(solution)/shard_map/ppermute | solution.py:161
  24.1 5.2 %collective-permute-start.9 = (bf16[64,512]{1,0:T(8,128)(2,1)S(1)}, bf16[64,512]{1,0:T(8,128)(2,1)S(1)}, u32[]{:S(2)}, u32[]{:S(2)}) collective-permute-start(bf16[64,512]{1,0:T(8,128)(2,1)S(1)} %get-tuple-element.16), channel_id=1, source_target_pairs={{0,3},{1,2},{2,1},{3,0},{4,7},{5,6},{6,5},{7,4},{8,11},{9,10},{10,... | collective-permute-start | bytes 196616 | tf_op jit(solution)/shard_map/ppermute | solution.py:161
  25.1 4.9 %collective-permute-start.10 = (bf16[64,512]{1,0:T(8,128)(2,1)S(1)}, bf16[64,512]{1,0:T(8,128)(2,1)S(1)}, u32[]{:S(2)}, u32[]{:S(2)}) collective-permute-start(bf16[64,512]{1,0:T(8,128)(2,1)S(1)} %get-tuple-element.17), channel_id=1, source_target_pairs={{0,1},{1,0},{2,3},{3,2},{4,5},{5,4},{6,7},{7,6},{8,9},{9,8},{10,11... | collective-permute-start | bytes 196616 | tf_op jit(solution)/shard_map/ppermute | solution.py:161
  30.1 3.1 %collective-permute-start.13 = (f32[2,64]{1,0:T(2,128)S(1)}, f32[2,64]{1,0:T(2,128)S(1)}, u32[]{:S(2)}, u32[]{:S(2)}) collective-permute-start(f32[2,64]{1,0:T(2,128)S(1)} %totals.1), channel_id=1, source_target_pairs={{0,24},{8,16},{16,8},{24,0},{1,25},{9,17},{17,9},{25,1},{2,26},{10... | collective-permute-start | bytes 1544 | tf_op jit(solution)/shard_map/ppermute | solution.py:161
  30.2 3.6 %collective-permute-start.12 = (f32[2,64]{1,0:T(2,128)S(1)}, f32[2,64]{1,0:T(2,128)S(1)}, u32[]{:S(2)}, u32[]{:S(2)}) collective-permute-start(f32[2,64]{1,0:T(2,128)S(1)} %totals.1), channel_id=1, source_target_pairs={{0,16},{8,24},{16,0},{24,8},{1,17},{9,25},{17,1},{25,9},{2,18},{10... | collective-permute-start | bytes 1544 | tf_op jit(solution)/shard_map/ppermute | solution.py:161
  31.8 2.1 %collective-permute-start.11 = (f32[2,64]{1,0:T(2,128)S(1)}, f32[2,64]{1,0:T(2,128)S(1)}, u32[]{:S(2)}, u32[]{:S(2)}) collective-permute-start(f32[2,64]{1,0:T(2,128)S(1)} %totals.1), channel_id=1, source_target_pairs={{0,8},{8,0},{16,24},{24,16},{1,9},{9,1},{17,25},{25,17},{2,10},{10... | collective-permute-start | bytes 1544 | tf_op jit(solution)/shard_map/ppermute | solution.py:161

commit v14 on v13

--- a/solution.py
+++ b/solution.py
@@ -118,9 +118,9 @@
             shares_ref[i * rows : (i + 1) * rows, at : at + pair] = (own + other).astype(jnp.bfloat16)
 
 
-def value_kernel(part, held, scen_count, *refs):
-    cores_refs, price_refs = refs[:2], refs[2:4]
-    out_refs, whole_ref = refs[4:-1], refs[-1]
+def own_value_kernel(part, held, scen_count, *refs):
+    cores_refs, price_ref = refs[:2], refs[2]
+    own_ref, later_ref, whole_ref = refs[3:]
     scen = lax.axis_index("scen")
     for i in range(scen_count):
         column = (scen ^ i) * part
@@ -129,13 +129,15 @@
             at = pl.ds(pl.multiple_of(b * BLOCK + column, part), part)
             whole_ref[at, :] = cores_refs[i % 2][row : row + part, :].astype(jnp.float32)
     width = held * BLOCK
-    total = None
-    for i, price_ref in enumerate(price_refs):
-        whole = whole_ref[i * width : (i + 1) * width, :].T.astype(jnp.bfloat16)
-        term = f32_dot(whole, price_ref[...], NT)
-        total = term if total is None else total + term
+    own_ref[...] = f32_dot(whole_ref[:width, :].T.astype(jnp.bfloat16), price_ref[...], NT)
+    later_ref[...] = whole_ref[width:, :].T.astype(jnp.bfloat16)
+
+
+def value_kernel(own_ref, later_ref, price_ref, *out_refs):
     for p, out_ref in enumerate(out_refs):
-        out_ref[...] = total[p * SET_DEV : (p + 1) * SET_DEV].astype(out_ref.dtype)
+        at = slice(p * SET_DEV, (p + 1) * SET_DEV)
+        total = own_ref[at, :] + f32_dot(later_ref[at, :], price_ref[...], NT)
+        out_ref[...] = total.astype(out_ref.dtype)
 
 
 def exposure_of(part_refs, date, rows):
@@ -210,7 +212,7 @@
         compiler_params=PARAMS,
         name="pack",
     )(pick, trade_weights, dependencies.T, netting[None])
-    order = column_flips[1:2] + column_flips[:1:-1]
+    order = column_flips[2:] + column_flips[1:2]
     packets = [packet] + [from_partner(packet, "fac", i) for i in order]
 
     packet, shocks = lax.optimization_barrier((packet, shocks))
@@ -256,20 +258,32 @@
     )(*parts)
     shares = [shares, from_partner(shares, "scen", 1)]
 
+    sets = share_shape[1]
+    own_value, later = pl.pallas_call(
+        functools.partial(own_value_kernel, part, held, scen_count),
+        out_shape=[
+            jax.ShapeDtypeStruct((sets, DATES * rows), jnp.float32),
+            jax.ShapeDtypeStruct((sets, width), jnp.bfloat16),
+        ],
+        in_specs=[VMEM] * 3,
+        out_specs=[VMEM] * 2,
+        scratch_shapes=[pltpu.VMEM((2 * width, sets), jnp.float32)],
+        compiler_params=PARAMS,
+        name="own_value",
+    )(*shares, pair_prices[0])
     parts = pl.pallas_call(
-        functools.partial(value_kernel, part, held, scen_count),
+        value_kernel,
         out_shape=[
             jax.ShapeDtypeStruct((SET_DEV, DATES * rows), jnp.bfloat16 if flip else jnp.float32)
             for flip in owner_flips
         ],
-        in_specs=[VMEM] * 4,
+        in_specs=[VMEM] * 3,
         out_specs=[VMEM] * len(owner_flips),
-        scratch_shapes=[pltpu.VMEM((2 * width, share_shape[1]), jnp.float32)],
         compiler_params=PARAMS,
         name="value",
-    )(*shares, *pair_prices)
+    )(own_value, later, pair_prices[1])
     sends = list(zip(parts[1:], owner_flips[1:]))
-    sends = sends[1:] + sends[:1]
+    sends = sends[2:] + sends[:2]
     parts = [parts[0]] + [from_partner(x, "fac", i) for x, i in sends]
 
     totals = pl.pallas_call(

time: 34.6 us -> 35.5 us (1.026)
  waiting for transfers between devices: 10.6 us -> 11.3 us
  Pallas kernels: 3.11 us -> 3.49 us
    ppermute x12, starting transfers between devices: 15.9 us -> 14.7 us  [from_partner(): return lax.ppermute(x, axis, [(i, i ^ flip) for i in range(count)])]
    ppermute x2, starting transfers between devices: 1.97 us -> 3.05 us  [from_both(): return lax.ppermute(x, ('scen', 'fac'), pairs)]
    ppermute x2, waiting for transfers between devices: 2.43 us -> 3.18 us  [from_both(): return lax.ppermute(x, ('scen', 'fac'), pairs)]
    pallas_call x1 -> x2, Pallas kernels: 0.4 us -> 0.77 us  [the longest x1 0.45 us: body(): pl.pallas_call(value_kernel, out_shape=[jax.ShapeDtypeStruct((SET_DEV, DA...]
  transfers between devices with their start and end apart: 14 -> 14, of which waited for: 10 -> 10; matrix products, arithmetic and copies ran while one was open for 0% -> 0% of each run, Pallas kernels for 6% -> 7%
where the time goes in v14:
time: 35.5 us; the launch traced here: 35.4 us
  starting transfers between devices  17.8 us (50%)
  waiting for transfers between devices  11.3 us (32%)
  Pallas kernels  3.49 us (10%)
  local copies, waits for them, and re-layouts  1.47 us (4%)
  between operations  0.8 us (2%)
  other arithmetic  0.57 us (2%)
    ppermute x12, starting transfers between devices, from_partner(): return lax.ppermute(x, axis, [(i, i ^ flip) for i in range(count)])  14.7 us
    ppermute x12, waiting for transfers between devices, from_partner(): return lax.ppermute(x, axis, [(i, i ^ flip) for i in range(count)])  8.1 us
    ppermute x2, waiting for transfers between devices, from_both(): return lax.ppermute(x, ('scen', 'fac'), pairs)  3.18 us
    ppermute x2, starting transfers between devices, from_both(): return lax.ppermute(x, ('scen', 'fac'), pairs)  3.05 us
    unnamed x22, local copies, waits for them, and re-layouts  1.47 us
    pallas_call x1, Pallas kernels, body(): pl.pallas_call(functools.partial(combine_kernel, part, held, owner_flips)...  0.9 us
  transfers between devices with their start and end apart: 14, of which 10 were waited for; matrix products, arithmetic and copies ran while one was open for 0% of the time, Pallas kernels for 7%

profile of v14, /device:TPU:0, one launch (start us, length us, event | category | flops | bytes accessed | tf_op | source)
XLA Modules:
  0.0 35.4 jit_solution(144998513340826854)
XLA Ops:
  0.7 0.8 %copy-done.4 = bf16[256,2,128]{2,1,0:T(2,128)(2,1)S(1)} copy-done((bf16[256,2,128]{2,1,0:T(2,128)(2,1)S(1)}, bf16[256,2,128]{2,1,0:T(2,128)(2,1)}, u32[]{:S(2)}) %copy-start.4) | copy-done | bytes 131096
  1.5 0.4 %pack.1.refs_1_ = bf16[80,256]{1,0:T(8,128)(2,1)S(1)} custom-call(bf16[32,128]{1,0:T(8,128)(2,1)S(1)} %pick.1.pick_ref, bf16[256,2,128]{2,1,0:T(2,128)(2,1)S(1)} %copy-done.4, s32[2,256]{1,0:T(2,128)S(1)} %bitcast.5, s32[1,256]{1,0:T(1,128)S(1)} %bitcast.6), custom_call_target="tpu_custom_call" | custom-call | tf_op jit(solution)/shard_map/pack/pallas_call | solution.py:207
  2.0 4.1 %collective-permute-start = (bf16[80,256]{1,0:T(8,128)(2,1)S(1)}, bf16[80,256]{1,0:T(8,128)(2,1)S(1)}, u32[]{:S(2)}, u32[]{:S(2)}) collective-permute-start(bf16[80,256]{1,0:T(8,128)(2,1)S(1)} %pack.1.refs_1_), channel_id=1, source_target_pairs={{0,4},{1,5},{2,6},{3,7},{4,0},{5,1},{6,2},{7,3},{8,12},{9,13},{10,... | collective-permute-start | bytes 122888 | tf_op jit(solution)/shard_map/ppermute | solution.py:163
  6.1 1.3 %collective-permute-start.1 = (bf16[80,256]{1,0:T(8,128)(2,1)S(1)}, bf16[80,256]{1,0:T(8,128)(2,1)S(1)}, u32[]{:S(2)}, u32[]{:S(2)}) collective-permute-start(bf16[80,256]{1,0:T(8,128)(2,1)S(1)} %pack.1.refs_1_), channel_id=1, source_target_pairs={{0,6},{1,7},{2,4},{3,5},{4,2},{5,3},{6,0},{7,1},{8,14},{9,15},{10,... | collective-permute-start | bytes 122888 | tf_op jit(solution)/shard_map/ppermute | solution.py:163
  7.4 0.2 collective-permute-start.2
  7.7 0.6 %copy-done.7 = f32[256]{0:T(256)S(1)} copy-done((f32[256]{0:T(256)S(1)}, f32[256]{0:T(256)}, u32[]{:S(2)}) %copy-start.7) | copy-done | bytes 1048
  8.3 0.5 %price.1.refs_2_ = bf16[512,256]{1,0:T(8,128)(2,1)S(1)} custom-call(bf16[2,256,256]{2,1,0:T(8,128)(2,1)S(1)} %copy-done.1, bf16[256,256]{1,0:T(8,128)(2,1)S(1)} %copy-done.3, f32[1,256]{1,0:T(1,128)S(1)} %bitcast.7, s32[2,256,256]{2,1,0:T(8,128)S(1)} %copy-done, bf16[2,256,256]{2,1,0:T(8,128)(2,1)S(1)} %copy-done.2, f32[1,256]{1,0:T(1,128)S(1)} %bitcast.8, ...), custom_call_target="tpu_custom_call" | custom-call | tf_op jit(solution)/shard_map/price/pallas_call | solution.py:219
  8.8 3.0 %collective-permute-start.7 = (bf16[512,256]{1,0:T(8,128)(2,1)S(1)}, bf16[512,256]{1,0:T(8,128)(2,1)S(1)}, u32[]{:S(2)}, u32[]{:S(2)}) collective-permute-start(bf16[512,256]{1,0:T(8,128)(2,1)S(1)} %price.1.refs_2_), channel_id=1, source_target_pairs={{0,6},{1,7},{2,4},{3,5},{4,2},{5,3},{6,0},{7,1},{8,14},{9,15},{10,... | collective-permute-start | bytes 786440 | tf_op jit(solution)/shard_map/ppermute | solution.py:163
  11.9 0.9 %combine.1 = (f32[128,256]{1,0:T(8,128)S(1)}, bf16[128,256]{1,0:T(8,128)(2,1)S(1)}, bf16[128,256]{1,0:T(8,128)(2,1)S(1)}) custom-call(s32[16]{0:T(128)S(1)} %copy-done.10, bf16[80,256]{1,0:T(8,128)(2,1)S(1)} %pack.1.refs_1_, bf16[80,256]{1,0:T(8,128)(2,1)S(1)} %collective-permute-done.refs_2_, bf16[80,256]{1,0:T(8,128)(2,1)S(1)} %collective-permute-done.1.refs_3_, ...), custom_call_target="tpu_custom_call" | custom-call | flops 1000000000 | tf_op jit(solution)/shard_map/combine/pallas_call | solution.py:229
  12.8 1.6 %collective-permute-start.3 = (bf16[128,256]{1,0:T(8,128)(2,1)S(1)}, bf16[128,256]{1,0:T(8,128)(2,1)S(1)}, u32[]{:S(2)}, u32[]{:S(2)}) collective-permute-start(bf16[128,256]{1,0:T(8,128)(2,1)S(1)} %get-tuple-element.13), channel_id=1, source_target_pairs={{0,1},{1,0},{2,3},{3,2},{4,5},{5,4},{6,7},{7,6},{8,9},{9,8},{10,11... | collective-permute-start | bytes 196616 | tf_op jit(solution)/shard_map/ppermute | solution.py:173
  14.3 1.5 %collective-permute-start.5 = (bf16[128,256]{1,0:T(8,128)(2,1)S(1)}, bf16[128,256]{1,0:T(8,128)(2,1)S(1)}, u32[]{:S(2)}, u32[]{:S(2)}) collective-permute-start(bf16[128,256]{1,0:T(8,128)(2,1)S(1)} %get-tuple-element.13), channel_id=1, source_target_pairs={{0,17},{1,16},{2,19},{3,18},{4,21},{5,20},{6,23},{7,22},{8,25},{9,... | collective-permute-start | bytes 196616 | tf_op jit(solution)/shard_map/ppermute | solution.py:173
  15.8 0.5 %collective-permute-start.4 = (bf16[128,256]{1,0:T(8,128)(2,1)S(1)}, bf16[128,256]{1,0:T(8,128)(2,1)S(1)}, u32[]{:S(2)}, u32[]{:S(2)}) collective-permute-start(bf16[128,256]{1,0:T(8,128)(2,1)S(1)} %get-tuple-element.14), channel_id=1, source_target_pairs={{0,16},{8,24},{16,0},{24,8},{1,17},{9,25},{17,1},{25,9},{2,18},{10... | collective-permute-start | bytes 196616 | tf_op jit(solution)/shard_map/ppermute | solution.py:163
  16.3 1.3 %collective-permute-done.3.refs_1_ = bf16[128,256]{1,0:T(8,128)(2,1)S(1)} collective-permute-done((bf16[128,256]{1,0:T(8,128)(2,1)S(1)}, bf16[128,256]{1,0:T(8,128)(2,1)S(1)}, u32[]{:S(2)}, u32[]{:S(2)}) %collective-permute-start.3) | collective-permute-done | bytes 65568 | tf_op jit(solution)/shard_map/ppermute | solution.py:173
  17.7 1.8 %collective-permute-done.5.refs_3_ = bf16[128,256]{1,0:T(8,128)(2,1)S(1)} collective-permute-done((bf16[128,256]{1,0:T(8,128)(2,1)S(1)}, bf16[128,256]{1,0:T(8,128)(2,1)S(1)}, u32[]{:S(2)}, u32[]{:S(2)}) %collective-permute-start.5) | collective-permute-done | bytes 65568 | tf_op jit(solution)/shard_map/ppermute | solution.py:173
  19.5 0.7 %collective-permute-done.4.refs_2_ = bf16[128,256]{1,0:T(8,128)(2,1)S(1)} collective-permute-done((bf16[128,256]{1,0:T(8,128)(2,1)S(1)}, bf16[128,256]{1,0:T(8,128)(2,1)S(1)}, u32[]{:S(2)}, u32[]{:S(2)}) %collective-permute-start.4) | collective-permute-done | bytes 65568 | tf_op jit(solution)/shard_map/ppermute | solution.py:163
  20.2 0.1 merge.1.refs_0_
  20.4 1.3 %collective-permute-done.6.refs_1_ = bf16[256,256]{1,0:T(8,128)(2,1)S(1)} collective-permute-done((bf16[256,256]{1,0:T(8,128)(2,1)S(1)}, bf16[256,256]{1,0:T(8,128)(2,1)S(1)}, u32[]{:S(2)}, u32[]{:S(2)}) %collective-permute-start.6) | collective-permute-done | bytes 131104 | tf_op jit(solution)/shard_map/ppermute | solution.py:163
  21.7 0.3 own_value.1
  22.1 0.4 %value.1 = (f32[64,512]{1,0:T(8,128)S(1)}, bf16[64,512]{1,0:T(8,128)(2,1)S(1)}, bf16[64,512]{1,0:T(8,128)(2,1)S(1)}, bf16[64,512]{1,0:T(8,128)(2,1)S(1)}) custom-call(f32[256,512]{1,0:T(8,128)S(1)} %get-tuple-element.16.own_ref, bf16[256,256]{1,0:T(8,128)(2,1)S(1)} %get-tuple-element.17.later_ref, bf16[512,256]{1,0:T(8,128)(2,1)S(1)} %collective-permute-done.7.price_ref), custom_call_target="tpu_custom_call" | custom-call | tf_op jit(solution)/shard_map/value/pallas_call | solution.py:274
  22.5 1.7 %collective-permute-start.10 = (bf16[64,512]{1,0:T(8,128)(2,1)S(1)}, bf16[64,512]{1,0:T(8,128)(2,1)S(1)}, u32[]{:S(2)}, u32[]{:S(2)}) collective-permute-start(bf16[64,512]{1,0:T(8,128)(2,1)S(1)} %get-tuple-element.21), channel_id=1, source_target_pairs={{0,2},{1,3},{2,0},{3,1},{4,6},{5,7},{6,4},{7,5},{8,10},{9,11},{10,... | collective-permute-start | bytes 196616 | tf_op jit(solution)/shard_map/ppermute | solution.py:163
  24.2 1.2 %collective-permute-start.8 = (bf16[64,512]{1,0:T(8,128)(2,1)S(1)}, bf16[64,512]{1,0:T(8,128)(2,1)S(1)}, u32[]{:S(2)}, u32[]{:S(2)}) collective-permute-start(bf16[64,512]{1,0:T(8,128)(2,1)S(1)} %get-tuple-element.19), channel_id=1, source_target_pairs={{0,3},{1,2},{2,1},{3,0},{4,7},{5,6},{6,5},{7,4},{8,11},{9,10},{10,... | collective-permute-start | bytes 196616 | tf_op jit(solution)/shard_map/ppermute | solution.py:163
  25.4 0.6 %collective-permute-start.9 = (bf16[64,512]{1,0:T(8,128)(2,1)S(1)}, bf16[64,512]{1,0:T(8,128)(2,1)S(1)}, u32[]{:S(2)}, u32[]{:S(2)}) collective-permute-start(bf16[64,512]{1,0:T(8,128)(2,1)S(1)} %get-tuple-element.20), channel_id=1, source_target_pairs={{0,1},{1,0},{2,3},{3,2},{4,5},{5,4},{6,7},{7,6},{8,9},{9,8},{10,11... | collective-permute-start | bytes 196616 | tf_op jit(solution)/shard_map/ppermute | solution.py:163
  26.1 1.0 %collective-permute-done.10.refs_3_ = bf16[64,512]{1,0:T(8,128)(2,1)S(1)} collective-permute-done((bf16[64,512]{1,0:T(8,128)(2,1)S(1)}, bf16[64,512]{1,0:T(8,128)(2,1)S(1)}, u32[]{:S(2)}, u32[]{:S(2)}) %collective-permute-start.10) | collective-permute-done | bytes 65568 | tf_op jit(solution)/shard_map/ppermute | solution.py:163
  27.1 2.3 %collective-permute-done.8.refs_1_ = bf16[64,512]{1,0:T(8,128)(2,1)S(1)} collective-permute-done((bf16[64,512]{1,0:T(8,128)(2,1)S(1)}, bf16[64,512]{1,0:T(8,128)(2,1)S(1)}, u32[]{:S(2)}, u32[]{:S(2)}) %collective-permute-start.8) | collective-permute-done | bytes 65568 | tf_op jit(solution)/shard_map/ppermute | solution.py:163
  29.4 0.7 %collective-permute-done.9.refs_2_ = bf16[64,512]{1,0:T(8,128)(2,1)S(1)} collective-permute-done((bf16[64,512]{1,0:T(8,128)(2,1)S(1)}, bf16[64,512]{1,0:T(8,128)(2,1)S(1)}, u32[]{:S(2)}, u32[]{:S(2)}) %collective-permute-start.9) | collective-permute-done | bytes 65568 | tf_op jit(solution)/shard_map/ppermute | solution.py:163
  30.0 0.1 totals.1
  30.2 1.6 %collective-permute-start.12 = (f32[2,64]{1,0:T(2,128)S(1)}, f32[2,64]{1,0:T(2,128)S(1)}, u32[]{:S(2)}, u32[]{:S(2)}) collective-permute-start(f32[2,64]{1,0:T(2,128)S(1)} %totals.1), channel_id=1, source_target_pairs={{0,16},{8,24},{16,0},{24,8},{1,17},{9,25},{17,1},{25,9},{2,18},{10... | collective-permute-start | bytes 1544 | tf_op jit(solution)/shard_map/ppermute | solution.py:163
  31.8 0.3 collective-permute-start.13
  32.1 0.7 %expose.1 = f32[2,64,256]{2,1,0:T(8,128)} custom-call(f32[64,512]{1,0:T(8,128)S(1)} %get-tuple-element.18.refs_0_, bf16[64,512]{1,0:T(8,128)(2,1)S(1)} %collective-permute-done.8.refs_1_, bf16[64,512]{1,0:T(8,128)(2,1)S(1)} %collective-permute-done.9.refs_2_, bf16[64,512]{1,0:T(8,128)(2,1)S(1)} %collective-permute-done.10.refs_3_), custom_call_target="tpu_custom_call" | custom-call | tf_op jit(solution)/shard_map/expose/pallas_call | solution.py:297
  32.8 1.1 %collective-permute-done.12 = f32[2,64]{1,0:T(2,128)S(1)} collective-permute-done((f32[2,64]{1,0:T(2,128)S(1)}, f32[2,64]{1,0:T(2,128)S(1)}, u32[]{:S(2)}, u32[]{:S(2)}) %collective-permute-start.12) | collective-permute-done | bytes 544 | tf_op jit(solution)/shard_map/ppermute | solution.py:163
  33.9 0.9 %collective-permute-done.13 = f32[2,64]{1,0:T(2,128)S(1)} collective-permute-done((f32[2,64]{1,0:T(2,128)S(1)}, f32[2,64]{1,0:T(2,128)S(1)}, u32[]{:S(2)}, u32[]{:S(2)}) %collective-permute-start.13) | collective-permute-done | bytes 544 | tf_op jit(solution)/shard_map/ppermute | solution.py:163
  34.8 0.6 %add_multiply_fusion = f32[2,64]{1,0:T(2,128)} fusion(f32[2,64]{1,0:T(2,128)S(1)} %collective-permute-done.12, f32[2,64]{1,0:T(2,128)S(1)} %collective-permute-done.13, f32[2,64]{1,0:T(2,128)S(1)} %totals.1, f32[2,64]{1,0:T(2,128)S(1)} %collective-permute-done.11), kind=kLoop, calls=%fused_computation | loop fusion | flops 512 | bytes 2560 | tf_op jit(solution)/shard_map/div | solution.py:310
  (28 shorter events, 0.3 us)
Async XLA Ops:
  0.6 0.9 %copy-start.4 = (bf16[256,2,128]{2,1,0:T(2,128)(2,1)S(1)}, bf16[256,2,128]{2,1,0:T(2,128)(2,1)}, u32[]{:S(2)}) copy-start(bf16[256,2,128]{2,1,0:T(2,128)(2,1)} %weights_ref.1) | copy-start | bytes 393220
  0.6 0.9 %copy-start.5 = (s32[256,2]{0,1:T(2,128)S(1)}, s32[256,2]{0,1:T(2,128)}, u32[]{:S(2)}) copy-start(s32[256,2]{0,1:T(2,128)} %param.18) | copy-start | bytes 6148
  0.7 0.9 %copy-start.6 = (s32[256]{0:T(256)S(1)}, s32[256]{0:T(256)}, u32[]{:S(2)}) copy-start(s32[256]{0:T(256)} %param.21) | copy-start | bytes 3076
  0.7 7.0 %copy-start = (s32[2,256,256]{2,1,0:T(8,128)S(1)}, s32[2,256,256]{2,1,0:T(8,128)}, u32[]{:S(2)}) copy-start(s32[2,256,256]{2,1,0:T(8,128)} %counts_ref.1) | copy-start | bytes 1572868
  0.7 7.0 %copy-start.1 = (bf16[2,256,256]{2,1,0:T(8,128)(2,1)S(1)}, bf16[2,256,256]{2,1,0:T(8,128)(2,1)}, u32[]{:S(2)}) copy-start(bf16[2,256,256]{2,1,0:T(8,128)(2,1)} %shocks_ref) | copy-start | bytes 786436
  0.7 7.0 %copy-start.2 = (bf16[2,256,256]{2,1,0:T(8,128)(2,1)S(1)}, bf16[2,256,256]{2,1,0:T(8,128)(2,1)}, u32[]{:S(2)}) copy-start(bf16[2,256,256]{2,1,0:T(8,128)(2,1)} %noise_ref.1) | copy-start | bytes 786436
  0.7 7.0 %copy-start.8 = (f32[256]{0:T(256)S(1)}, f32[256]{0:T(256)}, u32[]{:S(2)}) copy-start(f32[256]{0:T(256)} %param.16) | copy-start | bytes 3076
  0.7 7.0 %copy-start.9 = (f32[256]{0:T(256)S(1)}, f32[256]{0:T(256)}, u32[]{:S(2)}) copy-start(f32[256]{0:T(256)} %param.17) | copy-start | bytes 3076
  0.7 6.9 %copy-start.3 = (bf16[256,256]{1,0:T(8,128)(2,1)S(1)}, bf16[256,256]{1,0:T(8,128)(2,1)}, u32[]{:S(2)}) copy-start(bf16[256,256]{1,0:T(8,128)(2,1)} %loadings_ref.1) | copy-start | bytes 393220
  2.0 9.8 %collective-permute-start = (bf16[80,256]{1,0:T(8,128)(2,1)S(1)}, bf16[80,256]{1,0:T(8,128)(2,1)S(1)}, u32[]{:S(2)}, u32[]{:S(2)}) collective-permute-start(bf16[80,256]{1,0:T(8,128)(2,1)S(1)} %pack.1.refs_1_), channel_id=1, source_target_pairs={{0,4},{1,5},{2,6},{3,7},{4,0},{5,1},{6,2},{7,3},{8,12},{9,13},{10,... | collective-permute-start | bytes 122888 | tf_op jit(solution)/shard_map/ppermute | solution.py:163
  6.1 5.8 %collective-permute-start.1 = (bf16[80,256]{1,0:T(8,128)(2,1)S(1)}, bf16[80,256]{1,0:T(8,128)(2,1)S(1)}, u32[]{:S(2)}, u32[]{:S(2)}) collective-permute-start(bf16[80,256]{1,0:T(8,128)(2,1)S(1)} %pack.1.refs_1_), channel_id=1, source_target_pairs={{0,6},{1,7},{2,4},{3,5},{4,2},{5,3},{6,0},{7,1},{8,14},{9,15},{10,... | collective-permute-start | bytes 122888 | tf_op jit(solution)/shard_map/ppermute | solution.py:163
  7.4 4.5 %collective-permute-start.2 = (bf16[80,256]{1,0:T(8,128)(2,1)S(1)}, bf16[80,256]{1,0:T(8,128)(2,1)S(1)}, u32[]{:S(2)}, u32[]{:S(2)}) collective-permute-start(bf16[80,256]{1,0:T(8,128)(2,1)S(1)} %pack.1.refs_1_), channel_id=1, source_target_pairs={{0,2},{1,3},{2,0},{3,1},{4,6},{5,7},{6,4},{7,5},{8,10},{9,11},{10,... | collective-permute-start | bytes 122888 | tf_op jit(solution)/shard_map/ppermute | solution.py:163
  7.6 0.7 %copy-start.7 = (f32[256]{0:T(256)S(1)}, f32[256]{0:T(256)}, u32[]{:S(2)}) copy-start(f32[256]{0:T(256)} %param.13) | copy-start | bytes 3076
  8.3 3.6 %copy-start.10 = (s32[16]{0:T(128)S(1)}, s32[16]{0:T(128)}, u32[]{:S(2)}) copy-start(s32[16]{0:T(128)} %refs_0_.1) | copy-start | bytes 196
  8.8 13.3 %collective-permute-start.7 = (bf16[512,256]{1,0:T(8,128)(2,1)S(1)}, bf16[512,256]{1,0:T(8,128)(2,1)S(1)}, u32[]{:S(2)}, u32[]{:S(2)}) collective-permute-start(bf16[512,256]{1,0:T(8,128)(2,1)S(1)} %price.1.refs_2_), channel_id=1, source_target_pairs={{0,6},{1,7},{2,4},{3,5},{4,2},{5,3},{6,0},{7,1},{8,14},{9,15},{10,... | collective-permute-start | bytes 786440 | tf_op jit(solution)/shard_map/ppermute | solution.py:163
  12.8 4.9 %collective-permute-start.3 = (bf16[128,256]{1,0:T(8,128)(2,1)S(1)}, bf16[128,256]{1,0:T(8,128)(2,1)S(1)}, u32[]{:S(2)}, u32[]{:S(2)}) collective-permute-start(bf16[128,256]{1,0:T(8,128)(2,1)S(1)} %get-tuple-element.13), channel_id=1, source_target_pairs={{0,1},{1,0},{2,3},{3,2},{4,5},{5,4},{6,7},{7,6},{8,9},{9,8},{10,11... | collective-permute-start | bytes 196616 | tf_op jit(solution)/shard_map/ppermute | solution.py:173
  14.3 5.2 %collective-permute-start.5 = (bf16[128,256]{1,0:T(8,128)(2,1)S(1)}, bf16[128,256]{1,0:T(8,128)(2,1)S(1)}, u32[]{:S(2)}, u32[]{:S(2)}) collective-permute-start(bf16[128,256]{1,0:T(8,128)(2,1)S(1)} %get-tuple-element.13), channel_id=1, source_target_pairs={{0,17},{1,16},{2,19},{3,18},{4,21},{5,20},{6,23},{7,22},{8,25},{9,... | collective-permute-start | bytes 196616 | tf_op jit(solution)/shard_map/ppermute | solution.py:173
  15.8 4.4 %collective-permute-start.4 = (bf16[128,256]{1,0:T(8,128)(2,1)S(1)}, bf16[128,256]{1,0:T(8,128)(2,1)S(1)}, u32[]{:S(2)}, u32[]{:S(2)}) collective-permute-start(bf16[128,256]{1,0:T(8,128)(2,1)S(1)} %get-tuple-element.14), channel_id=1, source_target_pairs={{0,16},{8,24},{16,0},{24,8},{1,17},{9,25},{17,1},{25,9},{2,18},{10... | collective-permute-start | bytes 196616 | tf_op jit(solution)/shard_map/ppermute | solution.py:163
  20.3 1.4 %collective-permute-start.6 = (bf16[256,256]{1,0:T(8,128)(2,1)S(1)}, bf16[256,256]{1,0:T(8,128)(2,1)S(1)}, u32[]{:S(2)}, u32[]{:S(2)}) collective-permute-start(bf16[256,256]{1,0:T(8,128)(2,1)S(1)} %merge.1.refs_0_), channel_id=1, source_target_pairs={{0,8},{8,0},{16,24},{24,16},{1,9},{9,1},{17,25},{25,17},{2,10},{10... | collective-permute-start | bytes 393224 | tf_op jit(solution)/shard_map/ppermute | solution.py:163
  22.5 4.6 %collective-permute-start.10 = (bf16[64,512]{1,0:T(8,128)(2,1)S(1)}, bf16[64,512]{1,0:T(8,128)(2,1)S(1)}, u32[]{:S(2)}, u32[]{:S(2)}) collective-permute-start(bf16[64,512]{1,0:T(8,128)(2,1)S(1)} %get-tuple-element.21), channel_id=1, source_target_pairs={{0,2},{1,3},{2,0},{3,1},{4,6},{5,7},{6,4},{7,5},{8,10},{9,11},{10,... | collective-permute-start | bytes 196616 | tf_op jit(solution)/shard_map/ppermute | solution.py:163
  24.2 5.2 %collective-permute-start.8 = (bf16[64,512]{1,0:T(8,128)(2,1)S(1)}, bf16[64,512]{1,0:T(8,128)(2,1)S(1)}, u32[]{:S(2)}, u32[]{:S(2)}) collective-permute-start(bf16[64,512]{1,0:T(8,128)(2,1)S(1)} %get-tuple-element.19), channel_id=1, source_target_pairs={{0,3},{1,2},{2,1},{3,0},{4,7},{5,6},{6,5},{7,4},{8,11},{9,10},{10,... | collective-permute-start | bytes 196616 | tf_op jit(solution)/shard_map/ppermute | solution.py:163
  25.4 4.6 %collective-permute-start.9 = (bf16[64,512]{1,0:T(8,128)(2,1)S(1)}, bf16[64,512]{1,0:T(8,128)(2,1)S(1)}, u32[]{:S(2)}, u32[]{:S(2)}) collective-permute-start(bf16[64,512]{1,0:T(8,128)(2,1)S(1)} %get-tuple-element.20), channel_id=1, source_target_pairs={{0,1},{1,0},{2,3},{3,2},{4,5},{5,4},{6,7},{7,6},{8,9},{9,8},{10,11... | collective-permute-start | bytes 196616 | tf_op jit(solution)/shard_map/ppermute | solution.py:163
  30.2 2.6 %collective-permute-start.11 = (f32[2,64]{1,0:T(2,128)S(1)}, f32[2,64]{1,0:T(2,128)S(1)}, u32[]{:S(2)}, u32[]{:S(2)}) collective-permute-start(f32[2,64]{1,0:T(2,128)S(1)} %totals.1), channel_id=1, source_target_pairs={{0,8},{8,0},{16,24},{24,16},{1,9},{9,1},{17,25},{25,17},{2,10},{10... | collective-permute-start | bytes 1544 | tf_op jit(solution)/shard_map/ppermute | solution.py:163
  30.2 3.6 %collective-permute-start.12 = (f32[2,64]{1,0:T(2,128)S(1)}, f32[2,64]{1,0:T(2,128)S(1)}, u32[]{:S(2)}, u32[]{:S(2)}) collective-permute-start(f32[2,64]{1,0:T(2,128)S(1)} %totals.1), channel_id=1, source_target_pairs={{0,16},{8,24},{16,0},{24,8},{1,17},{9,25},{17,1},{25,9},{2,18},{10... | collective-permute-start | bytes 1544 | tf_op jit(solution)/shard_map/ppermute | solution.py:163
  31.8 3.0 %collective-permute-start.13 = (f32[2,64]{1,0:T(2,128)S(1)}, f32[2,64]{1,0:T(2,128)S(1)}, u32[]{:S(2)}, u32[]{:S(2)}) collective-permute-start(f32[2,64]{1,0:T(2,128)S(1)} %totals.1), channel_id=1, source_target_pairs={{0,24},{8,16},{16,8},{24,0},{1,25},{9,17},{17,9},{25,1},{2,26},{10... | collective-permute-start | bytes 1544 | tf_op jit(solution)/shard_map/ppermute | solution.py:163

commit v15 on v13

--- a/solution.py
+++ b/solution.py
@@ -34,7 +34,9 @@
     pick_ref[...] = pick.astype(jnp.float32).astype(jnp.bfloat16)
 
 
-def pack_kernel(part, pick_ref, weights_ref, deps_ref, netting_ref, packet_ref):
+def pack_kernel(part, *refs):
+    pick_ref, weights_ref, deps_ref, netting_ref = refs[:4]
+    factor_refs, packet_ref, factors_ref = refs[4:-2], refs[-2], refs[-1]
     for k in range(2):
         share = f32_dot(pick_ref[...], weights_ref[:, k, :], NT)
         packet_ref[k * part : (k + 1) * part, :] = share[:part].astype(jnp.bfloat16)
@@ -49,14 +51,16 @@
         axis=0,
     )
     packet_ref[2 * part :, :] = tags.astype(jnp.float32).astype(jnp.bfloat16)
-
-
-def price_kernel(shocks_ref, loadings_ref, vol_ref, counts_ref, noise_ref, mean_ref, dev_ref, out_ref):
+    for i, ref in enumerate(factor_refs):
+        factors_ref[i : i + 1, :] = ref[...]
+
+
+def price_kernel(shocks_ref, loadings_ref, counts_ref, noise_ref, factors_ref, out_ref):
     rows = shocks_ref.shape[1]
-    vol = vol_ref[...]
+    vol = factors_ref[0:1, :]
     drift = 0.5 * vol * vol
-    mean = mean_ref[...]
-    dev = dev_ref[...]
+    mean = factors_ref[1:2, :]
+    dev = factors_ref[2:3, :]
     loadings = loadings_ref[...]
     for i in range(0, rows, CHUNK):
         at = slice(i, i + CHUNK)
@@ -202,14 +206,25 @@
         cost_estimate=pl.CostEstimate(flops=10**10, bytes_accessed=0, transcendentals=0),
         name="pick",
     )()
-    packet = pl.pallas_call(
+    packet, factors = pl.pallas_call(
         functools.partial(pack_kernel, part),
-        out_shape=jax.ShapeDtypeStruct((2 * part + TAGS, trades), jnp.bfloat16),
-        in_specs=[VMEM] * 4,
-        out_specs=VMEM,
+        out_shape=[
+            jax.ShapeDtypeStruct((2 * part + TAGS, trades), jnp.bfloat16),
+            jax.ShapeDtypeStruct((3, width), jnp.float32),
+        ],
+        in_specs=[VMEM] * 7,
+        out_specs=[VMEM] * 2,
         compiler_params=PARAMS,
         name="pack",
-    )(pick, trade_weights, dependencies.T, netting[None])
+    )(
+        pick,
+        trade_weights,
+        dependencies.T,
+        netting[None],
+        vol[None],
+        jump_mean[None],
+        jump_vol[None],
+    )
     order = column_flips[1:2] + column_flips[:1:-1]
     packets = [packet] + [from_partner(packet, "fac", i) for i in order]
 
@@ -217,11 +232,11 @@
     prices = pl.pallas_call(
         price_kernel,
         out_shape=jax.ShapeDtypeStruct((DATES * rows, width), jnp.bfloat16),
-        in_specs=[VMEM] * 7,
+        in_specs=[VMEM] * 5,
         out_specs=VMEM,
         compiler_params=PARAMS,
         name="price",
-    )(shocks, loadings, vol[None], jump_counts, jump_noise, jump_mean[None], jump_vol[None])
+    )(shocks, loadings, jump_counts, jump_noise, factors)
     share_shape = (2 * held * part, len(owner_flips) * SET_DEV)
     column_trades = len(column_flips) * trades
     own, narrow, other = pl.pallas_call(

time: 34.6 us -> 34.2 us (0.988)
  local copies, waits for them, and re-layouts: 1.47 us -> 0.83 us
  waiting for transfers between devices: 10.6 us -> 11 us
    unnamed x22, local copies, waits for them, and re-layouts: 1.47 us -> 0.83 us
    ppermute x2, waiting for transfers between devices: 2.43 us -> 2.78 us  [from_both(): return lax.ppermute(x, ('scen', 'fac'), pairs)]
where the time goes in v15:
time: 34.2 us; the launch traced here: 34.1 us
  starting transfers between devices  17.8 us (52%)
  waiting for transfers between devices  11 us (32%)
  Pallas kernels  3.12 us (9%)
  local copies, waits for them, and re-layouts  0.83 us (2%)
  between operations  0.8 us (2%)
  other arithmetic  0.57 us (2%)
    ppermute x12, starting transfers between devices, from_partner(): return lax.ppermute(x, axis, [(i, i ^ flip) for i in range(count)])  15.8 us
    ppermute x12, waiting for transfers between devices, from_partner(): return lax.ppermute(x, axis, [(i, i ^ flip) for i in range(count)])  8.21 us
    ppermute x2, waiting for transfers between devices, from_both(): return lax.ppermute(x, ('scen', 'fac'), pairs)  2.78 us
    ppermute x2, starting transfers between devices, from_both(): return lax.ppermute(x, ('scen', 'fac'), pairs)  1.97 us
    pallas_call x1, Pallas kernels, body(): pl.pallas_call(functools.partial(combine_kernel, part, held, owner_flips)...  0.9 us
    unnamed x22, local copies, waits for them, and re-layouts  0.83 us
    pallas_call x1, Pallas kernels, body(): pl.pallas_call(functools.partial(expose_kernel, rows), out_shape=jax.Shap...  0.69 us
  transfers between devices with their start and end apart: 14, of which 10 were waited for; matrix products, arithmetic and copies ran while one was open for 0% of the time, Pallas kernels for 6%

profile of v15, /device:TPU:0, one launch (start us, length us, event | category | flops | bytes accessed | tf_op | source)
XLA Modules:
  0.0 34.1 jit_solution(15415999943252914324)
XLA Ops:
  0.8 0.8 %copy-done.3 = bf16[256,2,128]{2,1,0:T(2,128)(2,1)S(1)} copy-done((bf16[256,2,128]{2,1,0:T(2,128)(2,1)S(1)}, bf16[256,2,128]{2,1,0:T(2,128)(2,1)}, u32[]{:S(2)}) %copy-start.3) | copy-done | bytes 131096
  1.6 0.4 %pack.1 = (bf16[80,256]{1,0:T(8,128)(2,1)S(1)}, f32[3,256]{1,0:T(4,128)S(1)}) custom-call(bf16[32,128]{1,0:T(8,128)(2,1)S(1)} %pick.1.refs_0_, bf16[256,2,128]{2,1,0:T(2,128)(2,1)S(1)} %copy-done.3, s32[2,256]{1,0:T(2,128)S(1)} %bitcast.5, s32[1,256]{1,0:T(1,128)S(1)} %bitcast.6, f32[1,256]{1,0:T(1,128)S(1)} %bitcast.7, f32[1,256]{1,0:T(1,128)S(1)} %bitcast.8, ...), custom_call_target="tpu_custom_call" | custom-call | tf_op jit(solution)/shard_map/pack/pallas_call | solution.py:209
  2.0 4.1 %collective-permute-start.2 = (bf16[80,256]{1,0:T(8,128)(2,1)S(1)}, bf16[80,256]{1,0:T(8,128)(2,1)S(1)}, u32[]{:S(2)}, u32[]{:S(2)}) collective-permute-start(bf16[80,256]{1,0:T(8,128)(2,1)S(1)} %get-tuple-element.12.refs_1_), channel_id=1, source_target_pairs={{0,4},{1,5},{2,6},{3,7},{4,0},{5,1},{6,2},{7,3},{8,12},{9,13},{10,... | collective-permute-start | bytes 122888 | tf_op jit(solution)/shard_map/ppermute | solution.py:165
  6.1 1.3 %collective-permute-start.1 = (bf16[80,256]{1,0:T(8,128)(2,1)S(1)}, bf16[80,256]{1,0:T(8,128)(2,1)S(1)}, u32[]{:S(2)}, u32[]{:S(2)}) collective-permute-start(bf16[80,256]{1,0:T(8,128)(2,1)S(1)} %get-tuple-element.12.refs_1_), channel_id=1, source_target_pairs={{0,6},{1,7},{2,4},{3,5},{4,2},{5,3},{6,0},{7,1},{8,14},{9,15},{10,... | collective-permute-start | bytes 122888 | tf_op jit(solution)/shard_map/ppermute | solution.py:165
  7.4 0.2 collective-permute-start
  7.7 0.5 %price.1.refs_2_ = bf16[512,256]{1,0:T(8,128)(2,1)S(1)} custom-call(bf16[2,256,256]{2,1,0:T(8,128)(2,1)S(1)} %copy-done.1, bf16[256,256]{1,0:T(8,128)(2,1)S(1)} %copy-done.4, s32[2,256,256]{2,1,0:T(8,128)S(1)} %copy-done, bf16[2,256,256]{2,1,0:T(8,128)(2,1)S(1)} %copy-done.2, f32[3,256]{1,0:T(4,128)S(1)} %get-tuple-element.17.factors_ref), custom_call_target="tpu_custom_call" | custom-call | tf_op jit(solution)/shard_map/price/pallas_call | solution.py:232
  8.2 3.0 %collective-permute-start.7 = (bf16[512,256]{1,0:T(8,128)(2,1)S(1)}, bf16[512,256]{1,0:T(8,128)(2,1)S(1)}, u32[]{:S(2)}, u32[]{:S(2)}) collective-permute-start(bf16[512,256]{1,0:T(8,128)(2,1)S(1)} %price.1.refs_2_), channel_id=1, source_target_pairs={{0,6},{1,7},{2,4},{3,5},{4,2},{5,3},{6,0},{7,1},{8,14},{9,15},{10,... | collective-permute-start | bytes 786440 | tf_op jit(solution)/shard_map/ppermute | solution.py:165
  11.2 0.8 %collective-permute-done.1.refs_3_ = bf16[80,256]{1,0:T(8,128)(2,1)S(1)} collective-permute-done((bf16[80,256]{1,0:T(8,128)(2,1)S(1)}, bf16[80,256]{1,0:T(8,128)(2,1)S(1)}, u32[]{:S(2)}, u32[]{:S(2)}) %collective-permute-start.1) | collective-permute-done | bytes 40992 | tf_op jit(solution)/shard_map/ppermute | solution.py:165
  12.0 0.9 %combine.1 = (f32[128,256]{1,0:T(8,128)S(1)}, bf16[128,256]{1,0:T(8,128)(2,1)S(1)}, bf16[128,256]{1,0:T(8,128)(2,1)S(1)}) custom-call(s32[16]{0:T(128)S(1)} %copy-done.10, bf16[80,256]{1,0:T(8,128)(2,1)S(1)} %get-tuple-element.12.refs_1_, bf16[80,256]{1,0:T(8,128)(2,1)S(1)} %collective-permute-done.refs_2_, ...), custom_call_target="tpu_custom_call" | custom-call | flops 1000000000 | tf_op jit(solution)/shard_map/combine/pallas_call | solution.py:242
  12.9 1.6 %collective-permute-start.4 = (bf16[128,256]{1,0:T(8,128)(2,1)S(1)}, bf16[128,256]{1,0:T(8,128)(2,1)S(1)}, u32[]{:S(2)}, u32[]{:S(2)}) collective-permute-start(bf16[128,256]{1,0:T(8,128)(2,1)S(1)} %get-tuple-element.15), channel_id=1, source_target_pairs={{0,16},{8,24},{16,0},{24,8},{1,17},{9,25},{17,1},{25,9},{2,18},{10... | collective-permute-start | bytes 196616 | tf_op jit(solution)/shard_map/ppermute | solution.py:165
  14.5 1.4 %collective-permute-start.5 = (bf16[128,256]{1,0:T(8,128)(2,1)S(1)}, bf16[128,256]{1,0:T(8,128)(2,1)S(1)}, u32[]{:S(2)}, u32[]{:S(2)}) collective-permute-start(bf16[128,256]{1,0:T(8,128)(2,1)S(1)} %get-tuple-element.14), channel_id=1, source_target_pairs={{0,17},{1,16},{2,19},{3,18},{4,21},{5,20},{6,23},{7,22},{8,25},{9,... | collective-permute-start | bytes 196616 | tf_op jit(solution)/shard_map/ppermute | solution.py:175
  15.9 0.5 %collective-permute-start.3 = (bf16[128,256]{1,0:T(8,128)(2,1)S(1)}, bf16[128,256]{1,0:T(8,128)(2,1)S(1)}, u32[]{:S(2)}, u32[]{:S(2)}) collective-permute-start(bf16[128,256]{1,0:T(8,128)(2,1)S(1)} %get-tuple-element.14), channel_id=1, source_target_pairs={{0,1},{1,0},{2,3},{3,2},{4,5},{5,4},{6,7},{7,6},{8,9},{9,8},{10,11... | collective-permute-start | bytes 196616 | tf_op jit(solution)/shard_map/ppermute | solution.py:175
  16.5 0.9 %collective-permute-done.4.refs_2_ = bf16[128,256]{1,0:T(8,128)(2,1)S(1)} collective-permute-done((bf16[128,256]{1,0:T(8,128)(2,1)S(1)}, bf16[128,256]{1,0:T(8,128)(2,1)S(1)}, u32[]{:S(2)}, u32[]{:S(2)}) %collective-permute-start.4) | collective-permute-done | bytes 65568 | tf_op jit(solution)/shard_map/ppermute | solution.py:165
  17.4 2.2 %collective-permute-done.5.refs_3_ = bf16[128,256]{1,0:T(8,128)(2,1)S(1)} collective-permute-done((bf16[128,256]{1,0:T(8,128)(2,1)S(1)}, bf16[128,256]{1,0:T(8,128)(2,1)S(1)}, u32[]{:S(2)}, u32[]{:S(2)}) %collective-permute-start.5) | collective-permute-done | bytes 65568 | tf_op jit(solution)/shard_map/ppermute | solution.py:175
  19.6 0.5 %collective-permute-done.3.refs_1_ = bf16[128,256]{1,0:T(8,128)(2,1)S(1)} collective-permute-done((bf16[128,256]{1,0:T(8,128)(2,1)S(1)}, bf16[128,256]{1,0:T(8,128)(2,1)S(1)}, u32[]{:S(2)}, u32[]{:S(2)}) %collective-permute-start.3) | collective-permute-done | bytes 65568 | tf_op jit(solution)/shard_map/ppermute | solution.py:175
  20.2 0.1 merge.1.refs_0_
  20.3 0.1 collective-permute-start.6
  20.4 1.3 %collective-permute-done.6.refs_1_ = bf16[256,256]{1,0:T(8,128)(2,1)S(1)} collective-permute-done((bf16[256,256]{1,0:T(8,128)(2,1)S(1)}, bf16[256,256]{1,0:T(8,128)(2,1)S(1)}, u32[]{:S(2)}, u32[]{:S(2)}) %collective-permute-start.6) | collective-permute-done | bytes 131104 | tf_op jit(solution)/shard_map/ppermute | solution.py:165
  21.7 0.4 %value.1 = (f32[64,512]{1,0:T(8,128)S(1)}, bf16[64,512]{1,0:T(8,128)(2,1)S(1)}, bf16[64,512]{1,0:T(8,128)(2,1)S(1)}, bf16[64,512]{1,0:T(8,128)(2,1)S(1)}) custom-call(bf16[256,256]{1,0:T(8,128)(2,1)S(1)} %merge.1.refs_0_, bf16[256,256]{1,0:T(8,128)(2,1)S(1)} %collective-permute-done.6.refs_1_, bf16[512,256]{1,0:T(8,128)(2,1)S(1)} %price.1.refs_2_, ...), custom_call_target="tpu_custom_call" | custom-call | tf_op jit(solution)/shard_map/value/pallas_call | solution.py:274
  22.1 1.7 %collective-permute-start.8 = (bf16[64,512]{1,0:T(8,128)(2,1)S(1)}, bf16[64,512]{1,0:T(8,128)(2,1)S(1)}, u32[]{:S(2)}, u32[]{:S(2)}) collective-permute-start(bf16[64,512]{1,0:T(8,128)(2,1)S(1)} %get-tuple-element.19), channel_id=1, source_target_pairs={{0,2},{1,3},{2,0},{3,1},{4,6},{5,7},{6,4},{7,5},{8,10},{9,11},{10,... | collective-permute-start | bytes 196616 | tf_op jit(solution)/shard_map/ppermute | solution.py:165
  23.8 1.0 %collective-permute-start.9 = (bf16[64,512]{1,0:T(8,128)(2,1)S(1)}, bf16[64,512]{1,0:T(8,128)(2,1)S(1)}, u32[]{:S(2)}, u32[]{:S(2)}) collective-permute-start(bf16[64,512]{1,0:T(8,128)(2,1)S(1)} %get-tuple-element.20), channel_id=1, source_target_pairs={{0,3},{1,2},{2,1},{3,0},{4,7},{5,6},{6,5},{7,4},{8,11},{9,10},{10,... | collective-permute-start | bytes 196616 | tf_op jit(solution)/shard_map/ppermute | solution.py:165
  24.8 0.9 %collective-permute-start.10 = (bf16[64,512]{1,0:T(8,128)(2,1)S(1)}, bf16[64,512]{1,0:T(8,128)(2,1)S(1)}, u32[]{:S(2)}, u32[]{:S(2)}) collective-permute-start(bf16[64,512]{1,0:T(8,128)(2,1)S(1)} %get-tuple-element.21), channel_id=1, source_target_pairs={{0,1},{1,0},{2,3},{3,2},{4,5},{5,4},{6,7},{7,6},{8,9},{9,8},{10,11... | collective-permute-start | bytes 196616 | tf_op jit(solution)/shard_map/ppermute | solution.py:165
  25.7 1.0 %collective-permute-done.8.refs_1_ = bf16[64,512]{1,0:T(8,128)(2,1)S(1)} collective-permute-done((bf16[64,512]{1,0:T(8,128)(2,1)S(1)}, bf16[64,512]{1,0:T(8,128)(2,1)S(1)}, u32[]{:S(2)}, u32[]{:S(2)}) %collective-permute-start.8) | collective-permute-done | bytes 65568 | tf_op jit(solution)/shard_map/ppermute | solution.py:165
  26.7 2.4 %collective-permute-done.9.refs_2_ = bf16[64,512]{1,0:T(8,128)(2,1)S(1)} collective-permute-done((bf16[64,512]{1,0:T(8,128)(2,1)S(1)}, bf16[64,512]{1,0:T(8,128)(2,1)S(1)}, u32[]{:S(2)}, u32[]{:S(2)}) %collective-permute-start.9) | collective-permute-done | bytes 65568 | tf_op jit(solution)/shard_map/ppermute | solution.py:165
  29.0 0.6 %collective-permute-done.10.refs_3_ = bf16[64,512]{1,0:T(8,128)(2,1)S(1)} collective-permute-done((bf16[64,512]{1,0:T(8,128)(2,1)S(1)}, bf16[64,512]{1,0:T(8,128)(2,1)S(1)}, u32[]{:S(2)}, u32[]{:S(2)}) %collective-permute-start.10) | collective-permute-done | bytes 65568 | tf_op jit(solution)/shard_map/ppermute | solution.py:165
  29.7 0.1 totals.1
  29.9 1.6 %collective-permute-start.12 = (f32[2,64]{1,0:T(2,128)S(1)}, f32[2,64]{1,0:T(2,128)S(1)}, u32[]{:S(2)}, u32[]{:S(2)}) collective-permute-start(f32[2,64]{1,0:T(2,128)S(1)} %totals.1), channel_id=1, source_target_pairs={{0,16},{8,24},{16,0},{24,8},{1,17},{9,25},{17,1},{25,9},{2,18},{10... | collective-permute-start | bytes 1544 | tf_op jit(solution)/shard_map/ppermute | solution.py:165
  31.5 0.3 collective-permute-start.11
  31.7 0.7 %expose.1 = f32[2,64,256]{2,1,0:T(8,128)} custom-call(f32[64,512]{1,0:T(8,128)S(1)} %get-tuple-element.18.refs_0_, bf16[64,512]{1,0:T(8,128)(2,1)S(1)} %collective-permute-done.8.refs_1_, bf16[64,512]{1,0:T(8,128)(2,1)S(1)} %collective-permute-done.9.refs_2_, bf16[64,512]{1,0:T(8,128)(2,1)S(1)} %collective-permute-done.10.refs_3_), custom_call_target="tpu_custom_call" | custom-call | tf_op jit(solution)/shard_map/expose/pallas_call | solution.py:298
  32.4 0.4 %collective-permute-done.13 = f32[2,64]{1,0:T(2,128)S(1)} collective-permute-done((f32[2,64]{1,0:T(2,128)S(1)}, f32[2,64]{1,0:T(2,128)S(1)}, u32[]{:S(2)}, u32[]{:S(2)}) %collective-permute-start.13) | collective-permute-done | bytes 544 | tf_op jit(solution)/shard_map/ppermute | solution.py:165
  32.9 0.7 %collective-permute-done.12 = f32[2,64]{1,0:T(2,128)S(1)} collective-permute-done((f32[2,64]{1,0:T(2,128)S(1)}, f32[2,64]{1,0:T(2,128)S(1)}, u32[]{:S(2)}, u32[]{:S(2)}) %collective-permute-start.12) | collective-permute-done | bytes 544 | tf_op jit(solution)/shard_map/ppermute | solution.py:165
  33.5 0.6 %add_multiply_fusion = f32[2,64]{1,0:T(2,128)} fusion(f32[2,64]{1,0:T(2,128)S(1)} %collective-permute-done.12, f32[2,64]{1,0:T(2,128)S(1)} %collective-permute-done.13, f32[2,64]{1,0:T(2,128)S(1)} %totals.1, f32[2,64]{1,0:T(2,128)S(1)} %collective-permute-done.11), kind=kLoop, calls=%fused_computation | loop fusion | flops 512 | bytes 2560 | tf_op jit(solution)/shard_map/div | solution.py:311
  (27 shorter events, 0.1 us)
Async XLA Ops:
  0.6 0.9 %copy-start.3 = (bf16[256,2,128]{2,1,0:T(2,128)(2,1)S(1)}, bf16[256,2,128]{2,1,0:T(2,128)(2,1)}, u32[]{:S(2)}) copy-start(bf16[256,2,128]{2,1,0:T(2,128)(2,1)} %refs_1_.1) | copy-start | bytes 393220
  0.6 7.0 %copy-start = (s32[2,256,256]{2,1,0:T(8,128)S(1)}, s32[2,256,256]{2,1,0:T(8,128)}, u32[]{:S(2)}) copy-start(s32[2,256,256]{2,1,0:T(8,128)} %counts_ref.1) | copy-start | bytes 1572868
  0.7 0.9 %copy-start.5 = (s32[256,2]{0,1:T(2,128)S(1)}, s32[256,2]{0,1:T(2,128)}, u32[]{:S(2)}) copy-start(s32[256,2]{0,1:T(2,128)} %param.18) | copy-start | bytes 6148
  0.7 0.9 %copy-start.6 = (s32[256]{0:T(256)S(1)}, s32[256]{0:T(256)}, u32[]{:S(2)}) copy-start(s32[256]{0:T(256)} %param.21) | copy-start | bytes 3076
  0.7 0.9 %copy-start.7 = (f32[256]{0:T(256)S(1)}, f32[256]{0:T(256)}, u32[]{:S(2)}) copy-start(f32[256]{0:T(256)} %param.13) | copy-start | bytes 3076
  0.7 0.9 %copy-start.8 = (f32[256]{0:T(256)S(1)}, f32[256]{0:T(256)}, u32[]{:S(2)}) copy-start(f32[256]{0:T(256)} %param.16) | copy-start | bytes 3076
  0.7 0.9 %copy-start.9 = (f32[256]{0:T(256)S(1)}, f32[256]{0:T(256)}, u32[]{:S(2)}) copy-start(f32[256]{0:T(256)} %param.17) | copy-start | bytes 3076
  0.7 7.0 %copy-start.1 = (bf16[2,256,256]{2,1,0:T(8,128)(2,1)S(1)}, bf16[2,256,256]{2,1,0:T(8,128)(2,1)}, u32[]{:S(2)}) copy-start(bf16[2,256,256]{2,1,0:T(8,128)(2,1)} %shocks_ref) | copy-start | bytes 786436
  0.7 7.0 %copy-start.2 = (bf16[2,256,256]{2,1,0:T(8,128)(2,1)S(1)}, bf16[2,256,256]{2,1,0:T(8,128)(2,1)}, u32[]{:S(2)}) copy-start(bf16[2,256,256]{2,1,0:T(8,128)(2,1)} %noise_ref.1) | copy-start | bytes 786436
  0.7 6.9 %copy-start.4 = (bf16[256,256]{1,0:T(8,128)(2,1)S(1)}, bf16[256,256]{1,0:T(8,128)(2,1)}, u32[]{:S(2)}) copy-start(bf16[256,256]{1,0:T(8,128)(2,1)} %loadings_ref.1) | copy-start | bytes 393220
  2.0 9.2 %collective-permute-start.2 = (bf16[80,256]{1,0:T(8,128)(2,1)S(1)}, bf16[80,256]{1,0:T(8,128)(2,1)S(1)}, u32[]{:S(2)}, u32[]{:S(2)}) collective-permute-start(bf16[80,256]{1,0:T(8,128)(2,1)S(1)} %get-tuple-element.12.refs_1_), channel_id=1, source_target_pairs={{0,4},{1,5},{2,6},{3,7},{4,0},{5,1},{6,2},{7,3},{8,12},{9,13},{10,... | collective-permute-start | bytes 122888 | tf_op jit(solution)/shard_map/ppermute | solution.py:165
  6.1 5.9 %collective-permute-start.1 = (bf16[80,256]{1,0:T(8,128)(2,1)S(1)}, bf16[80,256]{1,0:T(8,128)(2,1)S(1)}, u32[]{:S(2)}, u32[]{:S(2)}) collective-permute-start(bf16[80,256]{1,0:T(8,128)(2,1)S(1)} %get-tuple-element.12.refs_1_), channel_id=1, source_target_pairs={{0,6},{1,7},{2,4},{3,5},{4,2},{5,3},{6,0},{7,1},{8,14},{9,15},{10,... | collective-permute-start | bytes 122888 | tf_op jit(solution)/shard_map/ppermute | solution.py:165
  7.4 4.6 %collective-permute-start = (bf16[80,256]{1,0:T(8,128)(2,1)S(1)}, bf16[80,256]{1,0:T(8,128)(2,1)S(1)}, u32[]{:S(2)}, u32[]{:S(2)}) collective-permute-start(bf16[80,256]{1,0:T(8,128)(2,1)S(1)} %get-tuple-element.12.refs_1_), channel_id=1, source_target_pairs={{0,2},{1,3},{2,0},{3,1},{4,6},{5,7},{6,4},{7,5},{8,10},{9,11},{10,... | collective-permute-start | bytes 122888 | tf_op jit(solution)/shard_map/ppermute | solution.py:165
  7.7 4.3 %copy-start.10 = (s32[16]{0:T(128)S(1)}, s32[16]{0:T(128)}, u32[]{:S(2)}) copy-start(s32[16]{0:T(128)} %refs_0_.1) | copy-start | bytes 196
  8.2 13.5 %collective-permute-start.7 = (bf16[512,256]{1,0:T(8,128)(2,1)S(1)}, bf16[512,256]{1,0:T(8,128)(2,1)S(1)}, u32[]{:S(2)}, u32[]{:S(2)}) collective-permute-start(bf16[512,256]{1,0:T(8,128)(2,1)S(1)} %price.1.refs_2_), channel_id=1, source_target_pairs={{0,6},{1,7},{2,4},{3,5},{4,2},{5,3},{6,0},{7,1},{8,14},{9,15},{10,... | collective-permute-start | bytes 786440 | tf_op jit(solution)/shard_map/ppermute | solution.py:165
  12.9 4.5 %collective-permute-start.4 = (bf16[128,256]{1,0:T(8,128)(2,1)S(1)}, bf16[128,256]{1,0:T(8,128)(2,1)S(1)}, u32[]{:S(2)}, u32[]{:S(2)}) collective-permute-start(bf16[128,256]{1,0:T(8,128)(2,1)S(1)} %get-tuple-element.15), channel_id=1, source_target_pairs={{0,16},{8,24},{16,0},{24,8},{1,17},{9,25},{17,1},{25,9},{2,18},{10... | collective-permute-start | bytes 196616 | tf_op jit(solution)/shard_map/ppermute | solution.py:165
  14.5 5.2 %collective-permute-start.5 = (bf16[128,256]{1,0:T(8,128)(2,1)S(1)}, bf16[128,256]{1,0:T(8,128)(2,1)S(1)}, u32[]{:S(2)}, u32[]{:S(2)}) collective-permute-start(bf16[128,256]{1,0:T(8,128)(2,1)S(1)} %get-tuple-element.14), channel_id=1, source_target_pairs={{0,17},{1,16},{2,19},{3,18},{4,21},{5,20},{6,23},{7,22},{8,25},{9,... | collective-permute-start | bytes 196616 | tf_op jit(solution)/shard_map/ppermute | solution.py:175
  15.9 4.3 %collective-permute-start.3 = (bf16[128,256]{1,0:T(8,128)(2,1)S(1)}, bf16[128,256]{1,0:T(8,128)(2,1)S(1)}, u32[]{:S(2)}, u32[]{:S(2)}) collective-permute-start(bf16[128,256]{1,0:T(8,128)(2,1)S(1)} %get-tuple-element.14), channel_id=1, source_target_pairs={{0,1},{1,0},{2,3},{3,2},{4,5},{5,4},{6,7},{7,6},{8,9},{9,8},{10,11... | collective-permute-start | bytes 196616 | tf_op jit(solution)/shard_map/ppermute | solution.py:175
  20.3 1.4 %collective-permute-start.6 = (bf16[256,256]{1,0:T(8,128)(2,1)S(1)}, bf16[256,256]{1,0:T(8,128)(2,1)S(1)}, u32[]{:S(2)}, u32[]{:S(2)}) collective-permute-start(bf16[256,256]{1,0:T(8,128)(2,1)S(1)} %merge.1.refs_0_), channel_id=1, source_target_pairs={{0,8},{8,0},{16,24},{24,16},{1,9},{9,1},{17,25},{25,17},{2,10},{10... | collective-permute-start | bytes 393224 | tf_op jit(solution)/shard_map/ppermute | solution.py:165
  22.1 4.6 %collective-permute-start.8 = (bf16[64,512]{1,0:T(8,128)(2,1)S(1)}, bf16[64,512]{1,0:T(8,128)(2,1)S(1)}, u32[]{:S(2)}, u32[]{:S(2)}) collective-permute-start(bf16[64,512]{1,0:T(8,128)(2,1)S(1)} %get-tuple-element.19), channel_id=1, source_target_pairs={{0,2},{1,3},{2,0},{3,1},{4,6},{5,7},{6,4},{7,5},{8,10},{9,11},{10,... | collective-permute-start | bytes 196616 | tf_op jit(solution)/shard_map/ppermute | solution.py:165
  23.8 5.2 %collective-permute-start.9 = (bf16[64,512]{1,0:T(8,128)(2,1)S(1)}, bf16[64,512]{1,0:T(8,128)(2,1)S(1)}, u32[]{:S(2)}, u32[]{:S(2)}) collective-permute-start(bf16[64,512]{1,0:T(8,128)(2,1)S(1)} %get-tuple-element.20), channel_id=1, source_target_pairs={{0,3},{1,2},{2,1},{3,0},{4,7},{5,6},{6,5},{7,4},{8,11},{9,10},{10,... | collective-permute-start | bytes 196616 | tf_op jit(solution)/shard_map/ppermute | solution.py:165
  24.8 4.9 %collective-permute-start.10 = (bf16[64,512]{1,0:T(8,128)(2,1)S(1)}, bf16[64,512]{1,0:T(8,128)(2,1)S(1)}, u32[]{:S(2)}, u32[]{:S(2)}) collective-permute-start(bf16[64,512]{1,0:T(8,128)(2,1)S(1)} %get-tuple-element.21), channel_id=1, source_target_pairs={{0,1},{1,0},{2,3},{3,2},{4,5},{5,4},{6,7},{7,6},{8,9},{9,8},{10,11... | collective-permute-start | bytes 196616 | tf_op jit(solution)/shard_map/ppermute | solution.py:165
  29.8 3.1 %collective-permute-start.13 = (f32[2,64]{1,0:T(2,128)S(1)}, f32[2,64]{1,0:T(2,128)S(1)}, u32[]{:S(2)}, u32[]{:S(2)}) collective-permute-start(f32[2,64]{1,0:T(2,128)S(1)} %totals.1), channel_id=1, source_target_pairs={{0,24},{8,16},{16,8},{24,0},{1,25},{9,17},{17,9},{25,1},{2,26},{10... | collective-permute-start | bytes 1544 | tf_op jit(solution)/shard_map/ppermute | solution.py:165
  29.9 3.6 %collective-permute-start.12 = (f32[2,64]{1,0:T(2,128)S(1)}, f32[2,64]{1,0:T(2,128)S(1)}, u32[]{:S(2)}, u32[]{:S(2)}) collective-permute-start(f32[2,64]{1,0:T(2,128)S(1)} %totals.1), channel_id=1, source_target_pairs={{0,16},{8,24},{16,0},{24,8},{1,17},{9,25},{17,1},{25,9},{2,18},{10... | collective-permute-start | bytes 1544 | tf_op jit(solution)/shard_map/ppermute | solution.py:165
  31.5 2.1 %collective-permute-start.11 = (f32[2,64]{1,0:T(2,128)S(1)}, f32[2,64]{1,0:T(2,128)S(1)}, u32[]{:S(2)}, u32[]{:S(2)}) collective-permute-start(f32[2,64]{1,0:T(2,128)S(1)} %totals.1), channel_id=1, source_target_pairs={{0,8},{8,0},{16,24},{24,16},{1,9},{9,1},{17,25},{25,17},{2,10},{10... | collective-permute-start | bytes 1544 | tf_op jit(solution)/shard_map/ppermute | solution.py:165

commit v16 on v15

--- a/solution.py
+++ b/solution.py
@@ -284,7 +284,7 @@
         name="value",
     )(*shares, *pair_prices)
     sends = list(zip(parts[1:], owner_flips[1:]))
-    sends = sends[1:] + sends[:1]
+    sends = sends[::-1]
     parts = [parts[0]] + [from_partner(x, "fac", i) for x, i in sends]
 
     totals = pl.pallas_call(

time: 34.2 us -> 33.6 us (0.982)
  waiting for transfers between devices: 11 us -> 10.3 us
    ppermute x12, waiting for transfers between devices: 8.21 us -> 7.54 us  [from_partner(): return lax.ppermute(x, axis, [(i, i ^ flip) for i in range(count)])]
  transfers between devices with their start and end apart: 14 -> 14, of which waited for: 10 -> 9; matrix products, arithmetic and copies ran while one was open for 0% -> 0% of each run, Pallas kernels for 6% -> 7%
where the time goes in v16:
time: 33.6 us; the launch traced here: 33.4 us
  starting transfers between devices  17.8 us (53%)
  waiting for transfers between devices  10.3 us (31%)
  Pallas kernels  3.12 us (9%)
  local copies, waits for them, and re-layouts  0.83 us (2%)
  between operations  0.8 us (2%)
  other arithmetic  0.57 us (2%)
    ppermute x12, starting transfers between devices, from_partner(): return lax.ppermute(x, axis, [(i, i ^ flip) for i in range(count)])  15.8 us
    ppermute x12, waiting for transfers between devices, from_partner(): return lax.ppermute(x, axis, [(i, i ^ flip) for i in range(count)])  7.54 us
    ppermute x2, waiting for transfers between devices, from_both(): return lax.ppermute(x, ('scen', 'fac'), pairs)  2.78 us
    ppermute x2, starting transfers between devices, from_both(): return lax.ppermute(x, ('scen', 'fac'), pairs)  1.97 us
    pallas_call x1, Pallas kernels, body(): pl.pallas_call(functools.partial(combine_kernel, part, held, owner_flips)...  0.9 us
    unnamed x22, local copies, waits for them, and re-layouts  0.83 us
    pallas_call x1, Pallas kernels, body(): pl.pallas_call(functools.partial(expose_kernel, rows), out_shape=jax.Shap...  0.69 us
  transfers between devices with their start and end apart: 14, of which 9 were waited for; matrix products, arithmetic and copies ran while one was open for 0% of the time, Pallas kernels for 7%

profile of v16, /device:TPU:0, one launch (start us, length us, event | category | flops | bytes accessed | tf_op | source)
XLA Modules:
  0.0 33.4 jit_solution(1855665065342079886)
XLA Ops:
  0.8 0.8 %copy-done.3 = bf16[256,2,128]{2,1,0:T(2,128)(2,1)S(1)} copy-done((bf16[256,2,128]{2,1,0:T(2,128)(2,1)S(1)}, bf16[256,2,128]{2,1,0:T(2,128)(2,1)}, u32[]{:S(2)}) %copy-start.3) | copy-done | bytes 131096
  1.6 0.4 %pack.1 = (bf16[80,256]{1,0:T(8,128)(2,1)S(1)}, f32[3,256]{1,0:T(4,128)S(1)}) custom-call(bf16[32,128]{1,0:T(8,128)(2,1)S(1)} %pick.1.refs_0_, bf16[256,2,128]{2,1,0:T(2,128)(2,1)S(1)} %copy-done.3, s32[2,256]{1,0:T(2,128)S(1)} %bitcast.5, s32[1,256]{1,0:T(1,128)S(1)} %bitcast.6, f32[1,256]{1,0:T(1,128)S(1)} %bitcast.7, f32[1,256]{1,0:T(1,128)S(1)} %bitcast.8, ...), custom_call_target="tpu_custom_call" | custom-call | tf_op jit(solution)/shard_map/pack/pallas_call | solution.py:209
  2.0 4.1 %collective-permute-start.2 = (bf16[80,256]{1,0:T(8,128)(2,1)S(1)}, bf16[80,256]{1,0:T(8,128)(2,1)S(1)}, u32[]{:S(2)}, u32[]{:S(2)}) collective-permute-start(bf16[80,256]{1,0:T(8,128)(2,1)S(1)} %get-tuple-element.12.refs_1_), channel_id=1, source_target_pairs={{0,4},{1,5},{2,6},{3,7},{4,0},{5,1},{6,2},{7,3},{8,12},{9,13},{10,... | collective-permute-start | bytes 122888 | tf_op jit(solution)/shard_map/ppermute | solution.py:165
  6.1 1.3 %collective-permute-start.1 = (bf16[80,256]{1,0:T(8,128)(2,1)S(1)}, bf16[80,256]{1,0:T(8,128)(2,1)S(1)}, u32[]{:S(2)}, u32[]{:S(2)}) collective-permute-start(bf16[80,256]{1,0:T(8,128)(2,1)S(1)} %get-tuple-element.12.refs_1_), channel_id=1, source_target_pairs={{0,6},{1,7},{2,4},{3,5},{4,2},{5,3},{6,0},{7,1},{8,14},{9,15},{10,... | collective-permute-start | bytes 122888 | tf_op jit(solution)/shard_map/ppermute | solution.py:165
  7.4 0.2 collective-permute-start
  7.7 0.0 copy-start.10
  7.7 0.5 %price.1.refs_2_ = bf16[512,256]{1,0:T(8,128)(2,1)S(1)} custom-call(bf16[2,256,256]{2,1,0:T(8,128)(2,1)S(1)} %copy-done.1, bf16[256,256]{1,0:T(8,128)(2,1)S(1)} %copy-done.4, s32[2,256,256]{2,1,0:T(8,128)S(1)} %copy-done, bf16[2,256,256]{2,1,0:T(8,128)(2,1)S(1)} %copy-done.2, f32[3,256]{1,0:T(4,128)S(1)} %get-tuple-element.17.factors_ref), custom_call_target="tpu_custom_call" | custom-call | tf_op jit(solution)/shard_map/price/pallas_call | solution.py:232
  8.2 3.0 %collective-permute-start.7 = (bf16[512,256]{1,0:T(8,128)(2,1)S(1)}, bf16[512,256]{1,0:T(8,128)(2,1)S(1)}, u32[]{:S(2)}, u32[]{:S(2)}) collective-permute-start(bf16[512,256]{1,0:T(8,128)(2,1)S(1)} %price.1.refs_2_), channel_id=1, source_target_pairs={{0,6},{1,7},{2,4},{3,5},{4,2},{5,3},{6,0},{7,1},{8,14},{9,15},{10,... | collective-permute-start | bytes 786440 | tf_op jit(solution)/shard_map/ppermute | solution.py:165
  11.2 0.8 %collective-permute-done.1.refs_3_ = bf16[80,256]{1,0:T(8,128)(2,1)S(1)} collective-permute-done((bf16[80,256]{1,0:T(8,128)(2,1)S(1)}, bf16[80,256]{1,0:T(8,128)(2,1)S(1)}, u32[]{:S(2)}, u32[]{:S(2)}) %collective-permute-start.1) | collective-permute-done | bytes 40992 | tf_op jit(solution)/shard_map/ppermute | solution.py:165
  12.0 0.9 %combine.1 = (f32[128,256]{1,0:T(8,128)S(1)}, bf16[128,256]{1,0:T(8,128)(2,1)S(1)}, bf16[128,256]{1,0:T(8,128)(2,1)S(1)}) custom-call(s32[16]{0:T(128)S(1)} %copy-done.10, bf16[80,256]{1,0:T(8,128)(2,1)S(1)} %get-tuple-element.12.refs_1_, bf16[80,256]{1,0:T(8,128)(2,1)S(1)} %collective-permute-done.refs_2_, ...), custom_call_target="tpu_custom_call" | custom-call | flops 1000000000 | tf_op jit(solution)/shard_map/combine/pallas_call | solution.py:242
  12.9 1.6 %collective-permute-start.4 = (bf16[128,256]{1,0:T(8,128)(2,1)S(1)}, bf16[128,256]{1,0:T(8,128)(2,1)S(1)}, u32[]{:S(2)}, u32[]{:S(2)}) collective-permute-start(bf16[128,256]{1,0:T(8,128)(2,1)S(1)} %get-tuple-element.15), channel_id=1, source_target_pairs={{0,16},{8,24},{16,0},{24,8},{1,17},{9,25},{17,1},{25,9},{2,18},{10... | collective-permute-start | bytes 196616 | tf_op jit(solution)/shard_map/ppermute | solution.py:165
  14.5 1.4 %collective-permute-start.5 = (bf16[128,256]{1,0:T(8,128)(2,1)S(1)}, bf16[128,256]{1,0:T(8,128)(2,1)S(1)}, u32[]{:S(2)}, u32[]{:S(2)}) collective-permute-start(bf16[128,256]{1,0:T(8,128)(2,1)S(1)} %get-tuple-element.14), channel_id=1, source_target_pairs={{0,17},{1,16},{2,19},{3,18},{4,21},{5,20},{6,23},{7,22},{8,25},{9,... | collective-permute-start | bytes 196616 | tf_op jit(solution)/shard_map/ppermute | solution.py:175
  15.9 0.5 %collective-permute-start.3 = (bf16[128,256]{1,0:T(8,128)(2,1)S(1)}, bf16[128,256]{1,0:T(8,128)(2,1)S(1)}, u32[]{:S(2)}, u32[]{:S(2)}) collective-permute-start(bf16[128,256]{1,0:T(8,128)(2,1)S(1)} %get-tuple-element.14), channel_id=1, source_target_pairs={{0,1},{1,0},{2,3},{3,2},{4,5},{5,4},{6,7},{7,6},{8,9},{9,8},{10,11... | collective-permute-start | bytes 196616 | tf_op jit(solution)/shard_map/ppermute | solution.py:175
  16.5 0.9 %collective-permute-done.4.refs_2_ = bf16[128,256]{1,0:T(8,128)(2,1)S(1)} collective-permute-done((bf16[128,256]{1,0:T(8,128)(2,1)S(1)}, bf16[128,256]{1,0:T(8,128)(2,1)S(1)}, u32[]{:S(2)}, u32[]{:S(2)}) %collective-permute-start.4) | collective-permute-done | bytes 65568 | tf_op jit(solution)/shard_map/ppermute | solution.py:165
  17.4 2.2 %collective-permute-done.5.refs_3_ = bf16[128,256]{1,0:T(8,128)(2,1)S(1)} collective-permute-done((bf16[128,256]{1,0:T(8,128)(2,1)S(1)}, bf16[128,256]{1,0:T(8,128)(2,1)S(1)}, u32[]{:S(2)}, u32[]{:S(2)}) %collective-permute-start.5) | collective-permute-done | bytes 65568 | tf_op jit(solution)/shard_map/ppermute | solution.py:175
  19.6 0.5 %collective-permute-done.3.refs_1_ = bf16[128,256]{1,0:T(8,128)(2,1)S(1)} collective-permute-done((bf16[128,256]{1,0:T(8,128)(2,1)S(1)}, bf16[128,256]{1,0:T(8,128)(2,1)S(1)}, u32[]{:S(2)}, u32[]{:S(2)}) %collective-permute-start.3) | collective-permute-done | bytes 65568 | tf_op jit(solution)/shard_map/ppermute | solution.py:175
  20.2 0.1 merge.1.refs_0_
  20.3 0.1 collective-permute-start.6
  20.4 1.3 %collective-permute-done.6.refs_1_ = bf16[256,256]{1,0:T(8,128)(2,1)S(1)} collective-permute-done((bf16[256,256]{1,0:T(8,128)(2,1)S(1)}, bf16[256,256]{1,0:T(8,128)(2,1)S(1)}, u32[]{:S(2)}, u32[]{:S(2)}) %collective-permute-start.6) | collective-permute-done | bytes 131104 | tf_op jit(solution)/shard_map/ppermute | solution.py:165
  21.7 0.4 %value.1 = (f32[64,512]{1,0:T(8,128)S(1)}, bf16[64,512]{1,0:T(8,128)(2,1)S(1)}, bf16[64,512]{1,0:T(8,128)(2,1)S(1)}, bf16[64,512]{1,0:T(8,128)(2,1)S(1)}) custom-call(bf16[256,256]{1,0:T(8,128)(2,1)S(1)} %merge.1.refs_0_, bf16[256,256]{1,0:T(8,128)(2,1)S(1)} %collective-permute-done.6.refs_1_, bf16[512,256]{1,0:T(8,128)(2,1)S(1)} %price.1.refs_2_, ...), custom_call_target="tpu_custom_call" | custom-call | tf_op jit(solution)/shard_map/value/pallas_call | solution.py:274
  22.1 2.6 %collective-permute-start.8 = (bf16[64,512]{1,0:T(8,128)(2,1)S(1)}, bf16[64,512]{1,0:T(8,128)(2,1)S(1)}, u32[]{:S(2)}, u32[]{:S(2)}) collective-permute-start(bf16[64,512]{1,0:T(8,128)(2,1)S(1)} %get-tuple-element.19), channel_id=1, source_target_pairs={{0,3},{1,2},{2,1},{3,0},{4,7},{5,6},{6,5},{7,4},{8,11},{9,10},{10,... | collective-permute-start | bytes 196616 | tf_op jit(solution)/shard_map/ppermute | solution.py:165
  24.7 0.9 %collective-permute-start.10 = (bf16[64,512]{1,0:T(8,128)(2,1)S(1)}, bf16[64,512]{1,0:T(8,128)(2,1)S(1)}, u32[]{:S(2)}, u32[]{:S(2)}) collective-permute-start(bf16[64,512]{1,0:T(8,128)(2,1)S(1)} %get-tuple-element.21), channel_id=1, source_target_pairs={{0,1},{1,0},{2,3},{3,2},{4,5},{5,4},{6,7},{7,6},{8,9},{9,8},{10,11... | collective-permute-start | bytes 196616 | tf_op jit(solution)/shard_map/ppermute | solution.py:165
  25.7 2.4 %collective-permute-done.8.refs_1_ = bf16[64,512]{1,0:T(8,128)(2,1)S(1)} collective-permute-done((bf16[64,512]{1,0:T(8,128)(2,1)S(1)}, bf16[64,512]{1,0:T(8,128)(2,1)S(1)}, u32[]{:S(2)}, u32[]{:S(2)}) %collective-permute-start.8) | collective-permute-done | bytes 65568 | tf_op jit(solution)/shard_map/ppermute | solution.py:165
  28.0 1.0 %collective-permute-done.9.refs_2_ = bf16[64,512]{1,0:T(8,128)(2,1)S(1)} collective-permute-done((bf16[64,512]{1,0:T(8,128)(2,1)S(1)}, bf16[64,512]{1,0:T(8,128)(2,1)S(1)}, u32[]{:S(2)}, u32[]{:S(2)}) %collective-permute-start.9) | collective-permute-done | bytes 65568 | tf_op jit(solution)/shard_map/ppermute | solution.py:165
  29.0 0.1 totals.1
  29.1 0.1 collective-permute-start.13
  29.3 1.5 %collective-permute-start.12 = (f32[2,64]{1,0:T(2,128)S(1)}, f32[2,64]{1,0:T(2,128)S(1)}, u32[]{:S(2)}, u32[]{:S(2)}) collective-permute-start(f32[2,64]{1,0:T(2,128)S(1)} %totals.1), channel_id=1, source_target_pairs={{0,16},{8,24},{16,0},{24,8},{1,17},{9,25},{17,1},{25,9},{2,18},{10... | collective-permute-start | bytes 1544 | tf_op jit(solution)/shard_map/ppermute | solution.py:165
  30.8 0.3 collective-permute-start.11
  31.1 0.7 %expose.1 = f32[2,64,256]{2,1,0:T(8,128)} custom-call(f32[64,512]{1,0:T(8,128)S(1)} %get-tuple-element.18.refs_0_, bf16[64,512]{1,0:T(8,128)(2,1)S(1)} %collective-permute-done.8.refs_1_, bf16[64,512]{1,0:T(8,128)(2,1)S(1)} %collective-permute-done.9.refs_2_, bf16[64,512]{1,0:T(8,128)(2,1)S(1)} %collective-permute-done.10.refs_3_), custom_call_target="tpu_custom_call" | custom-call | tf_op jit(solution)/shard_map/expose/pallas_call | solution.py:298
  31.7 0.4 %collective-permute-done.13 = f32[2,64]{1,0:T(2,128)S(1)} collective-permute-done((f32[2,64]{1,0:T(2,128)S(1)}, f32[2,64]{1,0:T(2,128)S(1)}, u32[]{:S(2)}, u32[]{:S(2)}) %collective-permute-start.13) | collective-permute-done | bytes 544 | tf_op jit(solution)/shard_map/ppermute | solution.py:165
  32.2 0.7 %collective-permute-done.12 = f32[2,64]{1,0:T(2,128)S(1)} collective-permute-done((f32[2,64]{1,0:T(2,128)S(1)}, f32[2,64]{1,0:T(2,128)S(1)}, u32[]{:S(2)}, u32[]{:S(2)}) %collective-permute-start.12) | collective-permute-done | bytes 544 | tf_op jit(solution)/shard_map/ppermute | solution.py:165
  32.8 0.6 %add_multiply_fusion = f32[2,64]{1,0:T(2,128)} fusion(f32[2,64]{1,0:T(2,128)S(1)} %collective-permute-done.12, f32[2,64]{1,0:T(2,128)S(1)} %collective-permute-done.13, f32[2,64]{1,0:T(2,128)S(1)} %totals.1, f32[2,64]{1,0:T(2,128)S(1)} %collective-permute-done.11), kind=kLoop, calls=%fused_computation | loop fusion | flops 512 | bytes 2560 | tf_op jit(solution)/shard_map/div | solution.py:311
  (27 shorter events, 0.1 us)
Async XLA Ops:
  0.6 0.9 %copy-start.3 = (bf16[256,2,128]{2,1,0:T(2,128)(2,1)S(1)}, bf16[256,2,128]{2,1,0:T(2,128)(2,1)}, u32[]{:S(2)}) copy-start(bf16[256,2,128]{2,1,0:T(2,128)(2,1)} %refs_1_.1) | copy-start | bytes 393220
  0.6 7.0 %copy-start = (s32[2,256,256]{2,1,0:T(8,128)S(1)}, s32[2,256,256]{2,1,0:T(8,128)}, u32[]{:S(2)}) copy-start(s32[2,256,256]{2,1,0:T(8,128)} %counts_ref.1) | copy-start | bytes 1572868
  0.7 0.9 %copy-start.5 = (s32[256,2]{0,1:T(2,128)S(1)}, s32[256,2]{0,1:T(2,128)}, u32[]{:S(2)}) copy-start(s32[256,2]{0,1:T(2,128)} %param.18) | copy-start | bytes 6148
  0.7 0.9 %copy-start.6 = (s32[256]{0:T(256)S(1)}, s32[256]{0:T(256)}, u32[]{:S(2)}) copy-start(s32[256]{0:T(256)} %param.21) | copy-start | bytes 3076
  0.7 0.9 %copy-start.7 = (f32[256]{0:T(256)S(1)}, f32[256]{0:T(256)}, u32[]{:S(2)}) copy-start(f32[256]{0:T(256)} %param.13) | copy-start | bytes 3076
  0.7 0.9 %copy-start.8 = (f32[256]{0:T(256)S(1)}, f32[256]{0:T(256)}, u32[]{:S(2)}) copy-start(f32[256]{0:T(256)} %param.16) | copy-start | bytes 3076
  0.7 0.9 %copy-start.9 = (f32[256]{0:T(256)S(1)}, f32[256]{0:T(256)}, u32[]{:S(2)}) copy-start(f32[256]{0:T(256)} %param.17) | copy-start | bytes 3076
  0.7 7.0 %copy-start.1 = (bf16[2,256,256]{2,1,0:T(8,128)(2,1)S(1)}, bf16[2,256,256]{2,1,0:T(8,128)(2,1)}, u32[]{:S(2)}) copy-start(bf16[2,256,256]{2,1,0:T(8,128)(2,1)} %shocks_ref) | copy-start | bytes 786436
  0.7 7.0 %copy-start.2 = (bf16[2,256,256]{2,1,0:T(8,128)(2,1)S(1)}, bf16[2,256,256]{2,1,0:T(8,128)(2,1)}, u32[]{:S(2)}) copy-start(bf16[2,256,256]{2,1,0:T(8,128)(2,1)} %noise_ref.1) | copy-start | bytes 786436
  0.7 6.9 %copy-start.4 = (bf16[256,256]{1,0:T(8,128)(2,1)S(1)}, bf16[256,256]{1,0:T(8,128)(2,1)}, u32[]{:S(2)}) copy-start(bf16[256,256]{1,0:T(8,128)(2,1)} %loadings_ref.1) | copy-start | bytes 393220
  2.0 9.2 %collective-permute-start.2 = (bf16[80,256]{1,0:T(8,128)(2,1)S(1)}, bf16[80,256]{1,0:T(8,128)(2,1)S(1)}, u32[]{:S(2)}, u32[]{:S(2)}) collective-permute-start(bf16[80,256]{1,0:T(8,128)(2,1)S(1)} %get-tuple-element.12.refs_1_), channel_id=1, source_target_pairs={{0,4},{1,5},{2,6},{3,7},{4,0},{5,1},{6,2},{7,3},{8,12},{9,13},{10,... | collective-permute-start | bytes 122888 | tf_op jit(solution)/shard_map/ppermute | solution.py:165
  6.1 5.9 %collective-permute-start.1 = (bf16[80,256]{1,0:T(8,128)(2,1)S(1)}, bf16[80,256]{1,0:T(8,128)(2,1)S(1)}, u32[]{:S(2)}, u32[]{:S(2)}) collective-permute-start(bf16[80,256]{1,0:T(8,128)(2,1)S(1)} %get-tuple-element.12.refs_1_), channel_id=1, source_target_pairs={{0,6},{1,7},{2,4},{3,5},{4,2},{5,3},{6,0},{7,1},{8,14},{9,15},{10,... | collective-permute-start | bytes 122888 | tf_op jit(solution)/shard_map/ppermute | solution.py:165
  7.4 4.6 %collective-permute-start = (bf16[80,256]{1,0:T(8,128)(2,1)S(1)}, bf16[80,256]{1,0:T(8,128)(2,1)S(1)}, u32[]{:S(2)}, u32[]{:S(2)}) collective-permute-start(bf16[80,256]{1,0:T(8,128)(2,1)S(1)} %get-tuple-element.12.refs_1_), channel_id=1, source_target_pairs={{0,2},{1,3},{2,0},{3,1},{4,6},{5,7},{6,4},{7,5},{8,10},{9,11},{10,... | collective-permute-start | bytes 122888 | tf_op jit(solution)/shard_map/ppermute | solution.py:165
  7.7 4.3 %copy-start.10 = (s32[16]{0:T(128)S(1)}, s32[16]{0:T(128)}, u32[]{:S(2)}) copy-start(s32[16]{0:T(128)} %refs_0_.1) | copy-start | bytes 196
  8.2 13.5 %collective-permute-start.7 = (bf16[512,256]{1,0:T(8,128)(2,1)S(1)}, bf16[512,256]{1,0:T(8,128)(2,1)S(1)}, u32[]{:S(2)}, u32[]{:S(2)}) collective-permute-start(bf16[512,256]{1,0:T(8,128)(2,1)S(1)} %price.1.refs_2_), channel_id=1, source_target_pairs={{0,6},{1,7},{2,4},{3,5},{4,2},{5,3},{6,0},{7,1},{8,14},{9,15},{10,... | collective-permute-start | bytes 786440 | tf_op jit(solution)/shard_map/ppermute | solution.py:165
  12.9 4.5 %collective-permute-start.4 = (bf16[128,256]{1,0:T(8,128)(2,1)S(1)}, bf16[128,256]{1,0:T(8,128)(2,1)S(1)}, u32[]{:S(2)}, u32[]{:S(2)}) collective-permute-start(bf16[128,256]{1,0:T(8,128)(2,1)S(1)} %get-tuple-element.15), channel_id=1, source_target_pairs={{0,16},{8,24},{16,0},{24,8},{1,17},{9,25},{17,1},{25,9},{2,18},{10... | collective-permute-start | bytes 196616 | tf_op jit(solution)/shard_map/ppermute | solution.py:165
  14.5 5.2 %collective-permute-start.5 = (bf16[128,256]{1,0:T(8,128)(2,1)S(1)}, bf16[128,256]{1,0:T(8,128)(2,1)S(1)}, u32[]{:S(2)}, u32[]{:S(2)}) collective-permute-start(bf16[128,256]{1,0:T(8,128)(2,1)S(1)} %get-tuple-element.14), channel_id=1, source_target_pairs={{0,17},{1,16},{2,19},{3,18},{4,21},{5,20},{6,23},{7,22},{8,25},{9,... | collective-permute-start | bytes 196616 | tf_op jit(solution)/shard_map/ppermute | solution.py:175
  15.9 4.3 %collective-permute-start.3 = (bf16[128,256]{1,0:T(8,128)(2,1)S(1)}, bf16[128,256]{1,0:T(8,128)(2,1)S(1)}, u32[]{:S(2)}, u32[]{:S(2)}) collective-permute-start(bf16[128,256]{1,0:T(8,128)(2,1)S(1)} %get-tuple-element.14), channel_id=1, source_target_pairs={{0,1},{1,0},{2,3},{3,2},{4,5},{5,4},{6,7},{7,6},{8,9},{9,8},{10,11... | collective-permute-start | bytes 196616 | tf_op jit(solution)/shard_map/ppermute | solution.py:175
  20.3 1.4 %collective-permute-start.6 = (bf16[256,256]{1,0:T(8,128)(2,1)S(1)}, bf16[256,256]{1,0:T(8,128)(2,1)S(1)}, u32[]{:S(2)}, u32[]{:S(2)}) collective-permute-start(bf16[256,256]{1,0:T(8,128)(2,1)S(1)} %merge.1.refs_0_), channel_id=1, source_target_pairs={{0,8},{8,0},{16,24},{24,16},{1,9},{9,1},{17,25},{25,17},{2,10},{10... | collective-permute-start | bytes 393224 | tf_op jit(solution)/shard_map/ppermute | solution.py:165
  22.1 5.9 %collective-permute-start.8 = (bf16[64,512]{1,0:T(8,128)(2,1)S(1)}, bf16[64,512]{1,0:T(8,128)(2,1)S(1)}, u32[]{:S(2)}, u32[]{:S(2)}) collective-permute-start(bf16[64,512]{1,0:T(8,128)(2,1)S(1)} %get-tuple-element.19), channel_id=1, source_target_pairs={{0,3},{1,2},{2,1},{3,0},{4,7},{5,6},{6,5},{7,4},{8,11},{9,10},{10,... | collective-permute-start | bytes 196616 | tf_op jit(solution)/shard_map/ppermute | solution.py:165
  24.7 4.3 %collective-permute-start.9 = (bf16[64,512]{1,0:T(8,128)(2,1)S(1)}, bf16[64,512]{1,0:T(8,128)(2,1)S(1)}, u32[]{:S(2)}, u32[]{:S(2)}) collective-permute-start(bf16[64,512]{1,0:T(8,128)(2,1)S(1)} %get-tuple-element.20), channel_id=1, source_target_pairs={{0,2},{1,3},{2,0},{3,1},{4,6},{5,7},{6,4},{7,5},{8,10},{9,11},{10,... | collective-permute-start | bytes 196616 | tf_op jit(solution)/shard_map/ppermute | solution.py:165
  24.7 4.3 %collective-permute-start.10 = (bf16[64,512]{1,0:T(8,128)(2,1)S(1)}, bf16[64,512]{1,0:T(8,128)(2,1)S(1)}, u32[]{:S(2)}, u32[]{:S(2)}) collective-permute-start(bf16[64,512]{1,0:T(8,128)(2,1)S(1)} %get-tuple-element.21), channel_id=1, source_target_pairs={{0,1},{1,0},{2,3},{3,2},{4,5},{5,4},{6,7},{7,6},{8,9},{9,8},{10,11... | collective-permute-start | bytes 196616 | tf_op jit(solution)/shard_map/ppermute | solution.py:165
  29.1 3.1 %collective-permute-start.13 = (f32[2,64]{1,0:T(2,128)S(1)}, f32[2,64]{1,0:T(2,128)S(1)}, u32[]{:S(2)}, u32[]{:S(2)}) collective-permute-start(f32[2,64]{1,0:T(2,128)S(1)} %totals.1), channel_id=1, source_target_pairs={{0,24},{8,16},{16,8},{24,0},{1,25},{9,17},{17,9},{25,1},{2,26},{10... | collective-permute-start | bytes 1544 | tf_op jit(solution)/shard_map/ppermute | solution.py:165
  29.3 3.6 %collective-permute-start.12 = (f32[2,64]{1,0:T(2,128)S(1)}, f32[2,64]{1,0:T(2,128)S(1)}, u32[]{:S(2)}, u32[]{:S(2)}) collective-permute-start(f32[2,64]{1,0:T(2,128)S(1)} %totals.1), channel_id=1, source_target_pairs={{0,16},{8,24},{16,0},{24,8},{1,17},{9,25},{17,1},{25,9},{2,18},{10... | collective-permute-start | bytes 1544 | tf_op jit(solution)/shard_map/ppermute | solution.py:165
  30.8 2.1 %collective-permute-start.11 = (f32[2,64]{1,0:T(2,128)S(1)}, f32[2,64]{1,0:T(2,128)S(1)}, u32[]{:S(2)}, u32[]{:S(2)}) collective-permute-start(f32[2,64]{1,0:T(2,128)S(1)} %totals.1), channel_id=1, source_target_pairs={{0,8},{8,0},{16,24},{24,16},{1,9},{9,1},{17,25},{25,17},{2,10},{10... | collective-permute-start | bytes 1544 | tf_op jit(solution)/shard_map/ppermute | solution.py:165

commit v17 on v16

--- a/solution.py
+++ b/solution.py
@@ -225,8 +225,7 @@
         jump_mean[None],
         jump_vol[None],
     )
-    order = column_flips[1:2] + column_flips[:1:-1]
-    packets = [packet] + [from_partner(packet, "fac", i) for i in order]
+    packets = [packet] + [from_partner(packet, "fac", i) for i in column_flips[1:]]
 
     packet, shocks = lax.optimization_barrier((packet, shocks))
     prices = pl.pallas_call(

time: 33.6 us -> 35.3 us (1.051)
  starting transfers between devices: 17.8 us -> 18.7 us
  waiting for transfers between devices: 10.3 us -> 11.1 us
    ppermute x12, starting transfers between devices: 15.8 us -> 16.7 us  [from_partner(): return lax.ppermute(x, axis, [(i, i ^ flip) for i in range(count)])]
    ppermute x12, waiting for transfers between devices: 7.54 us -> 8.17 us  [from_partner(): return lax.ppermute(x, axis, [(i, i ^ flip) for i in range(count)])]
  transfers between devices with their start and end apart: 14 -> 14, of which waited for: 9 -> 10; matrix products, arithmetic and copies ran while one was open for 0% -> 0% of each run, Pallas kernels for 7% -> 6%
where the time goes in v17:
time: 35.3 us; the launch traced here: 35.1 us
  starting transfers between devices  18.7 us (53%)
  waiting for transfers between devices  11.1 us (31%)
  Pallas kernels  3.12 us (9%)
  local copies, waits for them, and re-layouts  0.83 us (2%)
  between operations  0.8 us (2%)
  other arithmetic  0.57 us (2%)
    ppermute x12, starting transfers between devices, from_partner(): return lax.ppermute(x, axis, [(i, i ^ flip) for i in range(count)])  16.7 us
    ppermute x12, waiting for transfers between devices, from_partner(): return lax.ppermute(x, axis, [(i, i ^ flip) for i in range(count)])  8.17 us
    ppermute x2, waiting for transfers between devices, from_both(): return lax.ppermute(x, ('scen', 'fac'), pairs)  2.95 us
    ppermute x2, starting transfers between devices, from_both(): return lax.ppermute(x, ('scen', 'fac'), pairs)  1.97 us
    pallas_call x1, Pallas kernels, body(): pl.pallas_call(functools.partial(combine_kernel, part, held, owner_flips)...  0.9 us
    unnamed x22, local copies, waits for them, and re-layouts  0.83 us
  transfers between devices with their start and end apart: 14, of which 10 were waited for; matrix products, arithmetic and copies ran while one was open for 0% of the time, Pallas kernels for 6%

profile of v17, /device:TPU:0, one launch (start us, length us, event | category | flops | bytes accessed | tf_op | source)
XLA Modules:
  0.0 35.1 jit_solution(7286290542186233350)
XLA Ops:
  0.8 0.8 %copy-done.3 = bf16[256,2,128]{2,1,0:T(2,128)(2,1)S(1)} copy-done((bf16[256,2,128]{2,1,0:T(2,128)(2,1)S(1)}, bf16[256,2,128]{2,1,0:T(2,128)(2,1)}, u32[]{:S(2)}) %copy-start.3) | copy-done | bytes 131096
  1.6 0.4 %pack.1 = (bf16[80,256]{1,0:T(8,128)(2,1)S(1)}, f32[3,256]{1,0:T(4,128)S(1)}) custom-call(bf16[32,128]{1,0:T(8,128)(2,1)S(1)} %pick.1.refs_0_, bf16[256,2,128]{2,1,0:T(2,128)(2,1)S(1)} %copy-done.3, s32[2,256]{1,0:T(2,128)S(1)} %bitcast.5, s32[1,256]{1,0:T(1,128)S(1)} %bitcast.6, f32[1,256]{1,0:T(1,128)S(1)} %bitcast.7, f32[1,256]{1,0:T(1,128)S(1)} %bitcast.8, ...), custom_call_target="tpu_custom_call" | custom-call | tf_op jit(solution)/shard_map/pack/pallas_call | solution.py:209
  2.0 5.1 %collective-permute-start.2 = (bf16[80,256]{1,0:T(8,128)(2,1)S(1)}, bf16[80,256]{1,0:T(8,128)(2,1)S(1)}, u32[]{:S(2)}, u32[]{:S(2)}) collective-permute-start(bf16[80,256]{1,0:T(8,128)(2,1)S(1)} %get-tuple-element.12.refs_1_), channel_id=1, source_target_pairs={{0,6},{1,7},{2,4},{3,5},{4,2},{5,3},{6,0},{7,1},{8,14},{9,15},{10,... | collective-permute-start | bytes 122888 | tf_op jit(solution)/shard_map/ppermute | solution.py:165
  7.1 0.6 %collective-permute-start = (bf16[80,256]{1,0:T(8,128)(2,1)S(1)}, bf16[80,256]{1,0:T(8,128)(2,1)S(1)}, u32[]{:S(2)}, u32[]{:S(2)}) collective-permute-start(bf16[80,256]{1,0:T(8,128)(2,1)S(1)} %get-tuple-element.12.refs_1_), channel_id=1, source_target_pairs={{0,2},{1,3},{2,0},{3,1},{4,6},{5,7},{6,4},{7,5},{8,10},{9,11},{10,... | collective-permute-start | bytes 122888 | tf_op jit(solution)/shard_map/ppermute | solution.py:165
  7.8 0.5 %price.1.refs_2_ = bf16[512,256]{1,0:T(8,128)(2,1)S(1)} custom-call(bf16[2,256,256]{2,1,0:T(8,128)(2,1)S(1)} %copy-done.1, bf16[256,256]{1,0:T(8,128)(2,1)S(1)} %copy-done.4, s32[2,256,256]{2,1,0:T(8,128)S(1)} %copy-done, bf16[2,256,256]{2,1,0:T(8,128)(2,1)S(1)} %copy-done.2, f32[3,256]{1,0:T(4,128)S(1)} %get-tuple-element.17.factors_ref), custom_call_target="tpu_custom_call" | custom-call | tf_op jit(solution)/shard_map/price/pallas_call | solution.py:231
  8.3 3.8 %collective-permute-start.7 = (bf16[512,256]{1,0:T(8,128)(2,1)S(1)}, bf16[512,256]{1,0:T(8,128)(2,1)S(1)}, u32[]{:S(2)}, u32[]{:S(2)}) collective-permute-start(bf16[512,256]{1,0:T(8,128)(2,1)S(1)} %price.1.refs_2_), channel_id=1, source_target_pairs={{0,6},{1,7},{2,4},{3,5},{4,2},{5,3},{6,0},{7,1},{8,14},{9,15},{10,... | collective-permute-start | bytes 786440 | tf_op jit(solution)/shard_map/ppermute | solution.py:165
  12.1 1.6 %collective-permute-done.1.refs_3_ = bf16[80,256]{1,0:T(8,128)(2,1)S(1)} collective-permute-done((bf16[80,256]{1,0:T(8,128)(2,1)S(1)}, bf16[80,256]{1,0:T(8,128)(2,1)S(1)}, u32[]{:S(2)}, u32[]{:S(2)}) %collective-permute-start.1) | collective-permute-done | bytes 40992 | tf_op jit(solution)/shard_map/ppermute | solution.py:165
  13.7 0.9 %combine.1 = (f32[128,256]{1,0:T(8,128)S(1)}, bf16[128,256]{1,0:T(8,128)(2,1)S(1)}, bf16[128,256]{1,0:T(8,128)(2,1)S(1)}) custom-call(s32[16]{0:T(128)S(1)} %copy-done.10, bf16[80,256]{1,0:T(8,128)(2,1)S(1)} %get-tuple-element.12.refs_1_, bf16[80,256]{1,0:T(8,128)(2,1)S(1)} %collective-permute-done.refs_2_, ...), custom_call_target="tpu_custom_call" | custom-call | flops 1000000000 | tf_op jit(solution)/shard_map/combine/pallas_call | solution.py:241
  14.6 1.6 %collective-permute-start.4 = (bf16[128,256]{1,0:T(8,128)(2,1)S(1)}, bf16[128,256]{1,0:T(8,128)(2,1)S(1)}, u32[]{:S(2)}, u32[]{:S(2)}) collective-permute-start(bf16[128,256]{1,0:T(8,128)(2,1)S(1)} %get-tuple-element.15), channel_id=1, source_target_pairs={{0,16},{8,24},{16,0},{24,8},{1,17},{9,25},{17,1},{25,9},{2,18},{10... | collective-permute-start | bytes 196616 | tf_op jit(solution)/shard_map/ppermute | solution.py:165
  16.2 1.4 %collective-permute-start.5 = (bf16[128,256]{1,0:T(8,128)(2,1)S(1)}, bf16[128,256]{1,0:T(8,128)(2,1)S(1)}, u32[]{:S(2)}, u32[]{:S(2)}) collective-permute-start(bf16[128,256]{1,0:T(8,128)(2,1)S(1)} %get-tuple-element.14), channel_id=1, source_target_pairs={{0,17},{1,16},{2,19},{3,18},{4,21},{5,20},{6,23},{7,22},{8,25},{9,... | collective-permute-start | bytes 196616 | tf_op jit(solution)/shard_map/ppermute | solution.py:175
  17.6 0.5 %collective-permute-start.3 = (bf16[128,256]{1,0:T(8,128)(2,1)S(1)}, bf16[128,256]{1,0:T(8,128)(2,1)S(1)}, u32[]{:S(2)}, u32[]{:S(2)}) collective-permute-start(bf16[128,256]{1,0:T(8,128)(2,1)S(1)} %get-tuple-element.14), channel_id=1, source_target_pairs={{0,1},{1,0},{2,3},{3,2},{4,5},{5,4},{6,7},{7,6},{8,9},{9,8},{10,11... | collective-permute-start | bytes 196616 | tf_op jit(solution)/shard_map/ppermute | solution.py:175
  18.2 0.8 %collective-permute-done.4.refs_2_ = bf16[128,256]{1,0:T(8,128)(2,1)S(1)} collective-permute-done((bf16[128,256]{1,0:T(8,128)(2,1)S(1)}, bf16[128,256]{1,0:T(8,128)(2,1)S(1)}, u32[]{:S(2)}, u32[]{:S(2)}) %collective-permute-start.4) | collective-permute-done | bytes 65568 | tf_op jit(solution)/shard_map/ppermute | solution.py:165
  18.9 2.4 %collective-permute-done.5.refs_3_ = bf16[128,256]{1,0:T(8,128)(2,1)S(1)} collective-permute-done((bf16[128,256]{1,0:T(8,128)(2,1)S(1)}, bf16[128,256]{1,0:T(8,128)(2,1)S(1)}, u32[]{:S(2)}, u32[]{:S(2)}) %collective-permute-start.5) | collective-permute-done | bytes 65568 | tf_op jit(solution)/shard_map/ppermute | solution.py:175
  21.4 0.5 %collective-permute-done.3.refs_1_ = bf16[128,256]{1,0:T(8,128)(2,1)S(1)} collective-permute-done((bf16[128,256]{1,0:T(8,128)(2,1)S(1)}, bf16[128,256]{1,0:T(8,128)(2,1)S(1)}, u32[]{:S(2)}, u32[]{:S(2)}) %collective-permute-start.3) | collective-permute-done | bytes 65568 | tf_op jit(solution)/shard_map/ppermute | solution.py:175
  21.9 0.1 merge.1.refs_0_
  22.0 0.1 collective-permute-start.6
  22.1 1.3 %collective-permute-done.6.refs_1_ = bf16[256,256]{1,0:T(8,128)(2,1)S(1)} collective-permute-done((bf16[256,256]{1,0:T(8,128)(2,1)S(1)}, bf16[256,256]{1,0:T(8,128)(2,1)S(1)}, u32[]{:S(2)}, u32[]{:S(2)}) %collective-permute-start.6) | collective-permute-done | bytes 131104 | tf_op jit(solution)/shard_map/ppermute | solution.py:165
  23.4 0.4 %value.1 = (f32[64,512]{1,0:T(8,128)S(1)}, bf16[64,512]{1,0:T(8,128)(2,1)S(1)}, bf16[64,512]{1,0:T(8,128)(2,1)S(1)}, bf16[64,512]{1,0:T(8,128)(2,1)S(1)}) custom-call(bf16[256,256]{1,0:T(8,128)(2,1)S(1)} %merge.1.refs_0_, bf16[256,256]{1,0:T(8,128)(2,1)S(1)} %collective-permute-done.6.refs_1_, bf16[512,256]{1,0:T(8,128)(2,1)S(1)} %price.1.refs_2_, ...), custom_call_target="tpu_custom_call" | custom-call | tf_op jit(solution)/shard_map/value/pallas_call | solution.py:273
  23.8 0.8 %collective-permute-start.8 = (bf16[64,512]{1,0:T(8,128)(2,1)S(1)}, bf16[64,512]{1,0:T(8,128)(2,1)S(1)}, u32[]{:S(2)}, u32[]{:S(2)}) collective-permute-start(bf16[64,512]{1,0:T(8,128)(2,1)S(1)} %get-tuple-element.19), channel_id=1, source_target_pairs={{0,3},{1,2},{2,1},{3,0},{4,7},{5,6},{6,5},{7,4},{8,11},{9,10},{10,... | collective-permute-start | bytes 196616 | tf_op jit(solution)/shard_map/ppermute | solution.py:165
  24.7 1.7 %collective-permute-start.9 = (bf16[64,512]{1,0:T(8,128)(2,1)S(1)}, bf16[64,512]{1,0:T(8,128)(2,1)S(1)}, u32[]{:S(2)}, u32[]{:S(2)}) collective-permute-start(bf16[64,512]{1,0:T(8,128)(2,1)S(1)} %get-tuple-element.20), channel_id=1, source_target_pairs={{0,2},{1,3},{2,0},{3,1},{4,6},{5,7},{6,4},{7,5},{8,10},{9,11},{10,... | collective-permute-start | bytes 196616 | tf_op jit(solution)/shard_map/ppermute | solution.py:165
  26.3 1.1 %collective-permute-start.10 = (bf16[64,512]{1,0:T(8,128)(2,1)S(1)}, bf16[64,512]{1,0:T(8,128)(2,1)S(1)}, u32[]{:S(2)}, u32[]{:S(2)}) collective-permute-start(bf16[64,512]{1,0:T(8,128)(2,1)S(1)} %get-tuple-element.21), channel_id=1, source_target_pairs={{0,1},{1,0},{2,3},{3,2},{4,5},{5,4},{6,7},{7,6},{8,9},{9,8},{10,11... | collective-permute-start | bytes 196616 | tf_op jit(solution)/shard_map/ppermute | solution.py:165
  27.4 2.4 %collective-permute-done.8.refs_1_ = bf16[64,512]{1,0:T(8,128)(2,1)S(1)} collective-permute-done((bf16[64,512]{1,0:T(8,128)(2,1)S(1)}, bf16[64,512]{1,0:T(8,128)(2,1)S(1)}, u32[]{:S(2)}, u32[]{:S(2)}) %collective-permute-start.8) | collective-permute-done | bytes 65568 | tf_op jit(solution)/shard_map/ppermute | solution.py:165
  29.7 0.1 collective-permute-done.9.refs_2_
  29.8 0.7 %collective-permute-done.10.refs_3_ = bf16[64,512]{1,0:T(8,128)(2,1)S(1)} collective-permute-done((bf16[64,512]{1,0:T(8,128)(2,1)S(1)}, bf16[64,512]{1,0:T(8,128)(2,1)S(1)}, u32[]{:S(2)}, u32[]{:S(2)}) %collective-permute-start.10) | collective-permute-done | bytes 65568 | tf_op jit(solution)/shard_map/ppermute | solution.py:165
  30.6 0.1 totals.1
  30.7 0.3 collective-permute-start.13
  31.0 1.2 %collective-permute-start.12 = (f32[2,64]{1,0:T(2,128)S(1)}, f32[2,64]{1,0:T(2,128)S(1)}, u32[]{:S(2)}, u32[]{:S(2)}) collective-permute-start(f32[2,64]{1,0:T(2,128)S(1)} %totals.1), channel_id=1, source_target_pairs={{0,16},{8,24},{16,0},{24,8},{1,17},{9,25},{17,1},{25,9},{2,18},{10... | collective-permute-start | bytes 1544 | tf_op jit(solution)/shard_map/ppermute | solution.py:165
  32.1 0.5 %collective-permute-start.11 = (f32[2,64]{1,0:T(2,128)S(1)}, f32[2,64]{1,0:T(2,128)S(1)}, u32[]{:S(2)}, u32[]{:S(2)}) collective-permute-start(f32[2,64]{1,0:T(2,128)S(1)} %totals.1), channel_id=1, source_target_pairs={{0,8},{8,0},{16,24},{24,16},{1,9},{9,1},{17,25},{25,17},{2,10},{10... | collective-permute-start | bytes 1544 | tf_op jit(solution)/shard_map/ppermute | solution.py:165
  32.6 0.7 %expose.1 = f32[2,64,256]{2,1,0:T(8,128)} custom-call(f32[64,512]{1,0:T(8,128)S(1)} %get-tuple-element.18.refs_0_, bf16[64,512]{1,0:T(8,128)(2,1)S(1)} %collective-permute-done.8.refs_1_, bf16[64,512]{1,0:T(8,128)(2,1)S(1)} %collective-permute-done.9.refs_2_, bf16[64,512]{1,0:T(8,128)(2,1)S(1)} %collective-permute-done.10.refs_3_), custom_call_target="tpu_custom_call" | custom-call | tf_op jit(solution)/shard_map/expose/pallas_call | solution.py:297
  33.3 0.4 %collective-permute-done.13 = f32[2,64]{1,0:T(2,128)S(1)} collective-permute-done((f32[2,64]{1,0:T(2,128)S(1)}, f32[2,64]{1,0:T(2,128)S(1)}, u32[]{:S(2)}, u32[]{:S(2)}) %collective-permute-start.13) | collective-permute-done | bytes 544 | tf_op jit(solution)/shard_map/ppermute | solution.py:165
  33.8 0.8 %collective-permute-done.12 = f32[2,64]{1,0:T(2,128)S(1)} collective-permute-done((f32[2,64]{1,0:T(2,128)S(1)}, f32[2,64]{1,0:T(2,128)S(1)}, u32[]{:S(2)}, u32[]{:S(2)}) %collective-permute-start.12) | collective-permute-done | bytes 544 | tf_op jit(solution)/shard_map/ppermute | solution.py:165
  34.5 0.6 %add_multiply_fusion = f32[2,64]{1,0:T(2,128)} fusion(f32[2,64]{1,0:T(2,128)S(1)} %collective-permute-done.12, f32[2,64]{1,0:T(2,128)S(1)} %collective-permute-done.13, f32[2,64]{1,0:T(2,128)S(1)} %totals.1, f32[2,64]{1,0:T(2,128)S(1)} %collective-permute-done.11), kind=kLoop, calls=%fused_computation | loop fusion | flops 512 | bytes 2560 | tf_op jit(solution)/shard_map/div | solution.py:310
  (27 shorter events, 0.1 us)
Async XLA Ops:
  0.6 0.9 %copy-start.3 = (bf16[256,2,128]{2,1,0:T(2,128)(2,1)S(1)}, bf16[256,2,128]{2,1,0:T(2,128)(2,1)}, u32[]{:S(2)}) copy-start(bf16[256,2,128]{2,1,0:T(2,128)(2,1)} %refs_1_.1) | copy-start | bytes 393220
  0.6 7.1 %copy-start = (s32[2,256,256]{2,1,0:T(8,128)S(1)}, s32[2,256,256]{2,1,0:T(8,128)}, u32[]{:S(2)}) copy-start(s32[2,256,256]{2,1,0:T(8,128)} %counts_ref.1) | copy-start | bytes 1572868
  0.7 0.9 %copy-start.5 = (s32[256,2]{0,1:T(2,128)S(1)}, s32[256,2]{0,1:T(2,128)}, u32[]{:S(2)}) copy-start(s32[256,2]{0,1:T(2,128)} %param.18) | copy-start | bytes 6148
  0.7 0.9 %copy-start.6 = (s32[256]{0:T(256)S(1)}, s32[256]{0:T(256)}, u32[]{:S(2)}) copy-start(s32[256]{0:T(256)} %param.21) | copy-start | bytes 3076
  0.7 0.9 %copy-start.7 = (f32[256]{0:T(256)S(1)}, f32[256]{0:T(256)}, u32[]{:S(2)}) copy-start(f32[256]{0:T(256)} %param.13) | copy-start | bytes 3076
  0.7 0.9 %copy-start.8 = (f32[256]{0:T(256)S(1)}, f32[256]{0:T(256)}, u32[]{:S(2)}) copy-start(f32[256]{0:T(256)} %param.16) | copy-start | bytes 3076
  0.7 0.9 %copy-start.9 = (f32[256]{0:T(256)S(1)}, f32[256]{0:T(256)}, u32[]{:S(2)}) copy-start(f32[256]{0:T(256)} %param.17) | copy-start | bytes 3076
  0.7 7.0 %copy-start.1 = (bf16[2,256,256]{2,1,0:T(8,128)(2,1)S(1)}, bf16[2,256,256]{2,1,0:T(8,128)(2,1)}, u32[]{:S(2)}) copy-start(bf16[2,256,256]{2,1,0:T(8,128)(2,1)} %shocks_ref) | copy-start | bytes 786436
  0.7 7.0 %copy-start.2 = (bf16[2,256,256]{2,1,0:T(8,128)(2,1)S(1)}, bf16[2,256,256]{2,1,0:T(8,128)(2,1)}, u32[]{:S(2)}) copy-start(bf16[2,256,256]{2,1,0:T(8,128)(2,1)} %noise_ref.1) | copy-start | bytes 786436
  0.7 7.0 %copy-start.4 = (bf16[256,256]{1,0:T(8,128)(2,1)S(1)}, bf16[256,256]{1,0:T(8,128)(2,1)}, u32[]{:S(2)}) copy-start(bf16[256,256]{1,0:T(8,128)(2,1)} %loadings_ref.1) | copy-start | bytes 393220
  2.0 10.1 %collective-permute-start.2 = (bf16[80,256]{1,0:T(8,128)(2,1)S(1)}, bf16[80,256]{1,0:T(8,128)(2,1)S(1)}, u32[]{:S(2)}, u32[]{:S(2)}) collective-permute-start(bf16[80,256]{1,0:T(8,128)(2,1)S(1)} %get-tuple-element.12.refs_1_), channel_id=1, source_target_pairs={{0,6},{1,7},{2,4},{3,5},{4,2},{5,3},{6,0},{7,1},{8,14},{9,15},{10,... | collective-permute-start | bytes 122888 | tf_op jit(solution)/shard_map/ppermute | solution.py:165
  7.1 6.6 %collective-permute-start.1 = (bf16[80,256]{1,0:T(8,128)(2,1)S(1)}, bf16[80,256]{1,0:T(8,128)(2,1)S(1)}, u32[]{:S(2)}, u32[]{:S(2)}) collective-permute-start(bf16[80,256]{1,0:T(8,128)(2,1)S(1)} %get-tuple-element.12.refs_1_), channel_id=1, source_target_pairs={{0,4},{1,5},{2,6},{3,7},{4,0},{5,1},{6,2},{7,3},{8,12},{9,13},{10,... | collective-permute-start | bytes 122888 | tf_op jit(solution)/shard_map/ppermute | solution.py:165
  7.1 6.6 %collective-permute-start = (bf16[80,256]{1,0:T(8,128)(2,1)S(1)}, bf16[80,256]{1,0:T(8,128)(2,1)S(1)}, u32[]{:S(2)}, u32[]{:S(2)}) collective-permute-start(bf16[80,256]{1,0:T(8,128)(2,1)S(1)} %get-tuple-element.12.refs_1_), channel_id=1, source_target_pairs={{0,2},{1,3},{2,0},{3,1},{4,6},{5,7},{6,4},{7,5},{8,10},{9,11},{10,... | collective-permute-start | bytes 122888 | tf_op jit(solution)/shard_map/ppermute | solution.py:165
  7.8 5.9 %copy-start.10 = (s32[16]{0:T(128)S(1)}, s32[16]{0:T(128)}, u32[]{:S(2)}) copy-start(s32[16]{0:T(128)} %refs_0_.1) | copy-start | bytes 196
  8.3 15.2 %collective-permute-start.7 = (bf16[512,256]{1,0:T(8,128)(2,1)S(1)}, bf16[512,256]{1,0:T(8,128)(2,1)S(1)}, u32[]{:S(2)}, u32[]{:S(2)}) collective-permute-start(bf16[512,256]{1,0:T(8,128)(2,1)S(1)} %price.1.refs_2_), channel_id=1, source_target_pairs={{0,6},{1,7},{2,4},{3,5},{4,2},{5,3},{6,0},{7,1},{8,14},{9,15},{10,... | collective-permute-start | bytes 786440 | tf_op jit(solution)/shard_map/ppermute | solution.py:165
  14.6 4.3 %collective-permute-start.4 = (bf16[128,256]{1,0:T(8,128)(2,1)S(1)}, bf16[128,256]{1,0:T(8,128)(2,1)S(1)}, u32[]{:S(2)}, u32[]{:S(2)}) collective-permute-start(bf16[128,256]{1,0:T(8,128)(2,1)S(1)} %get-tuple-element.15), channel_id=1, source_target_pairs={{0,16},{8,24},{16,0},{24,8},{1,17},{9,25},{17,1},{25,9},{2,18},{10... | collective-permute-start | bytes 196616 | tf_op jit(solution)/shard_map/ppermute | solution.py:165
  16.2 5.2 %collective-permute-start.5 = (bf16[128,256]{1,0:T(8,128)(2,1)S(1)}, bf16[128,256]{1,0:T(8,128)(2,1)S(1)}, u32[]{:S(2)}, u32[]{:S(2)}) collective-permute-start(bf16[128,256]{1,0:T(8,128)(2,1)S(1)} %get-tuple-element.14), channel_id=1, source_target_pairs={{0,17},{1,16},{2,19},{3,18},{4,21},{5,20},{6,23},{7,22},{8,25},{9,... | collective-permute-start | bytes 196616 | tf_op jit(solution)/shard_map/ppermute | solution.py:175
  17.6 4.3 %collective-permute-start.3 = (bf16[128,256]{1,0:T(8,128)(2,1)S(1)}, bf16[128,256]{1,0:T(8,128)(2,1)S(1)}, u32[]{:S(2)}, u32[]{:S(2)}) collective-permute-start(bf16[128,256]{1,0:T(8,128)(2,1)S(1)} %get-tuple-element.14), channel_id=1, source_target_pairs={{0,1},{1,0},{2,3},{3,2},{4,5},{5,4},{6,7},{7,6},{8,9},{9,8},{10,11... | collective-permute-start | bytes 196616 | tf_op jit(solution)/shard_map/ppermute | solution.py:175
  22.0 1.4 %collective-permute-start.6 = (bf16[256,256]{1,0:T(8,128)(2,1)S(1)}, bf16[256,256]{1,0:T(8,128)(2,1)S(1)}, u32[]{:S(2)}, u32[]{:S(2)}) collective-permute-start(bf16[256,256]{1,0:T(8,128)(2,1)S(1)} %merge.1.refs_0_), channel_id=1, source_target_pairs={{0,8},{8,0},{16,24},{24,16},{1,9},{9,1},{17,25},{25,17},{2,10},{10... | collective-permute-start | bytes 393224 | tf_op jit(solution)/shard_map/ppermute | solution.py:165
  23.8 5.9 %collective-permute-start.8 = (bf16[64,512]{1,0:T(8,128)(2,1)S(1)}, bf16[64,512]{1,0:T(8,128)(2,1)S(1)}, u32[]{:S(2)}, u32[]{:S(2)}) collective-permute-start(bf16[64,512]{1,0:T(8,128)(2,1)S(1)} %get-tuple-element.19), channel_id=1, source_target_pairs={{0,3},{1,2},{2,1},{3,0},{4,7},{5,6},{6,5},{7,4},{8,11},{9,10},{10,... | collective-permute-start | bytes 196616 | tf_op jit(solution)/shard_map/ppermute | solution.py:165
  24.7 5.2 %collective-permute-start.9 = (bf16[64,512]{1,0:T(8,128)(2,1)S(1)}, bf16[64,512]{1,0:T(8,128)(2,1)S(1)}, u32[]{:S(2)}, u32[]{:S(2)}) collective-permute-start(bf16[64,512]{1,0:T(8,128)(2,1)S(1)} %get-tuple-element.20), channel_id=1, source_target_pairs={{0,2},{1,3},{2,0},{3,1},{4,6},{5,7},{6,4},{7,5},{8,10},{9,11},{10,... | collective-permute-start | bytes 196616 | tf_op jit(solution)/shard_map/ppermute | solution.py:165
  26.3 4.3 %collective-permute-start.10 = (bf16[64,512]{1,0:T(8,128)(2,1)S(1)}, bf16[64,512]{1,0:T(8,128)(2,1)S(1)}, u32[]{:S(2)}, u32[]{:S(2)}) collective-permute-start(bf16[64,512]{1,0:T(8,128)(2,1)S(1)} %get-tuple-element.21), channel_id=1, source_target_pairs={{0,1},{1,0},{2,3},{3,2},{4,5},{5,4},{6,7},{7,6},{8,9},{9,8},{10,11... | collective-permute-start | bytes 196616 | tf_op jit(solution)/shard_map/ppermute | solution.py:165
  30.7 3.1 %collective-permute-start.13 = (f32[2,64]{1,0:T(2,128)S(1)}, f32[2,64]{1,0:T(2,128)S(1)}, u32[]{:S(2)}, u32[]{:S(2)}) collective-permute-start(f32[2,64]{1,0:T(2,128)S(1)} %totals.1), channel_id=1, source_target_pairs={{0,24},{8,16},{16,8},{24,0},{1,25},{9,17},{17,9},{25,1},{2,26},{10... | collective-permute-start | bytes 1544 | tf_op jit(solution)/shard_map/ppermute | solution.py:165
  31.0 3.6 %collective-permute-start.12 = (f32[2,64]{1,0:T(2,128)S(1)}, f32[2,64]{1,0:T(2,128)S(1)}, u32[]{:S(2)}, u32[]{:S(2)}) collective-permute-start(f32[2,64]{1,0:T(2,128)S(1)} %totals.1), channel_id=1, source_target_pairs={{0,16},{8,24},{16,0},{24,8},{1,17},{9,25},{17,1},{25,9},{2,18},{10... | collective-permute-start | bytes 1544 | tf_op jit(solution)/shard_map/ppermute | solution.py:165
  32.1 2.4 %collective-permute-start.11 = (f32[2,64]{1,0:T(2,128)S(1)}, f32[2,64]{1,0:T(2,128)S(1)}, u32[]{:S(2)}, u32[]{:S(2)}) collective-permute-start(f32[2,64]{1,0:T(2,128)S(1)} %totals.1), channel_id=1, source_target_pairs={{0,8},{8,0},{16,24},{24,16},{1,9},{9,1},{17,25},{25,17},{2,10},{10... | collective-permute-start | bytes 1544 | tf_op jit(solution)/shard_map/ppermute | solution.py:165

commit v18 on v16

--- a/solution.py
+++ b/solution.py
@@ -35,15 +35,18 @@
 
 
 def pack_kernel(part, *refs):
-    pick_ref, weights_ref, deps_ref, netting_ref = refs[:4]
-    factor_refs, packet_ref, factors_ref = refs[4:-2], refs[-2], refs[-1]
+    slot_ref, pick_ref, weights_ref, deps_ref, netting_ref = refs[:5]
+    factor_refs, packet_ref, factors_ref = refs[5:-2], refs[-2], refs[-1]
     for k in range(2):
         share = f32_dot(pick_ref[...], weights_ref[:, k, :], NT)
         packet_ref[k * part : (k + 1) * part, :] = share[:part].astype(jnp.bfloat16)
     netting = netting_ref[...]
+    slots = jnp.zeros_like(deps_ref[...])
+    for b in range(slot_ref.shape[0]):
+        slots = jnp.where(deps_ref[...] == b, slot_ref[b], slots)
     tags = jnp.concatenate(
         [
-            deps_ref[...],
+            slots,
             netting // SET_DEV,
             netting % SET_DEV,
             jnp.zeros((TAGS - 4, netting.shape[1]), jnp.int32),
@@ -76,18 +79,13 @@
 
 
 def combine_kernel(part, held, flips, *refs):
-    slot_ref, packet_refs = refs[0], refs[1:-5]
+    packet_refs = refs[:-5]
     own_ref, narrow_ref, other_ref, chosen_ref, marks_ref = refs[-5:]
     fac = lax.axis_index("fac")
     names = []
     for flip in (0, PRICE_FLIP, SIDE_FLIP, SIDE_FLIP ^ PRICE_FLIP):
         for h in range(held):
-            slot = (fac ^ flip) * held + h
-
-            def find(b, name):
-                return jnp.where(slot_ref[b] == slot, b, name)
-
-            names.append(lax.fori_loop(0, slot_ref.shape[0], find, 0, unroll=True).astype(jnp.float32))
+            names.append(((fac ^ flip) * held + h).astype(jnp.float32))
     trades = packet_refs[0].shape[1]
     place = lax.broadcasted_iota(jnp.int32, (SET_DEV, trades), 0).astype(jnp.float32)
     for source, packet_ref in enumerate(packet_refs):
@@ -212,11 +210,12 @@
             jax.ShapeDtypeStruct((2 * part + TAGS, trades), jnp.bfloat16),
             jax.ShapeDtypeStruct((3, width), jnp.float32),
         ],
-        in_specs=[VMEM] * 7,
+        in_specs=[SMEM] + [VMEM] * 7,
         out_specs=[VMEM] * 2,
         compiler_params=PARAMS,
         name="pack",
     )(
+        block_slot,
         pick,
         trade_weights,
         dependencies.T,
@@ -246,7 +245,7 @@
             jax.ShapeDtypeStruct(share_shape, jnp.bfloat16),
             jax.ShapeDtypeStruct(share_shape, jnp.bfloat16),
         ],
-        in_specs=[SMEM] + [VMEM] * len(packets),
+        in_specs=[VMEM] * len(packets),
         out_specs=[VMEM] * 3,
         scratch_shapes=[
             pltpu.VMEM((2 * share_shape[0], column_trades), jnp.bfloat16),
@@ -255,7 +254,7 @@
         compiler_params=PARAMS,
         cost_estimate=pl.CostEstimate(flops=10**9, bytes_accessed=0, transcendentals=0),
         name="combine",
-    )(block_slot, *packets)
+    )(*packets)
     pair_prices = [prices, from_partner(prices, "fac", PRICE_FLIP)]
     parts = []
     for i in range(0, scen_count, 2):

time: 33.6 us -> 34.1 us (1.015)
    pallas_call x1, Pallas kernels: 0.42 us -> 0.97 us  [body(): pl.pallas_call(functools.partial(pack_kernel, part), out_shape=[jax.Shape...]
    pallas_call x1, Pallas kernels: 0.9 us -> 0.36 us  [body(): pl.pallas_call(functools.partial(combine_kernel, part, held, owner_flips)...]
  transfers between devices with their start and end apart: 14 -> 14, of which waited for: 9 -> 9; matrix products, arithmetic and copies ran while one was open for 0% -> 0% of each run, Pallas kernels for 7% -> 5%
where the time goes in v18:
time: 34.1 us; the launch traced here: 34 us
  starting transfers between devices  18 us (53%)
  waiting for transfers between devices  10.6 us (31%)
  Pallas kernels  3.13 us (9%)
  local copies, waits for them, and re-layouts  0.82 us (2%)
  between operations  0.82 us (2%)
  other arithmetic  0.57 us (2%)
    ppermute x12, starting transfers between devices, from_partner(): return lax.ppermute(x, axis, [(i, i ^ flip) for i in range(count)])  16 us
    ppermute x12, waiting for transfers between devices, from_partner(): return lax.ppermute(x, axis, [(i, i ^ flip) for i in range(count)])  7.85 us
    ppermute x2, waiting for transfers between devices, from_both(): return lax.ppermute(x, ('scen', 'fac'), pairs)  2.79 us
    ppermute x2, starting transfers between devices, from_both(): return lax.ppermute(x, ('scen', 'fac'), pairs)  1.96 us
    pallas_call x1, Pallas kernels, body(): pl.pallas_call(functools.partial(pack_kernel, part), out_shape=[jax.Shape...  0.97 us
    unnamed x22, local copies, waits for them, and re-layouts  0.82 us
    pallas_call x1, Pallas kernels, body(): pl.pallas_call(functools.partial(expose_kernel, rows), out_shape=jax.Shap...  0.69 us
  transfers between devices with their start and end apart: 14, of which 9 were waited for; matrix products, arithmetic and copies ran while one was open for 0% of the time, Pallas kernels for 5%

profile of v18, /device:TPU:0, one launch (start us, length us, event | category | flops | bytes accessed | tf_op | source)
XLA Modules:
  0.0 34.0 jit_solution(13505758612487185208)
XLA Ops:
  0.8 0.0 copy-start.4
  0.8 0.8 %copy-done.3 = bf16[256,2,128]{2,1,0:T(2,128)(2,1)S(1)} copy-done((bf16[256,2,128]{2,1,0:T(2,128)(2,1)S(1)}, bf16[256,2,128]{2,1,0:T(2,128)(2,1)}, u32[]{:S(2)}) %copy-start.3) | copy-done | bytes 131096
  1.6 1.0 %pack.1 = (bf16[80,256]{1,0:T(8,128)(2,1)S(1)}, f32[3,256]{1,0:T(4,128)S(1)}) custom-call(s32[16]{0:T(128)S(1)} %copy-done.10, bf16[32,128]{1,0:T(8,128)(2,1)S(1)} %pick.1.refs_1_, bf16[256,2,128]{2,1,0:T(2,128)(2,1)S(1)} %copy-done.3, s32[2,256]{1,0:T(2,128)S(1)} %bitcast.5, s32[1,256]{1,0:T(1,128)S(1)} %bitcast.6, f32[1,256]{1,0:T(1,128)S(1)} %bitcast.7, ...), custom_call_target="tpu_custom_call" | custom-call | tf_op jit(solution)/shard_map/pack/pallas_call | solution.py:207
  2.5 4.1 %collective-permute-start.2 = (bf16[80,256]{1,0:T(8,128)(2,1)S(1)}, bf16[80,256]{1,0:T(8,128)(2,1)S(1)}, u32[]{:S(2)}, u32[]{:S(2)}) collective-permute-start(bf16[80,256]{1,0:T(8,128)(2,1)S(1)} %get-tuple-element.12.refs_0_), channel_id=1, source_target_pairs={{0,4},{1,5},{2,6},{3,7},{4,0},{5,1},{6,2},{7,3},{8,12},{9,13},{10,... | collective-permute-start | bytes 122888 | tf_op jit(solution)/shard_map/ppermute | solution.py:163
  6.6 1.3 %collective-permute-start.1 = (bf16[80,256]{1,0:T(8,128)(2,1)S(1)}, bf16[80,256]{1,0:T(8,128)(2,1)S(1)}, u32[]{:S(2)}, u32[]{:S(2)}) collective-permute-start(bf16[80,256]{1,0:T(8,128)(2,1)S(1)} %get-tuple-element.12.refs_0_), channel_id=1, source_target_pairs={{0,6},{1,7},{2,4},{3,5},{4,2},{5,3},{6,0},{7,1},{8,14},{9,15},{10,... | collective-permute-start | bytes 122888 | tf_op jit(solution)/shard_map/ppermute | solution.py:163
  8.0 0.2 collective-permute-start
  8.2 0.5 %price.1.refs_2_ = bf16[512,256]{1,0:T(8,128)(2,1)S(1)} custom-call(bf16[2,256,256]{2,1,0:T(8,128)(2,1)S(1)} %copy-done.1, bf16[256,256]{1,0:T(8,128)(2,1)S(1)} %copy-done.4, s32[2,256,256]{2,1,0:T(8,128)S(1)} %copy-done, bf16[2,256,256]{2,1,0:T(8,128)(2,1)S(1)} %copy-done.2, f32[3,256]{1,0:T(4,128)S(1)} %get-tuple-element.17.factors_ref), custom_call_target="tpu_custom_call" | custom-call | tf_op jit(solution)/shard_map/price/pallas_call | solution.py:231
  8.7 3.0 %collective-permute-start.7 = (bf16[512,256]{1,0:T(8,128)(2,1)S(1)}, bf16[512,256]{1,0:T(8,128)(2,1)S(1)}, u32[]{:S(2)}, u32[]{:S(2)}) collective-permute-start(bf16[512,256]{1,0:T(8,128)(2,1)S(1)} %price.1.refs_2_), channel_id=1, source_target_pairs={{0,6},{1,7},{2,4},{3,5},{4,2},{5,3},{6,0},{7,1},{8,14},{9,15},{10,... | collective-permute-start | bytes 786440 | tf_op jit(solution)/shard_map/ppermute | solution.py:163
  11.7 0.8 %collective-permute-done.1.refs_2_ = bf16[80,256]{1,0:T(8,128)(2,1)S(1)} collective-permute-done((bf16[80,256]{1,0:T(8,128)(2,1)S(1)}, bf16[80,256]{1,0:T(8,128)(2,1)S(1)}, u32[]{:S(2)}, u32[]{:S(2)}) %collective-permute-start.1) | collective-permute-done | bytes 40992 | tf_op jit(solution)/shard_map/ppermute | solution.py:163
  12.6 0.4 %combine.1 = (f32[128,256]{1,0:T(8,128)S(1)}, bf16[128,256]{1,0:T(8,128)(2,1)S(1)}, bf16[128,256]{1,0:T(8,128)(2,1)S(1)}) custom-call(bf16[80,256]{1,0:T(8,128)(2,1)S(1)} %get-tuple-element.12.refs_0_, bf16[80,256]{1,0:T(8,128)(2,1)S(1)} %collective-permute-done.refs_1_, bf16[80,256]{1,0:T(8,128)(2,1)S(1)} %collective-permute-done.1.refs_2_, ...), custom_call_target="tpu_custom_call" | custom-call | flops 1000000000 | tf_op jit(solution)/shard_map/combine/pallas_call | solution.py:241
  12.9 1.6 %collective-permute-start.4 = (bf16[128,256]{1,0:T(8,128)(2,1)S(1)}, bf16[128,256]{1,0:T(8,128)(2,1)S(1)}, u32[]{:S(2)}, u32[]{:S(2)}) collective-permute-start(bf16[128,256]{1,0:T(8,128)(2,1)S(1)} %get-tuple-element.15), channel_id=1, source_target_pairs={{0,16},{8,24},{16,0},{24,8},{1,17},{9,25},{17,1},{25,9},{2,18},{10... | collective-permute-start | bytes 196616 | tf_op jit(solution)/shard_map/ppermute | solution.py:163
  14.5 1.4 %collective-permute-start.5 = (bf16[128,256]{1,0:T(8,128)(2,1)S(1)}, bf16[128,256]{1,0:T(8,128)(2,1)S(1)}, u32[]{:S(2)}, u32[]{:S(2)}) collective-permute-start(bf16[128,256]{1,0:T(8,128)(2,1)S(1)} %get-tuple-element.14), channel_id=1, source_target_pairs={{0,17},{1,16},{2,19},{3,18},{4,21},{5,20},{6,23},{7,22},{8,25},{9,... | collective-permute-start | bytes 196616 | tf_op jit(solution)/shard_map/ppermute | solution.py:173
  16.0 0.5 %collective-permute-start.3 = (bf16[128,256]{1,0:T(8,128)(2,1)S(1)}, bf16[128,256]{1,0:T(8,128)(2,1)S(1)}, u32[]{:S(2)}, u32[]{:S(2)}) collective-permute-start(bf16[128,256]{1,0:T(8,128)(2,1)S(1)} %get-tuple-element.14), channel_id=1, source_target_pairs={{0,1},{1,0},{2,3},{3,2},{4,5},{5,4},{6,7},{7,6},{8,9},{9,8},{10,11... | collective-permute-start | bytes 196616 | tf_op jit(solution)/shard_map/ppermute | solution.py:173
  16.5 0.9 %collective-permute-done.4.refs_2_ = bf16[128,256]{1,0:T(8,128)(2,1)S(1)} collective-permute-done((bf16[128,256]{1,0:T(8,128)(2,1)S(1)}, bf16[128,256]{1,0:T(8,128)(2,1)S(1)}, u32[]{:S(2)}, u32[]{:S(2)}) %collective-permute-start.4) | collective-permute-done | bytes 65568 | tf_op jit(solution)/shard_map/ppermute | solution.py:163
  17.4 2.3 %collective-permute-done.5.refs_3_ = bf16[128,256]{1,0:T(8,128)(2,1)S(1)} collective-permute-done((bf16[128,256]{1,0:T(8,128)(2,1)S(1)}, bf16[128,256]{1,0:T(8,128)(2,1)S(1)}, u32[]{:S(2)}, u32[]{:S(2)}) %collective-permute-start.5) | collective-permute-done | bytes 65568 | tf_op jit(solution)/shard_map/ppermute | solution.py:173
  19.7 0.5 %collective-permute-done.3.refs_1_ = bf16[128,256]{1,0:T(8,128)(2,1)S(1)} collective-permute-done((bf16[128,256]{1,0:T(8,128)(2,1)S(1)}, bf16[128,256]{1,0:T(8,128)(2,1)S(1)}, u32[]{:S(2)}, u32[]{:S(2)}) %collective-permute-start.3) | collective-permute-done | bytes 65568 | tf_op jit(solution)/shard_map/ppermute | solution.py:173
  20.2 0.1 merge.1.refs_0_
  20.3 0.1 collective-permute-start.6
  20.4 1.3 %collective-permute-done.6.refs_1_ = bf16[256,256]{1,0:T(8,128)(2,1)S(1)} collective-permute-done((bf16[256,256]{1,0:T(8,128)(2,1)S(1)}, bf16[256,256]{1,0:T(8,128)(2,1)S(1)}, u32[]{:S(2)}, u32[]{:S(2)}) %collective-permute-start.6) | collective-permute-done | bytes 131104 | tf_op jit(solution)/shard_map/ppermute | solution.py:163
  21.7 0.4 %value.1 = (f32[64,512]{1,0:T(8,128)S(1)}, bf16[64,512]{1,0:T(8,128)(2,1)S(1)}, bf16[64,512]{1,0:T(8,128)(2,1)S(1)}, bf16[64,512]{1,0:T(8,128)(2,1)S(1)}) custom-call(bf16[256,256]{1,0:T(8,128)(2,1)S(1)} %merge.1.refs_0_, bf16[256,256]{1,0:T(8,128)(2,1)S(1)} %collective-permute-done.6.refs_1_, bf16[512,256]{1,0:T(8,128)(2,1)S(1)} %price.1.refs_2_, ...), custom_call_target="tpu_custom_call" | custom-call | tf_op jit(solution)/shard_map/value/pallas_call | solution.py:273
  22.2 3.1 %collective-permute-start.8 = (bf16[64,512]{1,0:T(8,128)(2,1)S(1)}, bf16[64,512]{1,0:T(8,128)(2,1)S(1)}, u32[]{:S(2)}, u32[]{:S(2)}) collective-permute-start(bf16[64,512]{1,0:T(8,128)(2,1)S(1)} %get-tuple-element.19), channel_id=1, source_target_pairs={{0,3},{1,2},{2,1},{3,0},{4,7},{5,6},{6,5},{7,4},{8,11},{9,10},{10,... | collective-permute-start | bytes 196616 | tf_op jit(solution)/shard_map/ppermute | solution.py:163
  25.3 0.6 %collective-permute-start.10 = (bf16[64,512]{1,0:T(8,128)(2,1)S(1)}, bf16[64,512]{1,0:T(8,128)(2,1)S(1)}, u32[]{:S(2)}, u32[]{:S(2)}) collective-permute-start(bf16[64,512]{1,0:T(8,128)(2,1)S(1)} %get-tuple-element.21), channel_id=1, source_target_pairs={{0,1},{1,0},{2,3},{3,2},{4,5},{5,4},{6,7},{7,6},{8,9},{9,8},{10,11... | collective-permute-start | bytes 196616 | tf_op jit(solution)/shard_map/ppermute | solution.py:163
  25.9 2.3 %collective-permute-done.8.refs_1_ = bf16[64,512]{1,0:T(8,128)(2,1)S(1)} collective-permute-done((bf16[64,512]{1,0:T(8,128)(2,1)S(1)}, bf16[64,512]{1,0:T(8,128)(2,1)S(1)}, u32[]{:S(2)}, u32[]{:S(2)}) %collective-permute-start.8) | collective-permute-done | bytes 65568 | tf_op jit(solution)/shard_map/ppermute | solution.py:163
  28.2 1.3 %collective-permute-done.9.refs_2_ = bf16[64,512]{1,0:T(8,128)(2,1)S(1)} collective-permute-done((bf16[64,512]{1,0:T(8,128)(2,1)S(1)}, bf16[64,512]{1,0:T(8,128)(2,1)S(1)}, u32[]{:S(2)}, u32[]{:S(2)}) %collective-permute-start.9) | collective-permute-done | bytes 65568 | tf_op jit(solution)/shard_map/ppermute | solution.py:163
  29.6 0.1 totals.1
  29.7 0.1 collective-permute-start.13
  29.8 1.6 %collective-permute-start.12 = (f32[2,64]{1,0:T(2,128)S(1)}, f32[2,64]{1,0:T(2,128)S(1)}, u32[]{:S(2)}, u32[]{:S(2)}) collective-permute-start(f32[2,64]{1,0:T(2,128)S(1)} %totals.1), channel_id=1, source_target_pairs={{0,16},{8,24},{16,0},{24,8},{1,17},{9,25},{17,1},{25,9},{2,18},{10... | collective-permute-start | bytes 1544 | tf_op jit(solution)/shard_map/ppermute | solution.py:163
  31.4 0.3 collective-permute-start.11
  31.6 0.7 %expose.1 = f32[2,64,256]{2,1,0:T(8,128)} custom-call(f32[64,512]{1,0:T(8,128)S(1)} %get-tuple-element.18.refs_0_, bf16[64,512]{1,0:T(8,128)(2,1)S(1)} %collective-permute-done.8.refs_1_, bf16[64,512]{1,0:T(8,128)(2,1)S(1)} %collective-permute-done.9.refs_2_, bf16[64,512]{1,0:T(8,128)(2,1)S(1)} %collective-permute-done.10.refs_3_), custom_call_target="tpu_custom_call" | custom-call | tf_op jit(solution)/shard_map/expose/pallas_call | solution.py:297
  32.3 0.4 %collective-permute-done.13 = f32[2,64]{1,0:T(2,128)S(1)} collective-permute-done((f32[2,64]{1,0:T(2,128)S(1)}, f32[2,64]{1,0:T(2,128)S(1)}, u32[]{:S(2)}, u32[]{:S(2)}) %collective-permute-start.13) | collective-permute-done | bytes 544 | tf_op jit(solution)/shard_map/ppermute | solution.py:163
  32.7 0.7 %collective-permute-done.12 = f32[2,64]{1,0:T(2,128)S(1)} collective-permute-done((f32[2,64]{1,0:T(2,128)S(1)}, f32[2,64]{1,0:T(2,128)S(1)}, u32[]{:S(2)}, u32[]{:S(2)}) %collective-permute-start.12) | collective-permute-done | bytes 544 | tf_op jit(solution)/shard_map/ppermute | solution.py:163
  33.4 0.6 %add_multiply_fusion = f32[2,64]{1,0:T(2,128)} fusion(f32[2,64]{1,0:T(2,128)S(1)} %collective-permute-done.12, f32[2,64]{1,0:T(2,128)S(1)} %collective-permute-done.13, f32[2,64]{1,0:T(2,128)S(1)} %totals.1, f32[2,64]{1,0:T(2,128)S(1)} %collective-permute-done.11), kind=kLoop, calls=%fused_computation | loop fusion | flops 512 | bytes 2560 | tf_op jit(solution)/shard_map/div | solution.py:310
  (27 shorter events, 0.1 us)
Async XLA Ops:
  0.6 0.9 %copy-start.3 = (bf16[256,2,128]{2,1,0:T(2,128)(2,1)S(1)}, bf16[256,2,128]{2,1,0:T(2,128)(2,1)}, u32[]{:S(2)}) copy-start(bf16[256,2,128]{2,1,0:T(2,128)(2,1)} %refs_2_.1) | copy-start | bytes 393220
  0.6 7.6 %copy-start = (s32[2,256,256]{2,1,0:T(8,128)S(1)}, s32[2,256,256]{2,1,0:T(8,128)}, u32[]{:S(2)}) copy-start(s32[2,256,256]{2,1,0:T(8,128)} %counts_ref.1) | copy-start | bytes 1572868
  0.7 0.9 %copy-start.5 = (s32[256,2]{0,1:T(2,128)S(1)}, s32[256,2]{0,1:T(2,128)}, u32[]{:S(2)}) copy-start(s32[256,2]{0,1:T(2,128)} %param.18) | copy-start | bytes 6148
  0.7 0.9 %copy-start.6 = (s32[256]{0:T(256)S(1)}, s32[256]{0:T(256)}, u32[]{:S(2)}) copy-start(s32[256]{0:T(256)} %param.21) | copy-start | bytes 3076
  0.7 0.9 %copy-start.7 = (f32[256]{0:T(256)S(1)}, f32[256]{0:T(256)}, u32[]{:S(2)}) copy-start(f32[256]{0:T(256)} %param.13) | copy-start | bytes 3076
  0.7 0.9 %copy-start.8 = (f32[256]{0:T(256)S(1)}, f32[256]{0:T(256)}, u32[]{:S(2)}) copy-start(f32[256]{0:T(256)} %param.16) | copy-start | bytes 3076
  0.7 0.9 %copy-start.9 = (f32[256]{0:T(256)S(1)}, f32[256]{0:T(256)}, u32[]{:S(2)}) copy-start(f32[256]{0:T(256)} %param.17) | copy-start | bytes 3076
  0.7 0.9 %copy-start.10 = (s32[16]{0:T(128)S(1)}, s32[16]{0:T(128)}, u32[]{:S(2)}) copy-start(s32[16]{0:T(128)} %refs_0_.1) | copy-start | bytes 196
  0.7 7.5 %copy-start.1 = (bf16[2,256,256]{2,1,0:T(8,128)(2,1)S(1)}, bf16[2,256,256]{2,1,0:T(8,128)(2,1)}, u32[]{:S(2)}) copy-start(bf16[2,256,256]{2,1,0:T(8,128)(2,1)} %shocks_ref) | copy-start | bytes 786436
  0.7 7.5 %copy-start.2 = (bf16[2,256,256]{2,1,0:T(8,128)(2,1)S(1)}, bf16[2,256,256]{2,1,0:T(8,128)(2,1)}, u32[]{:S(2)}) copy-start(bf16[2,256,256]{2,1,0:T(8,128)(2,1)} %noise_ref.1) | copy-start | bytes 786436
  0.8 7.5 %copy-start.4 = (bf16[256,256]{1,0:T(8,128)(2,1)S(1)}, bf16[256,256]{1,0:T(8,128)(2,1)}, u32[]{:S(2)}) copy-start(bf16[256,256]{1,0:T(8,128)(2,1)} %loadings_ref.1) | copy-start | bytes 393220
  2.5 9.2 %collective-permute-start.2 = (bf16[80,256]{1,0:T(8,128)(2,1)S(1)}, bf16[80,256]{1,0:T(8,128)(2,1)S(1)}, u32[]{:S(2)}, u32[]{:S(2)}) collective-permute-start(bf16[80,256]{1,0:T(8,128)(2,1)S(1)} %get-tuple-element.12.refs_0_), channel_id=1, source_target_pairs={{0,4},{1,5},{2,6},{3,7},{4,0},{5,1},{6,2},{7,3},{8,12},{9,13},{10,... | collective-permute-start | bytes 122888 | tf_op jit(solution)/shard_map/ppermute | solution.py:163
  6.6 5.9 %collective-permute-start.1 = (bf16[80,256]{1,0:T(8,128)(2,1)S(1)}, bf16[80,256]{1,0:T(8,128)(2,1)S(1)}, u32[]{:S(2)}, u32[]{:S(2)}) collective-permute-start(bf16[80,256]{1,0:T(8,128)(2,1)S(1)} %get-tuple-element.12.refs_0_), channel_id=1, source_target_pairs={{0,6},{1,7},{2,4},{3,5},{4,2},{5,3},{6,0},{7,1},{8,14},{9,15},{10,... | collective-permute-start | bytes 122888 | tf_op jit(solution)/shard_map/ppermute | solution.py:163
  8.0 4.6 %collective-permute-start = (bf16[80,256]{1,0:T(8,128)(2,1)S(1)}, bf16[80,256]{1,0:T(8,128)(2,1)S(1)}, u32[]{:S(2)}, u32[]{:S(2)}) collective-permute-start(bf16[80,256]{1,0:T(8,128)(2,1)S(1)} %get-tuple-element.12.refs_0_), channel_id=1, source_target_pairs={{0,2},{1,3},{2,0},{3,1},{4,6},{5,7},{6,4},{7,5},{8,10},{9,11},{10,... | collective-permute-start | bytes 122888 | tf_op jit(solution)/shard_map/ppermute | solution.py:163
  8.7 13.0 %collective-permute-start.7 = (bf16[512,256]{1,0:T(8,128)(2,1)S(1)}, bf16[512,256]{1,0:T(8,128)(2,1)S(1)}, u32[]{:S(2)}, u32[]{:S(2)}) collective-permute-start(bf16[512,256]{1,0:T(8,128)(2,1)S(1)} %price.1.refs_2_), channel_id=1, source_target_pairs={{0,6},{1,7},{2,4},{3,5},{4,2},{5,3},{6,0},{7,1},{8,14},{9,15},{10,... | collective-permute-start | bytes 786440 | tf_op jit(solution)/shard_map/ppermute | solution.py:163
  12.9 4.5 %collective-permute-start.4 = (bf16[128,256]{1,0:T(8,128)(2,1)S(1)}, bf16[128,256]{1,0:T(8,128)(2,1)S(1)}, u32[]{:S(2)}, u32[]{:S(2)}) collective-permute-start(bf16[128,256]{1,0:T(8,128)(2,1)S(1)} %get-tuple-element.15), channel_id=1, source_target_pairs={{0,16},{8,24},{16,0},{24,8},{1,17},{9,25},{17,1},{25,9},{2,18},{10... | collective-permute-start | bytes 196616 | tf_op jit(solution)/shard_map/ppermute | solution.py:163
  14.5 5.2 %collective-permute-start.5 = (bf16[128,256]{1,0:T(8,128)(2,1)S(1)}, bf16[128,256]{1,0:T(8,128)(2,1)S(1)}, u32[]{:S(2)}, u32[]{:S(2)}) collective-permute-start(bf16[128,256]{1,0:T(8,128)(2,1)S(1)} %get-tuple-element.14), channel_id=1, source_target_pairs={{0,17},{1,16},{2,19},{3,18},{4,21},{5,20},{6,23},{7,22},{8,25},{9,... | collective-permute-start | bytes 196616 | tf_op jit(solution)/shard_map/ppermute | solution.py:173
  16.0 4.3 %collective-permute-start.3 = (bf16[128,256]{1,0:T(8,128)(2,1)S(1)}, bf16[128,256]{1,0:T(8,128)(2,1)S(1)}, u32[]{:S(2)}, u32[]{:S(2)}) collective-permute-start(bf16[128,256]{1,0:T(8,128)(2,1)S(1)} %get-tuple-element.14), channel_id=1, source_target_pairs={{0,1},{1,0},{2,3},{3,2},{4,5},{5,4},{6,7},{7,6},{8,9},{9,8},{10,11... | collective-permute-start | bytes 196616 | tf_op jit(solution)/shard_map/ppermute | solution.py:173
  20.3 1.4 %collective-permute-start.6 = (bf16[256,256]{1,0:T(8,128)(2,1)S(1)}, bf16[256,256]{1,0:T(8,128)(2,1)S(1)}, u32[]{:S(2)}, u32[]{:S(2)}) collective-permute-start(bf16[256,256]{1,0:T(8,128)(2,1)S(1)} %merge.1.refs_0_), channel_id=1, source_target_pairs={{0,8},{8,0},{16,24},{24,16},{1,9},{9,1},{17,25},{25,17},{2,10},{10... | collective-permute-start | bytes 393224 | tf_op jit(solution)/shard_map/ppermute | solution.py:163
  22.2 6.1 %collective-permute-start.8 = (bf16[64,512]{1,0:T(8,128)(2,1)S(1)}, bf16[64,512]{1,0:T(8,128)(2,1)S(1)}, u32[]{:S(2)}, u32[]{:S(2)}) collective-permute-start(bf16[64,512]{1,0:T(8,128)(2,1)S(1)} %get-tuple-element.19), channel_id=1, source_target_pairs={{0,3},{1,2},{2,1},{3,0},{4,7},{5,6},{6,5},{7,4},{8,11},{9,10},{10,... | collective-permute-start | bytes 196616 | tf_op jit(solution)/shard_map/ppermute | solution.py:163
  25.3 4.3 %collective-permute-start.9 = (bf16[64,512]{1,0:T(8,128)(2,1)S(1)}, bf16[64,512]{1,0:T(8,128)(2,1)S(1)}, u32[]{:S(2)}, u32[]{:S(2)}) collective-permute-start(bf16[64,512]{1,0:T(8,128)(2,1)S(1)} %get-tuple-element.20), channel_id=1, source_target_pairs={{0,2},{1,3},{2,0},{3,1},{4,6},{5,7},{6,4},{7,5},{8,10},{9,11},{10,... | collective-permute-start | bytes 196616 | tf_op jit(solution)/shard_map/ppermute | solution.py:163
  25.3 4.3 %collective-permute-start.10 = (bf16[64,512]{1,0:T(8,128)(2,1)S(1)}, bf16[64,512]{1,0:T(8,128)(2,1)S(1)}, u32[]{:S(2)}, u32[]{:S(2)}) collective-permute-start(bf16[64,512]{1,0:T(8,128)(2,1)S(1)} %get-tuple-element.21), channel_id=1, source_target_pairs={{0,1},{1,0},{2,3},{3,2},{4,5},{5,4},{6,7},{7,6},{8,9},{9,8},{10,11... | collective-permute-start | bytes 196616 | tf_op jit(solution)/shard_map/ppermute | solution.py:163
  29.7 3.1 %collective-permute-start.13 = (f32[2,64]{1,0:T(2,128)S(1)}, f32[2,64]{1,0:T(2,128)S(1)}, u32[]{:S(2)}, u32[]{:S(2)}) collective-permute-start(f32[2,64]{1,0:T(2,128)S(1)} %totals.1), channel_id=1, source_target_pairs={{0,24},{8,16},{16,8},{24,0},{1,25},{9,17},{17,9},{25,1},{2,26},{10... | collective-permute-start | bytes 1544 | tf_op jit(solution)/shard_map/ppermute | solution.py:163
  29.8 3.6 %collective-permute-start.12 = (f32[2,64]{1,0:T(2,128)S(1)}, f32[2,64]{1,0:T(2,128)S(1)}, u32[]{:S(2)}, u32[]{:S(2)}) collective-permute-start(f32[2,64]{1,0:T(2,128)S(1)} %totals.1), channel_id=1, source_target_pairs={{0,16},{8,24},{16,0},{24,8},{1,17},{9,25},{17,1},{25,9},{2,18},{10... | collective-permute-start | bytes 1544 | tf_op jit(solution)/shard_map/ppermute | solution.py:163
  31.4 2.1 %collective-permute-start.11 = (f32[2,64]{1,0:T(2,128)S(1)}, f32[2,64]{1,0:T(2,128)S(1)}, u32[]{:S(2)}, u32[]{:S(2)}) collective-permute-start(f32[2,64]{1,0:T(2,128)S(1)} %totals.1), channel_id=1, source_target_pairs={{0,8},{8,0},{16,24},{24,16},{1,9},{9,1},{17,25},{25,17},{2,10},{10... | collective-permute-start | bytes 1544 | tf_op jit(solution)/shard_map/ppermute | solution.py:163
